TPU v7x, 32 devices: a whole 2x2x4 slice. The times are simulated.
32 devices in a mesh: groups: 2 (over x), shard: 16 (over z, y, core).
Axes of the slice: x: 2, y: 2, z: 4, core: 2. Of those that a mesh axis runs over, the one named last changes fastest.
Arguments:
- query_grads: bfloat16 [32, 16, 4096], P(('groups', 'shard')), parts along dimension 0, may hold values from -6 to 6
- cand_grads: bfloat16 [64, 16, 4096], P(('groups', 'shard')), parts along dimension 0, may hold values from -0.0234375 to 0.0234375
- basis_out: bfloat16 [16, 64, 64], P('shard'), may hold values from -0.75 to 0.75
- basis_in: bfloat16 [16, 64, 64], P('shard'), may hold values from -0.75 to 0.75
- eigvals: float32 [16, 4096], P('shard'), may hold values from 0.1 to 10
- layer_map: int32 [16], replicated, may hold values from 0 to 15, each once
- cand_rows: int32 [64], P('groups'), parts along dimension 0, may hold values from 0 to 31, each once
- cand_lists: int32 [32, 384], P(('groups', 'shard')), parts along dimension 0, may hold values from 0 to 31
- list_lengths: int32 [32], P(('groups', 'shard')), parts along dimension 0, may hold values from 1 to 384, 2048 in all
Outputs:
- preconditioned: bfloat16 [32, 16, 4096], P(('groups', 'shard')), parts along dimension 0
- scores: float32 [32, 384], P(('groups', 'shard')), parts along dimension 0
There are 2 independent parts, one for each index of `groups`. A program takes and returns all parts, laid end to end along the dimension named above; an argument that names none is the same for every part. Nothing has to cross between parts.
Inputs may be any that keep to these rules, and one draw needn't show every extreme that they name: Slot s of basis_out, basis_in and eigvals holds module layer_map[s]; slot s lies on index s // 1 of shard; each module once. cand_grads row cand_rows[c] holds candidate c, on index cand_rows[c] // 2 of shard; each row once. `cand_lists`: A candidate may be named several times in one list; entries at positions list_lengths[q] and beyond are padding. `list_lengths`: within each attribution job (each index of groups) the 16 lengths sum to 2048, a mean of 128; the whole array, holding all jobs, sums to that times the number of jobs.
All inputs are finite; a program needn't handle non-finite values.
Results may differ from a plain program's by a relative error of at most 0.013.
Values may be sent and summed in bfloat16 or wider, within the bound.
No kernel may reach another device: no remote copies, remote signals or barrier semaphores. Data moves between devices by JAX's collectives and lax.ppermute only.
A program may use at most 64 MiB of HBM per device.

v0:
```python
import jax
import jax.numpy as jnp
from jax import lax
from jax.sharding import PartitionSpec as P

damping = 0.1


def precondition(grads, out_basis, in_basis, eigen):
    rows_count, modules_here, flat_size = grads.shape
    side_out = out_basis.shape[1]
    side_in = in_basis.shape[1]
    matrices = grads.reshape(rows_count, modules_here, side_out, side_in)
    applied = jnp.einsum(
        "rmoi,mij->rmoj", matrices, in_basis, preferred_element_type=jnp.float32
    ).astype(jnp.bfloat16)
    rotated = jnp.einsum("mop,rmoj->rmpj", out_basis, applied, preferred_element_type=jnp.float32)
    scaled = (rotated / (eigen.reshape(modules_here, side_out, side_in)[None] + damping)).astype(
        jnp.bfloat16
    )
    returned = jnp.einsum(
        "rmpj,mij->rmpi", scaled, in_basis, preferred_element_type=jnp.float32
    ).astype(jnp.bfloat16)
    precond = jnp.einsum(
        "mop,rmpi->rmoi", out_basis, returned, preferred_element_type=jnp.float32
    ).astype(jnp.bfloat16)
    return precond.reshape(rows_count, modules_here, flat_size)


def body(
    query_grads,
    cand_grads,
    basis_out,
    basis_in,
    eigvals,
    layer_map,
    cand_rows,
    cand_lists,
    list_lengths,
):
    inverse = jnp.argsort(layer_map)
    query_slot = jnp.take(query_grads, layer_map, axis=1)
    cand_slot = jnp.take(cand_grads, layer_map, axis=1)
    query_here, cand_here = (
        lax.all_to_all(query_slot, "shard", split_axis=1, concat_axis=0, tiled=True),
        lax.all_to_all(cand_slot, "shard", split_axis=1, concat_axis=0, tiled=True),
    )
    precond_here = precondition(query_here, basis_out, basis_in, eigvals)
    precond_home = lax.all_to_all(precond_here, "shard", split_axis=0, concat_axis=1, tiled=True)
    preconditioned = jnp.take(precond_home, inverse, axis=1)
    summed = lax.psum_scatter(
        jnp.einsum("qmk,rmk->qr", precond_here, cand_here, preferred_element_type=jnp.float32),
        "shard",
        scatter_dimension=0,
        tiled=True,
    )
    positions = jnp.take(cand_rows, cand_lists)
    picked = jnp.take_along_axis(summed, positions, axis=1)
    in_list = jnp.arange(picked.shape[1], dtype=jnp.int32)[None, :] < list_lengths[:, None]
    scores = jnp.where(in_list, picked, jnp.zeros_like(picked))
    return (preconditioned, scores)


def solution(mesh):
    return jax.shard_map(
        body,
        mesh=mesh,
        in_specs=(
            P(("groups", "shard"), None, None),
            P(("groups", "shard"), None, None),
            P("shard", None, None),
            P("shard", None, None),
            P("shard", None),
            P(),
            P("groups"),
            P(("groups", "shard"), None),
            P(("groups", "shard")),
        ),
        out_specs=(P(("groups", "shard"), None, None), P(("groups", "shard"), None)),
        check_vma=False,
    )
```

profile of v0, /device:TPU:0, one launch (start us, length us, event | category | flops | bytes accessed | tf_op | source)
XLA Modules:
  0.0 119.0 jit_solution(9558312946934065267)
XLA Ops:
  0.7 0.7 compare_select_fusion.16
  1.4 1.7 %gather_fusion.1 = bf16[16,4096]{1,0:T(8,128)(2,1)S(1)} fusion(bf16[16,4096]{1,0:T(8,128)(2,1)} %bitcast.130, s32[1024]{0:T(1024)S(1)} %pad_clamp_fusion.1), kind=kCustom, calls=%fused_computation.clone | custom fusion | bytes 262208 | tf_op jit(solution)/shard_map/jit(_take)/gather | solution.py:42
  3.2 0.2 copy.41
  3.4 0.5 broadcast.564
  3.9 1.4 %reduce.110 = bf16[16,4096]{1,0:T(8,128)(2,1)S(1)} reduce(bf16[16,1,4096]{2,1,0:T(2,128)(2,1)S(1)} %bitcast.131, bf16[]{:T(256)} %broadcast.564), dimensions={1}, to_apply=%bitcast.127.reduce_sub_computation | reduce | bytes 262146
  5.3 0.7 reshape.557
  6.1 7.5 %all-to-all-start = ((bf16[16,2,2048]{2,1,0:T(2,128)(2,1)}), bf16[16,2,2048]{2,1,0:T(2,128)(2,1)S(1)}, u32[]{:S(2)}, u32[]{:S(2)}) async-start(bf16[16,2,2048]{2,1,0:T(2,128)(2,1)} %reshape.557), calls=%async_computation | async-start | bytes 262144 | tf_op jit(solution)/shard_map/all_to_all | solution.py:45
  13.6 1.3 %sort.17 = (s32[16]{0:T(128)}, s32[16]{0:T(128)S(1)}) sort(s32[16]{0:T(128)S(1)} %copy-done.6, s32[16]{0:T(128)S(1)} %iota.8), dimensions={0}, to_apply=%region_0.2 | sort | flops 64 | bytes 256 | tf_op jit(solution)/shard_map/jit(argsort)/sort | solution.py:41
  15.0 1.3 %gather_fusion = bf16[16,2,4096]{2,0,1:T(8,128)(2,1)S(1)} fusion(bf16[2,16,4096]{2,1,0:T(8,128)(2,1)S(1)} %copy-done, s32[1024]{0:T(1024)S(1)} %pad_clamp_fusion.1), kind=kCustom, calls=%fused_computation.2 | custom fusion | bytes 524352 | tf_op jit(solution)/shard_map/jit(_take)/gather | solution.py:43
  16.3 0.1 select_bitcast_fusion
  16.4 0.5 copy-done.1
  17.0 0.7 fusion.15
  17.7 0.7 copy-done.5
  18.4 4.3 %fusion.10 = (s32[384]{0:T(512)S(1)}, s32[1,384]{1,0:T(1,128)S(1)}) fusion(s32[]{:T(128)} %bitcast.38, s32[]{:T(128)} %bitcast.39, s32[]{:T(128)} %bitcast.40, s32[]{:T(128)} %bitcast.41, s32[]{:T(128)} %bitcast.42, s32[]{:T(128)} %bitcast.44, s32[]{:T(128)} %bitcast.43, s32[1,384]{1,0:T(1,128)S(1)} %copy-done.5), kind=kLoop, calls=%fused_computation.95 | loop fusion | flops 5760 | bytes 4636 | tf_op jit(solution)/shard_map/jit(_take)/gather | solution.py:57
  22.7 0.1 compare_reduce_fusion.49
  22.8 0.7 fusion.14
  23.6 1.0 copy.33
  24.5 15.7 %select_select_fusion.1 = s32[384]{0:T(512)S(1)} fusion(pred[384]{0:T(512)(128)(4,1)S(1)} %get-tuple-element.53, pred[384]{0:T(512)(128)(4,1)S(1)} %get-tuple-element.52, pred[384]{0:T(512)(128)(4,1)S(1)} %get-tuple-element.54, pred[384]{0:T(512)(128)(4,1)S(1)} %get-tuple-element.51, pred[384]{0:T(512)(128)(4,1)S(1)} %get-tuple-element.50, ...), kind=kLoop, calls=%fused_computation.92 | loop fusion | flops 9600 | bytes 12772 | tf_op jit(solution)/shard_map/jit(_take)/gather | solution.py:57
  40.2 6.0 %all-to-all-start.2 = ((bf16[2,16,4096]{2,0,1:T(2,128)(2,1)}), bf16[2,16,4096]{2,0,1:T(2,128)(2,1)S(1)}, u32[]{:S(2)}, u32[]{:S(2)}) async-start(bf16[2,16,4096]{2,0,1:T(2,128)(2,1)} %copy.33), calls=%async_computation.2 | async-start | bytes 524288 | tf_op jit(solution)/shard_map/all_to_all | solution.py:46
  47.1 0.6 copy-done.7
  47.8 0.6 dynamic-slice
  48.4 0.1 reshape.558
  48.5 0.7 bitcast_reduce_fusion
  49.2 0.2 reshape.139
  49.5 0.4 copy-done.2
  50.0 0.4 fusion.3
  50.4 0.5 fusion
  50.9 0.2 copy.30
  51.1 0.2 reshape.490
  51.2 0.3 reshape.144
  51.5 1.4 %reduce.111 = bf16[16,4096]{1,0:T(8,128)(2,1)S(1)} reduce(bf16[16,1,4096]{2,1,0:T(2,128)(2,1)S(1)} %reshape.490, bf16[]{:T(256)} %broadcast.564), dimensions={1}, to_apply=%reshape.490.reduce_sub_computation | reduce | bytes 262146 | tf_op jit(solution)/shard_map/reshape | solution.py:27
  52.9 0.7 reshape.559
  53.6 2.7 %all-to-all-done.2 = bf16[2,16,4096]{2,0,1:T(2,128)(2,1)S(1)} async-done(((bf16[2,16,4096]{2,0,1:T(2,128)(2,1)}), bf16[2,16,4096]{2,0,1:T(2,128)(2,1)S(1)}, u32[]{:S(2)}, u32[]{:S(2)}) %all-to-all-start.2) | async-done | bytes 262176 | tf_op jit(solution)/shard_map/all_to_all | solution.py:46
  56.3 3.5 %all-to-all-start.1 = ((bf16[16,2,2048]{2,1,0:T(2,128)(2,1)}), bf16[16,2,2048]{2,1,0:T(2,128)(2,1)S(1)}, u32[]{:S(2)}, u32[]{:S(2)}) async-start(bf16[16,2,2048]{2,1,0:T(2,128)(2,1)} %reshape.559), calls=%async_computation.1 | async-start | bytes 262144 | tf_op jit(solution)/shard_map/all_to_all | solution.py:49
  59.8 0.1 reshape.145
  59.9 0.2 fusion.16
  60.1 34.3 %all-reduce = f32[16,32]{1,0:T(8,128)S(1)} all-reduce(f32[16,32]{1,0:T(8,128)S(1)} %fusion.16), channel_id=2, replica_groups=mesh['groups'=2,'shard'=16] {'shard'}, use_global_device_ids=true, to_apply=%region_1.3.clone | all-reduce | flops 512 | bytes 4096
  94.5 0.6 constant_dynamic-slice_fusion
  95.1 0.7 fusion.13
  95.8 0.7 fusion.12
  96.6 0.1 reshape.560
  96.7 0.2 copy.40
  96.8 4.5 %fusion.11 = (f32[384]{0:T(512)S(1)}, s32[1,384]{1,0:T(1,128)S(1)}) fusion(f32[]{:T(128)} %bitcast.74, f32[]{:T(128)} %bitcast.75, f32[]{:T(128)} %bitcast.76, f32[]{:T(128)} %bitcast.77, f32[]{:T(128)} %bitcast.78, f32[]{:T(128)} %bitcast.80, f32[]{:T(128)} %bitcast.79, s32[384]{0:T(512)S(1)} %select_select_fusion.1, s32[1,384]{1,0:T(1,128)S(1)} %get-tuple-element.58), kind=kLoop, calls=%fused_computation.96 | loop fusion | flops 7296 | bytes 6172 | tf_op jit(solution)/shard_map/jit(take_along_axis)/gather | solution.py:58
  101.3 0.1 compare_reduce_fusion.24
  101.5 0.6 gather_fusion.2
  102.1 0.7 bitcast_select_fusion
  102.8 15.6 %select_select_fusion = f32[384]{0:T(512)S(1)} fusion(pred[384]{0:T(512)(128)(4,1)S(1)} %get-tuple-element.28, pred[384]{0:T(512)(128)(4,1)S(1)} %get-tuple-element.27, pred[384]{0:T(512)(128)(4,1)S(1)} %get-tuple-element.29, pred[384]{0:T(512)(128)(4,1)S(1)} %get-tuple-element.26, pred[384]{0:T(512)(128)(4,1)S(1)} %get-tuple-element.25, ...), kind=kLoop, calls=%fused_computation.91 | loop fusion | flops 9600 | bytes 12772 | tf_op jit(solution)/shard_map/jit(take_along_axis)/gather | solution.py:58
  118.4 0.6 compare_select_fusion.14
  (24 shorter events, 0.4 us)
Async XLA Ops:
  0.6 14.4 %copy-start = (bf16[2,16,4096]{2,1,0:T(8,128)(2,1)S(1)}, bf16[2,16,4096]{2,1,0:T(8,128)(2,1)}, u32[]{:S(2)}) copy-start(bf16[2,16,4096]{2,1,0:T(8,128)(2,1)} %param.12) | copy-start | bytes 786436
  0.6 0.7 copy-start.6
  6.0 8.9 %copy-start.4 = (f32[1,4096]{1,0:T(1,128)S(1)}, f32[1,4096]{1,0:T(1,128)}, u32[]{:S(2)}) copy-start(f32[1,4096]{1,0:T(1,128)} %param.15) | copy-start | bytes 49156
  6.1 34.2 %all-to-all-start = ((bf16[16,2,2048]{2,1,0:T(2,128)(2,1)}), bf16[16,2,2048]{2,1,0:T(2,128)(2,1)S(1)}, u32[]{:S(2)}, u32[]{:S(2)}) async-start(bf16[16,2,2048]{2,1,0:T(2,128)(2,1)} %reshape.557), calls=%async_computation | async-start | bytes 262144 | tf_op jit(solution)/shard_map/all_to_all | solution.py:45
  16.3 0.7 copy-start.1
  17.7 0.7 copy-start.5
  40.2 16.1 %all-to-all-start.2 = ((bf16[2,16,4096]{2,0,1:T(2,128)(2,1)}), bf16[2,16,4096]{2,0,1:T(2,128)(2,1)S(1)}, u32[]{:S(2)}, u32[]{:S(2)}) async-start(bf16[2,16,4096]{2,0,1:T(2,128)(2,1)} %copy.33), calls=%async_computation.2 | async-start | bytes 524288 | tf_op jit(solution)/shard_map/all_to_all | solution.py:46
  47.1 0.7 copy-start.7
  49.2 0.7 copy-start.2
  49.2 0.7 copy-start.3
  56.3 40.2 %all-to-all-start.1 = ((bf16[16,2,2048]{2,1,0:T(2,128)(2,1)}), bf16[16,2,2048]{2,1,0:T(2,128)(2,1)S(1)}, u32[]{:S(2)}, u32[]{:S(2)}) async-start(bf16[16,2,2048]{2,1,0:T(2,128)(2,1)} %reshape.559), calls=%async_computation.1 | async-start | bytes 262144 | tf_op jit(solution)/shard_map/all_to_all | solution.py:49
where the time goes:
time: 120 us; the launch traced here: 119 us
  other arithmetic  46.7 us (39%)
  blocking collectives  34.3 us (29%)
  starting transfers between devices  17 us (14%)
  local copies, waits for them, and re-layouts  15.5 us (13%)
  waiting for transfers between devices  2.7 us (2%)
  between operations  1.62 us (1%)
    unnamed x1, blocking collectives  34.3 us
    gather x3, other arithmetic, body(): picked = jnp.take_along_axis(summed, positions, axis=1)  20.2 us
    gather x3, other arithmetic, body(): positions = jnp.take(cand_rows, cand_lists)  20.1 us
    all_to_all x1, starting transfers between devices, body(): lax.all_to_all(query_slot, 'shard', split_axis=1, concat_axis=0, tiled=True)  7.52 us
    all_to_all x1, starting transfers between devices, body(): lax.all_to_all(cand_slot, 'shard', split_axis=1, concat_axis=0, tiled=True)  6.02 us
    unnamed x24, local copies, waits for them, and re-layouts  5.99 us
    all_to_all x1, starting transfers between devices, body(): lax.all_to_all(precond_here, 'shard', split_axis=0, concat_axis=1, tiled=...  3.51 us
    all_to_all x1, waiting for transfers between devices, body(): lax.all_to_all(cand_slot, 'shard', split_axis=1, concat_axis=0, tiled=True)  2.69 us
  transfers between devices with their start and end apart: 3, of which 1 were waited for; matrix products, arithmetic and copies ran while one was open for 28% of the time, Pallas kernels for 0%

commit v1 on v0

v1 whole, which is shorter than its diff:
```python
import functools

import jax
import jax.numpy as jnp
from jax import lax
from jax.experimental import pallas as pl
from jax.experimental.pallas import tpu as pltpu
from jax.sharding import PartitionSpec as P

damping = 0.1
LANES = 128
PIECES = 3
f32, bf16 = jnp.float32, jnp.bfloat16


def iota(shape, axis):
    return lax.broadcasted_iota(jnp.int32, shape, axis)


def dot(a, b, dims=((1,), (0,))):
    return lax.dot_general(a, b, (dims, ((), ())), preferred_element_type=f32)


def holds(layer_row, modules):
    slots = layer_row.shape[1]
    return (iota((modules, slots), 0) == layer_row).astype(f32).astype(bf16)


def pack(layer_ref, query_ref, cand_ref, out_ref, wide):
    modules, flat = query_ref.shape[1:]
    slots, height, _ = out_ref.shape
    tall = flat // LANES
    one_hot = holds(layer_ref[...], modules)
    sources = [query_ref[r] for r in range(query_ref.shape[0])]
    sources += [cand_ref[r] for r in range(cand_ref.shape[0])]
    for r, rows in enumerate(sources):
        by_slot = dot(one_hot, rows, ((0,), (0,)))
        for j in range(tall):
            wide[pl.ds(r * tall + j, slots, stride=height), :] = by_slot[:, j * LANES : (j + 1) * LANES]
    out_ref[...] = wide[...].reshape(out_ref.shape).astype(bf16)


def half(left, right):
    return jnp.where(iota(left.shape, 1) < LANES // 2, left, right)


def swap(block):
    return pltpu.roll(block, LANES // 2, 1)


def work(moved_ref, out_basis_ref, in_basis_ref, eigen_ref, out_ref, cands, homes):
    sources, height, _ = moved_ref.shape
    _, send, _ = out_ref.shape
    side = out_basis_ref.shape[0]
    tall = side // 2
    per = height // tall - 1
    count = sources * per
    out_basis = out_basis_ref[...]
    in_basis = in_basis_ref[...]

    order = (iota((side, side), 1) == 2 * (iota((side, side), 0) % tall) + iota((side, side), 0) // tall)
    order = order.astype(f32).astype(bf16)
    basis = dot(dot(order, out_basis).astype(bf16), order, ((1,), (1,))).astype(bf16)
    twice = (iota((LANES, side), 0) % side == iota((LANES, side), 1)).astype(f32).astype(bf16)
    spread = dot(dot(twice, in_basis).astype(bf16), twice, ((1,), (1,)))
    same = iota((LANES, LANES), 0) // side == iota((LANES, LANES), 1) // side
    inner = jnp.where(same, spread, 0.0).astype(bf16)
    eigen = eigen_ref[...]
    turned = swap(eigen)
    factor = 1.0 / (jnp.concatenate([half(eigen, turned), half(turned, eigen)], axis=0) + damping)

    pairs = []
    for p in range(sources // 2):
        a = moved_ref[2 * p, :tall, :].astype(f32)
        b = moved_ref[2 * p + 1, :tall, :].astype(f32)
        pairs.append(jnp.concatenate([half(a, swap(b)), half(swap(a), b)], axis=0).astype(bf16))

    def stack(wide):
        return jnp.concatenate([wide[:, p * LANES : (p + 1) * LANES] for p in range(len(pairs))], axis=0)

    def spread_out(rows):
        return jnp.concatenate([rows[p * side : (p + 1) * side] for p in range(len(pairs))], axis=1)

    applied = spread_out(dot(jnp.concatenate(pairs, axis=0), inner).astype(bf16))
    rotated = stack(dot(basis, applied, ((0,), (0,))))
    scaled = (rotated.reshape(len(pairs), side, LANES) * factor[None]).reshape(rotated.shape).astype(bf16)
    returned = spread_out(dot(scaled, inner, ((1,), (1,))).astype(bf16))
    precond = dot(basis, returned).astype(bf16).astype(f32)
    for p in range(len(pairs)):
        top = precond[:tall, p * LANES : (p + 1) * LANES]
        low = precond[tall:, p * LANES : (p + 1) * LANES]
        homes[pl.ds(2 * p * send, tall), :] = half(top, swap(low))
        homes[pl.ds((2 * p + 1) * send, tall), :] = half(swap(top), low)

    for d in range(sources):
        cands[pl.ds(d * per * tall, per * tall), :] = moved_ref[d, tall:, :].astype(f32)
    queries_flat = jnp.concatenate(
        [homes[pl.ds(j, sources, stride=send), :].astype(bf16) for j in range(tall)], axis=1
    )
    cands_flat = jnp.concatenate(
        [cands[pl.ds(j, count, stride=tall), :].astype(bf16) for j in range(tall)], axis=1
    )
    rest = dot(queries_flat, cands_flat, ((1,), (1,)))
    wide = -(-count // LANES)
    if wide * LANES > count:
        rest = jnp.concatenate([rest, jnp.zeros((sources, wide * LANES - count), f32)], axis=1)
    for k in range(PIECES):
        piece = rest.astype(bf16).astype(f32)
        rest = rest - piece
        for t in range(wide):
            homes[pl.ds(tall + k * wide + t, sources, stride=send), :] = piece[:, t * LANES : (t + 1) * LANES]
    for row in range(tall + PIECES * wide, send):
        homes[pl.ds(row, sources, stride=send), :] = jnp.zeros((sources, LANES), f32)
    out_ref[...] = homes[...].reshape(out_ref.shape).astype(bf16)


def upright(row):
    n = row.shape[1]
    return jnp.sum(jnp.where(iota((n, n), 0) == iota((n, n), 1), row, 0.0), axis=1, keepdims=True)


def finish(length_ref, layer_ref, rows_ref, lists_ref, home_ref, precond_ref, scores_ref, wide):
    slots, send, _ = home_ref.shape
    modules, flat = precond_ref.shape[1:]
    count = rows_ref.shape[1]
    tall = flat // LANES
    wide[...] = home_ref[...].reshape(wide.shape).astype(f32)
    by_slot = jnp.concatenate([wide[pl.ds(j, slots, stride=send), :].astype(bf16) for j in range(tall)], axis=1)
    precond_ref[0] = dot(holds(layer_ref[...], modules), by_slot).astype(bf16)
    groups = -(-count // LANES)
    parts = []
    for t in range(groups):
        pieces = [wide[pl.ds(tall + k * groups + t, slots, stride=send), :] for k in range(PIECES)]
        parts.append(jnp.sum((pieces[2] + pieces[1]) + pieces[0], axis=0, keepdims=True))
    dense = parts[0] if groups == 1 else jnp.concatenate(parts, axis=1)
    dense = dense[:, :count]
    by_cand = jnp.sum(
        jnp.where(iota((count, count), 0) == rows_ref[...], upright(dense), 0.0), axis=0, keepdims=True
    )
    lists = lists_ref[...]
    longest = lists.shape[1]
    picked = jnp.sum(
        jnp.where(iota((count, longest), 0) == lists, upright(by_cand), 0.0), axis=0, keepdims=True
    )
    scores_ref[...] = jnp.where(iota((1, longest), 1) < length_ref[0], picked, 0.0)


VMEM = pl.BlockSpec(memory_space=pltpu.VMEM)
SMEM = pl.BlockSpec(memory_space=pltpu.SMEM)
PARAMS = pltpu.CompilerParams(vmem_limit_bytes=40 * 1024 * 1024)


def body(
    query_grads,
    cand_grads,
    basis_out,
    basis_in,
    eigvals,
    layer_map,
    cand_rows,
    cand_lists,
    list_lengths,
):
    own, modules, flat = query_grads.shape
    per = cand_grads.shape[0]
    slots = layer_map.shape[0]
    tall = flat // LANES
    count = cand_rows.shape[0]
    layer_row = layer_map.reshape(1, slots)
    height = (own + per) * tall
    send = tall + -(-PIECES * -(-count // LANES) // 16) * 16

    packed = pl.pallas_call(
        pack,
        out_shape=jax.ShapeDtypeStruct((slots, height, LANES), bf16),
        in_specs=[VMEM] * 3,
        out_specs=VMEM,
        scratch_shapes=[pltpu.VMEM((slots * height, LANES), f32)],
        compiler_params=PARAMS,
        name="pack",
    )(layer_row, query_grads, cand_grads)
    moved = lax.all_to_all(packed, "shard", split_axis=0, concat_axis=0, tiled=True)
    sources = moved.shape[0]
    homes = pl.pallas_call(
        work,
        out_shape=jax.ShapeDtypeStruct((sources, send, LANES), bf16),
        in_specs=[VMEM] * 4,
        out_specs=VMEM,
        scratch_shapes=[pltpu.VMEM((sources * per * tall, LANES), f32), pltpu.VMEM((sources * send, LANES), f32)],
        compiler_params=PARAMS,
        name="work",
    )(
        moved,
        basis_out.reshape(basis_out.shape[1:]),
        basis_in.reshape(basis_in.shape[1:]),
        eigvals.reshape(tall, LANES),
    )
    home = lax.all_to_all(homes, "shard", split_axis=0, concat_axis=0, tiled=True)
    return pl.pallas_call(
        finish,
        out_shape=(
            jax.ShapeDtypeStruct(query_grads.shape, bf16),
            jax.ShapeDtypeStruct(cand_lists.shape, f32),
        ),
        in_specs=[SMEM] + [VMEM] * 4,
        out_specs=(VMEM, VMEM),
        scratch_shapes=[pltpu.VMEM((slots * send, LANES), f32)],
        compiler_params=PARAMS,
        name="finish",
    )(list_lengths, layer_row, cand_rows.reshape(1, count), cand_lists, home)


def solution(mesh):
    return jax.shard_map(
        body,
        mesh=mesh,
        in_specs=(
            P(("groups", "shard"), None, None),
            P(("groups", "shard"), None, None),
            P("shard", None, None),
            P("shard", None, None),
            P("shard", None),
            P(),
            P("groups"),
            P(("groups", "shard"), None),
            P(("groups", "shard")),
        ),
        out_specs=(P(("groups", "shard"), None, None), P(("groups", "shard"), None)),
        check_vma=False,
    )
```

time: 120 us -> 39.3 us (0.33)
  other arithmetic: 46.7 us -> 0 us
  blocking collectives: 34.3 us -> 19.5 us
  starting transfers between devices: 17 us -> 3.53 us
  local copies, waits for them, and re-layouts: 15.5 us -> 2.53 us
  waiting for transfers between devices: 2.7 us -> 8.3 us
  Pallas kernels: 0 us -> 3.67 us
    gather x8 -> x0, other arithmetic: 40.4 us -> none  [the longest x3 20.2 us: body(): picked = jnp.take_along_axis(summed, positions, axis=1)]
    unnamed x1 -> x0, blocking collectives: 34.3 us -> none
    all_to_all x0 -> x1, blocking collectives: none -> 19.5 us  [body(): lax.all_to_all(packed, 'shard', split_axis=0, concat_axis=0, tiled=True)]
    all_to_all x3 -> x1, starting transfers between devices: 17 us -> 3.53 us  [body(): lax.all_to_all(homes, 'shard', split_axis=0, concat_axis=0, tiled=True)]
    gather x7 -> x0, local copies, waits for them, and re-layouts: 6.49 us -> none  [the longest x1 1.67 us: body(): query_slot = jnp.take(query_grads, layer_map, axis=1)]
    all_to_all x3 -> x1, waiting for transfers between devices: 2.7 us -> 8.3 us  [body(): lax.all_to_all(homes, 'shard', split_axis=0, concat_axis=0, tiled=True)]
    pallas_call x0 -> x3, Pallas kernels: none -> 3.67 us  [the longest x1 2.11 us: body(): pl.pallas_call(work, out_shape=jax.ShapeDtypeStruct((sources, send, LANES...]
    unnamed x24 -> x16, local copies, waits for them, and re-layouts: 5.99 us -> 2.53 us
  transfers between devices with their start and end apart: 3 -> 1, of which waited for: 1 -> 1; matrix products, arithmetic and copies ran while one was open for 28% -> 0% of each run, Pallas kernels for 0% -> 0%
where the time goes in v1:
time: 39.3 us; the launch traced here: 38.9 us
  blocking collectives  19.5 us (50%)
  waiting for transfers between devices  8.3 us (21%)
  Pallas kernels  3.67 us (9%)
  starting transfers between devices  3.53 us (9%)
  local copies, waits for them, and re-layouts  2.53 us (6%)
  between operations  1.36 us (3%)
    all_to_all x1, blocking collectives, body(): lax.all_to_all(packed, 'shard', split_axis=0, concat_axis=0, tiled=True)  19.5 us
    all_to_all x1, waiting for transfers between devices, body(): lax.all_to_all(homes, 'shard', split_axis=0, concat_axis=0, tiled=True)  8.3 us
    all_to_all x1, starting transfers between devices, body(): lax.all_to_all(homes, 'shard', split_axis=0, concat_axis=0, tiled=True)  3.53 us
    unnamed x16, local copies, waits for them, and re-layouts  2.53 us
    pallas_call x1, Pallas kernels, body(): pl.pallas_call(work, out_shape=jax.ShapeDtypeStruct((sources, send, LANES...  2.11 us
    pallas_call x1, Pallas kernels, body(): pl.pallas_call(finish, out_shape=(jax.ShapeDtypeStruct(query_grads.shape,...  0.88 us
  transfers between devices with their start and end apart: 1, of which 1 were waited for; matrix products, arithmetic and copies ran while one was open for 0% of the time, Pallas kernels for 0%

profile of v1, /device:TPU:0, one launch (start us, length us, event | category | flops | bytes accessed | tf_op | source)
XLA Modules:
  0.0 38.9 jit_solution(14950982184247961852)
XLA Ops:
  0.6 0.0 copy-start.5
  0.6 0.6 %copy-done.5 = s32[16]{0:T(128)S(1)} copy-done((s32[16]{0:T(128)S(1)}, s32[16]{0:T(128)}, u32[]{:S(2)}) %copy-start.5) | copy-done | bytes 88
  1.3 0.0 copy-start
  1.3 0.9 %copy-done = bf16[2,16,4096]{2,1,0:T(8,128)(2,1)S(1)} copy-done((bf16[2,16,4096]{2,1,0:T(8,128)(2,1)S(1)}, bf16[2,16,4096]{2,1,0:T(8,128)(2,1)}, u32[]{:S(2)}) %copy-start) | copy-done | bytes 262168
  2.2 0.0 copy-start.1
  2.2 0.9 %copy-done.1 = bf16[1,16,4096]{2,1,0:T(8,128)(2,1)S(1)} copy-done((bf16[1,16,4096]{2,1,0:T(8,128)(2,1)S(1)}, bf16[1,16,4096]{2,1,0:T(8,128)(2,1)}, u32[]{:S(2)}) %copy-start.1) | copy-done | bytes 131096
  3.1 0.7 %pack.1 = bf16[16,96,128]{2,1,0:T(8,128)(2,1)S(1)} custom-call(s32[1,16]{1,0:T(1,128)S(1)} %bitcast.8, bf16[1,16,4096]{2,1,0:T(8,128)(2,1)S(1)} %copy-done.1, bf16[2,16,4096]{2,1,0:T(8,128)(2,1)S(1)} %copy-done), custom_call_target="tpu_custom_call" | custom-call | tf_op jit(solution)/shard_map/pack/pallas_call | solution.py:173
  3.8 0.0 copy-start.2
  3.8 0.0 copy-start.3
  3.9 0.0 copy-start.4
  3.9 19.5 %all_to_all.10.moved_ref = bf16[16,96,128]{2,1,0:T(8,128)(2,1)S(1)} all-to-all(bf16[16,96,128]{2,1,0:T(8,128)(2,1)S(1)} %pack.1), channel_id=1, replica_groups=mesh['groups'=2,'shard'=16] {'shard'}, dimensions={0} | all-to-all | bytes 786432 | tf_op jit(solution)/shard_map/all_to_all | solution.py:182
  23.4 0.0 copy-done.2
  23.4 0.0 copy-done.3
  23.4 0.0 copy-done.4
  23.4 2.1 %work.1 = bf16[16,48,128]{2,1,0:T(8,128)(2,1)} custom-call(bf16[16,96,128]{2,1,0:T(8,128)(2,1)S(1)} %all_to_all.10.moved_ref, bf16[64,64]{1,0:T(8,128)(2,1)S(1)} %bitcast.5, bf16[64,64]{1,0:T(8,128)(2,1)S(1)} %bitcast.6, f32[32,128]{1,0:T(8,128)S(1)} %bitcast.7), custom_call_target="tpu_custom_call" | custom-call | tf_op jit(solution)/shard_map/work/pallas_call | solution.py:184
  25.5 3.5 %all-to-all-start.1 = ((bf16[16,48,128]{2,1,0:T(8,128)(2,1)}), bf16[16,48,128]{2,1,0:T(8,128)(2,1)S(1)}, u32[]{:S(2)}, u32[]{:S(2)}) async-start(bf16[16,48,128]{2,1,0:T(8,128)(2,1)} %work.1), calls=%async_computation.1 | async-start | bytes 393216 | tf_op jit(solution)/shard_map/all_to_all | solution.py:198
  29.0 0.0 copy-start.6
  29.7 0.0 copy-start.7
  29.7 8.3 %all-to-all-done.1.home_ref = bf16[16,48,128]{2,1,0:T(8,128)(2,1)S(1)} async-done(((bf16[16,48,128]{2,1,0:T(8,128)(2,1)}), bf16[16,48,128]{2,1,0:T(8,128)(2,1)S(1)}, u32[]{:S(2)}, u32[]{:S(2)}) %all-to-all-start.1) | async-done | bytes 196640 | tf_op jit(solution)/shard_map/all_to_all | solution.py:198
  38.0 0.0 copy-done.6
  38.0 0.0 copy-done.7
  38.0 0.9 %finish.1 = (bf16[1,16,4096]{2,1,0:T(8,128)(2,1)}, f32[1,384]{1,0:T(1,128)}) custom-call(s32[1]{0:T(128)S(6)} %copy.11.length_ref, s32[1,16]{1,0:T(1,128)S(1)} %bitcast.9, s32[1,32]{1,0:T(1,128)S(1)} %bitcast.10, s32[1,384]{1,0:T(1,128)S(1)} %copy-done.6, bf16[16,48,128]{2,1,0:T(8,128)(2,1)S(1)} %all-to-all-done.1.home_ref), custom_call_target="tpu_custom_call" | custom-call | tf_op jit(solution)/shard_map/finish/pallas_call | solution.py:199
Async XLA Ops:
  0.6 0.7 %copy-start.5 = (s32[16]{0:T(128)S(1)}, s32[16]{0:T(128)}, u32[]{:S(2)}) copy-start(s32[16]{0:T(128)} %param.14) | copy-start | bytes 196
  1.3 0.9 %copy-start = (bf16[2,16,4096]{2,1,0:T(8,128)(2,1)S(1)}, bf16[2,16,4096]{2,1,0:T(8,128)(2,1)}, u32[]{:S(2)}) copy-start(bf16[2,16,4096]{2,1,0:T(8,128)(2,1)} %cand_ref.1) | copy-start | bytes 786436
  2.2 0.9 %copy-start.1 = (bf16[1,16,4096]{2,1,0:T(8,128)(2,1)S(1)}, bf16[1,16,4096]{2,1,0:T(8,128)(2,1)}, u32[]{:S(2)}) copy-start(bf16[1,16,4096]{2,1,0:T(8,128)(2,1)} %query_ref.1) | copy-start | bytes 393220
  3.8 19.6 %copy-start.2 = (bf16[1,64,64]{2,1,0:T(8,128)(2,1)S(1)}, bf16[1,64,64]{2,1,0:T(8,128)(2,1)}, u32[]{:S(2)}) copy-start(bf16[1,64,64]{2,1,0:T(8,128)(2,1)} %param.11) | copy-start | bytes 24580
  3.8 19.5 %copy-start.3 = (bf16[1,64,64]{2,1,0:T(8,128)(2,1)S(1)}, bf16[1,64,64]{2,1,0:T(8,128)(2,1)}, u32[]{:S(2)}) copy-start(bf16[1,64,64]{2,1,0:T(8,128)(2,1)} %param.12) | copy-start | bytes 24580
  3.9 19.5 %copy-start.4 = (f32[1,4096]{1,0:T(1,128)S(1)}, f32[1,4096]{1,0:T(1,128)}, u32[]{:S(2)}) copy-start(f32[1,4096]{1,0:T(1,128)} %param.13) | copy-start | bytes 49156
  25.5 12.5 %all-to-all-start.1 = ((bf16[16,48,128]{2,1,0:T(8,128)(2,1)}), bf16[16,48,128]{2,1,0:T(8,128)(2,1)S(1)}, u32[]{:S(2)}, u32[]{:S(2)}) async-start(bf16[16,48,128]{2,1,0:T(8,128)(2,1)} %work.1), calls=%async_computation.1 | async-start | bytes 393216 | tf_op jit(solution)/shard_map/all_to_all | solution.py:198
  29.0 9.0 %copy-start.6 = (s32[1,384]{1,0:T(1,128)S(1)}, s32[1,384]{1,0:T(1,128)}, u32[]{:S(2)}) copy-start(s32[1,384]{1,0:T(1,128)} %lists_ref.1) | copy-start | bytes 4612
  29.7 8.3 %copy-start.7 = (s32[32]{0:T(128)S(1)}, s32[32]{0:T(128)}, u32[]{:S(2)}) copy-start(s32[32]{0:T(128)} %param.15) | copy-start | bytes 388

commit v2 on v1

--- a/solution.py
+++ b/solution.py
@@ -26,7 +26,17 @@
     return (iota((modules, slots), 0) == layer_row).astype(f32).astype(bf16)
 
 
-def pack(layer_ref, query_ref, cand_ref, out_ref, wide):
+def pack(layer_hbm, query_hbm, cand_hbm, out_ref, layer_ref, query_ref, cand_ref, wide, sems):
+    arrivals = [
+        pltpu.make_async_copy(source, target, sems.at[i])
+        for i, (source, target) in enumerate(
+            ((layer_hbm, layer_ref), (query_hbm, query_ref), (cand_hbm, cand_ref))
+        )
+    ]
+    for arrival in arrivals:
+        arrival.start()
+    for arrival in arrivals:
+        arrival.wait()
     modules, flat = query_ref.shape[1:]
     slots, height, _ = out_ref.shape
     tall = flat // LANES
@@ -146,8 +156,10 @@
 
 
 VMEM = pl.BlockSpec(memory_space=pltpu.VMEM)
+HBM = pl.BlockSpec(memory_space=pltpu.HBM)
 SMEM = pl.BlockSpec(memory_space=pltpu.SMEM)
 PARAMS = pltpu.CompilerParams(vmem_limit_bytes=40 * 1024 * 1024)
+FULL = pltpu.CompilerParams(vmem_limit_bytes=56 * 1024 * 1024)
 
 
 def body(
@@ -173,10 +185,16 @@
     packed = pl.pallas_call(
         pack,
         out_shape=jax.ShapeDtypeStruct((slots, height, LANES), bf16),
-        in_specs=[VMEM] * 3,
+        in_specs=[HBM] * 3,
         out_specs=VMEM,
-        scratch_shapes=[pltpu.VMEM((slots * height, LANES), f32)],
-        compiler_params=PARAMS,
+        scratch_shapes=[
+            pltpu.VMEM(layer_row.shape, jnp.int32),
+            pltpu.VMEM(query_grads.shape, bf16),
+            pltpu.VMEM(cand_grads.shape, bf16),
+            pltpu.VMEM((slots * height, LANES), f32),
+            pltpu.SemaphoreType.DMA((3,)),
+        ],
+        compiler_params=FULL,
         name="pack",
     )(layer_row, query_grads, cand_grads)
     moved = lax.all_to_all(packed, "shard", split_axis=0, concat_axis=0, tiled=True)

time: 39.3 us -> 38.8 us (0.987)
  local copies, waits for them, and re-layouts: 2.53 us -> 0.04 us
  Pallas kernels: 3.67 us -> 5.48 us
    unnamed x16 -> x12, local copies, waits for them, and re-layouts: 2.53 us -> 0.04 us
    pallas_call x1, Pallas kernels: 0.68 us -> 2.5 us  [body(): pl.pallas_call(pack, out_shape=jax.ShapeDtypeStruct((slots, height, LANES...]
where the time goes in v2:
time: 38.8 us; the launch traced here: 38.4 us
  blocking collectives  19.7 us (51%)
  waiting for transfers between devices  8.29 us (21%)
  Pallas kernels  5.48 us (14%)
  starting transfers between devices  3.53 us (9%)
  between operations  1.36 us (4%)
    all_to_all x1, blocking collectives, body(): lax.all_to_all(packed, 'shard', split_axis=0, concat_axis=0, tiled=True)  19.7 us
    all_to_all x1, waiting for transfers between devices, body(): lax.all_to_all(homes, 'shard', split_axis=0, concat_axis=0, tiled=True)  8.29 us
    all_to_all x1, starting transfers between devices, body(): lax.all_to_all(homes, 'shard', split_axis=0, concat_axis=0, tiled=True)  3.53 us
    pallas_call x1, Pallas kernels, body(): pl.pallas_call(pack, out_shape=jax.ShapeDtypeStruct((slots, height, LANES...  2.5 us
    pallas_call x1, Pallas kernels, body(): pl.pallas_call(work, out_shape=jax.ShapeDtypeStruct((sources, send, LANES...  2.11 us
    pallas_call x1, Pallas kernels, body(): pl.pallas_call(finish, out_shape=(jax.ShapeDtypeStruct(query_grads.shape,...  0.88 us
  transfers between devices with their start and end apart: 1, of which 1 were waited for; matrix products, arithmetic and copies ran while one was open for 0% of the time, Pallas kernels for 0%

profile of v2, /device:TPU:0, one launch (start us, length us, event | category | flops | bytes accessed | tf_op | source)
XLA Modules:
  0.0 38.4 jit_solution(3771670769930779165)
XLA Ops:
  0.6 2.5 %pack.1 = bf16[16,96,128]{2,1,0:T(8,128)(2,1)} custom-call(s32[1,16]{1,0:T(1,128)} %bitcast.8, bf16[1,16,4096]{2,1,0:T(8,128)(2,1)} %query_hbm.1, bf16[2,16,4096]{2,1,0:T(8,128)(2,1)} %cand_hbm.1), custom_call_target="tpu_custom_call" | custom-call | tf_op jit(solution)/shard_map/pack/pallas_call | solution.py:185
  3.1 0.0 copy-start
  3.1 0.0 copy-start.1
  3.2 0.0 copy-start.2
  3.2 19.7 %all_to_all.10.moved_ref = bf16[16,96,128]{2,1,0:T(8,128)(2,1)S(1)} all-to-all(bf16[16,96,128]{2,1,0:T(8,128)(2,1)} %pack.1), channel_id=1, replica_groups=mesh['groups'=2,'shard'=16] {'shard'}, dimensions={0} | all-to-all | bytes 786432 | tf_op jit(solution)/shard_map/all_to_all | solution.py:200
  22.9 0.0 copy-done
  22.9 0.0 copy-done.1
  22.9 0.0 copy-done.2
  22.9 2.1 %work.1 = bf16[16,48,128]{2,1,0:T(8,128)(2,1)} custom-call(bf16[16,96,128]{2,1,0:T(8,128)(2,1)S(1)} %all_to_all.10.moved_ref, bf16[64,64]{1,0:T(8,128)(2,1)S(1)} %bitcast.5, bf16[64,64]{1,0:T(8,128)(2,1)S(1)} %bitcast.6, f32[32,128]{1,0:T(8,128)S(1)} %bitcast.7), custom_call_target="tpu_custom_call" | custom-call | tf_op jit(solution)/shard_map/work/pallas_call | solution.py:202
  25.0 3.5 %all-to-all-start.1 = ((bf16[16,48,128]{2,1,0:T(8,128)(2,1)}), bf16[16,48,128]{2,1,0:T(8,128)(2,1)S(1)}, u32[]{:S(2)}, u32[]{:S(2)}) async-start(bf16[16,48,128]{2,1,0:T(8,128)(2,1)} %work.1), calls=%async_computation.1 | async-start | bytes 393216 | tf_op jit(solution)/shard_map/all_to_all | solution.py:216
  28.5 0.0 copy-start.4
  29.2 0.0 copy-start.3
  29.2 0.0 copy-start.5
  29.2 8.3 %all-to-all-done.1.home_ref = bf16[16,48,128]{2,1,0:T(8,128)(2,1)S(1)} async-done(((bf16[16,48,128]{2,1,0:T(8,128)(2,1)}), bf16[16,48,128]{2,1,0:T(8,128)(2,1)S(1)}, u32[]{:S(2)}, u32[]{:S(2)}) %all-to-all-start.1) | async-done | bytes 196640 | tf_op jit(solution)/shard_map/all_to_all | solution.py:216
  37.5 0.0 copy-done.4
  37.5 0.0 copy-done.3
  37.5 0.0 copy-done.5
  37.5 0.9 %finish.1 = (bf16[1,16,4096]{2,1,0:T(8,128)(2,1)}, f32[1,384]{1,0:T(1,128)}) custom-call(s32[1]{0:T(128)S(6)} %copy.11.length_ref, s32[1,16]{1,0:T(1,128)S(1)} %bitcast.9, s32[1,32]{1,0:T(1,128)S(1)} %bitcast.10, s32[1,384]{1,0:T(1,128)S(1)} %copy-done.4, bf16[16,48,128]{2,1,0:T(8,128)(2,1)S(1)} %all-to-all-done.1.home_ref), custom_call_target="tpu_custom_call" | custom-call | tf_op jit(solution)/shard_map/finish/pallas_call | solution.py:217
Async XLA Ops:
  3.1 19.8 %copy-start = (bf16[1,64,64]{2,1,0:T(8,128)(2,1)S(1)}, bf16[1,64,64]{2,1,0:T(8,128)(2,1)}, u32[]{:S(2)}) copy-start(bf16[1,64,64]{2,1,0:T(8,128)(2,1)} %param.11) | copy-start | bytes 24580
  3.1 19.7 %copy-start.1 = (bf16[1,64,64]{2,1,0:T(8,128)(2,1)S(1)}, bf16[1,64,64]{2,1,0:T(8,128)(2,1)}, u32[]{:S(2)}) copy-start(bf16[1,64,64]{2,1,0:T(8,128)(2,1)} %param.12) | copy-start | bytes 24580
  3.2 19.7 %copy-start.2 = (f32[1,4096]{1,0:T(1,128)S(1)}, f32[1,4096]{1,0:T(1,128)}, u32[]{:S(2)}) copy-start(f32[1,4096]{1,0:T(1,128)} %param.13) | copy-start | bytes 49156
  25.0 12.5 %all-to-all-start.1 = ((bf16[16,48,128]{2,1,0:T(8,128)(2,1)}), bf16[16,48,128]{2,1,0:T(8,128)(2,1)S(1)}, u32[]{:S(2)}, u32[]{:S(2)}) async-start(bf16[16,48,128]{2,1,0:T(8,128)(2,1)} %work.1), calls=%async_computation.1 | async-start | bytes 393216 | tf_op jit(solution)/shard_map/all_to_all | solution.py:216
  28.5 9.0 %copy-start.4 = (s32[1,384]{1,0:T(1,128)S(1)}, s32[1,384]{1,0:T(1,128)}, u32[]{:S(2)}) copy-start(s32[1,384]{1,0:T(1,128)} %lists_ref.1) | copy-start | bytes 4612
  29.2 8.3 %copy-start.3 = (s32[16]{0:T(128)S(1)}, s32[16]{0:T(128)}, u32[]{:S(2)}) copy-start(s32[16]{0:T(128)} %param.14) | copy-start | bytes 196
  29.2 8.3 %copy-start.5 = (s32[32]{0:T(128)S(1)}, s32[32]{0:T(128)}, u32[]{:S(2)}) copy-start(s32[32]{0:T(128)} %param.15) | copy-start | bytes 388

commit v3 on v2

v3 whole, which is shorter than its diff:
```python
import functools

import jax
import jax.numpy as jnp
from jax import lax
from jax.experimental import pallas as pl
from jax.experimental.pallas import tpu as pltpu
from jax.sharding import PartitionSpec as P

damping = 0.1
LANES = 128
EIGEN_PIECES = 2
f32, bf16 = jnp.float32, jnp.bfloat16


def iota(shape, axis):
    return lax.broadcasted_iota(jnp.int32, shape, axis)


def dot(a, b, dims=((1,), (0,))):
    return lax.dot_general(a, b, (dims, ((), ())), preferred_element_type=f32)


def holds(layer_row, modules):
    slots = layer_row.shape[1]
    return (iota((modules, slots), 0) == layer_row).astype(f32).astype(bf16)


def half(left, right):
    return jnp.where(iota(left.shape, 1) < LANES // 2, left, right)


def swap(block):
    return pltpu.roll(block, LANES // 2, 1)


def paired(a, b):
    return jnp.concatenate([half(a, swap(b)), half(swap(a), b)], axis=0)


def unpaired(block):
    tall = block.shape[0] // 2
    top, low = block[:tall], block[tall:]
    return half(top, swap(low)), half(swap(top), low)


def reorder(out_basis):
    side = out_basis.shape[0]
    tall = side // 2
    order = iota((side, side), 1) == 2 * (iota((side, side), 0) % tall) + iota((side, side), 0) // tall
    order = order.astype(f32).astype(bf16)
    return dot(dot(order, out_basis).astype(bf16), order, ((1,), (1,)))


def widen(basis, where):
    side = basis.shape[0]
    spot = (iota((side, LANES), 0) + where * side == iota((side, LANES), 1)).astype(f32).astype(bf16)
    return dot(basis, spot)


def pack(
    layer_hbm, query_hbm, cand_hbm, out_basis_ref, in_basis_ref, eigen_ref,
    out_ref, shared_ref, layer_ref, query_ref, cand_ref, wide, sems,
):
    arrivals = [
        pltpu.make_async_copy(source, target, sems.at[i])
        for i, (source, target) in enumerate(
            ((layer_hbm, layer_ref), (query_hbm, query_ref), (cand_hbm, cand_ref))
        )
    ]
    for arrival in arrivals:
        arrival.start()
    side = out_basis_ref.shape[0]
    tall = side // 2
    eigen = eigen_ref[...]
    shared_ref[:side, :] = (
        widen(reorder(out_basis_ref[...]).astype(bf16), 0) + widen(in_basis_ref[...], 1)
    ).astype(bf16)
    for k in range(EIGEN_PIECES):
        piece = eigen.astype(bf16)
        eigen = eigen - piece.astype(f32)
        shared_ref[side + k * tall : side + (k + 1) * tall, :] = piece
    for arrival in arrivals:
        arrival.wait()
    modules, flat = query_ref.shape[1:]
    slots, height, _ = out_ref.shape
    one_hot = holds(layer_ref[...], modules)
    sources = [query_ref[r] for r in range(query_ref.shape[0])]
    sources += [cand_ref[r] for r in range(cand_ref.shape[0])]
    for r, rows in enumerate(sources):
        by_slot = dot(one_hot, rows, ((0,), (0,)))
        for j in range(tall):
            wide[pl.ds(r * tall + j, slots, stride=height), :] = by_slot[:, j * LANES : (j + 1) * LANES]
    out_ref[...] = wide[...].reshape(out_ref.shape).astype(bf16)


def at_home(packed_ref, gathered_ref, layer_ref, precond_ref, wide):
    slots = packed_ref.shape[0]
    modules, flat = precond_ref.shape[1:]
    tall = flat // LANES
    side = 2 * tall
    for p in range(slots // 2):
        a, b = 2 * p, 2 * p + 1
        basis_a, basis_b = gathered_ref[a, :side, :].astype(f32), gathered_ref[b, :side, :].astype(f32)
        zero = jnp.zeros_like(basis_a)
        turned_b = swap(basis_b)
        inner = jnp.concatenate([half(swap(basis_a), zero), half(zero, basis_b)], axis=0).astype(bf16)
        tower = jnp.concatenate([basis_a[:, :side], basis_b[:, :side]], axis=0).astype(bf16)
        beside = half(basis_a, turned_b).astype(bf16)
        eigens = []
        for s in (a, b):
            pieces = [
                gathered_ref[s, side + k * tall : side + (k + 1) * tall, :].astype(f32)
                for k in range(EIGEN_PIECES)
            ]
            eigens.append(sum(pieces[1:], pieces[0]))
        divisor = paired(*eigens) + damping
        query = paired(packed_ref[a, :tall, :].astype(f32), packed_ref[b, :tall, :].astype(f32)).astype(bf16)

        def apart(block):
            return jnp.concatenate([half(block, zero), half(zero, block)], axis=0).astype(bf16)

        applied = dot(query, inner).astype(bf16).astype(f32)
        rotated = dot(tower, apart(applied), ((0,), (0,)))
        scaled = (rotated / divisor).astype(bf16)
        returned = dot(scaled, inner, ((1,), (1,))).astype(bf16).astype(f32)
        precond_a, precond_b = unpaired(dot(beside, apart(returned)))
        wide[pl.ds(a * tall, tall), :] = precond_a
        wide[pl.ds(b * tall, tall), :] = precond_b
    by_slot = jnp.concatenate([wide[pl.ds(j, slots, stride=tall), :].astype(bf16) for j in range(tall)], axis=1)
    precond_ref[0] = dot(holds(layer_ref[...], modules), by_slot).astype(bf16)


def work(moved_ref, out_basis_ref, in_basis_ref, eigen_ref, out_ref, cands, queries):
    sources, height, _ = moved_ref.shape
    side = out_basis_ref.shape[0]
    tall = side // 2
    per = height // tall - 1
    count = sources * per
    basis = reorder(out_basis_ref[...]).astype(bf16)
    in_basis = in_basis_ref[...]
    inner = jnp.concatenate([widen(in_basis, 0), widen(in_basis, 1)], axis=0).astype(bf16)
    eigen = eigen_ref[...]
    factor = 1.0 / (paired(eigen, eigen) + damping)
    pairs = [
        paired(moved_ref[2 * p, :tall, :].astype(f32), moved_ref[2 * p + 1, :tall, :].astype(f32)).astype(bf16)
        for p in range(sources // 2)
    ]

    def stack(wide):
        return jnp.concatenate([wide[:, p * LANES : (p + 1) * LANES] for p in range(len(pairs))], axis=0)

    def spread_out(rows):
        return jnp.concatenate([rows[p * side : (p + 1) * side] for p in range(len(pairs))], axis=1)

    applied = spread_out(dot(jnp.concatenate(pairs, axis=0), inner).astype(bf16))
    rotated = stack(dot(basis, applied, ((0,), (0,))))
    scaled = (rotated.reshape(len(pairs), side, LANES) * factor[None]).reshape(rotated.shape).astype(bf16)
    returned = spread_out(dot(scaled, inner, ((1,), (1,))).astype(bf16))
    precond = dot(basis, returned).astype(bf16).astype(f32)
    for p in range(len(pairs)):
        a, b = unpaired(precond[:, p * LANES : (p + 1) * LANES])
        queries[pl.ds(2 * p * tall, tall), :] = a
        queries[pl.ds((2 * p + 1) * tall, tall), :] = b

    for d in range(sources):
        cands[pl.ds(d * per * tall, per * tall), :] = moved_ref[d, tall:, :].astype(f32)
    queries_flat = jnp.concatenate(
        [queries[pl.ds(j, sources, stride=tall), :].astype(bf16) for j in range(tall)], axis=1
    )
    cands_flat = jnp.concatenate(
        [cands[pl.ds(j, count, stride=tall), :].astype(bf16) for j in range(tall)], axis=1
    )
    partial = dot(queries_flat, cands_flat, ((1,), (1,)))
    width = out_ref.shape[2]
    if width > count:
        partial = jnp.concatenate([partial, jnp.zeros((sources, width - count), f32)], axis=1)
    out_ref[...] = partial.reshape(out_ref.shape)


def upright(row):
    n = row.shape[1]
    return jnp.sum(jnp.where(iota((n, n), 0) == iota((n, n), 1), row, 0.0), axis=1, keepdims=True)


def finish(length_ref, rows_ref, lists_ref, partial_ref, scores_ref):
    count = rows_ref.shape[1]
    dense = jnp.sum(partial_ref[...], axis=0)[:, :count]
    by_cand = jnp.sum(
        jnp.where(iota((count, count), 0) == rows_ref[...], upright(dense), 0.0), axis=0, keepdims=True
    )
    lists = lists_ref[...]
    longest = lists.shape[1]
    picked = jnp.sum(
        jnp.where(iota((count, longest), 0) == lists, upright(by_cand), 0.0), axis=0, keepdims=True
    )
    scores_ref[...] = jnp.where(iota((1, longest), 1) < length_ref[0], picked, 0.0)


VMEM = pl.BlockSpec(memory_space=pltpu.VMEM)
HBM = pl.BlockSpec(memory_space=pltpu.HBM)
SMEM = pl.BlockSpec(memory_space=pltpu.SMEM)
PARAMS = pltpu.CompilerParams(vmem_limit_bytes=40 * 1024 * 1024)
FULL = pltpu.CompilerParams(vmem_limit_bytes=56 * 1024 * 1024)


def body(
    query_grads,
    cand_grads,
    basis_out,
    basis_in,
    eigvals,
    layer_map,
    cand_rows,
    cand_lists,
    list_lengths,
):
    own, modules, flat = query_grads.shape
    per = cand_grads.shape[0]
    slots = layer_map.shape[0]
    tall = flat // LANES
    count = cand_rows.shape[0]
    layer_row = layer_map.reshape(1, slots)
    height = (own + per) * tall
    side = basis_out.shape[1]
    width = -(-count // LANES) * LANES
    out_basis = basis_out.reshape(basis_out.shape[1:])
    in_basis = basis_in.reshape(basis_in.shape[1:])
    eigen = eigvals.reshape(tall, LANES)

    packed, shared = pl.pallas_call(
        pack,
        out_shape=(
            jax.ShapeDtypeStruct((slots, height, LANES), bf16),
            jax.ShapeDtypeStruct((side + EIGEN_PIECES * tall, LANES), bf16),
        ),
        in_specs=[HBM] * 3 + [VMEM] * 3,
        out_specs=(VMEM, VMEM),
        scratch_shapes=[
            pltpu.VMEM(layer_row.shape, jnp.int32),
            pltpu.VMEM(query_grads.shape, bf16),
            pltpu.VMEM(cand_grads.shape, bf16),
            pltpu.VMEM((slots * height, LANES), f32),
            pltpu.SemaphoreType.DMA((3,)),
        ],
        compiler_params=FULL,
        name="pack",
    )(layer_row, query_grads, cand_grads, out_basis, in_basis, eigen)
    gathered = lax.all_gather(shared, "shard", axis=0, tiled=False)
    moved = lax.all_to_all(packed, "shard", split_axis=0, concat_axis=0, tiled=True)
    sources = moved.shape[0]
    partial = pl.pallas_call(
        work,
        out_shape=jax.ShapeDtypeStruct((sources, 1, width), f32),
        in_specs=[VMEM] * 4,
        out_specs=VMEM,
        scratch_shapes=[pltpu.VMEM((sources * per * tall, LANES), f32), pltpu.VMEM((sources * tall, LANES), f32)],
        compiler_params=PARAMS,
        name="work",
    )(moved, out_basis, in_basis, eigen)
    partials = lax.all_to_all(partial, "shard", split_axis=0, concat_axis=0, tiled=True)
    precond = pl.pallas_call(
        at_home,
        out_shape=jax.ShapeDtypeStruct(query_grads.shape, bf16),
        in_specs=[VMEM] * 3,
        out_specs=VMEM,
        scratch_shapes=[pltpu.VMEM((slots * tall, LANES), f32)],
        compiler_params=PARAMS,
        cost_estimate=pl.CostEstimate(
            flops=8 * slots * side * LANES * LANES, bytes_accessed=4 * slots * height * LANES, transcendentals=0
        ),
        name="at_home",
    )(packed, gathered, layer_row)
    scores = pl.pallas_call(
        finish,
        out_shape=jax.ShapeDtypeStruct(cand_lists.shape, f32),
        in_specs=[SMEM] + [VMEM] * 3,
        out_specs=VMEM,
        compiler_params=PARAMS,
        name="finish",
    )(list_lengths, cand_rows.reshape(1, count), cand_lists, partials)
    return precond, scores


def solution(mesh):
    return jax.shard_map(
        body,
        mesh=mesh,
        in_specs=(
            P(("groups", "shard"), None, None),
            P(("groups", "shard"), None, None),
            P("shard", None, None),
            P("shard", None, None),
            P("shard", None),
            P(),
            P("groups"),
            P(("groups", "shard"), None),
            P(("groups", "shard")),
        ),
        out_specs=(P(("groups", "shard"), None, None), P(("groups", "shard"), None)),
        check_vma=False,
    )
```

time: 38.8 us -> 60 us (1.55)
  blocking collectives: 19.7 us -> 43 us
  waiting for transfers between devices: 8.29 us -> 0.01 us
  Pallas kernels: 5.48 us -> 10.2 us
  local copies, waits for them, and re-layouts: 0.04 us -> 1.35 us
    all_gather x0 -> x1, blocking collectives: none -> 23.3 us  [body(): gathered = lax.all_gather(shared, 'shard', axis=0, tiled=False)]
    all_to_all x1, waiting for transfers between devices: 8.29 us -> 0.01 us  [body(): lax.all_to_all(partial, 'shard', split_axis=0, concat_axis=0, tiled=True)]
    pallas_call x3 -> x4, Pallas kernels: 5.48 us -> 10.2 us  [the longest x1 4.33 us: body(): pl.pallas_call(at_home, out_shape=jax.ShapeDtypeStruct(query_grads.shape,...]
    unnamed x12 -> x16, local copies, waits for them, and re-layouts: 0.04 us -> 1.35 us
  transfers between devices with their start and end apart: 1 -> 1, of which waited for: 1 -> 0; matrix products, arithmetic and copies ran while one was open for 0% -> 0% of each run, Pallas kernels for 0% -> 7%
where the time goes in v3:
time: 60 us; the launch traced here: 59.6 us
  blocking collectives  43 us (72%)
  Pallas kernels  10.2 us (17%)
  starting transfers between devices  3.65 us (6%)
  between operations  1.36 us (2%)
  local copies, waits for them, and re-layouts  1.35 us (2%)
    all_gather x1, blocking collectives, body(): gathered = lax.all_gather(shared, 'shard', axis=0, tiled=False)  23.3 us
    all_to_all x1, blocking collectives, body(): lax.all_to_all(packed, 'shard', split_axis=0, concat_axis=0, tiled=True)  19.7 us
    pallas_call x1, Pallas kernels, body(): pl.pallas_call(at_home, out_shape=jax.ShapeDtypeStruct(query_grads.shape,...  4.33 us
    all_to_all x1, starting transfers between devices, body(): lax.all_to_all(partial, 'shard', split_axis=0, concat_axis=0, tiled=True)  3.65 us
    pallas_call x1, Pallas kernels, body(): pl.pallas_call(pack, out_shape=(jax.ShapeDtypeStruct((slots, height, LANE...  3.23 us
    pallas_call x1, Pallas kernels, body(): pl.pallas_call(work, out_shape=jax.ShapeDtypeStruct((sources, 1, width),...  1.92 us
    unnamed x16, local copies, waits for them, and re-layouts  1.35 us
  transfers between devices with their start and end apart: 1, of which 0 were waited for; matrix products, arithmetic and copies ran while one was open for 0% of the time, Pallas kernels for 7%

profile of v3, /device:TPU:0, one launch (start us, length us, event | category | flops | bytes accessed | tf_op | source)
XLA Modules:
  0.0 59.6 jit_solution(11842232420229220992)
XLA Ops:
  0.6 3.2 %pack.1 = (bf16[16,96,128]{2,1,0:T(8,128)(2,1)}, bf16[128,128]{1,0:T(8,128)(2,1)}) custom-call(s32[1,16]{1,0:T(1,128)} %bitcast.13, bf16[1,16,4096]{2,1,0:T(8,128)(2,1)} %query_hbm.1, bf16[2,16,4096]{2,1,0:T(8,128)(2,1)} %cand_hbm.1, bf16[64,64]{1,0:T(8,128)(2,1)} %bitcast.7, bf16[64,64]{1,0:T(8,128)(2,1)} %bitcast.9, f32[32,128]{1,0:T(8,128)} %bitcast.11), custom_call_target="tpu_custom_call" | custom-call | tf_op jit(solution)/shard_map/pack/pallas_call | solution.py:231
  3.9 0.0 copy-start.1
  3.9 0.0 copy-start.2
  3.9 0.0 copy-start.3
  3.9 19.7 %all_to_all.10.moved_ref = bf16[16,96,128]{2,1,0:T(8,128)(2,1)S(1)} all-to-all(bf16[16,96,128]{2,1,0:T(8,128)(2,1)} %get-tuple-element.4.packed_ref), channel_id=1, replica_groups=mesh['groups'=2,'shard'=16] {'shard'}, dimensions={0} | all-to-all | bytes 786432 | tf_op jit(solution)/shard_map/all_to_all | solution.py:250
  23.6 0.0 copy-done.1
  23.6 0.0 copy-done.2
  23.7 0.0 copy-done.3
  23.7 0.0 copy-start.7
  23.7 1.9 %work.1 = f32[16,1,128]{2,1,0:T(1,128)} custom-call(bf16[16,96,128]{2,1,0:T(8,128)(2,1)S(1)} %all_to_all.10.moved_ref, bf16[64,64]{1,0:T(8,128)(2,1)S(1)} %bitcast.8, bf16[64,64]{1,0:T(8,128)(2,1)S(1)} %bitcast.10, f32[32,128]{1,0:T(8,128)S(1)} %bitcast.12), custom_call_target="tpu_custom_call" | custom-call | tf_op jit(solution)/shard_map/work/pallas_call | solution.py:252
  25.6 0.0 copy-start
  25.6 3.7 %all-to-all-start.1 = ((f32[16,1,128]{2,1,0:T(1,128)}), f32[16,1,128]{2,1,0:T(1,128)S(1)}, u32[]{:S(2)}, u32[]{:S(2)}) async-start(f32[16,1,128]{2,1,0:T(1,128)} %work.1), calls=%async_computation.1 | async-start | bytes 16384 | tf_op jit(solution)/shard_map/all_to_all | solution.py:261
  29.3 0.0 copy-done.7
  29.3 23.3 %all-gather = bf16[2048,128]{1,0:T(8,128)(2,1)S(1)} all-gather(bf16[128,128]{1,0:T(8,128)(2,1)S(1)} %copy-done.7), channel_id=2, replica_groups=mesh['groups'=2,'shard'=16] {'shard'}, dimensions={0}, use_global_device_ids=true | all-gather | bytes 557056 | tf_op jit(solution)/shard_map/all_gather | solution.py:249
  53.2 0.0 copy-start.4
  53.2 0.0 copy-done
  53.2 0.6 %copy-done.4 = s32[16]{0:T(128)S(1)} copy-done((s32[16]{0:T(128)S(1)}, s32[16]{0:T(128)}, u32[]{:S(2)}) %copy-start.4) | copy-done | bytes 88
  53.8 0.0 copy-start.6
  53.8 4.3 %at_home.1 = bf16[1,16,4096]{2,1,0:T(8,128)(2,1)} custom-call(bf16[16,96,128]{2,1,0:T(8,128)(2,1)S(1)} %copy-done, bf16[16,128,128]{2,1,0:T(8,128)(2,1)S(1)} %bitcast.6, s32[1,16]{1,0:T(1,128)S(1)} %bitcast.14), custom_call_target="tpu_custom_call" | custom-call | flops 134217728 | bytes 786432 | tf_op jit(solution)/shard_map/at_home/pallas_call | solution.py:262
  58.2 0.0 copy-start.5
  58.2 0.0 all-to-all-done.1.partial_ref
  58.2 0.0 copy-done.6
  58.2 0.7 %copy-done.5 = s32[1,384]{1,0:T(1,128)S(1)} copy-done((s32[1,384]{1,0:T(1,128)S(1)}, s32[1,384]{1,0:T(1,128)}, u32[]{:S(2)}) %copy-start.5) | copy-done | bytes 1560
  58.8 0.8 %finish.1 = f32[1,384]{1,0:T(1,128)} custom-call(s32[1]{0:T(128)S(6)} %copy.11.length_ref, s32[1,32]{1,0:T(1,128)S(1)} %bitcast.15, s32[1,384]{1,0:T(1,128)S(1)} %copy-done.5, f32[16,1,128]{2,1,0:T(1,128)S(1)} %all-to-all-done.1.partial_ref), custom_call_target="tpu_custom_call" | custom-call | tf_op jit(solution)/shard_map/finish/pallas_call | solution.py:274
Async XLA Ops:
  3.9 19.8 %copy-start.1 = (bf16[1,64,64]{2,1,0:T(8,128)(2,1)S(1)}, bf16[1,64,64]{2,1,0:T(8,128)(2,1)}, u32[]{:S(2)}) copy-start(bf16[1,64,64]{2,1,0:T(8,128)(2,1)} %param.11) | copy-start | bytes 24580
  3.9 19.8 %copy-start.2 = (bf16[1,64,64]{2,1,0:T(8,128)(2,1)S(1)}, bf16[1,64,64]{2,1,0:T(8,128)(2,1)}, u32[]{:S(2)}) copy-start(bf16[1,64,64]{2,1,0:T(8,128)(2,1)} %param.12) | copy-start | bytes 24580
  3.9 19.8 %copy-start.3 = (f32[1,4096]{1,0:T(1,128)S(1)}, f32[1,4096]{1,0:T(1,128)}, u32[]{:S(2)}) copy-start(f32[1,4096]{1,0:T(1,128)} %param.13) | copy-start | bytes 49156
  23.7 5.6 %copy-start.7 = (bf16[128,128]{1,0:T(8,128)(2,1)S(1)}, bf16[128,128]{1,0:T(8,128)(2,1)}, u32[]{:S(2)}) copy-start(bf16[128,128]{1,0:T(8,128)(2,1)} %get-tuple-element.5) | copy-start | bytes 98308
  25.6 27.6 %copy-start = (bf16[16,96,128]{2,1,0:T(8,128)(2,1)S(1)}, bf16[16,96,128]{2,1,0:T(8,128)(2,1)}, u32[]{:S(2)}) copy-start(bf16[16,96,128]{2,1,0:T(8,128)(2,1)} %get-tuple-element.4.packed_ref) | copy-start | bytes 1179652
  25.6 32.6 %all-to-all-start.1 = ((f32[16,1,128]{2,1,0:T(1,128)}), f32[16,1,128]{2,1,0:T(1,128)S(1)}, u32[]{:S(2)}, u32[]{:S(2)}) async-start(f32[16,1,128]{2,1,0:T(1,128)} %work.1), calls=%async_computation.1 | async-start | bytes 16384 | tf_op jit(solution)/shard_map/all_to_all | solution.py:261
  53.2 0.7 %copy-start.4 = (s32[16]{0:T(128)S(1)}, s32[16]{0:T(128)}, u32[]{:S(2)}) copy-start(s32[16]{0:T(128)} %param.14) | copy-start | bytes 196
  53.8 4.3 %copy-start.6 = (s32[32]{0:T(128)S(1)}, s32[32]{0:T(128)}, u32[]{:S(2)}) copy-start(s32[32]{0:T(128)} %param.15) | copy-start | bytes 388
  58.2 0.7 %copy-start.5 = (s32[1,384]{1,0:T(1,128)S(1)}, s32[1,384]{1,0:T(1,128)}, u32[]{:S(2)}) copy-start(s32[1,384]{1,0:T(1,128)} %lists_ref.1) | copy-start | bytes 4612

commit v4 on v2

--- a/solution.py
+++ b/solution.py
@@ -26,7 +26,8 @@
     return (iota((modules, slots), 0) == layer_row).astype(f32).astype(bf16)
 
 
-def pack(layer_hbm, query_hbm, cand_hbm, out_ref, layer_ref, query_ref, cand_ref, wide, sems):
+def pack(direct, layer_hbm, query_hbm, cand_hbm, *refs):
+    *out_refs, layer_ref, query_ref, cand_ref, wide, sems = refs
     arrivals = [
         pltpu.make_async_copy(source, target, sems.at[i])
         for i, (source, target) in enumerate(
@@ -38,16 +39,26 @@
     for arrival in arrivals:
         arrival.wait()
     modules, flat = query_ref.shape[1:]
-    slots, height, _ = out_ref.shape
+    slots = layer_ref.shape[1]
+    height = out_refs[0].shape[-2]
     tall = flat // LANES
     one_hot = holds(layer_ref[...], modules)
+    if direct:
+        me = lax.axis_index("shard")
+        partner = iota((slots, slots), 0) == (iota((slots, slots), 1) ^ me)
+        one_hot = dot(one_hot, partner.astype(f32).astype(bf16)).astype(bf16)
     sources = [query_ref[r] for r in range(query_ref.shape[0])]
     sources += [cand_ref[r] for r in range(cand_ref.shape[0])]
     for r, rows in enumerate(sources):
         by_slot = dot(one_hot, rows, ((0,), (0,)))
         for j in range(tall):
             wide[pl.ds(r * tall + j, slots, stride=height), :] = by_slot[:, j * LANES : (j + 1) * LANES]
-    out_ref[...] = wide[...].reshape(out_ref.shape).astype(bf16)
+    for k in range(slots):
+        block = wide[pl.ds(k * height, height), :].astype(bf16)
+        if direct:
+            out_refs[k][...] = block
+        else:
+            out_refs[0][k] = block
 
 
 def half(left, right):
@@ -58,8 +69,18 @@
     return pltpu.roll(block, LANES // 2, 1)
 
 
-def work(moved_ref, out_basis_ref, in_basis_ref, eigen_ref, out_ref, cands, homes):
-    sources, height, _ = moved_ref.shape
+def work(direct, *refs):
+    *moved_refs, out_basis_ref, in_basis_ref, eigen_ref, out_ref, cands, homes = refs
+    sources = out_ref.shape[0]
+    height = moved_refs[0].shape[-2]
+    me = lax.axis_index("shard") if direct else 0
+
+    def arrived(k, rows):
+        return (moved_refs[k][rows, :] if direct else moved_refs[0][k, rows, :]).astype(f32)
+
+    def place(k, size):
+        return pl.multiple_of((k ^ me) * size, 8) if direct else k * size
+
     _, send, _ = out_ref.shape
     side = out_basis_ref.shape[0]
     tall = side // 2
@@ -81,8 +102,8 @@
 
     pairs = []
     for p in range(sources // 2):
-        a = moved_ref[2 * p, :tall, :].astype(f32)
-        b = moved_ref[2 * p + 1, :tall, :].astype(f32)
+        a = arrived(2 * p, slice(0, tall))
+        b = arrived(2 * p + 1, slice(0, tall))
         pairs.append(jnp.concatenate([half(a, swap(b)), half(swap(a), b)], axis=0).astype(bf16))
 
     def stack(wide):
@@ -99,11 +120,11 @@
     for p in range(len(pairs)):
         top = precond[:tall, p * LANES : (p + 1) * LANES]
         low = precond[tall:, p * LANES : (p + 1) * LANES]
-        homes[pl.ds(2 * p * send, tall), :] = half(top, swap(low))
-        homes[pl.ds((2 * p + 1) * send, tall), :] = half(swap(top), low)
+        homes[pl.ds(place(2 * p, send), tall), :] = half(top, swap(low))
+        homes[pl.ds(place(2 * p + 1, send), tall), :] = half(swap(top), low)
 
     for d in range(sources):
-        cands[pl.ds(d * per * tall, per * tall), :] = moved_ref[d, tall:, :].astype(f32)
+        cands[pl.ds(place(d, per * tall), per * tall), :] = arrived(d, slice(tall, height))
     queries_flat = jnp.concatenate(
         [homes[pl.ds(j, sources, stride=send), :].astype(bf16) for j in range(tall)], axis=1
     )
@@ -182,11 +203,16 @@
     height = (own + per) * tall
     send = tall + -(-PIECES * -(-count // LANES) // 16) * 16
 
+    sources = lax.axis_size("shard")
+    direct = sources <= 16
+    block = jax.ShapeDtypeStruct((height, LANES), bf16)
+    blocks = [block] * slots if direct else [jax.ShapeDtypeStruct((slots, height, LANES), bf16)]
+
     packed = pl.pallas_call(
-        pack,
-        out_shape=jax.ShapeDtypeStruct((slots, height, LANES), bf16),
+        functools.partial(pack, direct),
+        out_shape=blocks,
         in_specs=[HBM] * 3,
-        out_specs=VMEM,
+        out_specs=[VMEM] * len(blocks),
         scratch_shapes=[
             pltpu.VMEM(layer_row.shape, jnp.int32),
             pltpu.VMEM(query_grads.shape, bf16),
@@ -197,18 +223,22 @@
         compiler_params=FULL,
         name="pack",
     )(layer_row, query_grads, cand_grads)
-    moved = lax.all_to_all(packed, "shard", split_axis=0, concat_axis=0, tiled=True)
-    sources = moved.shape[0]
+    if direct:
+        moved = [packed[0]] + [
+            lax.ppermute(packed[k], "shard", [(i, i ^ k) for i in range(sources)]) for k in range(1, sources)
+        ]
+    else:
+        moved = [lax.all_to_all(packed[0], "shard", split_axis=0, concat_axis=0, tiled=True)]
     homes = pl.pallas_call(
-        work,
+        functools.partial(work, direct),
         out_shape=jax.ShapeDtypeStruct((sources, send, LANES), bf16),
-        in_specs=[VMEM] * 4,
+        in_specs=[VMEM] * (len(moved) + 3),
         out_specs=VMEM,
         scratch_shapes=[pltpu.VMEM((sources * per * tall, LANES), f32), pltpu.VMEM((sources * send, LANES), f32)],
         compiler_params=PARAMS,
         name="work",
     )(
-        moved,
+        *moved,
         basis_out.reshape(basis_out.shape[1:]),
         basis_in.reshape(basis_in.shape[1:]),
         eigvals.reshape(tall, LANES),

time: 38.8 us -> 46.8 us (1.21)
  starting transfers between devices: 3.53 us -> 26.8 us
  blocking collectives: 19.7 us -> 0 us
  waiting for transfers between devices: 8.29 us -> 12.8 us
    ppermute x0 -> x15, starting transfers between devices: none -> 23.3 us  [body(): lax.ppermute(packed[k], 'shard', [(i, i ^ k) for i in range(sources)])]
    all_to_all x1 -> x0, blocking collectives: 19.7 us -> none  [body(): lax.all_to_all(packed, 'shard', split_axis=0, concat_axis=0, tiled=True)]
    ppermute x0 -> x15, waiting for transfers between devices: none -> 4.51 us  [body(): lax.ppermute(packed[k], 'shard', [(i, i ^ k) for i in range(sources)])]
  transfers between devices with their start and end apart: 1 -> 16, of which waited for: 1 -> 5; matrix products, arithmetic and copies ran while one was open for 0% -> 0% of each run, Pallas kernels for 0% -> 0%
where the time goes in v4:
time: 46.8 us; the launch traced here: 46.6 us
  starting transfers between devices  26.8 us (57%)
  waiting for transfers between devices  12.8 us (27%)
  Pallas kernels  5.56 us (12%)
  between operations  1.4 us (3%)
    ppermute x15, starting transfers between devices, body(): lax.ppermute(packed[k], 'shard', [(i, i ^ k) for i in range(sources)])  23.3 us
    all_to_all x1, waiting for transfers between devices, body(): lax.all_to_all(homes, 'shard', split_axis=0, concat_axis=0, tiled=True)  8.27 us
    ppermute x15, waiting for transfers between devices, body(): lax.ppermute(packed[k], 'shard', [(i, i ^ k) for i in range(sources)])  4.51 us
    all_to_all x1, starting transfers between devices, body(): lax.all_to_all(homes, 'shard', split_axis=0, concat_axis=0, tiled=True)  3.52 us
    pallas_call x1, Pallas kernels, body(): pl.pallas_call(functools.partial(pack, direct), out_shape=blocks, in_spec...  2.59 us
    pallas_call x1, Pallas kernels, body(): pl.pallas_call(functools.partial(work, direct), out_shape=jax.ShapeDtypeS...  2.09 us
  transfers between devices with their start and end apart: 16, of which 5 were waited for; matrix products, arithmetic and copies ran while one was open for 0% of the time, Pallas kernels for 0%

profile of v4, /device:TPU:0, one launch (start us, length us, event | category | flops | bytes accessed | tf_op | source)
XLA Modules:
  0.0 46.6 jit_solution(10632987791618925971)
XLA Ops:
  0.6 0.0 copy-start.1
  0.6 0.0 copy-start.2
  0.7 0.0 copy-start.3
  0.7 2.6 %pack.1 = (bf16[96,128]{1,0:T(8,128)(2,1)}, bf16[96,128]{1,0:T(8,128)(2,1)}, bf16[96,128]{1,0:T(8,128)(2,1)}, bf16[96,128]{1,0:T(8,128)(2,1)}, bf16[96,128]{1,0:...) custom-call(s32[1,16]{1,0:T(1,128)} %bitcast.8, ...), custom_call_target="tpu_custom_call" | custom-call | tf_op jit(solution)/shard_map/pack/pallas_call | solution.py:211
  3.3 0.0 copy-start
  3.3 0.5 %collective-permute-start = (bf16[96,128]{1,0:T(8,128)(2,1)}, bf16[96,128]{1,0:T(8,128)(2,1)S(1)}, u32[]{:S(2)}, u32[]{:S(2)}) collective-permute-start(bf16[96,128]{1,0:T(8,128)(2,1)} %get-tuple-element.19), channel_id=1, source_target_pairs={{0,1},{1,0},{2,3},{3,2},{4,5},{5,4},{6,7},{7,6},{8,9},{9,8},{10,11... | collective-permute-start | bytes 73736 | tf_op jit(solution)/shard_map/ppermute | solution.py:228
  3.8 2.6 %collective-permute-start.1 = (bf16[96,128]{1,0:T(8,128)(2,1)}, bf16[96,128]{1,0:T(8,128)(2,1)S(1)}, u32[]{:S(2)}, u32[]{:S(2)}) collective-permute-start(bf16[96,128]{1,0:T(8,128)(2,1)} %get-tuple-element.20), channel_id=1, source_target_pairs={{0,2},{1,3},{2,0},{3,1},{4,6},{5,7},{6,4},{7,5},{8,10},{9,11},{10,... | collective-permute-start | bytes 73736 | tf_op jit(solution)/shard_map/ppermute | solution.py:228
  6.4 2.3 %collective-permute-start.10 = (bf16[96,128]{1,0:T(8,128)(2,1)}, bf16[96,128]{1,0:T(8,128)(2,1)S(1)}, u32[]{:S(2)}, u32[]{:S(2)}) collective-permute-start(bf16[96,128]{1,0:T(8,128)(2,1)} %get-tuple-element.29), channel_id=1, source_target_pairs={{0,11},{1,10},{2,9},{3,8},{4,15},{5,14},{6,13},{7,12},{8,3},{9,2},... | collective-permute-start | bytes 73736 | tf_op jit(solution)/shard_map/ppermute | solution.py:228
  8.7 1.4 %collective-permute-start.11 = (bf16[96,128]{1,0:T(8,128)(2,1)}, bf16[96,128]{1,0:T(8,128)(2,1)S(1)}, u32[]{:S(2)}, u32[]{:S(2)}) collective-permute-start(bf16[96,128]{1,0:T(8,128)(2,1)} %get-tuple-element.30), channel_id=1, source_target_pairs={{0,12},{1,13},{2,14},{3,15},{4,8},{5,9},{6,10},{7,11},{8,4},{9,5},... | collective-permute-start | bytes 73736 | tf_op jit(solution)/shard_map/ppermute | solution.py:228
  10.0 2.1 %collective-permute-start.12 = (bf16[96,128]{1,0:T(8,128)(2,1)}, bf16[96,128]{1,0:T(8,128)(2,1)S(1)}, u32[]{:S(2)}, u32[]{:S(2)}) collective-permute-start(bf16[96,128]{1,0:T(8,128)(2,1)} %get-tuple-element.31), channel_id=1, source_target_pairs={{0,13},{1,12},{2,15},{3,14},{4,9},{5,8},{6,11},{7,10},{8,5},{9,4},... | collective-permute-start | bytes 73736 | tf_op jit(solution)/shard_map/ppermute | solution.py:228
  12.2 0.0 collective-permute-done.refs_1_
  12.2 2.3 %collective-permute-start.13 = (bf16[96,128]{1,0:T(8,128)(2,1)}, bf16[96,128]{1,0:T(8,128)(2,1)S(1)}, u32[]{:S(2)}, u32[]{:S(2)}) collective-permute-start(bf16[96,128]{1,0:T(8,128)(2,1)} %get-tuple-element.32), channel_id=1, source_target_pairs={{0,14},{1,15},{2,12},{3,13},{4,10},{5,11},{6,8},{7,9},{8,6},{9,7},... | collective-permute-start | bytes 73736 | tf_op jit(solution)/shard_map/ppermute | solution.py:228
  14.5 0.0 collective-permute-done.1.refs_2_
  14.5 2.2 %collective-permute-start.14 = (bf16[96,128]{1,0:T(8,128)(2,1)}, bf16[96,128]{1,0:T(8,128)(2,1)S(1)}, u32[]{:S(2)}, u32[]{:S(2)}) collective-permute-start(bf16[96,128]{1,0:T(8,128)(2,1)} %get-tuple-element.33), channel_id=1, source_target_pairs={{0,15},{1,14},{2,13},{3,12},{4,11},{5,10},{6,9},{7,8},{8,7},{9,6},... | collective-permute-start | bytes 73736 | tf_op jit(solution)/shard_map/ppermute | solution.py:228
  16.7 0.0 collective-permute-done.10.refs_11_
  16.7 1.5 %collective-permute-start.2 = (bf16[96,128]{1,0:T(8,128)(2,1)}, bf16[96,128]{1,0:T(8,128)(2,1)S(1)}, u32[]{:S(2)}, u32[]{:S(2)}) collective-permute-start(bf16[96,128]{1,0:T(8,128)(2,1)} %get-tuple-element.21), channel_id=1, source_target_pairs={{0,3},{1,2},{2,1},{3,0},{4,7},{5,6},{6,5},{7,4},{8,11},{9,10},{10,... | collective-permute-start | bytes 73736 | tf_op jit(solution)/shard_map/ppermute | solution.py:228
  18.1 0.0 collective-permute-done.11.refs_12_
  18.2 0.0 collective-permute-start.3
  18.2 0.0 collective-permute-done.12.refs_13_
  18.2 1.5 %collective-permute-start.4 = (bf16[96,128]{1,0:T(8,128)(2,1)}, bf16[96,128]{1,0:T(8,128)(2,1)S(1)}, u32[]{:S(2)}, u32[]{:S(2)}) collective-permute-start(bf16[96,128]{1,0:T(8,128)(2,1)} %get-tuple-element.23), channel_id=1, source_target_pairs={{0,5},{1,4},{2,7},{3,6},{4,1},{5,0},{6,3},{7,2},{8,13},{9,12},{10,... | collective-permute-start | bytes 73736 | tf_op jit(solution)/shard_map/ppermute | solution.py:228
  19.7 0.0 collective-permute-done.13.refs_14_
  19.7 0.5 %collective-permute-start.5 = (bf16[96,128]{1,0:T(8,128)(2,1)}, bf16[96,128]{1,0:T(8,128)(2,1)S(1)}, u32[]{:S(2)}, u32[]{:S(2)}) collective-permute-start(bf16[96,128]{1,0:T(8,128)(2,1)} %get-tuple-element.24), channel_id=1, source_target_pairs={{0,6},{1,7},{2,4},{3,5},{4,2},{5,3},{6,0},{7,1},{8,14},{9,15},{10,... | collective-permute-start | bytes 73736 | tf_op jit(solution)/shard_map/ppermute | solution.py:228
  20.2 0.5 %collective-permute-done.14.refs_15_ = bf16[96,128]{1,0:T(8,128)(2,1)S(1)} collective-permute-done((bf16[96,128]{1,0:T(8,128)(2,1)}, bf16[96,128]{1,0:T(8,128)(2,1)S(1)}, u32[]{:S(2)}, u32[]{:S(2)}) %collective-permute-start.14) | collective-permute-done | bytes 24608 | tf_op jit(solution)/shard_map/ppermute | solution.py:228
  20.7 1.9 %collective-permute-start.6 = (bf16[96,128]{1,0:T(8,128)(2,1)}, bf16[96,128]{1,0:T(8,128)(2,1)S(1)}, u32[]{:S(2)}, u32[]{:S(2)}) collective-permute-start(bf16[96,128]{1,0:T(8,128)(2,1)} %get-tuple-element.25), channel_id=1, source_target_pairs={{0,7},{1,6},{2,5},{3,4},{4,3},{5,2},{6,1},{7,0},{8,15},{9,14},{10,... | collective-permute-start | bytes 73736 | tf_op jit(solution)/shard_map/ppermute | solution.py:228
  22.6 0.0 collective-permute-done.2.refs_3_
  22.6 0.9 %collective-permute-start.7 = (bf16[96,128]{1,0:T(8,128)(2,1)}, bf16[96,128]{1,0:T(8,128)(2,1)S(1)}, u32[]{:S(2)}, u32[]{:S(2)}) collective-permute-start(bf16[96,128]{1,0:T(8,128)(2,1)} %get-tuple-element.26), channel_id=1, source_target_pairs={{0,8},{1,9},{2,10},{3,11},{4,12},{5,13},{6,14},{7,15},{8,0},{9,1},... | collective-permute-start | bytes 73736 | tf_op jit(solution)/shard_map/ppermute | solution.py:228
  23.4 0.0 collective-permute-done.3.refs_4_
  23.5 1.5 %collective-permute-start.8 = (bf16[96,128]{1,0:T(8,128)(2,1)}, bf16[96,128]{1,0:T(8,128)(2,1)S(1)}, u32[]{:S(2)}, u32[]{:S(2)}) collective-permute-start(bf16[96,128]{1,0:T(8,128)(2,1)} %get-tuple-element.27), channel_id=1, source_target_pairs={{0,9},{1,8},{2,11},{3,10},{4,13},{5,12},{6,15},{7,14},{8,1},{9,0},... | collective-permute-start | bytes 73736 | tf_op jit(solution)/shard_map/ppermute | solution.py:228
  25.0 0.0 collective-permute-done.4.refs_5_
  25.0 2.1 %collective-permute-start.9 = (bf16[96,128]{1,0:T(8,128)(2,1)}, bf16[96,128]{1,0:T(8,128)(2,1)S(1)}, u32[]{:S(2)}, u32[]{:S(2)}) collective-permute-start(bf16[96,128]{1,0:T(8,128)(2,1)} %get-tuple-element.28), channel_id=1, source_target_pairs={{0,10},{1,11},{2,8},{3,9},{4,14},{5,15},{6,12},{7,13},{8,2},{9,3},... | collective-permute-start | bytes 73736 | tf_op jit(solution)/shard_map/ppermute | solution.py:228
  27.1 0.0 collective-permute-done.5.refs_6_
  27.1 0.0 collective-permute-done.6.refs_7_
  27.1 0.4 collective-permute-done.7.refs_8_
  27.5 0.3 collective-permute-done.8.refs_9_
  27.8 3.3 %collective-permute-done.9.refs_10_ = bf16[96,128]{1,0:T(8,128)(2,1)S(1)} collective-permute-done((bf16[96,128]{1,0:T(8,128)(2,1)}, bf16[96,128]{1,0:T(8,128)(2,1)S(1)}, u32[]{:S(2)}, u32[]{:S(2)}) %collective-permute-start.9) | collective-permute-done | bytes 24608 | tf_op jit(solution)/shard_map/ppermute | solution.py:228
  31.1 0.0 copy-done.1
  31.1 0.0 copy-done.2
  31.1 0.0 copy-done.3
  31.1 0.0 copy-done
  31.1 2.1 %work.1 = bf16[16,48,128]{2,1,0:T(8,128)(2,1)} custom-call(bf16[96,128]{1,0:T(8,128)(2,1)S(1)} %copy-done, bf16[96,128]{1,0:T(8,128)(2,1)S(1)} %collective-permute-done.refs_1_, bf16[96,128]{1,0:T(8,128)(2,1)S(1)} %collective-permute-done.1.refs_2_, bf16[96,128]{1,0:T(8,128)(2,1)S(1)} %collective-permute-done.2.refs_3_, ...), custom_call_target="tpu_custom_call" | custom-call | tf_op jit(solution)/shard_map/work/pallas_call | solution.py:232
  33.2 3.5 %all-to-all-start = ((bf16[16,48,128]{2,1,0:T(8,128)(2,1)}), bf16[16,48,128]{2,1,0:T(8,128)(2,1)S(1)}, u32[]{:S(2)}, u32[]{:S(2)}) async-start(bf16[16,48,128]{2,1,0:T(8,128)(2,1)} %work.1), calls=%async_computation | async-start | bytes 393216 | tf_op jit(solution)/shard_map/all_to_all | solution.py:246
  36.7 0.0 copy-start.5
  37.4 0.0 copy-start.4
  37.4 0.0 copy-start.6
  37.4 8.3 %all-to-all-done.home_ref = bf16[16,48,128]{2,1,0:T(8,128)(2,1)S(1)} async-done(((bf16[16,48,128]{2,1,0:T(8,128)(2,1)}), bf16[16,48,128]{2,1,0:T(8,128)(2,1)S(1)}, u32[]{:S(2)}, u32[]{:S(2)}) %all-to-all-start) | async-done | bytes 196640 | tf_op jit(solution)/shard_map/all_to_all | solution.py:246
  45.7 0.0 copy-done.5
  45.7 0.0 copy-done.4
  45.7 0.9 %finish.1 = (bf16[1,16,4096]{2,1,0:T(8,128)(2,1)}, f32[1,384]{1,0:T(1,128)}) custom-call(s32[1]{0:T(128)S(6)} %copy.11.length_ref, s32[1,16]{1,0:T(1,128)S(1)} %bitcast.9, s32[1,32]{1,0:T(1,128)S(1)} %bitcast.10, s32[1,384]{1,0:T(1,128)S(1)} %copy-done.5, bf16[16,48,128]{2,1,0:T(8,128)(2,1)S(1)} %all-to-all-done.home_ref), custom_call_target="tpu_custom_call" | custom-call | tf_op jit(solution)/shard_map/finish/pallas_call | solution.py:247
  (1 shorter events, 0.0 us)
Async XLA Ops:
  0.6 30.5 %copy-start.1 = (bf16[1,64,64]{2,1,0:T(8,128)(2,1)S(1)}, bf16[1,64,64]{2,1,0:T(8,128)(2,1)}, u32[]{:S(2)}) copy-start(bf16[1,64,64]{2,1,0:T(8,128)(2,1)} %param.11) | copy-start | bytes 24580
  0.6 30.4 %copy-start.2 = (bf16[1,64,64]{2,1,0:T(8,128)(2,1)S(1)}, bf16[1,64,64]{2,1,0:T(8,128)(2,1)}, u32[]{:S(2)}) copy-start(bf16[1,64,64]{2,1,0:T(8,128)(2,1)} %param.12) | copy-start | bytes 24580
  0.7 30.4 %copy-start.3 = (f32[1,4096]{1,0:T(1,128)S(1)}, f32[1,4096]{1,0:T(1,128)}, u32[]{:S(2)}) copy-start(f32[1,4096]{1,0:T(1,128)} %param.13) | copy-start | bytes 49156
  3.3 27.8 %copy-start = (bf16[96,128]{1,0:T(8,128)(2,1)S(1)}, bf16[96,128]{1,0:T(8,128)(2,1)}, u32[]{:S(2)}) copy-start(bf16[96,128]{1,0:T(8,128)(2,1)} %get-tuple-element.18.refs_0_) | copy-start | bytes 73732
  3.3 8.9 %collective-permute-start = (bf16[96,128]{1,0:T(8,128)(2,1)}, bf16[96,128]{1,0:T(8,128)(2,1)S(1)}, u32[]{:S(2)}, u32[]{:S(2)}) collective-permute-start(bf16[96,128]{1,0:T(8,128)(2,1)} %get-tuple-element.19), channel_id=1, source_target_pairs={{0,1},{1,0},{2,3},{3,2},{4,5},{5,4},{6,7},{7,6},{8,9},{9,8},{10,11... | collective-permute-start | bytes 73736 | tf_op jit(solution)/shard_map/ppermute | solution.py:228
  3.8 10.7 %collective-permute-start.1 = (bf16[96,128]{1,0:T(8,128)(2,1)}, bf16[96,128]{1,0:T(8,128)(2,1)S(1)}, u32[]{:S(2)}, u32[]{:S(2)}) collective-permute-start(bf16[96,128]{1,0:T(8,128)(2,1)} %get-tuple-element.20), channel_id=1, source_target_pairs={{0,2},{1,3},{2,0},{3,1},{4,6},{5,7},{6,4},{7,5},{8,10},{9,11},{10,... | collective-permute-start | bytes 73736 | tf_op jit(solution)/shard_map/ppermute | solution.py:228
  6.4 10.3 %collective-permute-start.10 = (bf16[96,128]{1,0:T(8,128)(2,1)}, bf16[96,128]{1,0:T(8,128)(2,1)S(1)}, u32[]{:S(2)}, u32[]{:S(2)}) collective-permute-start(bf16[96,128]{1,0:T(8,128)(2,1)} %get-tuple-element.29), channel_id=1, source_target_pairs={{0,11},{1,10},{2,9},{3,8},{4,15},{5,14},{6,13},{7,12},{8,3},{9,2},... | collective-permute-start | bytes 73736 | tf_op jit(solution)/shard_map/ppermute | solution.py:228
  8.7 9.5 %collective-permute-start.11 = (bf16[96,128]{1,0:T(8,128)(2,1)}, bf16[96,128]{1,0:T(8,128)(2,1)S(1)}, u32[]{:S(2)}, u32[]{:S(2)}) collective-permute-start(bf16[96,128]{1,0:T(8,128)(2,1)} %get-tuple-element.30), channel_id=1, source_target_pairs={{0,12},{1,13},{2,14},{3,15},{4,8},{5,9},{6,10},{7,11},{8,4},{9,5},... | collective-permute-start | bytes 73736 | tf_op jit(solution)/shard_map/ppermute | solution.py:228
  10.0 8.1 %collective-permute-start.12 = (bf16[96,128]{1,0:T(8,128)(2,1)}, bf16[96,128]{1,0:T(8,128)(2,1)S(1)}, u32[]{:S(2)}, u32[]{:S(2)}) collective-permute-start(bf16[96,128]{1,0:T(8,128)(2,1)} %get-tuple-element.31), channel_id=1, source_target_pairs={{0,13},{1,12},{2,15},{3,14},{4,9},{5,8},{6,11},{7,10},{8,5},{9,4},... | collective-permute-start | bytes 73736 | tf_op jit(solution)/shard_map/ppermute | solution.py:228
  12.2 7.5 %collective-permute-start.13 = (bf16[96,128]{1,0:T(8,128)(2,1)}, bf16[96,128]{1,0:T(8,128)(2,1)S(1)}, u32[]{:S(2)}, u32[]{:S(2)}) collective-permute-start(bf16[96,128]{1,0:T(8,128)(2,1)} %get-tuple-element.32), channel_id=1, source_target_pairs={{0,14},{1,15},{2,12},{3,13},{4,10},{5,11},{6,8},{7,9},{8,6},{9,7},... | collective-permute-start | bytes 73736 | tf_op jit(solution)/shard_map/ppermute | solution.py:228
  14.5 6.2 %collective-permute-start.14 = (bf16[96,128]{1,0:T(8,128)(2,1)}, bf16[96,128]{1,0:T(8,128)(2,1)S(1)}, u32[]{:S(2)}, u32[]{:S(2)}) collective-permute-start(bf16[96,128]{1,0:T(8,128)(2,1)} %get-tuple-element.33), channel_id=1, source_target_pairs={{0,15},{1,14},{2,13},{3,12},{4,11},{5,10},{6,9},{7,8},{8,7},{9,6},... | collective-permute-start | bytes 73736 | tf_op jit(solution)/shard_map/ppermute | solution.py:228
  16.7 5.9 %collective-permute-start.2 = (bf16[96,128]{1,0:T(8,128)(2,1)}, bf16[96,128]{1,0:T(8,128)(2,1)S(1)}, u32[]{:S(2)}, u32[]{:S(2)}) collective-permute-start(bf16[96,128]{1,0:T(8,128)(2,1)} %get-tuple-element.21), channel_id=1, source_target_pairs={{0,3},{1,2},{2,1},{3,0},{4,7},{5,6},{6,5},{7,4},{8,11},{9,10},{10,... | collective-permute-start | bytes 73736 | tf_op jit(solution)/shard_map/ppermute | solution.py:228
  18.2 5.3 %collective-permute-start.3 = (bf16[96,128]{1,0:T(8,128)(2,1)}, bf16[96,128]{1,0:T(8,128)(2,1)S(1)}, u32[]{:S(2)}, u32[]{:S(2)}) collective-permute-start(bf16[96,128]{1,0:T(8,128)(2,1)} %get-tuple-element.22), channel_id=1, source_target_pairs={{0,4},{1,5},{2,6},{3,7},{4,0},{5,1},{6,2},{7,3},{8,12},{9,13},{10,... | collective-permute-start | bytes 73736 | tf_op jit(solution)/shard_map/ppermute | solution.py:228
  18.2 6.8 %collective-permute-start.4 = (bf16[96,128]{1,0:T(8,128)(2,1)}, bf16[96,128]{1,0:T(8,128)(2,1)S(1)}, u32[]{:S(2)}, u32[]{:S(2)}) collective-permute-start(bf16[96,128]{1,0:T(8,128)(2,1)} %get-tuple-element.23), channel_id=1, source_target_pairs={{0,5},{1,4},{2,7},{3,6},{4,1},{5,0},{6,3},{7,2},{8,13},{9,12},{10,... | collective-permute-start | bytes 73736 | tf_op jit(solution)/shard_map/ppermute | solution.py:228
  19.7 7.4 %collective-permute-start.5 = (bf16[96,128]{1,0:T(8,128)(2,1)}, bf16[96,128]{1,0:T(8,128)(2,1)S(1)}, u32[]{:S(2)}, u32[]{:S(2)}) collective-permute-start(bf16[96,128]{1,0:T(8,128)(2,1)} %get-tuple-element.24), channel_id=1, source_target_pairs={{0,6},{1,7},{2,4},{3,5},{4,2},{5,3},{6,0},{7,1},{8,14},{9,15},{10,... | collective-permute-start | bytes 73736 | tf_op jit(solution)/shard_map/ppermute | solution.py:228
  20.7 6.4 %collective-permute-start.6 = (bf16[96,128]{1,0:T(8,128)(2,1)}, bf16[96,128]{1,0:T(8,128)(2,1)S(1)}, u32[]{:S(2)}, u32[]{:S(2)}) collective-permute-start(bf16[96,128]{1,0:T(8,128)(2,1)} %get-tuple-element.25), channel_id=1, source_target_pairs={{0,7},{1,6},{2,5},{3,4},{4,3},{5,2},{6,1},{7,0},{8,15},{9,14},{10,... | collective-permute-start | bytes 73736 | tf_op jit(solution)/shard_map/ppermute | solution.py:228
  22.6 4.9 %collective-permute-start.7 = (bf16[96,128]{1,0:T(8,128)(2,1)}, bf16[96,128]{1,0:T(8,128)(2,1)S(1)}, u32[]{:S(2)}, u32[]{:S(2)}) collective-permute-start(bf16[96,128]{1,0:T(8,128)(2,1)} %get-tuple-element.26), channel_id=1, source_target_pairs={{0,8},{1,9},{2,10},{3,11},{4,12},{5,13},{6,14},{7,15},{8,0},{9,1},... | collective-permute-start | bytes 73736 | tf_op jit(solution)/shard_map/ppermute | solution.py:228
  23.5 4.4 %collective-permute-start.8 = (bf16[96,128]{1,0:T(8,128)(2,1)}, bf16[96,128]{1,0:T(8,128)(2,1)S(1)}, u32[]{:S(2)}, u32[]{:S(2)}) collective-permute-start(bf16[96,128]{1,0:T(8,128)(2,1)} %get-tuple-element.27), channel_id=1, source_target_pairs={{0,9},{1,8},{2,11},{3,10},{4,13},{5,12},{6,15},{7,14},{8,1},{9,0},... | collective-permute-start | bytes 73736 | tf_op jit(solution)/shard_map/ppermute | solution.py:228
  25.0 6.1 %collective-permute-start.9 = (bf16[96,128]{1,0:T(8,128)(2,1)}, bf16[96,128]{1,0:T(8,128)(2,1)S(1)}, u32[]{:S(2)}, u32[]{:S(2)}) collective-permute-start(bf16[96,128]{1,0:T(8,128)(2,1)} %get-tuple-element.28), channel_id=1, source_target_pairs={{0,10},{1,11},{2,8},{3,9},{4,14},{5,15},{6,12},{7,13},{8,2},{9,3},... | collective-permute-start | bytes 73736 | tf_op jit(solution)/shard_map/ppermute | solution.py:228
  33.2 12.5 %all-to-all-start = ((bf16[16,48,128]{2,1,0:T(8,128)(2,1)}), bf16[16,48,128]{2,1,0:T(8,128)(2,1)S(1)}, u32[]{:S(2)}, u32[]{:S(2)}) async-start(bf16[16,48,128]{2,1,0:T(8,128)(2,1)} %work.1), calls=%async_computation | async-start | bytes 393216 | tf_op jit(solution)/shard_map/all_to_all | solution.py:246
  36.7 9.0 %copy-start.5 = (s32[1,384]{1,0:T(1,128)S(1)}, s32[1,384]{1,0:T(1,128)}, u32[]{:S(2)}) copy-start(s32[1,384]{1,0:T(1,128)} %lists_ref.1) | copy-start | bytes 4612
  37.4 8.3 %copy-start.4 = (s32[16]{0:T(128)S(1)}, s32[16]{0:T(128)}, u32[]{:S(2)}) copy-start(s32[16]{0:T(128)} %param.14) | copy-start | bytes 196
  37.4 8.3 %copy-start.6 = (s32[32]{0:T(128)S(1)}, s32[32]{0:T(128)}, u32[]{:S(2)}) copy-start(s32[32]{0:T(128)} %param.15) | copy-start | bytes 388

commit v5 on v1

v5 whole, which is shorter than its diff:
```python
import functools

import jax
import jax.numpy as jnp
from jax import lax
from jax.experimental import pallas as pl
from jax.experimental.pallas import tpu as pltpu
from jax.sharding import PartitionSpec as P

damping = 0.1
LANES = 128
TALL = 32
f32, bf16 = jnp.float32, jnp.bfloat16


def iota(shape, axis):
    return lax.broadcasted_iota(jnp.int32, shape, axis)


def dot(a, b, dims=((1,), (0,))):
    return lax.dot_general(a, b, (dims, ((), ())), preferred_element_type=f32)


def holds(layer_row, modules):
    slots = layer_row.shape[1]
    return (iota((modules, slots), 0) == layer_row).astype(f32).astype(bf16)


def lay_out(layer_row, sources, out_ref, wide):
    modules, flat = sources[0].shape
    slots, height, _ = out_ref.shape
    tall = flat // LANES
    one_hot = holds(layer_row, modules)
    for r, rows in enumerate(sources):
        by_slot = dot(one_hot, rows, ((0,), (0,)))
        for j in range(tall):
            wide[pl.ds(r * tall + j, slots, stride=height), :] = by_slot[:, j * LANES : (j + 1) * LANES]
    out_ref[...] = wide[...].reshape(out_ref.shape).astype(bf16)


def pack_queries(layer_hbm, query_hbm, out_ref, layer_ref, query_ref, wide, sems):
    arrivals = [
        pltpu.make_async_copy(source, target, sems.at[i])
        for i, (source, target) in enumerate(((layer_hbm, layer_ref), (query_hbm, query_ref)))
    ]
    for arrival in arrivals:
        arrival.start()
    for arrival in arrivals:
        arrival.wait()
    lay_out(layer_ref[...], [query_ref[r] for r in range(query_ref.shape[0])], out_ref, wide)


def pack_cands(layer_ref, cand_ref, out_ref, wide):
    lay_out(layer_ref[...], [cand_ref[r] for r in range(cand_ref.shape[0])], out_ref, wide)


def half(left, right):
    return jnp.where(iota(left.shape, 1) < LANES // 2, left, right)


def swap(block):
    return pltpu.roll(block, LANES // 2, 1)


def work(moved_ref, out_basis_ref, in_basis_ref, eigen_ref, out_ref):
    sources, tall, _ = moved_ref.shape
    side = out_basis_ref.shape[0]
    out_basis = out_basis_ref[...]
    in_basis = in_basis_ref[...]

    order = (iota((side, side), 1) == 2 * (iota((side, side), 0) % tall) + iota((side, side), 0) // tall)
    order = order.astype(f32).astype(bf16)
    basis = dot(dot(order, out_basis).astype(bf16), order, ((1,), (1,))).astype(bf16)
    twice = (iota((LANES, side), 0) % side == iota((LANES, side), 1)).astype(f32).astype(bf16)
    spread = dot(dot(twice, in_basis).astype(bf16), twice, ((1,), (1,)))
    same = iota((LANES, LANES), 0) // side == iota((LANES, LANES), 1) // side
    inner = jnp.where(same, spread, 0.0).astype(bf16)
    eigen = eigen_ref[...]
    turned = swap(eigen)
    factor = 1.0 / (jnp.concatenate([half(eigen, turned), half(turned, eigen)], axis=0) + damping)

    pairs = []
    for p in range(sources // 2):
        a = moved_ref[2 * p].astype(f32)
        b = moved_ref[2 * p + 1].astype(f32)
        pairs.append(jnp.concatenate([half(a, swap(b)), half(swap(a), b)], axis=0).astype(bf16))

    def stack(wide):
        return jnp.concatenate([wide[:, p * LANES : (p + 1) * LANES] for p in range(len(pairs))], axis=0)

    def spread_out(rows):
        return jnp.concatenate([rows[p * side : (p + 1) * side] for p in range(len(pairs))], axis=1)

    applied = spread_out(dot(jnp.concatenate(pairs, axis=0), inner).astype(bf16))
    rotated = stack(dot(basis, applied, ((0,), (0,))))
    scaled = (rotated.reshape(len(pairs), side, LANES) * factor[None]).reshape(rotated.shape).astype(bf16)
    returned = spread_out(dot(scaled, inner, ((1,), (1,))).astype(bf16))
    precond = dot(basis, returned).astype(bf16).astype(f32)
    for p in range(len(pairs)):
        top = precond[:tall, p * LANES : (p + 1) * LANES]
        low = precond[tall:, p * LANES : (p + 1) * LANES]
        out_ref[2 * p] = half(top, swap(low)).astype(bf16)
        out_ref[2 * p + 1] = half(swap(top), low).astype(bf16)


def flatten(block_ref, wide):
    wide[...] = block_ref[...].reshape(wide.shape).astype(f32)
    count = wide.shape[0] // TALL
    return jnp.concatenate(
        [wide[pl.ds(j, count, stride=TALL), :].astype(bf16) for j in range(TALL)], axis=1
    )


def compare(precond_ref, moved_ref, out_ref, queries, cands):
    partial = dot(flatten(precond_ref, queries), flatten(moved_ref, cands), ((1,), (1,)))
    sources, count = partial.shape
    width = out_ref.shape[2]
    if width > count:
        partial = jnp.concatenate([partial, jnp.zeros((sources, width - count), f32)], axis=1)
    out_ref[...] = partial.reshape(out_ref.shape)


def come_home(layer_ref, home_ref, precond_ref, wide):
    precond_ref[0] = dot(holds(layer_ref[...], precond_ref.shape[1]), flatten(home_ref, wide)).astype(bf16)


def upright(row):
    n = row.shape[1]
    return jnp.sum(jnp.where(iota((n, n), 0) == iota((n, n), 1), row, 0.0), axis=1, keepdims=True)


def finish(length_ref, rows_ref, lists_ref, partial_ref, scores_ref):
    count = rows_ref.shape[1]
    dense = jnp.sum(partial_ref[...], axis=0)[:, :count]
    by_cand = jnp.sum(
        jnp.where(iota((count, count), 0) == rows_ref[...], upright(dense), 0.0), axis=0, keepdims=True
    )
    lists = lists_ref[...]
    longest = lists.shape[1]
    picked = jnp.sum(
        jnp.where(iota((count, longest), 0) == lists, upright(by_cand), 0.0), axis=0, keepdims=True
    )
    scores_ref[...] = jnp.where(iota((1, longest), 1) < length_ref[0], picked, 0.0)


VMEM = pl.BlockSpec(memory_space=pltpu.VMEM)
HBM = pl.BlockSpec(memory_space=pltpu.HBM)
SMEM = pl.BlockSpec(memory_space=pltpu.SMEM)
PARAMS = pltpu.CompilerParams(vmem_limit_bytes=40 * 1024 * 1024)
FULL = pltpu.CompilerParams(vmem_limit_bytes=56 * 1024 * 1024)


def body(
    query_grads,
    cand_grads,
    basis_out,
    basis_in,
    eigvals,
    layer_map,
    cand_rows,
    cand_lists,
    list_lengths,
):
    own, modules, flat = query_grads.shape
    per = cand_grads.shape[0]
    slots = layer_map.shape[0]
    tall = flat // LANES
    count = cand_rows.shape[0]
    layer_row = layer_map.reshape(1, slots)
    width = -(-count // LANES) * LANES

    def swap_over(x):
        return lax.all_to_all(x, "shard", split_axis=0, concat_axis=0, tiled=True)

    def scratch(rows):
        return pltpu.VMEM((rows * tall, LANES), f32)

    packed_queries = pl.pallas_call(
        pack_queries,
        out_shape=jax.ShapeDtypeStruct((slots, own * tall, LANES), bf16),
        in_specs=[HBM] * 2,
        out_specs=VMEM,
        scratch_shapes=[
            pltpu.VMEM(layer_row.shape, jnp.int32),
            pltpu.VMEM(query_grads.shape, bf16),
            scratch(slots * own),
            pltpu.SemaphoreType.DMA((2,)),
        ],
        compiler_params=FULL,
        name="pack_queries",
    )(layer_row, query_grads)
    moved_queries = swap_over(packed_queries)
    packed_cands = pl.pallas_call(
        pack_cands,
        out_shape=jax.ShapeDtypeStruct((slots, per * tall, LANES), bf16),
        in_specs=[VMEM] * 2,
        out_specs=VMEM,
        scratch_shapes=[scratch(slots * per)],
        compiler_params=PARAMS,
        name="pack_cands",
    )(layer_row, cand_grads)
    moved_cands = swap_over(packed_cands)
    sources = moved_queries.shape[0]
    precond = pl.pallas_call(
        work,
        out_shape=jax.ShapeDtypeStruct(moved_queries.shape, bf16),
        in_specs=[VMEM] * 4,
        out_specs=VMEM,
        compiler_params=PARAMS,
        name="work",
    )(
        moved_queries,
        basis_out.reshape(basis_out.shape[1:]),
        basis_in.reshape(basis_in.shape[1:]),
        eigvals.reshape(tall, LANES),
    )
    home = swap_over(precond)
    partial = pl.pallas_call(
        compare,
        out_shape=jax.ShapeDtypeStruct((sources, 1, width), f32),
        in_specs=[VMEM] * 2,
        out_specs=VMEM,
        scratch_shapes=[scratch(sources * own), scratch(sources * per)],
        compiler_params=PARAMS,
        name="compare",
    )(precond, moved_cands)
    partials = swap_over(partial)
    preconditioned = pl.pallas_call(
        come_home,
        out_shape=jax.ShapeDtypeStruct(query_grads.shape, bf16),
        in_specs=[VMEM] * 2,
        out_specs=VMEM,
        scratch_shapes=[scratch(slots * own)],
        compiler_params=PARAMS,
        name="come_home",
    )(layer_row, home)
    scores = pl.pallas_call(
        finish,
        out_shape=jax.ShapeDtypeStruct(cand_lists.shape, f32),
        in_specs=[SMEM] + [VMEM] * 3,
        out_specs=VMEM,
        compiler_params=PARAMS,
        name="finish",
    )(list_lengths, cand_rows.reshape(1, count), cand_lists, partials)
    return preconditioned, scores


def solution(mesh):
    return jax.shard_map(
        body,
        mesh=mesh,
        in_specs=(
            P(("groups", "shard"), None, None),
            P(("groups", "shard"), None, None),
            P("shard", None, None),
            P("shard", None, None),
            P("shard", None),
            P(),
            P("groups"),
            P(("groups", "shard"), None),
            P(("groups", "shard")),
        ),
        out_specs=(P(("groups", "shard"), None, None), P(("groups", "shard"), None)),
        check_vma=False,
    )
```

time: 39.3 us -> 54.2 us (1.38)
  blocking collectives: 19.5 us -> 0 us
  waiting for transfers between devices: 8.3 us -> 25.6 us
  starting transfers between devices: 3.53 us -> 18 us
  Pallas kernels: 3.67 us -> 8.59 us
  local copies, waits for them, and re-layouts: 2.53 us -> 0.03 us
    all_to_all x1 -> x0, blocking collectives: 19.5 us -> none  [body(): lax.all_to_all(packed, 'shard', split_axis=0, concat_axis=0, tiled=True)]
    all_to_all x1 -> x4, waiting for transfers between devices: 8.3 us -> 25.6 us  [swap_over(): return lax.all_to_all(x, 'shard', split_axis=0, concat_axis=0, tiled=True)]
    all_to_all x1 -> x4, starting transfers between devices: 3.53 us -> 18 us  [swap_over(): return lax.all_to_all(x, 'shard', split_axis=0, concat_axis=0, tiled=True)]
    pallas_call x3 -> x6, Pallas kernels: 3.67 us -> 8.59 us  [the longest x1 2.12 us: body(): pl.pallas_call(compare, out_shape=jax.ShapeDtypeStruct((sources, 1, width...]
    unnamed x16 -> x14, local copies, waits for them, and re-layouts: 2.53 us -> 0.03 us
  transfers between devices with their start and end apart: 1 -> 4, of which waited for: 1 -> 4; matrix products, arithmetic and copies ran while one was open for 0% -> 0% of each run, Pallas kernels for 0% -> 11%
where the time goes in v5:
time: 54.2 us; the launch traced here: 53.7 us
  waiting for transfers between devices  25.6 us (47%)
  starting transfers between devices  18 us (33%)
  Pallas kernels  8.59 us (16%)
  between operations  1.39 us (3%)
    all_to_all x4, waiting for transfers between devices, swap_over(): return lax.all_to_all(x, 'shard', split_axis=0, concat_axis=0, tiled=True)  25.6 us
    all_to_all x4, starting transfers between devices, swap_over(): return lax.all_to_all(x, 'shard', split_axis=0, concat_axis=0, tiled=True)  18 us
    pallas_call x1, Pallas kernels, body(): pl.pallas_call(compare, out_shape=jax.ShapeDtypeStruct((sources, 1, width...  2.12 us
    pallas_call x1, Pallas kernels, body(): pl.pallas_call(pack_queries, out_shape=jax.ShapeDtypeStruct((slots, own *...  1.98 us
    pallas_call x1, Pallas kernels, body(): pl.pallas_call(work, out_shape=jax.ShapeDtypeStruct(moved_queries.shape,...  1.57 us
    pallas_call x1, Pallas kernels, body(): pl.pallas_call(pack_cands, out_shape=jax.ShapeDtypeStruct((slots, per * t...  1.23 us
  transfers between devices with their start and end apart: 4, of which 4 were waited for; matrix products, arithmetic and copies ran while one was open for 0% of the time, Pallas kernels for 11%

profile of v5, /device:TPU:0, one launch (start us, length us, event | category | flops | bytes accessed | tf_op | source)
XLA Modules:
  0.0 53.7 jit_solution(17970729126477981087)
XLA Ops:
  0.6 0.0 copy-start
  0.6 2.0 %pack_queries.1 = bf16[16,32,128]{2,1,0:T(8,128)(2,1)} custom-call(s32[1,16]{1,0:T(1,128)} %bitcast.8, bf16[1,16,4096]{2,1,0:T(8,128)(2,1)} %query_hbm.1), custom_call_target="tpu_custom_call" | custom-call | tf_op jit(solution)/shard_map/pack_queries/pallas_call | solution.py:178
  2.6 0.0 copy-start.4
  2.6 7.4 %all-to-all-start = ((bf16[16,32,128]{2,1,0:T(8,128)(2,1)}), bf16[16,32,128]{2,1,0:T(8,128)(2,1)S(1)}, u32[]{:S(2)}, u32[]{:S(2)}) async-start(bf16[16,32,128]{2,1,0:T(8,128)(2,1)} %pack_queries.1), calls=%async_computation | async-start | bytes 262144 | tf_op jit(solution)/shard_map/all_to_all | solution.py:173
  10.0 0.0 copy-done
  10.1 0.0 copy-done.4
  10.1 1.2 %pack_cands.1 = bf16[16,64,128]{2,1,0:T(8,128)(2,1)} custom-call(s32[1,16]{1,0:T(1,128)S(1)} %bitcast.9, bf16[2,16,4096]{2,1,0:T(8,128)(2,1)S(1)} %copy-done), custom_call_target="tpu_custom_call" | custom-call | tf_op jit(solution)/shard_map/pack_cands/pallas_call | solution.py:193
  11.3 6.7 %all-to-all-done.moved_ref = bf16[16,32,128]{2,1,0:T(8,128)(2,1)S(1)} async-done(((bf16[16,32,128]{2,1,0:T(8,128)(2,1)}), bf16[16,32,128]{2,1,0:T(8,128)(2,1)S(1)}, u32[]{:S(2)}, u32[]{:S(2)}) %all-to-all-start) | async-done | bytes 131104 | tf_op jit(solution)/shard_map/all_to_all | solution.py:173
  18.0 0.0 copy-start.1
  18.0 0.0 copy-start.2
  18.0 0.0 copy-start.3
  18.0 3.7 %all-to-all-start.2 = ((bf16[16,64,128]{2,1,0:T(8,128)(2,1)}), bf16[16,64,128]{2,1,0:T(8,128)(2,1)S(1)}, u32[]{:S(2)}, u32[]{:S(2)}) async-start(bf16[16,64,128]{2,1,0:T(8,128)(2,1)} %pack_cands.1), calls=%async_computation.2 | async-start | bytes 524288 | tf_op jit(solution)/shard_map/all_to_all | solution.py:173
  21.7 0.0 copy-done.1
  21.7 0.0 copy-done.2
  21.7 0.0 copy-done.3
  21.7 1.6 %work.1.precond_ref = bf16[16,32,128]{2,1,0:T(8,128)(2,1)} custom-call(bf16[16,32,128]{2,1,0:T(8,128)(2,1)S(1)} %all-to-all-done.moved_ref, bf16[64,64]{1,0:T(8,128)(2,1)S(1)} %bitcast.5, bf16[64,64]{1,0:T(8,128)(2,1)S(1)} %bitcast.6, f32[32,128]{1,0:T(8,128)S(1)} %bitcast.7), custom_call_target="tpu_custom_call" | custom-call | tf_op jit(solution)/shard_map/work/pallas_call | solution.py:204
  23.3 8.4 %all-to-all-done.2.moved_ref = bf16[16,64,128]{2,1,0:T(8,128)(2,1)S(1)} async-done(((bf16[16,64,128]{2,1,0:T(8,128)(2,1)}), bf16[16,64,128]{2,1,0:T(8,128)(2,1)S(1)}, u32[]{:S(2)}, u32[]{:S(2)}) %all-to-all-start.2) | async-done | bytes 262176 | tf_op jit(solution)/shard_map/all_to_all | solution.py:173
  31.7 3.5 %all-to-all-start.1 = ((bf16[16,32,128]{2,1,0:T(8,128)(2,1)}), bf16[16,32,128]{2,1,0:T(8,128)(2,1)S(1)}, u32[]{:S(2)}, u32[]{:S(2)}) async-start(bf16[16,32,128]{2,1,0:T(8,128)(2,1)} %work.1.precond_ref), calls=%async_computation.1 | async-start | bytes 262144 | tf_op jit(solution)/shard_map/all_to_all | solution.py:173
  35.2 2.1 %compare.1 = f32[16,1,128]{2,1,0:T(1,128)} custom-call(bf16[16,32,128]{2,1,0:T(8,128)(2,1)} %work.1.precond_ref, bf16[16,64,128]{2,1,0:T(8,128)(2,1)S(1)} %all-to-all-done.2.moved_ref), custom_call_target="tpu_custom_call" | custom-call | tf_op jit(solution)/shard_map/compare/pallas_call | solution.py:218
  37.3 5.8 %all-to-all-done.1.home_ref = bf16[16,32,128]{2,1,0:T(8,128)(2,1)S(1)} async-done(((bf16[16,32,128]{2,1,0:T(8,128)(2,1)}), bf16[16,32,128]{2,1,0:T(8,128)(2,1)S(1)}, u32[]{:S(2)}, u32[]{:S(2)}) %all-to-all-start.1) | async-done | bytes 131104 | tf_op jit(solution)/shard_map/all_to_all | solution.py:173
  43.1 3.5 %all-to-all-start.3 = ((f32[16,1,128]{2,1,0:T(1,128)}), f32[16,1,128]{2,1,0:T(1,128)S(1)}, u32[]{:S(2)}, u32[]{:S(2)}) async-start(f32[16,1,128]{2,1,0:T(1,128)} %compare.1), calls=%async_computation.3 | async-start | bytes 16384 | tf_op jit(solution)/shard_map/all_to_all | solution.py:173
  47.2 0.0 copy-start.6
  47.2 0.9 %come_home.1 = bf16[1,16,4096]{2,1,0:T(8,128)(2,1)} custom-call(s32[1,16]{1,0:T(1,128)S(1)} %bitcast.10, bf16[16,32,128]{2,1,0:T(8,128)(2,1)S(1)} %all-to-all-done.1.home_ref), custom_call_target="tpu_custom_call" | custom-call | tf_op jit(solution)/shard_map/come_home/pallas_call | solution.py:228
  48.1 0.0 copy-start.5
  48.1 4.8 %all-to-all-done.3.partial_ref = f32[16,1,128]{2,1,0:T(1,128)S(1)} async-done(((f32[16,1,128]{2,1,0:T(1,128)}), f32[16,1,128]{2,1,0:T(1,128)S(1)}, u32[]{:S(2)}, u32[]{:S(2)}) %all-to-all-start.3) | async-done | bytes 8224 | tf_op jit(solution)/shard_map/all_to_all | solution.py:173
  52.9 0.0 copy-done.6
  52.9 0.0 copy-done.5
  52.9 0.8 %finish.1 = f32[1,384]{1,0:T(1,128)} custom-call(s32[1]{0:T(128)S(6)} %copy.11.length_ref, s32[1,32]{1,0:T(1,128)S(1)} %bitcast.11, s32[1,384]{1,0:T(1,128)S(1)} %copy-done.5, f32[16,1,128]{2,1,0:T(1,128)S(1)} %all-to-all-done.3.partial_ref), custom_call_target="tpu_custom_call" | custom-call | tf_op jit(solution)/shard_map/finish/pallas_call | solution.py:237
Async XLA Ops:
  0.6 9.4 %copy-start = (bf16[2,16,4096]{2,1,0:T(8,128)(2,1)S(1)}, bf16[2,16,4096]{2,1,0:T(8,128)(2,1)}, u32[]{:S(2)}) copy-start(bf16[2,16,4096]{2,1,0:T(8,128)(2,1)} %cand_ref.1) | copy-start | bytes 786436
  2.6 7.4 %copy-start.4 = (s32[16]{0:T(128)S(1)}, s32[16]{0:T(128)}, u32[]{:S(2)}) copy-start(s32[16]{0:T(128)} %param.14) | copy-start | bytes 196
  2.6 15.3 %all-to-all-start = ((bf16[16,32,128]{2,1,0:T(8,128)(2,1)}), bf16[16,32,128]{2,1,0:T(8,128)(2,1)S(1)}, u32[]{:S(2)}, u32[]{:S(2)}) async-start(bf16[16,32,128]{2,1,0:T(8,128)(2,1)} %pack_queries.1), calls=%async_computation | async-start | bytes 262144 | tf_op jit(solution)/shard_map/all_to_all | solution.py:173
  18.0 3.7 %copy-start.1 = (bf16[1,64,64]{2,1,0:T(8,128)(2,1)S(1)}, bf16[1,64,64]{2,1,0:T(8,128)(2,1)}, u32[]{:S(2)}) copy-start(bf16[1,64,64]{2,1,0:T(8,128)(2,1)} %param.11) | copy-start | bytes 24580
  18.0 3.7 %copy-start.2 = (bf16[1,64,64]{2,1,0:T(8,128)(2,1)S(1)}, bf16[1,64,64]{2,1,0:T(8,128)(2,1)}, u32[]{:S(2)}) copy-start(bf16[1,64,64]{2,1,0:T(8,128)(2,1)} %param.12) | copy-start | bytes 24580
  18.0 3.7 %copy-start.3 = (f32[1,4096]{1,0:T(1,128)S(1)}, f32[1,4096]{1,0:T(1,128)}, u32[]{:S(2)}) copy-start(f32[1,4096]{1,0:T(1,128)} %param.13) | copy-start | bytes 49156
  18.0 13.7 %all-to-all-start.2 = ((bf16[16,64,128]{2,1,0:T(8,128)(2,1)}), bf16[16,64,128]{2,1,0:T(8,128)(2,1)S(1)}, u32[]{:S(2)}, u32[]{:S(2)}) async-start(bf16[16,64,128]{2,1,0:T(8,128)(2,1)} %pack_cands.1), calls=%async_computation.2 | async-start | bytes 524288 | tf_op jit(solution)/shard_map/all_to_all | solution.py:173
  31.7 11.4 %all-to-all-start.1 = ((bf16[16,32,128]{2,1,0:T(8,128)(2,1)}), bf16[16,32,128]{2,1,0:T(8,128)(2,1)S(1)}, u32[]{:S(2)}, u32[]{:S(2)}) async-start(bf16[16,32,128]{2,1,0:T(8,128)(2,1)} %work.1.precond_ref), calls=%async_computation.1 | async-start | bytes 262144 | tf_op jit(solution)/shard_map/all_to_all | solution.py:173
  43.1 9.8 %all-to-all-start.3 = ((f32[16,1,128]{2,1,0:T(1,128)}), f32[16,1,128]{2,1,0:T(1,128)S(1)}, u32[]{:S(2)}, u32[]{:S(2)}) async-start(f32[16,1,128]{2,1,0:T(1,128)} %compare.1), calls=%async_computation.3 | async-start | bytes 16384 | tf_op jit(solution)/shard_map/all_to_all | solution.py:173
  47.2 5.7 %copy-start.6 = (s32[32]{0:T(128)S(1)}, s32[32]{0:T(128)}, u32[]{:S(2)}) copy-start(s32[32]{0:T(128)} %param.15) | copy-start | bytes 388
  48.1 4.8 %copy-start.5 = (s32[1,384]{1,0:T(1,128)S(1)}, s32[1,384]{1,0:T(1,128)}, u32[]{:S(2)}) copy-start(s32[1,384]{1,0:T(1,128)} %lists_ref.1) | copy-start | bytes 4612

commit v6 on v2

--- a/solution.py
+++ b/solution.py
@@ -21,8 +21,14 @@
     return lax.dot_general(a, b, (dims, ((), ())), preferred_element_type=f32)
 
 
+def first_of(slots):
+    return slots // 4
+
+
 def holds(layer_row, modules):
     slots = layer_row.shape[1]
+    first = first_of(slots)
+    layer_row = jnp.concatenate([layer_row[:, first:], layer_row[:, :first]], axis=1)
     return (iota((modules, slots), 0) == layer_row).astype(f32).astype(bf16)
 
 
@@ -144,8 +150,11 @@
         parts.append(jnp.sum((pieces[2] + pieces[1]) + pieces[0], axis=0, keepdims=True))
     dense = parts[0] if groups == 1 else jnp.concatenate(parts, axis=1)
     dense = dense[:, :count]
+    ahead = first_of(slots) * (count // slots)
+    place = rows_ref[...] - ahead
+    place = jnp.where(place < 0, place + count, place)
     by_cand = jnp.sum(
-        jnp.where(iota((count, count), 0) == rows_ref[...], upright(dense), 0.0), axis=0, keepdims=True
+        jnp.where(iota((count, count), 0) == place, upright(dense), 0.0), axis=0, keepdims=True
     )
     lists = lists_ref[...]
     longest = lists.shape[1]
@@ -180,7 +189,14 @@
     count = cand_rows.shape[0]
     layer_row = layer_map.reshape(1, slots)
     height = (own + per) * tall
-    send = tall + -(-PIECES * -(-count // LANES) // 16) * 16
+    send = tall + -(-PIECES * -(-count // LANES) // 8) * 8
+    order = [(first_of(slots) + k) % slots for k in range(slots)]
+
+    def swap_over(x):
+        return lax.all_to_all(
+            x, "shard", split_axis=0, concat_axis=0, tiled=True, axis_index_groups=[order]
+        )
+
 
     packed = pl.pallas_call(
         pack,
@@ -197,7 +213,7 @@
         compiler_params=FULL,
         name="pack",
     )(layer_row, query_grads, cand_grads)
-    moved = lax.all_to_all(packed, "shard", split_axis=0, concat_axis=0, tiled=True)
+    moved = swap_over(packed)
     sources = moved.shape[0]
     homes = pl.pallas_call(
         work,
@@ -213,7 +229,7 @@
         basis_in.reshape(basis_in.shape[1:]),
         eigvals.reshape(tall, LANES),
     )
-    home = lax.all_to_all(homes, "shard", split_axis=0, concat_axis=0, tiled=True)
+    home = swap_over(homes)
     return pl.pallas_call(
         finish,
         out_shape=(

time: 38.8 us -> 36.6 us (0.943)
  waiting for transfers between devices: 8.29 us -> 6.39 us
  blocking collectives: 19.7 us -> 18.8 us
  starting transfers between devices: 3.53 us -> 4.1 us
    all_to_all x1, waiting for transfers between devices: 8.29 us -> 6.39 us  [swap_over(): lax.all_to_all(x, 'shard', split_axis=0, concat_axis=0, tiled=True, axis_...]
    all_to_all x1, blocking collectives: 19.7 us -> 18.8 us  [swap_over(): lax.all_to_all(x, 'shard', split_axis=0, concat_axis=0, tiled=True, axis_...]
    all_to_all x1, starting transfers between devices: 3.53 us -> 4.1 us  [swap_over(): lax.all_to_all(x, 'shard', split_axis=0, concat_axis=0, tiled=True, axis_...]
where the time goes in v6:
time: 36.6 us; the launch traced here: 36.2 us
  blocking collectives  18.8 us (51%)
  waiting for transfers between devices  6.39 us (17%)
  Pallas kernels  5.48 us (15%)
  starting transfers between devices  4.1 us (11%)
  between operations  1.35 us (4%)
    all_to_all x1, blocking collectives, swap_over(): lax.all_to_all(x, 'shard', split_axis=0, concat_axis=0, tiled=True, axis_...  18.8 us
    all_to_all x1, waiting for transfers between devices, swap_over(): lax.all_to_all(x, 'shard', split_axis=0, concat_axis=0, tiled=True, axis_...  6.39 us
    all_to_all x1, starting transfers between devices, swap_over(): lax.all_to_all(x, 'shard', split_axis=0, concat_axis=0, tiled=True, axis_...  4.1 us
    pallas_call x1, Pallas kernels, body(): pl.pallas_call(pack, out_shape=jax.ShapeDtypeStruct((slots, height, LANES...  2.56 us
    pallas_call x1, Pallas kernels, body(): pl.pallas_call(work, out_shape=jax.ShapeDtypeStruct((sources, send, LANES...  2.03 us
    pallas_call x1, Pallas kernels, body(): pl.pallas_call(finish, out_shape=(jax.ShapeDtypeStruct(query_grads.shape,...  0.89 us
  transfers between devices with their start and end apart: 1, of which 1 were waited for; matrix products, arithmetic and copies ran while one was open for 0% of the time, Pallas kernels for 0%

profile of v6, /device:TPU:0, one launch (start us, length us, event | category | flops | bytes accessed | tf_op | source)
XLA Modules:
  0.0 36.2 jit_solution(2354442125575013367)
XLA Ops:
  0.6 2.6 %pack.1 = bf16[16,96,128]{2,1,0:T(8,128)(2,1)} custom-call(s32[1,16]{1,0:T(1,128)} %bitcast.8, bf16[1,16,4096]{2,1,0:T(8,128)(2,1)} %query_hbm.1, bf16[2,16,4096]{2,1,0:T(8,128)(2,1)} %cand_hbm.1), custom_call_target="tpu_custom_call" | custom-call | tf_op jit(solution)/shard_map/pack/pallas_call | solution.py:201
  3.2 0.0 copy-start
  3.2 0.0 copy-start.1
  3.2 0.0 copy-start.2
  3.2 18.8 %all_to_all.10.moved_ref = bf16[16,96,128]{2,1,0:T(8,128)(2,1)S(1)} all-to-all(bf16[16,96,128]{2,1,0:T(8,128)(2,1)} %pack.1), channel_id=1, replica_groups={{4,5,6,7,8,9,10,11,12,13,14,15,0,1,2,3},{20,21,22,23,24,25,26,27,28,29,..., dimensions={0} | all-to-all | bytes 786432 | tf_op jit(solution)/shard_map/all_to_all | solution.py:196
  22.1 0.0 copy-done
  22.1 0.0 copy-done.1
  22.1 0.0 copy-done.2
  22.1 2.0 %work.1 = bf16[16,40,128]{2,1,0:T(8,128)(2,1)} custom-call(bf16[16,96,128]{2,1,0:T(8,128)(2,1)S(1)} %all_to_all.10.moved_ref, bf16[64,64]{1,0:T(8,128)(2,1)S(1)} %bitcast.5, bf16[64,64]{1,0:T(8,128)(2,1)S(1)} %bitcast.6, f32[32,128]{1,0:T(8,128)S(1)} %bitcast.7), custom_call_target="tpu_custom_call" | custom-call | tf_op jit(solution)/shard_map/work/pallas_call | solution.py:218
  24.1 4.1 %all-to-all-start.1 = ((bf16[16,40,128]{2,1,0:T(8,128)(2,1)}), bf16[16,40,128]{2,1,0:T(8,128)(2,1)S(1)}, u32[]{:S(2)}, u32[]{:S(2)}) async-start(bf16[16,40,128]{2,1,0:T(8,128)(2,1)} %work.1), calls=%async_computation.1 | async-start | bytes 327680 | tf_op jit(solution)/shard_map/all_to_all | solution.py:196
  28.2 0.0 copy-start.4
  28.9 0.0 copy-start.3
  28.9 0.0 copy-start.5
  28.9 6.4 %all-to-all-done.1.home_ref = bf16[16,40,128]{2,1,0:T(8,128)(2,1)S(1)} async-done(((bf16[16,40,128]{2,1,0:T(8,128)(2,1)}), bf16[16,40,128]{2,1,0:T(8,128)(2,1)S(1)}, u32[]{:S(2)}, u32[]{:S(2)}) %all-to-all-start.1) | async-done | bytes 163872 | tf_op jit(solution)/shard_map/all_to_all | solution.py:196
  35.3 0.0 copy-done.4
  35.3 0.0 copy-done.3
  35.3 0.0 copy-done.5
  35.3 0.9 %finish.1 = (bf16[1,16,4096]{2,1,0:T(8,128)(2,1)}, f32[1,384]{1,0:T(1,128)}) custom-call(s32[1]{0:T(128)S(6)} %copy.11.length_ref, s32[1,16]{1,0:T(1,128)S(1)} %bitcast.9, s32[1,32]{1,0:T(1,128)S(1)} %bitcast.10, s32[1,384]{1,0:T(1,128)S(1)} %copy-done.4, bf16[16,40,128]{2,1,0:T(8,128)(2,1)S(1)} %all-to-all-done.1.home_ref), custom_call_target="tpu_custom_call" | custom-call | tf_op jit(solution)/shard_map/finish/pallas_call | solution.py:233
Async XLA Ops:
  3.2 18.9 %copy-start = (bf16[1,64,64]{2,1,0:T(8,128)(2,1)S(1)}, bf16[1,64,64]{2,1,0:T(8,128)(2,1)}, u32[]{:S(2)}) copy-start(bf16[1,64,64]{2,1,0:T(8,128)(2,1)} %param.11) | copy-start | bytes 24580
  3.2 18.9 %copy-start.1 = (bf16[1,64,64]{2,1,0:T(8,128)(2,1)S(1)}, bf16[1,64,64]{2,1,0:T(8,128)(2,1)}, u32[]{:S(2)}) copy-start(bf16[1,64,64]{2,1,0:T(8,128)(2,1)} %param.12) | copy-start | bytes 24580
  3.2 18.8 %copy-start.2 = (f32[1,4096]{1,0:T(1,128)S(1)}, f32[1,4096]{1,0:T(1,128)}, u32[]{:S(2)}) copy-start(f32[1,4096]{1,0:T(1,128)} %param.13) | copy-start | bytes 49156
  24.1 11.2 %all-to-all-start.1 = ((bf16[16,40,128]{2,1,0:T(8,128)(2,1)}), bf16[16,40,128]{2,1,0:T(8,128)(2,1)S(1)}, u32[]{:S(2)}, u32[]{:S(2)}) async-start(bf16[16,40,128]{2,1,0:T(8,128)(2,1)} %work.1), calls=%async_computation.1 | async-start | bytes 327680 | tf_op jit(solution)/shard_map/all_to_all | solution.py:196
  28.2 7.1 %copy-start.4 = (s32[1,384]{1,0:T(1,128)S(1)}, s32[1,384]{1,0:T(1,128)}, u32[]{:S(2)}) copy-start(s32[1,384]{1,0:T(1,128)} %lists_ref.1) | copy-start | bytes 4612
  28.9 6.4 %copy-start.3 = (s32[16]{0:T(128)S(1)}, s32[16]{0:T(128)}, u32[]{:S(2)}) copy-start(s32[16]{0:T(128)} %param.14) | copy-start | bytes 196
  28.9 6.4 %copy-start.5 = (s32[32]{0:T(128)S(1)}, s32[32]{0:T(128)}, u32[]{:S(2)}) copy-start(s32[32]{0:T(128)} %param.15) | copy-start | bytes 388

commit v7 on v6

--- a/solution.py
+++ b/solution.py
@@ -22,7 +22,7 @@
 
 
 def first_of(slots):
-    return slots // 4
+    return slots - 2
 
 
 def holds(layer_row, modules):

time: 36.6 us -> 36.9 us (level)
  starting transfers between devices: 4.1 us -> 7.77 us
  waiting for transfers between devices: 6.39 us -> 3.85 us
  blocking collectives: 18.8 us -> 18 us
    all_to_all x1, starting transfers between devices: 4.1 us -> 7.77 us  [swap_over(): lax.all_to_all(x, 'shard', split_axis=0, concat_axis=0, tiled=True, axis_...]
    all_to_all x1, waiting for transfers between devices: 6.39 us -> 3.85 us  [swap_over(): lax.all_to_all(x, 'shard', split_axis=0, concat_axis=0, tiled=True, axis_...]
    all_to_all x1, blocking collectives: 18.8 us -> 18 us  [swap_over(): lax.all_to_all(x, 'shard', split_axis=0, concat_axis=0, tiled=True, axis_...]
where the time goes in v7:
time: 36.9 us; the launch traced here: 36.5 us
  blocking collectives  18 us (49%)
  starting transfers between devices  7.77 us (21%)
  Pallas kernels  5.48 us (15%)
  waiting for transfers between devices  3.85 us (10%)
  between operations  1.35 us (4%)
    all_to_all x1, blocking collectives, swap_over(): lax.all_to_all(x, 'shard', split_axis=0, concat_axis=0, tiled=True, axis_...  18 us
    all_to_all x1, starting transfers between devices, swap_over(): lax.all_to_all(x, 'shard', split_axis=0, concat_axis=0, tiled=True, axis_...  7.77 us
    all_to_all x1, waiting for transfers between devices, swap_over(): lax.all_to_all(x, 'shard', split_axis=0, concat_axis=0, tiled=True, axis_...  3.85 us
    pallas_call x1, Pallas kernels, body(): pl.pallas_call(pack, out_shape=jax.ShapeDtypeStruct((slots, height, LANES...  2.56 us
    pallas_call x1, Pallas kernels, body(): pl.pallas_call(work, out_shape=jax.ShapeDtypeStruct((sources, send, LANES...  2.03 us
    pallas_call x1, Pallas kernels, body(): pl.pallas_call(finish, out_shape=(jax.ShapeDtypeStruct(query_grads.shape,...  0.89 us
  transfers between devices with their start and end apart: 1, of which 1 were waited for; matrix products, arithmetic and copies ran while one was open for 0% of the time, Pallas kernels for 0%

profile of v7, /device:TPU:0, one launch (start us, length us, event | category | flops | bytes accessed | tf_op | source)
XLA Modules:
  0.0 36.5 jit_solution(16163018922266079448)
XLA Ops:
  0.6 2.6 %pack.1 = bf16[16,96,128]{2,1,0:T(8,128)(2,1)} custom-call(s32[1,16]{1,0:T(1,128)} %bitcast.8, bf16[1,16,4096]{2,1,0:T(8,128)(2,1)} %query_hbm.1, bf16[2,16,4096]{2,1,0:T(8,128)(2,1)} %cand_hbm.1), custom_call_target="tpu_custom_call" | custom-call | tf_op jit(solution)/shard_map/pack/pallas_call | solution.py:201
  3.2 0.0 copy-start
  3.2 0.0 copy-start.1
  3.2 0.0 copy-start.2
  3.2 18.0 %all_to_all.10.moved_ref = bf16[16,96,128]{2,1,0:T(8,128)(2,1)S(1)} all-to-all(bf16[16,96,128]{2,1,0:T(8,128)(2,1)} %pack.1), channel_id=1, replica_groups={{14,15,0,1,2,3,4,5,6,7,8,9,10,11,12,13},{30,31,16,17,18,19,20,21,22,23,..., dimensions={0} | all-to-all | bytes 786432 | tf_op jit(solution)/shard_map/all_to_all | solution.py:196
  21.3 0.0 copy-done
  21.3 0.0 copy-done.1
  21.3 0.0 copy-done.2
  21.3 2.0 %work.1 = bf16[16,40,128]{2,1,0:T(8,128)(2,1)} custom-call(bf16[16,96,128]{2,1,0:T(8,128)(2,1)S(1)} %all_to_all.10.moved_ref, bf16[64,64]{1,0:T(8,128)(2,1)S(1)} %bitcast.5, bf16[64,64]{1,0:T(8,128)(2,1)S(1)} %bitcast.6, f32[32,128]{1,0:T(8,128)S(1)} %bitcast.7), custom_call_target="tpu_custom_call" | custom-call | tf_op jit(solution)/shard_map/work/pallas_call | solution.py:218
  23.3 7.8 %all-to-all-start.1 = ((bf16[16,40,128]{2,1,0:T(8,128)(2,1)}), bf16[16,40,128]{2,1,0:T(8,128)(2,1)S(1)}, u32[]{:S(2)}, u32[]{:S(2)}) async-start(bf16[16,40,128]{2,1,0:T(8,128)(2,1)} %work.1), calls=%async_computation.1 | async-start | bytes 327680 | tf_op jit(solution)/shard_map/all_to_all | solution.py:196
  31.1 0.0 copy-start.4
  31.7 0.0 copy-start.3
  31.7 0.0 copy-start.5
  31.8 3.9 %all-to-all-done.1.home_ref = bf16[16,40,128]{2,1,0:T(8,128)(2,1)S(1)} async-done(((bf16[16,40,128]{2,1,0:T(8,128)(2,1)}), bf16[16,40,128]{2,1,0:T(8,128)(2,1)S(1)}, u32[]{:S(2)}, u32[]{:S(2)}) %all-to-all-start.1) | async-done | bytes 163872 | tf_op jit(solution)/shard_map/all_to_all | solution.py:196
  35.6 0.0 copy-done.4
  35.6 0.0 copy-done.3
  35.6 0.0 copy-done.5
  35.6 0.9 %finish.1 = (bf16[1,16,4096]{2,1,0:T(8,128)(2,1)}, f32[1,384]{1,0:T(1,128)}) custom-call(s32[1]{0:T(128)S(6)} %copy.11.length_ref, s32[1,16]{1,0:T(1,128)S(1)} %bitcast.9, s32[1,32]{1,0:T(1,128)S(1)} %bitcast.10, s32[1,384]{1,0:T(1,128)S(1)} %copy-done.4, bf16[16,40,128]{2,1,0:T(8,128)(2,1)S(1)} %all-to-all-done.1.home_ref), custom_call_target="tpu_custom_call" | custom-call | tf_op jit(solution)/shard_map/finish/pallas_call | solution.py:233
Async XLA Ops:
  3.2 18.1 %copy-start = (bf16[1,64,64]{2,1,0:T(8,128)(2,1)S(1)}, bf16[1,64,64]{2,1,0:T(8,128)(2,1)}, u32[]{:S(2)}) copy-start(bf16[1,64,64]{2,1,0:T(8,128)(2,1)} %param.11) | copy-start | bytes 24580
  3.2 18.1 %copy-start.1 = (bf16[1,64,64]{2,1,0:T(8,128)(2,1)S(1)}, bf16[1,64,64]{2,1,0:T(8,128)(2,1)}, u32[]{:S(2)}) copy-start(bf16[1,64,64]{2,1,0:T(8,128)(2,1)} %param.12) | copy-start | bytes 24580
  3.2 18.0 %copy-start.2 = (f32[1,4096]{1,0:T(1,128)S(1)}, f32[1,4096]{1,0:T(1,128)}, u32[]{:S(2)}) copy-start(f32[1,4096]{1,0:T(1,128)} %param.13) | copy-start | bytes 49156
  23.3 12.3 %all-to-all-start.1 = ((bf16[16,40,128]{2,1,0:T(8,128)(2,1)}), bf16[16,40,128]{2,1,0:T(8,128)(2,1)S(1)}, u32[]{:S(2)}, u32[]{:S(2)}) async-start(bf16[16,40,128]{2,1,0:T(8,128)(2,1)} %work.1), calls=%async_computation.1 | async-start | bytes 327680 | tf_op jit(solution)/shard_map/all_to_all | solution.py:196
  31.1 4.5 %copy-start.4 = (s32[1,384]{1,0:T(1,128)S(1)}, s32[1,384]{1,0:T(1,128)}, u32[]{:S(2)}) copy-start(s32[1,384]{1,0:T(1,128)} %lists_ref.1) | copy-start | bytes 4612
  31.7 3.9 %copy-start.3 = (s32[16]{0:T(128)S(1)}, s32[16]{0:T(128)}, u32[]{:S(2)}) copy-start(s32[16]{0:T(128)} %param.14) | copy-start | bytes 196
  31.7 3.9 %copy-start.5 = (s32[32]{0:T(128)S(1)}, s32[32]{0:T(128)}, u32[]{:S(2)}) copy-start(s32[32]{0:T(128)} %param.15) | copy-start | bytes 388

commit v8 on v2

--- a/solution.py
+++ b/solution.py
@@ -21,8 +21,18 @@
     return lax.dot_general(a, b, (dims, ((), ())), preferred_element_type=f32)
 
 
-def holds(layer_row, modules):
+def order_of(slots, first):
+    return [(first + k) % slots for k in range(slots)]
+
+
+def firsts(slots):
+    return slots // 4, slots - 2
+
+
+def holds(layer_row, modules, first):
     slots = layer_row.shape[1]
+    if first:
+        layer_row = jnp.concatenate([layer_row[:, first:], layer_row[:, :first]], axis=1)
     return (iota((modules, slots), 0) == layer_row).astype(f32).astype(bf16)
 
 
@@ -35,16 +45,16 @@
     ]
     for arrival in arrivals:
         arrival.start()
-    for arrival in arrivals:
-        arrival.wait()
+    arrivals[0].wait()
     modules, flat = query_ref.shape[1:]
     slots, height, _ = out_ref.shape
     tall = flat // LANES
-    one_hot = holds(layer_ref[...], modules)
-    sources = [query_ref[r] for r in range(query_ref.shape[0])]
-    sources += [cand_ref[r] for r in range(cand_ref.shape[0])]
-    for r, rows in enumerate(sources):
-        by_slot = dot(one_hot, rows, ((0,), (0,)))
+    one_hot = holds(layer_ref[...], modules, firsts(slots)[0])
+    sources = [(query_ref, r) for r in range(query_ref.shape[0])] + [(cand_ref, r) for r in range(cand_ref.shape[0])]
+    for r, (ref, row) in enumerate(sources):
+        if row == 0:
+            arrivals[1 if ref is query_ref else 2].wait()
+        by_slot = dot(one_hot, ref[row], ((0,), (0,)))
         for j in range(tall):
             wide[pl.ds(r * tall + j, slots, stride=height), :] = by_slot[:, j * LANES : (j + 1) * LANES]
     out_ref[...] = wide[...].reshape(out_ref.shape).astype(bf16)
@@ -65,6 +75,9 @@
     tall = side // 2
     per = height // tall - 1
     count = sources * per
+    arrive, leave = firsts(sources)
+    devices = order_of(sources, arrive)
+    places = [(d - leave) % sources for d in devices]
     out_basis = out_basis_ref[...]
     in_basis = in_basis_ref[...]
 
@@ -99,11 +112,11 @@
     for p in range(len(pairs)):
         top = precond[:tall, p * LANES : (p + 1) * LANES]
         low = precond[tall:, p * LANES : (p + 1) * LANES]
-        homes[pl.ds(2 * p * send, tall), :] = half(top, swap(low))
-        homes[pl.ds((2 * p + 1) * send, tall), :] = half(swap(top), low)
-
-    for d in range(sources):
-        cands[pl.ds(d * per * tall, per * tall), :] = moved_ref[d, tall:, :].astype(f32)
+        homes[pl.ds(places[2 * p] * send, tall), :] = half(top, swap(low))
+        homes[pl.ds(places[2 * p + 1] * send, tall), :] = half(swap(top), low)
+
+    for k, d in enumerate(devices):
+        cands[pl.ds(d * per * tall, per * tall), :] = moved_ref[k, tall:, :].astype(f32)
     queries_flat = jnp.concatenate(
         [homes[pl.ds(j, sources, stride=send), :].astype(bf16) for j in range(tall)], axis=1
     )
@@ -136,7 +149,7 @@
     tall = flat // LANES
     wide[...] = home_ref[...].reshape(wide.shape).astype(f32)
     by_slot = jnp.concatenate([wide[pl.ds(j, slots, stride=send), :].astype(bf16) for j in range(tall)], axis=1)
-    precond_ref[0] = dot(holds(layer_ref[...], modules), by_slot).astype(bf16)
+    precond_ref[0] = dot(holds(layer_ref[...], modules, firsts(slots)[1]), by_slot).astype(bf16)
     groups = -(-count // LANES)
     parts = []
     for t in range(groups):
@@ -159,7 +172,6 @@
 HBM = pl.BlockSpec(memory_space=pltpu.HBM)
 SMEM = pl.BlockSpec(memory_space=pltpu.SMEM)
 PARAMS = pltpu.CompilerParams(vmem_limit_bytes=40 * 1024 * 1024)
-FULL = pltpu.CompilerParams(vmem_limit_bytes=56 * 1024 * 1024)
 
 
 def body(
@@ -180,11 +192,19 @@
     count = cand_rows.shape[0]
     layer_row = layer_map.reshape(1, slots)
     height = (own + per) * tall
-    send = tall + -(-PIECES * -(-count // LANES) // 16) * 16
+    send = tall + -(-PIECES * -(-count // LANES) // 8) * 8
+
+    def in_hbm(x):
+        return pltpu.with_memory_space_constraint(x, pltpu.HBM)
+
+    def swap_over(x, first):
+        groups = [order_of(slots, first)]
+        return lax.all_to_all(x, "shard", split_axis=0, concat_axis=0, tiled=True, axis_index_groups=groups)
+
 
     packed = pl.pallas_call(
         pack,
-        out_shape=jax.ShapeDtypeStruct((slots, height, LANES), bf16),
+        out_shape=pltpu.VMEM((slots, height, LANES), bf16),
         in_specs=[HBM] * 3,
         out_specs=VMEM,
         scratch_shapes=[
@@ -194,10 +214,10 @@
             pltpu.VMEM((slots * height, LANES), f32),
             pltpu.SemaphoreType.DMA((3,)),
         ],
-        compiler_params=FULL,
+        compiler_params=PARAMS,
         name="pack",
-    )(layer_row, query_grads, cand_grads)
-    moved = lax.all_to_all(packed, "shard", split_axis=0, concat_axis=0, tiled=True)
+    )(in_hbm(layer_row), in_hbm(query_grads), in_hbm(cand_grads))
+    moved = swap_over(packed, firsts(slots)[0])
     sources = moved.shape[0]
     homes = pl.pallas_call(
         work,
@@ -213,7 +233,7 @@
         basis_in.reshape(basis_in.shape[1:]),
         eigvals.reshape(tall, LANES),
     )
-    home = lax.all_to_all(homes, "shard", split_axis=0, concat_axis=0, tiled=True)
+    home = swap_over(homes, firsts(slots)[1])
     return pl.pallas_call(
         finish,
         out_shape=(

time: 38.8 us -> 34.8 us (0.90)
  waiting for transfers between devices: 8.29 us -> 3.83 us
  starting transfers between devices: 3.53 us -> 6.01 us
  blocking collectives: 19.7 us -> 18.6 us
  Pallas kernels: 5.48 us -> 4.6 us
    all_to_all x1, waiting for transfers between devices: 8.29 us -> 3.83 us  [swap_over(): lax.all_to_all(x, 'shard', split_axis=0, concat_axis=0, tiled=True, axis_...]
    all_to_all x1, starting transfers between devices: 3.53 us -> 6.01 us  [swap_over(): lax.all_to_all(x, 'shard', split_axis=0, concat_axis=0, tiled=True, axis_...]
    all_to_all x1, blocking collectives: 19.7 us -> 18.6 us  [swap_over(): lax.all_to_all(x, 'shard', split_axis=0, concat_axis=0, tiled=True, axis_...]
    pallas_call x1, Pallas kernels: 2.5 us -> 1.67 us  [body(): pl.pallas_call(pack, out_shape=pltpu.VMEM((slots, height, LANES), bf16),...]
where the time goes in v8:
time: 34.8 us; the launch traced here: 34.4 us
  blocking collectives  18.6 us (53%)
  starting transfers between devices  6.01 us (17%)
  Pallas kernels  4.6 us (13%)
  waiting for transfers between devices  3.83 us (11%)
  between operations  1.35 us (4%)
    all_to_all x1, blocking collectives, swap_over(): lax.all_to_all(x, 'shard', split_axis=0, concat_axis=0, tiled=True, axis_...  18.6 us
    all_to_all x1, starting transfers between devices, swap_over(): lax.all_to_all(x, 'shard', split_axis=0, concat_axis=0, tiled=True, axis_...  6.01 us
    all_to_all x1, waiting for transfers between devices, swap_over(): lax.all_to_all(x, 'shard', split_axis=0, concat_axis=0, tiled=True, axis_...  3.83 us
    pallas_call x1, Pallas kernels, body(): pl.pallas_call(work, out_shape=jax.ShapeDtypeStruct((sources, send, LANES...  2.03 us
    pallas_call x1, Pallas kernels, body(): pl.pallas_call(pack, out_shape=pltpu.VMEM((slots, height, LANES), bf16),...  1.67 us
    pallas_call x1, Pallas kernels, body(): pl.pallas_call(finish, out_shape=(jax.ShapeDtypeStruct(query_grads.shape,...  0.89 us
  transfers between devices with their start and end apart: 1, of which 1 were waited for; matrix products, arithmetic and copies ran while one was open for 0% of the time, Pallas kernels for 0%

profile of v8, /device:TPU:0, one launch (start us, length us, event | category | flops | bytes accessed | tf_op | source)
XLA Modules:
  0.0 34.4 jit_solution(15840710811212542947)
XLA Ops:
  0.6 1.7 %pack.1 = bf16[16,96,128]{2,1,0:T(8,128)(2,1)S(1)} custom-call(s32[1,16]{1,0:T(1,128)} %bitcast.8, bf16[1,16,4096]{2,1,0:T(8,128)(2,1)} %query_hbm.1, bf16[2,16,4096]{2,1,0:T(8,128)(2,1)} %cand_hbm.1), custom_call_target="tpu_custom_call" | custom-call | tf_op jit(solution)/shard_map/pack/pallas_call | solution.py:205
  2.3 0.0 copy-start
  2.3 0.0 copy-start.1
  2.3 0.0 copy-start.2
  2.3 18.6 %all_to_all.10.moved_ref = bf16[16,96,128]{2,1,0:T(8,128)(2,1)S(1)} all-to-all(bf16[16,96,128]{2,1,0:T(8,128)(2,1)S(1)} %pack.1), channel_id=1, replica_groups={{4,5,6,7,8,9,10,11,12,13,14,15,0,1,2,3},{20,21,22,23,24,25,26,27,28,29,..., dimensions={0} | all-to-all | bytes 786432 | tf_op jit(solution)/shard_map/all_to_all | solution.py:202
  21.0 0.0 copy-done
  21.0 0.0 copy-done.1
  21.0 0.0 copy-done.2
  21.0 2.0 %work.1 = bf16[16,40,128]{2,1,0:T(8,128)(2,1)} custom-call(bf16[16,96,128]{2,1,0:T(8,128)(2,1)S(1)} %all_to_all.10.moved_ref, bf16[64,64]{1,0:T(8,128)(2,1)S(1)} %bitcast.5, bf16[64,64]{1,0:T(8,128)(2,1)S(1)} %bitcast.6, f32[32,128]{1,0:T(8,128)S(1)} %bitcast.7), custom_call_target="tpu_custom_call" | custom-call | tf_op jit(solution)/shard_map/work/pallas_call | solution.py:222
  23.0 6.0 %all-to-all-start.1 = ((bf16[16,40,128]{2,1,0:T(8,128)(2,1)}), bf16[16,40,128]{2,1,0:T(8,128)(2,1)S(1)}, u32[]{:S(2)}, u32[]{:S(2)}) async-start(bf16[16,40,128]{2,1,0:T(8,128)(2,1)} %work.1), calls=%async_computation.1 | async-start | bytes 327680 | tf_op jit(solution)/shard_map/all_to_all | solution.py:202
  29.0 0.0 copy-start.4
  29.7 0.0 copy-start.3
  29.7 0.0 copy-start.5
  29.7 3.8 %all-to-all-done.1.home_ref = bf16[16,40,128]{2,1,0:T(8,128)(2,1)S(1)} async-done(((bf16[16,40,128]{2,1,0:T(8,128)(2,1)}), bf16[16,40,128]{2,1,0:T(8,128)(2,1)S(1)}, u32[]{:S(2)}, u32[]{:S(2)}) %all-to-all-start.1) | async-done | bytes 163872 | tf_op jit(solution)/shard_map/all_to_all | solution.py:202
  33.5 0.0 copy-done.4
  33.5 0.0 copy-done.3
  33.5 0.0 copy-done.5
  33.5 0.9 %finish.1 = (bf16[1,16,4096]{2,1,0:T(8,128)(2,1)}, f32[1,384]{1,0:T(1,128)}) custom-call(s32[1]{0:T(128)S(6)} %copy.11.length_ref, s32[1,16]{1,0:T(1,128)S(1)} %bitcast.9, s32[1,32]{1,0:T(1,128)S(1)} %bitcast.10, s32[1,384]{1,0:T(1,128)S(1)} %copy-done.4, bf16[16,40,128]{2,1,0:T(8,128)(2,1)S(1)} %all-to-all-done.1.home_ref), custom_call_target="tpu_custom_call" | custom-call | tf_op jit(solution)/shard_map/finish/pallas_call | solution.py:237
Async XLA Ops:
  2.3 18.7 %copy-start = (bf16[1,64,64]{2,1,0:T(8,128)(2,1)S(1)}, bf16[1,64,64]{2,1,0:T(8,128)(2,1)}, u32[]{:S(2)}) copy-start(bf16[1,64,64]{2,1,0:T(8,128)(2,1)} %param.11) | copy-start | bytes 24580
  2.3 18.6 %copy-start.1 = (bf16[1,64,64]{2,1,0:T(8,128)(2,1)S(1)}, bf16[1,64,64]{2,1,0:T(8,128)(2,1)}, u32[]{:S(2)}) copy-start(bf16[1,64,64]{2,1,0:T(8,128)(2,1)} %param.12) | copy-start | bytes 24580
  2.3 18.6 %copy-start.2 = (f32[1,4096]{1,0:T(1,128)S(1)}, f32[1,4096]{1,0:T(1,128)}, u32[]{:S(2)}) copy-start(f32[1,4096]{1,0:T(1,128)} %param.13) | copy-start | bytes 49156
  23.0 10.5 %all-to-all-start.1 = ((bf16[16,40,128]{2,1,0:T(8,128)(2,1)}), bf16[16,40,128]{2,1,0:T(8,128)(2,1)S(1)}, u32[]{:S(2)}, u32[]{:S(2)}) async-start(bf16[16,40,128]{2,1,0:T(8,128)(2,1)} %work.1), calls=%async_computation.1 | async-start | bytes 327680 | tf_op jit(solution)/shard_map/all_to_all | solution.py:202
  29.0 4.5 %copy-start.4 = (s32[1,384]{1,0:T(1,128)S(1)}, s32[1,384]{1,0:T(1,128)}, u32[]{:S(2)}) copy-start(s32[1,384]{1,0:T(1,128)} %lists_ref.1) | copy-start | bytes 4612
  29.7 3.9 %copy-start.3 = (s32[16]{0:T(128)S(1)}, s32[16]{0:T(128)}, u32[]{:S(2)}) copy-start(s32[16]{0:T(128)} %param.14) | copy-start | bytes 196
  29.7 3.8 %copy-start.5 = (s32[32]{0:T(128)S(1)}, s32[32]{0:T(128)}, u32[]{:S(2)}) copy-start(s32[32]{0:T(128)} %param.15) | copy-start | bytes 388

commit v9 on v0

v9 whole, which is shorter than its diff:
```python
import jax
import jax.numpy as jnp
from jax import lax
from jax.experimental import pallas as pl
from jax.experimental.pallas import tpu as pltpu
from jax.sharding import PartitionSpec as P

damping = 0.1
LANES = 128
SUBLANES = 8
PIECES = 3
f32, bf16 = jnp.float32, jnp.bfloat16


def iota(shape, axis):
    return lax.broadcasted_iota(jnp.int32, shape, axis)


def dot(a, b, dims=((1,), (0,))):
    return lax.dot_general(a, b, (dims, ((), ())), preferred_element_type=f32)


def mask(condition):
    return condition.astype(f32).astype(bf16)


def order_of(slots, first):
    return [(first + k) % slots for k in range(slots)]


def firsts(slots):
    return slots // 4, slots - 2


def gather_rows(tall):
    size = SUBLANES * tall
    row = iota((size, size), 0)
    return mask(row // SUBLANES + tall * (row % SUBLANES) == iota((size, size), 1))


def scatter_rows(tall):
    size = SUBLANES * tall
    row = iota((size, size), 0)
    return mask(row // tall + SUBLANES * (row % tall) == iota((size, size), 1))


def half(left, right):
    return jnp.where(iota(left.shape, 1) < LANES // 2, left, right)


def swap(block):
    return pltpu.roll(block, LANES // 2, 1)


def unpaired(block):
    tall = block.shape[0] // 2
    top, low = block[:tall], block[tall:]
    return half(top, swap(low)), half(swap(top), low)


def pack(layer_hbm, query_hbm, cand_hbm, out_ref, layer_ref, query_ref, cand_ref, by_module, sems):
    arrivals = [
        pltpu.make_async_copy(source, target, sems.at[i])
        for i, (source, target) in enumerate(
            ((query_hbm, query_ref), (cand_hbm, cand_ref), (layer_hbm, layer_ref))
        )
    ]
    for arrival in arrivals:
        arrival.start()
    modules, flat = query_ref.shape[1:]
    slots = out_ref.shape[0]
    tall = flat // LANES
    scatter = scatter_rows(tall)
    sources = [(query_ref, r) for r in range(query_ref.shape[0])] + [(cand_ref, r) for r in range(cand_ref.shape[0])]
    for r, (ref, row) in enumerate(sources):
        if row == 0:
            arrivals[0 if ref is query_ref else 1].wait()
        rows = ref[row].astype(f32)
        columns = []
        for m in range(0, modules, SUBLANES):
            tiles = [rows[m : m + SUBLANES, j * LANES : (j + 1) * LANES] for j in range(tall)]
            columns.append(jnp.concatenate(tiles, axis=0).astype(bf16))
        blocks = dot(scatter, jnp.concatenate(columns, axis=1)).astype(bf16)
        for m in range(modules):
            c, g = m % SUBLANES, m // SUBLANES
            by_module[m, r * tall : (r + 1) * tall, :] = blocks[c * tall : (c + 1) * tall, g * LANES : (g + 1) * LANES]
    arrivals[2].wait()
    for k, s in enumerate(order_of(slots, firsts(slots)[0])):
        out_ref[k] = by_module[layer_ref[s]]


def upright(row, count):
    shape = (count, row.shape[1])
    return jnp.sum(jnp.where(iota(shape, 0) == iota(shape, 1), row, 0.0), axis=1, keepdims=True)


def prepare(
    length_ref, out_basis_ref, in_basis_ref, eigen_ref, rows_ref, lists_ref, after_ref,
    enter_ref, outer_ref, inner_ref, factor_ref, gather_ref, chosen_ref,
):
    del after_ref
    out_basis, in_basis = out_basis_ref[...], in_basis_ref[...]
    side = out_basis.shape[0]
    tall = side // 2
    size = enter_ref.shape[0]
    order = mask(iota((side, side), 1) == 2 * (iota((side, side), 0) % tall) + iota((side, side), 0) // tall)
    basis = dot(dot(order, out_basis).astype(bf16), order, ((1,), (1,))).astype(bf16)
    spread = mask(iota((size, side), 0) % side == iota((size, side), 1))
    row, column = iota((size, size), 0) // side, iota((size, size), 1) // side
    outer = dot(dot(spread, basis).astype(bf16), spread, ((1,), (1,)))
    inner = dot(dot(spread, in_basis).astype(bf16), spread, ((1,), (1,)))
    outer_ref[...] = jnp.where(row == column, outer, 0.0).astype(bf16)
    inner_ref[...] = jnp.where(row == column, inner, 0.0).astype(bf16)
    enter_ref[...] = jnp.where(row == 2 * (column % 2) + column // 2, inner, 0.0).astype(bf16)
    eigen = eigen_ref[...]
    turned = swap(eigen)
    factor_ref[...] = 1.0 / (jnp.concatenate([half(eigen, turned), half(turned, eigen)], axis=0) + damping)
    gather_ref[...] = gather_rows(tall)

    count = rows_ref.shape[1]
    lists = lists_ref[...]
    longest = lists.shape[1]
    rows = upright(rows_ref[...].astype(f32), count)
    place = jnp.sum(jnp.where(iota((count, longest), 0) == lists, rows, 0.0), axis=0, keepdims=True)
    place = jnp.where(iota((1, longest), 1) < length_ref[0], place.astype(jnp.int32), -1)
    chosen_ref[...] = (iota((count, longest), 0) == place).astype(f32)


def work(moved_ref, enter_ref, outer_ref, inner_ref, factor_ref, gather_ref, out_ref, tails):
    sources, height, _ = moved_ref.shape
    _, send, _ = out_ref.shape
    size = enter_ref.shape[0]
    side, tall = size // 4, size // SUBLANES
    per = height // tall - 1
    count = sources * per
    pairs = sources // 2
    stacks = pairs // 4
    arrive, leave = firsts(sources)
    places = [(d - leave) % sources for d in order_of(sources, arrive)]
    outer, inner, gather = outer_ref[...], inner_ref[...], gather_ref[...]
    factor = factor_ref[...]

    queries = [jnp.concatenate([moved_ref[2 * p, :tall, :], moved_ref[2 * p + 1, :tall, :]], axis=1) for p in range(pairs)]
    entered = dot(jnp.concatenate(queries, axis=0), enter_ref[...]).astype(bf16)
    columns = []
    for t in range(stacks):
        tiles = []
        for p in range(4 * t, 4 * t + 4):
            rows = entered[p * tall : (p + 1) * tall]
            tiles += [rows[:, :LANES], rows[:, LANES:]]
        columns.append(jnp.concatenate(tiles, axis=0))
    rotated = dot(outer, jnp.concatenate(columns, axis=1), ((0,), (0,)))
    tile = jnp.concatenate([jnp.concatenate([factor] * 4, axis=0)] * 2, axis=1)
    scaled = [
        (rotated[:, t * LANES : (t + 2) * LANES] * tile).astype(bf16) for t in range(0, stacks, 2)
    ]
    returned = dot(jnp.concatenate(scaled, axis=0), inner, ((1,), (1,))).astype(bf16)
    returned = jnp.concatenate([returned[t * size : (t + 1) * size] for t in range(stacks // 2)], axis=1)
    precond = dot(outer, returned).astype(bf16).astype(f32)

    homes = [None] * sources
    for p in range(pairs):
        t, u = p // 4, p % 4
        block = precond[u * side : (u + 1) * side, t * LANES : (t + 1) * LANES]
        homes[places[2 * p]], homes[places[2 * p + 1]] = unpaired(block)

    def flat(blocks):
        groups = [
            jnp.concatenate(blocks[g : g + SUBLANES], axis=0).astype(bf16) for g in range(0, len(blocks), SUBLANES)
        ]
        turned = dot(gather, jnp.concatenate(groups, axis=1))
        return jnp.concatenate(
            [
                jnp.concatenate(
                    [
                        turned[j * SUBLANES : (j + 1) * SUBLANES, g * LANES : (g + 1) * LANES]
                        for g in range(len(groups))
                    ],
                    axis=0,
                ).astype(bf16)
                for j in range(tall)
            ],
            axis=1,
        )

    cands = [
        moved_ref[(d - arrive) % sources, (1 + c) * tall : (2 + c) * tall, :]
        for d in range(sources)
        for c in range(per)
    ]
    rest = dot(flat(homes), flat(cands), ((1,), (1,)))
    wide = -(-count // LANES)
    if wide * LANES > count:
        rest = jnp.concatenate([rest, jnp.zeros((sources, wide * LANES - count), f32)], axis=1)
    tail = send - tall
    tails[...] = jnp.zeros_like(tails)
    for k in range(PIECES):
        piece = rest.astype(bf16).astype(f32)
        rest = rest - piece
        for t in range(wide):
            tails[pl.ds(k * wide + t, sources, stride=tail), :] = piece[:, t * LANES : (t + 1) * LANES]
    for k in range(sources):
        out_ref[k] = jnp.concatenate([homes[k], tails[k * tail : (k + 1) * tail, :]], axis=0).astype(bf16)


def finish(layer_ref, home_ref, gather_ref, chosen_ref, precond_ref, scores_ref, by_module):
    slots, send, _ = home_ref.shape
    modules, flat = precond_ref.shape[1:]
    count = chosen_ref.shape[0]
    tall = flat // LANES
    totals = None
    for k, s in enumerate(order_of(slots, firsts(slots)[1])):
        block = home_ref[k].astype(f32)
        by_module[layer_ref[s]] = block[:tall].astype(bf16)
        totals = block[tall:] if totals is None else totals + block[tall:]
    groups = [
        jnp.concatenate([by_module[m + c] for c in range(SUBLANES)], axis=0) for m in range(0, modules, SUBLANES)
    ]
    turned = dot(gather_ref[...], jnp.concatenate(groups, axis=1))
    for j in range(tall):
        tiles = [turned[j * SUBLANES : (j + 1) * SUBLANES, g * LANES : (g + 1) * LANES] for g in range(len(groups))]
        precond_ref[0, :, j * LANES : (j + 1) * LANES] = jnp.concatenate(tiles, axis=0).astype(bf16)
    wide = -(-count // LANES)
    parts = [
        sum((totals[k * wide + t : k * wide + t + 1] for k in range(1, PIECES)), totals[t : t + 1]) for t in range(wide)
    ]
    dense = parts[0] if wide == 1 else jnp.concatenate(parts, axis=1)
    scores_ref[...] = jnp.sum(
        jnp.where(chosen_ref[...] > 0.0, upright(dense, count), 0.0), axis=0, keepdims=True
    )


HBM = pl.BlockSpec(memory_space=pltpu.HBM)
ANY = pl.BlockSpec(memory_space=pl.ANY)
SMEM = pl.BlockSpec(memory_space=pltpu.SMEM)
VMEM = pl.BlockSpec(memory_space=pltpu.VMEM)
PARAMS = pltpu.CompilerParams(vmem_limit_bytes=40 * 1024 * 1024)


def body(
    query_grads,
    cand_grads,
    basis_out,
    basis_in,
    eigvals,
    layer_map,
    cand_rows,
    cand_lists,
    list_lengths,
):
    own, modules, flat = query_grads.shape
    per = cand_grads.shape[0]
    slots = layer_map.shape[0]
    tall = flat // LANES
    side = basis_out.shape[1]
    size = SUBLANES * tall
    count = cand_rows.shape[0]
    height = (own + per) * tall
    send = tall + -(-PIECES * -(-count // LANES) // SUBLANES) * SUBLANES

    def in_hbm(x):
        return pltpu.with_memory_space_constraint(x, pltpu.HBM)

    def swap_over(x, first):
        groups = [order_of(slots, first)]
        return lax.all_to_all(x, "shard", split_axis=0, concat_axis=0, tiled=True, axis_index_groups=groups)

    packed = pl.pallas_call(
        pack,
        out_shape=pltpu.VMEM((slots, height, LANES), bf16),
        in_specs=[HBM] * 3,
        out_specs=VMEM,
        scratch_shapes=[
            pltpu.SMEM(layer_map.shape, jnp.int32),
            pltpu.VMEM(query_grads.shape, bf16),
            pltpu.VMEM(cand_grads.shape, bf16),
            pltpu.VMEM((modules, height, LANES), bf16),
            pltpu.SemaphoreType.DMA((3,)),
        ],
        compiler_params=PARAMS,
        name="pack",
    )(in_hbm(layer_map), in_hbm(query_grads), in_hbm(cand_grads))
    square = jax.ShapeDtypeStruct((size, size), bf16)
    enter, outer, inner, factor, gather, chosen = pl.pallas_call(
        prepare,
        out_shape=(
            square,
            square,
            square,
            jax.ShapeDtypeStruct((side, LANES), f32),
            square,
            jax.ShapeDtypeStruct((count, cand_lists.shape[1]), f32),
        ),
        in_specs=[SMEM] + [VMEM] * 5 + [ANY],
        out_specs=[VMEM] * 6,
        compiler_params=PARAMS,
        name="prepare",
    )(
        list_lengths,
        basis_out.reshape(basis_out.shape[1:]),
        basis_in.reshape(basis_in.shape[1:]),
        eigvals.reshape(tall, LANES),
        cand_rows.reshape(1, count),
        cand_lists,
        packed,
    )
    moved = swap_over(packed, firsts(slots)[0])
    homes = pl.pallas_call(
        work,
        out_shape=jax.ShapeDtypeStruct((slots, send, LANES), bf16),
        in_specs=[VMEM] * 6,
        out_specs=VMEM,
        scratch_shapes=[pltpu.VMEM((slots * (send - tall), LANES), f32)],
        compiler_params=PARAMS,
        name="work",
    )(moved, enter, outer, inner, factor, gather)
    home = swap_over(homes, firsts(slots)[1])
    return pl.pallas_call(
        finish,
        out_shape=(
            jax.ShapeDtypeStruct(query_grads.shape, bf16),
            jax.ShapeDtypeStruct(cand_lists.shape, f32),
        ),
        in_specs=[SMEM] + [VMEM] * 3,
        out_specs=(VMEM, VMEM),
        scratch_shapes=[pltpu.VMEM((modules, tall, LANES), bf16)],
        compiler_params=PARAMS,
        name="finish",
    )(layer_map, home, gather, chosen)


def solution(mesh):
    return jax.shard_map(
        body,
        mesh=mesh,
        in_specs=(
            P(("groups", "shard"), None, None),
            P(("groups", "shard"), None, None),
            P("shard", None, None),
            P("shard", None, None),
            P("shard", None),
            P(),
            P("groups"),
            P(("groups", "shard"), None),
            P(("groups", "shard")),
        ),
        out_specs=(P(("groups", "shard"), None, None), P(("groups", "shard"), None)),
        check_vma=False,
    )
```

time: 120 us -> 35.6 us (0.30)
  other arithmetic: 46.7 us -> 0 us
  blocking collectives: 34.3 us -> 10.3 us
  local copies, waits for them, and re-layouts: 15.5 us -> 1.31 us
  starting transfers between devices: 17 us -> 8 us
  waiting for transfers between devices: 2.7 us -> 8.92 us
  Pallas kernels: 0 us -> 5.34 us
    gather x8 -> x0, other arithmetic: 40.4 us -> none  [the longest x3 20.2 us: body(): picked = jnp.take_along_axis(summed, positions, axis=1)]
    unnamed x1 -> x0, blocking collectives: 34.3 us -> none
    all_to_all x0 -> x1, blocking collectives: none -> 10.3 us  [swap_over(): lax.all_to_all(x, 'shard', split_axis=0, concat_axis=0, tiled=True, axis_...]
    all_to_all x3 -> x1, starting transfers between devices: 17 us -> 8 us  [swap_over(): lax.all_to_all(x, 'shard', split_axis=0, concat_axis=0, tiled=True, axis_...]
    gather x7 -> x0, local copies, waits for them, and re-layouts: 6.49 us -> none  [the longest x1 1.67 us: body(): query_slot = jnp.take(query_grads, layer_map, axis=1)]
    all_to_all x3 -> x1, waiting for transfers between devices: 2.7 us -> 8.92 us  [swap_over(): lax.all_to_all(x, 'shard', split_axis=0, concat_axis=0, tiled=True, axis_...]
    pallas_call x0 -> x4, Pallas kernels: none -> 5.34 us  [the longest x1 2.13 us: body(): pl.pallas_call(pack, out_shape=pltpu.VMEM((slots, height, LANES), bf16),...]
    unnamed x24 -> x12, local copies, waits for them, and re-layouts: 5.99 us -> 1.31 us
  transfers between devices with their start and end apart: 3 -> 1, of which waited for: 1 -> 1; matrix products, arithmetic and copies ran while one was open for 28% -> 0% of each run, Pallas kernels for 0% -> 2%
where the time goes in v9:
time: 35.6 us; the launch traced here: 35.3 us
  blocking collectives  10.3 us (29%)
  waiting for transfers between devices  8.92 us (25%)
  starting transfers between devices  8 us (22%)
  Pallas kernels  5.34 us (15%)
  between operations  1.37 us (4%)
  local copies, waits for them, and re-layouts  1.31 us (4%)
    all_to_all x1, blocking collectives, swap_over(): lax.all_to_all(x, 'shard', split_axis=0, concat_axis=0, tiled=True, axis_...  10.3 us
    all_to_all x1, waiting for transfers between devices, swap_over(): lax.all_to_all(x, 'shard', split_axis=0, concat_axis=0, tiled=True, axis_...  8.92 us
    all_to_all x1, starting transfers between devices, swap_over(): lax.all_to_all(x, 'shard', split_axis=0, concat_axis=0, tiled=True, axis_...  8 us
    pallas_call x1, Pallas kernels, body(): pl.pallas_call(pack, out_shape=pltpu.VMEM((slots, height, LANES), bf16),...  2.13 us
    pallas_call x1, Pallas kernels, body(): pl.pallas_call(finish, out_shape=(jax.ShapeDtypeStruct(query_grads.shape,...  1.41 us
    unnamed x12, local copies, waits for them, and re-layouts  1.31 us
    pallas_call x1, Pallas kernels, body(): pl.pallas_call(work, out_shape=jax.ShapeDtypeStruct((slots, send, LANES),...  1.23 us
  transfers between devices with their start and end apart: 1, of which 1 were waited for; matrix products, arithmetic and copies ran while one was open for 0% of the time, Pallas kernels for 2%

profile of v9, /device:TPU:0, one launch (start us, length us, event | category | flops | bytes accessed | tf_op | source)
XLA Modules:
  0.0 35.3 jit_solution(7561152033280422710)
XLA Ops:
  0.6 2.1 %pack.1.after_ref = bf16[16,96,128]{2,1,0:T(8,128)(2,1)} custom-call(s32[16]{0:T(128)} %layer_ref.1, bf16[1,16,4096]{2,1,0:T(8,128)(2,1)} %query_hbm.1, bf16[2,16,4096]{2,1,0:T(8,128)(2,1)} %cand_hbm.1), custom_call_target="tpu_custom_call" | custom-call | tf_op jit(solution)/shard_map/pack/pallas_call | solution.py:268
  2.8 0.0 copy-start
  2.8 0.0 copy-start.1
  2.8 0.0 copy-start.2
  2.8 8.0 %all-to-all-start = ((bf16[16,96,128]{2,1,0:T(8,128)(2,1)}), bf16[16,96,128]{2,1,0:T(8,128)(2,1)S(1)}, u32[]{:S(2)}, u32[]{:S(2)}) async-start(bf16[16,96,128]{2,1,0:T(8,128)(2,1)} %pack.1.after_ref), calls=%async_computation | async-start | bytes 786432 | tf_op jit(solution)/shard_map/all_to_all | solution.py:266
  11.5 0.0 copy-start.4
  11.5 0.0 copy-start.5
  11.5 0.0 copy-done
  11.5 0.0 copy-done.1
  11.5 0.0 copy-done.2
  11.5 0.6 %copy-done.4 = s32[1,384]{1,0:T(1,128)S(1)} copy-done((s32[1,384]{1,0:T(1,128)S(1)}, s32[1,384]{1,0:T(1,128)}, u32[]{:S(2)}) %copy-start.4) | copy-done | bytes 1560
  12.1 0.0 copy-done.5
  12.1 0.6 %prepare.1 = (bf16[256,256]{1,0:T(8,128)(2,1)S(1)}, bf16[256,256]{1,0:T(8,128)(2,1)S(1)}, bf16[256,256]{1,0:T(8,128)(2,1)S(1)}, f32[64,128]{1,0:T(8,128)S(1)}, b...) custom-call(s32[1]{0:T(128)S(6)} %copy.11.length_ref, bf16[64,64]{1,0:T(8,128)(2,1)S(1)} %bitcast.4, ...), custom_call_target="tpu_custom_call" | custom-call | tf_op jit(solution)/shard_map/prepare/pallas_call | solution.py:284
  12.7 8.9 %all-to-all-done.moved_ref = bf16[16,96,128]{2,1,0:T(8,128)(2,1)S(1)} async-done(((bf16[16,96,128]{2,1,0:T(8,128)(2,1)}), bf16[16,96,128]{2,1,0:T(8,128)(2,1)S(1)}, u32[]{:S(2)}, u32[]{:S(2)}) %all-to-all-start) | async-done | bytes 393248 | tf_op jit(solution)/shard_map/all_to_all | solution.py:266
  21.6 1.2 %work.1 = bf16[16,40,128]{2,1,0:T(8,128)(2,1)S(1)} custom-call(bf16[16,96,128]{2,1,0:T(8,128)(2,1)S(1)} %all-to-all-done.moved_ref, bf16[256,256]{1,0:T(8,128)(2,1)S(1)} %get-tuple-element.8.enter_ref, bf16[256,256]{1,0:T(8,128)(2,1)S(1)} %get-tuple-element.9.outer_ref, bf16[256,256]{1,0:T(8,128)(2,1)S(1)} %get-tuple-element.10.inner_ref, ...), custom_call_target="tpu_custom_call" | custom-call | tf_op jit(solution)/shard_map/work/pallas_call | solution.py:308
  22.9 10.3 %all_to_all.10.home_ref = bf16[16,40,128]{2,1,0:T(8,128)(2,1)S(1)} all-to-all(bf16[16,40,128]{2,1,0:T(8,128)(2,1)S(1)} %work.1), channel_id=1, replica_groups={{14,15,0,1,2,3,4,5,6,7,8,9,10,11,12,13},{30,31,16,17,18,19,20,21,22,23,..., dimensions={0} | all-to-all | bytes 327680 | tf_op jit(solution)/shard_map/all_to_all | solution.py:266
  33.2 0.0 copy-start.3
  33.2 0.7 %copy-done.3 = s32[16]{0:T(128)S(1)} copy-done((s32[16]{0:T(128)S(1)}, s32[16]{0:T(128)}, u32[]{:S(2)}) %copy-start.3) | copy-done | bytes 88
  33.9 1.4 %finish.1 = (bf16[1,16,4096]{2,1,0:T(8,128)(2,1)}, f32[1,384]{1,0:T(1,128)}) custom-call(s32[16]{0:T(128)S(1)} %copy-done.3, bf16[16,40,128]{2,1,0:T(8,128)(2,1)S(1)} %all_to_all.10.home_ref, bf16[256,256]{1,0:T(8,128)(2,1)S(1)} %get-tuple-element.12.gather_ref, f32[32,384]{1,0:T(8,128)S(1)} %get-tuple-element.13.chosen_ref), custom_call_target="tpu_custom_call" | custom-call | tf_op jit(solution)/shard_map/finish/pallas_call | solution.py:318
Async XLA Ops:
  2.8 8.7 %copy-start = (bf16[1,64,64]{2,1,0:T(8,128)(2,1)S(1)}, bf16[1,64,64]{2,1,0:T(8,128)(2,1)}, u32[]{:S(2)}) copy-start(bf16[1,64,64]{2,1,0:T(8,128)(2,1)} %param.11) | copy-start | bytes 24580
  2.8 8.7 %copy-start.1 = (bf16[1,64,64]{2,1,0:T(8,128)(2,1)S(1)}, bf16[1,64,64]{2,1,0:T(8,128)(2,1)}, u32[]{:S(2)}) copy-start(bf16[1,64,64]{2,1,0:T(8,128)(2,1)} %param.12) | copy-start | bytes 24580
  2.8 8.7 %copy-start.2 = (f32[1,4096]{1,0:T(1,128)S(1)}, f32[1,4096]{1,0:T(1,128)}, u32[]{:S(2)}) copy-start(f32[1,4096]{1,0:T(1,128)} %param.13) | copy-start | bytes 49156
  2.8 18.8 %all-to-all-start = ((bf16[16,96,128]{2,1,0:T(8,128)(2,1)}), bf16[16,96,128]{2,1,0:T(8,128)(2,1)S(1)}, u32[]{:S(2)}, u32[]{:S(2)}) async-start(bf16[16,96,128]{2,1,0:T(8,128)(2,1)} %pack.1.after_ref), calls=%async_computation | async-start | bytes 786432 | tf_op jit(solution)/shard_map/all_to_all | solution.py:266
  11.5 0.7 %copy-start.4 = (s32[1,384]{1,0:T(1,128)S(1)}, s32[1,384]{1,0:T(1,128)}, u32[]{:S(2)}) copy-start(s32[1,384]{1,0:T(1,128)} %lists_ref.1) | copy-start | bytes 4612
  11.5 0.7 %copy-start.5 = (s32[32]{0:T(128)S(1)}, s32[32]{0:T(128)}, u32[]{:S(2)}) copy-start(s32[32]{0:T(128)} %param.15) | copy-start | bytes 388
  33.2 0.7 %copy-start.3 = (s32[16]{0:T(128)S(1)}, s32[16]{0:T(128)}, u32[]{:S(2)}) copy-start(s32[16]{0:T(128)} %layer_ref.1) | copy-start | bytes 196

commit v10 on v9

--- a/solution.py
+++ b/solution.py
@@ -38,12 +38,6 @@
     return mask(row // SUBLANES + tall * (row % SUBLANES) == iota((size, size), 1))
 
 
-def scatter_rows(tall):
-    size = SUBLANES * tall
-    row = iota((size, size), 0)
-    return mask(row // tall + SUBLANES * (row % tall) == iota((size, size), 1))
-
-
 def half(left, right):
     return jnp.where(iota(left.shape, 1) < LANES // 2, left, right)
 
@@ -58,35 +52,37 @@
     return half(top, swap(low)), half(swap(top), low)
 
 
-def pack(layer_hbm, query_hbm, cand_hbm, out_ref, layer_ref, query_ref, cand_ref, by_module, sems):
+def holds(layer_row, modules, first):
+    slots = layer_row.shape[1]
+    if first:
+        layer_row = jnp.concatenate([layer_row[:, first:], layer_row[:, :first]], axis=1)
+    return mask(iota((modules, slots), 0) == layer_row)
+
+
+def pack(layer_hbm, query_hbm, cand_hbm, out_ref, layer_ref, query_ref, cand_ref, wide, sems):
     arrivals = [
         pltpu.make_async_copy(source, target, sems.at[i])
         for i, (source, target) in enumerate(
-            ((query_hbm, query_ref), (cand_hbm, cand_ref), (layer_hbm, layer_ref))
+            ((layer_hbm, layer_ref), (query_hbm, query_ref), (cand_hbm, cand_ref))
         )
     ]
     for arrival in arrivals:
         arrival.start()
+    arrivals[0].wait()
     modules, flat = query_ref.shape[1:]
-    slots = out_ref.shape[0]
+    slots, height, _ = out_ref.shape
     tall = flat // LANES
-    scatter = scatter_rows(tall)
+    step = height + 1
+    one_hot = holds(layer_ref[...], modules, firsts(slots)[0])
     sources = [(query_ref, r) for r in range(query_ref.shape[0])] + [(cand_ref, r) for r in range(cand_ref.shape[0])]
     for r, (ref, row) in enumerate(sources):
         if row == 0:
-            arrivals[0 if ref is query_ref else 1].wait()
-        rows = ref[row].astype(f32)
-        columns = []
-        for m in range(0, modules, SUBLANES):
-            tiles = [rows[m : m + SUBLANES, j * LANES : (j + 1) * LANES] for j in range(tall)]
-            columns.append(jnp.concatenate(tiles, axis=0).astype(bf16))
-        blocks = dot(scatter, jnp.concatenate(columns, axis=1)).astype(bf16)
-        for m in range(modules):
-            c, g = m % SUBLANES, m // SUBLANES
-            by_module[m, r * tall : (r + 1) * tall, :] = blocks[c * tall : (c + 1) * tall, g * LANES : (g + 1) * LANES]
-    arrivals[2].wait()
-    for k, s in enumerate(order_of(slots, firsts(slots)[0])):
-        out_ref[k] = by_module[layer_ref[s]]
+            arrivals[1 if ref is query_ref else 2].wait()
+        by_slot = dot(one_hot, ref[row], ((0,), (0,)))
+        for j in range(tall):
+            wide[pl.ds(r * tall + j, slots, stride=step), :] = by_slot[:, j * LANES : (j + 1) * LANES]
+    for k in range(slots):
+        out_ref[k] = wide[pl.ds(k * step, height), :].astype(bf16)
 
 
 def upright(row, count):
@@ -95,8 +91,8 @@
 
 
 def prepare(
-    length_ref, out_basis_ref, in_basis_ref, eigen_ref, rows_ref, lists_ref, after_ref,
-    enter_ref, outer_ref, inner_ref, factor_ref, gather_ref, chosen_ref,
+    length_ref, layer_ref, out_basis_ref, in_basis_ref, eigen_ref, rows_ref, lists_ref, after_ref,
+    enter_ref, outer_ref, inner_ref, factor_ref, gather_ref, holds_ref, chosen_ref,
 ):
     del after_ref
     out_basis, in_basis = out_basis_ref[...], in_basis_ref[...]
@@ -116,6 +112,8 @@
     turned = swap(eigen)
     factor_ref[...] = 1.0 / (jnp.concatenate([half(eigen, turned), half(turned, eigen)], axis=0) + damping)
     gather_ref[...] = gather_rows(tall)
+    modules, slots = holds_ref.shape
+    holds_ref[...] = holds(layer_ref[...], modules, firsts(slots)[1])
 
     count = rows_ref.shape[1]
     lists = lists_ref[...]
@@ -203,28 +201,22 @@
         out_ref[k] = jnp.concatenate([homes[k], tails[k * tail : (k + 1) * tail, :]], axis=0).astype(bf16)
 
 
-def finish(layer_ref, home_ref, gather_ref, chosen_ref, precond_ref, scores_ref, by_module):
+def finish(home_ref, holds_ref, chosen_ref, precond_ref, scores_ref, wide):
     slots, send, _ = home_ref.shape
-    modules, flat = precond_ref.shape[1:]
+    _, flat = precond_ref.shape[1:]
     count = chosen_ref.shape[0]
     tall = flat // LANES
-    totals = None
-    for k, s in enumerate(order_of(slots, firsts(slots)[1])):
-        block = home_ref[k].astype(f32)
-        by_module[layer_ref[s]] = block[:tall].astype(bf16)
-        totals = block[tall:] if totals is None else totals + block[tall:]
-    groups = [
-        jnp.concatenate([by_module[m + c] for c in range(SUBLANES)], axis=0) for m in range(0, modules, SUBLANES)
-    ]
-    turned = dot(gather_ref[...], jnp.concatenate(groups, axis=1))
-    for j in range(tall):
-        tiles = [turned[j * SUBLANES : (j + 1) * SUBLANES, g * LANES : (g + 1) * LANES] for g in range(len(groups))]
-        precond_ref[0, :, j * LANES : (j + 1) * LANES] = jnp.concatenate(tiles, axis=0).astype(bf16)
-    wide = -(-count // LANES)
-    parts = [
-        sum((totals[k * wide + t : k * wide + t + 1] for k in range(1, PIECES)), totals[t : t + 1]) for t in range(wide)
-    ]
-    dense = parts[0] if wide == 1 else jnp.concatenate(parts, axis=1)
+    step = send + 1
+    for k in range(slots):
+        wide[pl.ds(k * step, send), :] = home_ref[k].astype(f32)
+    by_slot = jnp.concatenate([wide[pl.ds(j, slots, stride=step), :].astype(bf16) for j in range(tall)], axis=1)
+    precond_ref[0] = dot(holds_ref[...], by_slot).astype(bf16)
+    groups = -(-count // LANES)
+    parts = []
+    for t in range(groups):
+        pieces = [wide[pl.ds(tall + k * groups + t, slots, stride=step), :] for k in range(PIECES)]
+        parts.append(jnp.sum((pieces[2] + pieces[1]) + pieces[0], axis=0, keepdims=True))
+    dense = parts[0] if groups == 1 else jnp.concatenate(parts, axis=1)
     scores_ref[...] = jnp.sum(
         jnp.where(chosen_ref[...] > 0.0, upright(dense, count), 0.0), axis=0, keepdims=True
     )
@@ -251,6 +243,7 @@
     own, modules, flat = query_grads.shape
     per = cand_grads.shape[0]
     slots = layer_map.shape[0]
+    layer_row = layer_map.reshape(1, slots)
     tall = flat // LANES
     side = basis_out.shape[1]
     size = SUBLANES * tall
@@ -271,17 +264,17 @@
         in_specs=[HBM] * 3,
         out_specs=VMEM,
         scratch_shapes=[
-            pltpu.SMEM(layer_map.shape, jnp.int32),
+            pltpu.VMEM(layer_row.shape, jnp.int32),
             pltpu.VMEM(query_grads.shape, bf16),
             pltpu.VMEM(cand_grads.shape, bf16),
-            pltpu.VMEM((modules, height, LANES), bf16),
+            pltpu.VMEM((slots * (height + 1), LANES), f32),
             pltpu.SemaphoreType.DMA((3,)),
         ],
         compiler_params=PARAMS,
         name="pack",
-    )(in_hbm(layer_map), in_hbm(query_grads), in_hbm(cand_grads))
+    )(in_hbm(layer_row), in_hbm(query_grads), in_hbm(cand_grads))
     square = jax.ShapeDtypeStruct((size, size), bf16)
-    enter, outer, inner, factor, gather, chosen = pl.pallas_call(
+    enter, outer, inner, factor, gather, held, chosen = pl.pallas_call(
         prepare,
         out_shape=(
             square,
@@ -289,14 +282,16 @@
             square,
             jax.ShapeDtypeStruct((side, LANES), f32),
             square,
+            jax.ShapeDtypeStruct((modules, slots), bf16),
             jax.ShapeDtypeStruct((count, cand_lists.shape[1]), f32),
         ),
-        in_specs=[SMEM] + [VMEM] * 5 + [ANY],
-        out_specs=[VMEM] * 6,
+        in_specs=[SMEM] + [VMEM] * 6 + [ANY],
+        out_specs=[VMEM] * 7,
         compiler_params=PARAMS,
         name="prepare",
     )(
         list_lengths,
+        layer_row,
         basis_out.reshape(basis_out.shape[1:]),
         basis_in.reshape(basis_in.shape[1:]),
         eigvals.reshape(tall, LANES),
@@ -321,12 +316,12 @@
             jax.ShapeDtypeStruct(query_grads.shape, bf16),
             jax.ShapeDtypeStruct(cand_lists.shape, f32),
         ),
-        in_specs=[SMEM] + [VMEM] * 3,
+        in_specs=[VMEM] * 3,
         out_specs=(VMEM, VMEM),
-        scratch_shapes=[pltpu.VMEM((modules, tall, LANES), bf16)],
+        scratch_shapes=[pltpu.VMEM((slots * (send + 1), LANES), f32)],
         compiler_params=PARAMS,
         name="finish",
-    )(layer_map, home, gather, chosen)
+    )(home, held, chosen)
 
 
 def solution(mesh):

time: 35.6 us -> 34.3 us (0.963)
  local copies, waits for them, and re-layouts: 1.31 us -> 0.65 us
  Pallas kernels: 5.34 us -> 4.7 us
    unnamed x12, local copies, waits for them, and re-layouts: 1.31 us -> 0.65 us
    pallas_call x1, Pallas kernels: 1.41 us -> 0.84 us  [body(): pl.pallas_call(finish, out_shape=(jax.ShapeDtypeStruct(query_grads.shape,...]
where the time goes in v10:
time: 34.3 us; the launch traced here: 34 us
  blocking collectives  10.3 us (30%)
  waiting for transfers between devices  8.91 us (26%)
  starting transfers between devices  8.01 us (23%)
  Pallas kernels  4.7 us (14%)
  between operations  1.38 us (4%)
  local copies, waits for them, and re-layouts  0.65 us (2%)
    all_to_all x1, blocking collectives, swap_over(): lax.all_to_all(x, 'shard', split_axis=0, concat_axis=0, tiled=True, axis_...  10.3 us
    all_to_all x1, waiting for transfers between devices, swap_over(): lax.all_to_all(x, 'shard', split_axis=0, concat_axis=0, tiled=True, axis_...  8.91 us
    all_to_all x1, starting transfers between devices, swap_over(): lax.all_to_all(x, 'shard', split_axis=0, concat_axis=0, tiled=True, axis_...  8.01 us
    pallas_call x1, Pallas kernels, body(): pl.pallas_call(pack, out_shape=pltpu.VMEM((slots, height, LANES), bf16),...  2.07 us
    pallas_call x1, Pallas kernels, body(): pl.pallas_call(work, out_shape=jax.ShapeDtypeStruct((slots, send, LANES),...  1.23 us
    pallas_call x1, Pallas kernels, body(): pl.pallas_call(finish, out_shape=(jax.ShapeDtypeStruct(query_grads.shape,...  0.84 us
  transfers between devices with their start and end apart: 1, of which 1 were waited for; matrix products, arithmetic and copies ran while one was open for 0% of the time, Pallas kernels for 2%

profile of v10, /device:TPU:0, one launch (start us, length us, event | category | flops | bytes accessed | tf_op | source)
XLA Modules:
  0.0 34.0 jit_solution(4003406367270659951)
XLA Ops:
  0.6 2.1 %pack.1.after_ref = bf16[16,96,128]{2,1,0:T(8,128)(2,1)} custom-call(s32[1,16]{1,0:T(1,128)} %bitcast.8, bf16[1,16,4096]{2,1,0:T(8,128)(2,1)} %query_hbm.1, bf16[2,16,4096]{2,1,0:T(8,128)(2,1)} %cand_hbm.1), custom_call_target="tpu_custom_call" | custom-call | tf_op jit(solution)/shard_map/pack/pallas_call | solution.py:261
  2.7 0.0 copy-start
  2.7 0.0 copy-start.1
  2.7 0.0 copy-start.2
  2.7 8.0 %all-to-all-start = ((bf16[16,96,128]{2,1,0:T(8,128)(2,1)}), bf16[16,96,128]{2,1,0:T(8,128)(2,1)S(1)}, u32[]{:S(2)}, u32[]{:S(2)}) async-start(bf16[16,96,128]{2,1,0:T(8,128)(2,1)} %pack.1.after_ref), calls=%async_computation | async-start | bytes 786432 | tf_op jit(solution)/shard_map/all_to_all | solution.py:259
  11.4 0.0 copy-start.4
  11.4 0.0 copy-start.3
  11.4 0.0 copy-start.5
  11.4 0.0 copy-done
  11.5 0.0 copy-done.1
  11.5 0.0 copy-done.2
  11.5 0.6 %copy-done.4 = s32[1,384]{1,0:T(1,128)S(1)} copy-done((s32[1,384]{1,0:T(1,128)S(1)}, s32[1,384]{1,0:T(1,128)}, u32[]{:S(2)}) %copy-start.4) | copy-done | bytes 1560
  12.1 0.0 copy-done.3
  12.1 0.0 copy-done.5
  12.1 0.6 %prepare.1 = (bf16[256,256]{1,0:T(8,128)(2,1)S(1)}, bf16[256,256]{1,0:T(8,128)(2,1)S(1)}, bf16[256,256]{1,0:T(8,128)(2,1)S(1)}, f32[64,128]{1,0:T(8,128)S(1)}, b...) custom-call(s32[1]{0:T(128)S(6)} %copy.11.length_ref, s32[1,16]{1,0:T(1,128)S(1)} %bitcast.9, ...), custom_call_target="tpu_custom_call" | custom-call | tf_op jit(solution)/shard_map/prepare/pallas_call | solution.py:277
  12.7 8.9 %all-to-all-done.moved_ref = bf16[16,96,128]{2,1,0:T(8,128)(2,1)S(1)} async-done(((bf16[16,96,128]{2,1,0:T(8,128)(2,1)}), bf16[16,96,128]{2,1,0:T(8,128)(2,1)S(1)}, u32[]{:S(2)}, u32[]{:S(2)}) %all-to-all-start) | async-done | bytes 393248 | tf_op jit(solution)/shard_map/all_to_all | solution.py:259
  21.6 1.2 %work.1 = bf16[16,40,128]{2,1,0:T(8,128)(2,1)S(1)} custom-call(bf16[16,96,128]{2,1,0:T(8,128)(2,1)S(1)} %all-to-all-done.moved_ref, bf16[256,256]{1,0:T(8,128)(2,1)S(1)} %get-tuple-element.9.enter_ref, bf16[256,256]{1,0:T(8,128)(2,1)S(1)} %get-tuple-element.10.outer_ref, bf16[256,256]{1,0:T(8,128)(2,1)S(1)} %get-tuple-element.11.inner_ref, ...), custom_call_target="tpu_custom_call" | custom-call | tf_op jit(solution)/shard_map/work/pallas_call | solution.py:303
  22.8 10.3 %all_to_all.10.home_ref = bf16[16,40,128]{2,1,0:T(8,128)(2,1)S(1)} all-to-all(bf16[16,40,128]{2,1,0:T(8,128)(2,1)S(1)} %work.1), channel_id=1, replica_groups={{14,15,0,1,2,3,4,5,6,7,8,9,10,11,12,13},{30,31,16,17,18,19,20,21,22,23,..., dimensions={0} | all-to-all | bytes 327680 | tf_op jit(solution)/shard_map/all_to_all | solution.py:259
  33.1 0.8 %finish.1 = (bf16[1,16,4096]{2,1,0:T(8,128)(2,1)}, f32[1,384]{1,0:T(1,128)}) custom-call(bf16[16,40,128]{2,1,0:T(8,128)(2,1)S(1)} %all_to_all.10.home_ref, bf16[16,16]{1,0:T(8,128)(2,1)S(1)} %get-tuple-element.14.holds_ref, f32[32,384]{1,0:T(8,128)S(1)} %get-tuple-element.15.chosen_ref), custom_call_target="tpu_custom_call" | custom-call | tf_op jit(solution)/shard_map/finish/pallas_call | solution.py:313
Async XLA Ops:
  2.7 8.7 %copy-start = (bf16[1,64,64]{2,1,0:T(8,128)(2,1)S(1)}, bf16[1,64,64]{2,1,0:T(8,128)(2,1)}, u32[]{:S(2)}) copy-start(bf16[1,64,64]{2,1,0:T(8,128)(2,1)} %param.11) | copy-start | bytes 24580
  2.7 8.7 %copy-start.1 = (bf16[1,64,64]{2,1,0:T(8,128)(2,1)S(1)}, bf16[1,64,64]{2,1,0:T(8,128)(2,1)}, u32[]{:S(2)}) copy-start(bf16[1,64,64]{2,1,0:T(8,128)(2,1)} %param.12) | copy-start | bytes 24580
  2.7 8.7 %copy-start.2 = (f32[1,4096]{1,0:T(1,128)S(1)}, f32[1,4096]{1,0:T(1,128)}, u32[]{:S(2)}) copy-start(f32[1,4096]{1,0:T(1,128)} %param.13) | copy-start | bytes 49156
  2.7 18.8 %all-to-all-start = ((bf16[16,96,128]{2,1,0:T(8,128)(2,1)}), bf16[16,96,128]{2,1,0:T(8,128)(2,1)S(1)}, u32[]{:S(2)}, u32[]{:S(2)}) async-start(bf16[16,96,128]{2,1,0:T(8,128)(2,1)} %pack.1.after_ref), calls=%async_computation | async-start | bytes 786432 | tf_op jit(solution)/shard_map/all_to_all | solution.py:259
  11.4 0.7 %copy-start.4 = (s32[1,384]{1,0:T(1,128)S(1)}, s32[1,384]{1,0:T(1,128)}, u32[]{:S(2)}) copy-start(s32[1,384]{1,0:T(1,128)} %lists_ref.1) | copy-start | bytes 4612
  11.4 0.7 %copy-start.3 = (s32[16]{0:T(128)S(1)}, s32[16]{0:T(128)}, u32[]{:S(2)}) copy-start(s32[16]{0:T(128)} %param.14) | copy-start | bytes 196
  11.4 0.7 %copy-start.5 = (s32[32]{0:T(128)S(1)}, s32[32]{0:T(128)}, u32[]{:S(2)}) copy-start(s32[32]{0:T(128)} %param.15) | copy-start | bytes 388

commit v11 on v10

--- a/solution.py
+++ b/solution.py
@@ -29,7 +29,7 @@
 
 
 def firsts(slots):
-    return slots // 4, slots - 2
+    return slots * 5 // 8, slots * 5 // 8
 
 
 def gather_rows(tall):
@@ -59,7 +59,7 @@
     return mask(iota((modules, slots), 0) == layer_row)
 
 
-def pack(layer_hbm, query_hbm, cand_hbm, out_ref, layer_ref, query_ref, cand_ref, wide, sems):
+def pack(layer_hbm, query_hbm, cand_hbm, out_hbm, layer_ref, query_ref, cand_ref, wide, ready, sems):
     arrivals = [
         pltpu.make_async_copy(source, target, sems.at[i])
         for i, (source, target) in enumerate(
@@ -70,19 +70,28 @@
         arrival.start()
     arrivals[0].wait()
     modules, flat = query_ref.shape[1:]
-    slots, height, _ = out_ref.shape
+    slots = out_hbm.shape[0]
     tall = flat // LANES
-    step = height + 1
+    step = tall + 1
     one_hot = holds(layer_ref[...], modules, firsts(slots)[0])
     sources = [(query_ref, r) for r in range(query_ref.shape[0])] + [(cand_ref, r) for r in range(cand_ref.shape[0])]
+    departures = []
     for r, (ref, row) in enumerate(sources):
         if row == 0:
             arrivals[1 if ref is query_ref else 2].wait()
         by_slot = dot(one_hot, ref[row], ((0,), (0,)))
+        base = r * slots * step
         for j in range(tall):
-            wide[pl.ds(r * tall + j, slots, stride=step), :] = by_slot[:, j * LANES : (j + 1) * LANES]
-    for k in range(slots):
-        out_ref[k] = wide[pl.ds(k * step, height), :].astype(bf16)
+            wide[pl.ds(base + j, slots, stride=step), :] = by_slot[:, j * LANES : (j + 1) * LANES]
+        part = pl.ds(r * tall, tall)
+        for k in range(slots):
+            ready[k, part, :] = wide[pl.ds(base + k * step, tall), :].astype(bf16)
+        departures.append(
+            pltpu.make_async_copy(ready.at[:, part, :], out_hbm.at[:, part, :], sems.at[len(arrivals) + r])
+        )
+        departures[-1].start()
+    for departure in departures:
+        departure.wait()
 
 
 def upright(row, count):
@@ -201,7 +210,7 @@
         out_ref[k] = jnp.concatenate([homes[k], tails[k * tail : (k + 1) * tail, :]], axis=0).astype(bf16)
 
 
-def finish(home_ref, holds_ref, chosen_ref, precond_ref, scores_ref, wide):
+def finish(home_ref, holds_ref, chosen_ref, precond_hbm, scores_ref, wide, precond_ref, sem):
     slots, send, _ = home_ref.shape
     _, flat = precond_ref.shape[1:]
     count = chosen_ref.shape[0]
@@ -211,6 +220,8 @@
         wide[pl.ds(k * step, send), :] = home_ref[k].astype(f32)
     by_slot = jnp.concatenate([wide[pl.ds(j, slots, stride=step), :].astype(bf16) for j in range(tall)], axis=1)
     precond_ref[0] = dot(holds_ref[...], by_slot).astype(bf16)
+    departure = pltpu.make_async_copy(precond_ref, precond_hbm, sem)
+    departure.start()
     groups = -(-count // LANES)
     parts = []
     for t in range(groups):
@@ -220,6 +231,7 @@
     scores_ref[...] = jnp.sum(
         jnp.where(chosen_ref[...] > 0.0, upright(dense, count), 0.0), axis=0, keepdims=True
     )
+    departure.wait()
 
 
 HBM = pl.BlockSpec(memory_space=pltpu.HBM)
@@ -260,15 +272,16 @@
 
     packed = pl.pallas_call(
         pack,
-        out_shape=pltpu.VMEM((slots, height, LANES), bf16),
+        out_shape=jax.ShapeDtypeStruct((slots, height, LANES), bf16),
         in_specs=[HBM] * 3,
-        out_specs=VMEM,
+        out_specs=HBM,
         scratch_shapes=[
             pltpu.VMEM(layer_row.shape, jnp.int32),
             pltpu.VMEM(query_grads.shape, bf16),
             pltpu.VMEM(cand_grads.shape, bf16),
-            pltpu.VMEM((slots * (height + 1), LANES), f32),
-            pltpu.SemaphoreType.DMA((3,)),
+            pltpu.VMEM(((own + per) * slots * (tall + 1), LANES), f32),
+            pltpu.VMEM((slots, height, LANES), bf16),
+            pltpu.SemaphoreType.DMA((3 + own + per,)),
         ],
         compiler_params=PARAMS,
         name="pack",
@@ -317,8 +330,12 @@
             jax.ShapeDtypeStruct(cand_lists.shape, f32),
         ),
         in_specs=[VMEM] * 3,
-        out_specs=(VMEM, VMEM),
-        scratch_shapes=[pltpu.VMEM((slots * (send + 1), LANES), f32)],
+        out_specs=(HBM, VMEM),
+        scratch_shapes=[
+            pltpu.VMEM((slots * (send + 1), LANES), f32),
+            pltpu.VMEM(query_grads.shape, bf16),
+            pltpu.SemaphoreType.DMA,
+        ],
         compiler_params=PARAMS,
         name="finish",
     )(home, held, chosen)

time: 34.3 us -> 34.2 us (level)
  waiting for transfers between devices: 8.91 us -> 7.11 us
  blocking collectives: 10.3 us -> 10.9 us
  Pallas kernels: 4.7 us -> 5.23 us
  starting transfers between devices: 8.01 us -> 8.51 us
    all_to_all x1, waiting for transfers between devices: 8.91 us -> 7.11 us  [swap_over(): lax.all_to_all(x, 'shard', split_axis=0, concat_axis=0, tiled=True, axis_...]
    all_to_all x1, blocking collectives: 10.3 us -> 10.9 us  [swap_over(): lax.all_to_all(x, 'shard', split_axis=0, concat_axis=0, tiled=True, axis_...]
    pallas_call x1, Pallas kernels: 0.84 us -> 1.4 us  [body(): pl.pallas_call(finish, out_shape=(jax.ShapeDtypeStruct(query_grads.shape,...]
    all_to_all x1, starting transfers between devices: 8.01 us -> 8.51 us  [swap_over(): lax.all_to_all(x, 'shard', split_axis=0, concat_axis=0, tiled=True, axis_...]
where the time goes in v11:
time: 34.2 us; the launch traced here: 33.8 us
  blocking collectives  10.9 us (32%)
  starting transfers between devices  8.51 us (25%)
  waiting for transfers between devices  7.11 us (21%)
  Pallas kernels  5.23 us (15%)
  between operations  1.38 us (4%)
  local copies, waits for them, and re-layouts  0.65 us (2%)
    all_to_all x1, blocking collectives, swap_over(): lax.all_to_all(x, 'shard', split_axis=0, concat_axis=0, tiled=True, axis_...  10.9 us
    all_to_all x1, starting transfers between devices, swap_over(): lax.all_to_all(x, 'shard', split_axis=0, concat_axis=0, tiled=True, axis_...  8.51 us
    all_to_all x1, waiting for transfers between devices, swap_over(): lax.all_to_all(x, 'shard', split_axis=0, concat_axis=0, tiled=True, axis_...  7.11 us
    pallas_call x1, Pallas kernels, body(): pl.pallas_call(pack, out_shape=jax.ShapeDtypeStruct((slots, height, LANES...  2.04 us
    pallas_call x1, Pallas kernels, body(): pl.pallas_call(finish, out_shape=(jax.ShapeDtypeStruct(query_grads.shape,...  1.4 us
    pallas_call x1, Pallas kernels, body(): pl.pallas_call(work, out_shape=jax.ShapeDtypeStruct((slots, send, LANES),...  1.22 us
  transfers between devices with their start and end apart: 1, of which 1 were waited for; matrix products, arithmetic and copies ran while one was open for 0% of the time, Pallas kernels for 2%

profile of v11, /device:TPU:0, one launch (start us, length us, event | category | flops | bytes accessed | tf_op | source)
XLA Modules:
  0.0 33.8 jit_solution(12729572489912516962)
XLA Ops:
  0.6 2.0 %pack.1.after_ref = bf16[16,96,128]{2,1,0:T(8,128)(2,1)} custom-call(s32[1,16]{1,0:T(1,128)} %bitcast.8, bf16[1,16,4096]{2,1,0:T(8,128)(2,1)} %query_hbm.1, bf16[2,16,4096]{2,1,0:T(8,128)(2,1)} %cand_hbm.1), custom_call_target="tpu_custom_call" | custom-call | tf_op jit(solution)/shard_map/pack/pallas_call | solution.py:273
  2.7 0.0 copy-start
  2.7 0.0 copy-start.1
  2.7 0.0 copy-start.2
  2.7 8.5 %all-to-all-start = ((bf16[16,96,128]{2,1,0:T(8,128)(2,1)}), bf16[16,96,128]{2,1,0:T(8,128)(2,1)S(1)}, u32[]{:S(2)}, u32[]{:S(2)}) async-start(bf16[16,96,128]{2,1,0:T(8,128)(2,1)} %pack.1.after_ref), calls=%async_computation | async-start | bytes 786432 | tf_op jit(solution)/shard_map/all_to_all | solution.py:271
  11.9 0.0 copy-start.4
  11.9 0.0 copy-start.3
  11.9 0.0 copy-start.5
  11.9 0.0 copy-done
  11.9 0.0 copy-done.1
  11.9 0.0 copy-done.2
  12.0 0.6 %copy-done.4 = s32[1,384]{1,0:T(1,128)S(1)} copy-done((s32[1,384]{1,0:T(1,128)S(1)}, s32[1,384]{1,0:T(1,128)}, u32[]{:S(2)}) %copy-start.4) | copy-done | bytes 1560
  12.6 0.0 copy-done.3
  12.6 0.0 copy-done.5
  12.6 0.6 %prepare.1 = (bf16[256,256]{1,0:T(8,128)(2,1)S(1)}, bf16[256,256]{1,0:T(8,128)(2,1)S(1)}, bf16[256,256]{1,0:T(8,128)(2,1)S(1)}, f32[64,128]{1,0:T(8,128)S(1)}, b...) custom-call(s32[1]{0:T(128)S(6)} %copy.11.length_ref, s32[1,16]{1,0:T(1,128)S(1)} %bitcast.9, ...), custom_call_target="tpu_custom_call" | custom-call | tf_op jit(solution)/shard_map/prepare/pallas_call | solution.py:290
  13.1 7.1 %all-to-all-done.moved_ref = bf16[16,96,128]{2,1,0:T(8,128)(2,1)S(1)} async-done(((bf16[16,96,128]{2,1,0:T(8,128)(2,1)}), bf16[16,96,128]{2,1,0:T(8,128)(2,1)S(1)}, u32[]{:S(2)}, u32[]{:S(2)}) %all-to-all-start) | async-done | bytes 393248 | tf_op jit(solution)/shard_map/all_to_all | solution.py:271
  20.2 1.2 %work.1 = bf16[16,40,128]{2,1,0:T(8,128)(2,1)S(1)} custom-call(bf16[16,96,128]{2,1,0:T(8,128)(2,1)S(1)} %all-to-all-done.moved_ref, bf16[256,256]{1,0:T(8,128)(2,1)S(1)} %get-tuple-element.9.enter_ref, bf16[256,256]{1,0:T(8,128)(2,1)S(1)} %get-tuple-element.10.outer_ref, bf16[256,256]{1,0:T(8,128)(2,1)S(1)} %get-tuple-element.11.inner_ref, ...), custom_call_target="tpu_custom_call" | custom-call | tf_op jit(solution)/shard_map/work/pallas_call | solution.py:316
  21.5 10.9 %all_to_all.10.home_ref = bf16[16,40,128]{2,1,0:T(8,128)(2,1)S(1)} all-to-all(bf16[16,40,128]{2,1,0:T(8,128)(2,1)S(1)} %work.1), channel_id=1, replica_groups={{10,11,12,13,14,15,0,1,2,3,4,5,6,7,8,9},{26,27,28,29,30,31,16,17,18,19,..., dimensions={0} | all-to-all | bytes 327680 | tf_op jit(solution)/shard_map/all_to_all | solution.py:271
  32.4 1.4 %finish.1 = (bf16[1,16,4096]{2,1,0:T(8,128)(2,1)}, f32[1,384]{1,0:T(1,128)}) custom-call(bf16[16,40,128]{2,1,0:T(8,128)(2,1)S(1)} %all_to_all.10.home_ref, bf16[16,16]{1,0:T(8,128)(2,1)S(1)} %get-tuple-element.14.holds_ref, f32[32,384]{1,0:T(8,128)S(1)} %get-tuple-element.15.chosen_ref), custom_call_target="tpu_custom_call" | custom-call | tf_op jit(solution)/shard_map/finish/pallas_call | solution.py:326
Async XLA Ops:
  2.7 9.2 %copy-start = (bf16[1,64,64]{2,1,0:T(8,128)(2,1)S(1)}, bf16[1,64,64]{2,1,0:T(8,128)(2,1)}, u32[]{:S(2)}) copy-start(bf16[1,64,64]{2,1,0:T(8,128)(2,1)} %param.11) | copy-start | bytes 24580
  2.7 9.2 %copy-start.1 = (bf16[1,64,64]{2,1,0:T(8,128)(2,1)S(1)}, bf16[1,64,64]{2,1,0:T(8,128)(2,1)}, u32[]{:S(2)}) copy-start(bf16[1,64,64]{2,1,0:T(8,128)(2,1)} %param.12) | copy-start | bytes 24580
  2.7 9.2 %copy-start.2 = (f32[1,4096]{1,0:T(1,128)S(1)}, f32[1,4096]{1,0:T(1,128)}, u32[]{:S(2)}) copy-start(f32[1,4096]{1,0:T(1,128)} %param.13) | copy-start | bytes 49156
  2.7 17.5 %all-to-all-start = ((bf16[16,96,128]{2,1,0:T(8,128)(2,1)}), bf16[16,96,128]{2,1,0:T(8,128)(2,1)S(1)}, u32[]{:S(2)}, u32[]{:S(2)}) async-start(bf16[16,96,128]{2,1,0:T(8,128)(2,1)} %pack.1.after_ref), calls=%async_computation | async-start | bytes 786432 | tf_op jit(solution)/shard_map/all_to_all | solution.py:271
  11.9 0.7 %copy-start.4 = (s32[1,384]{1,0:T(1,128)S(1)}, s32[1,384]{1,0:T(1,128)}, u32[]{:S(2)}) copy-start(s32[1,384]{1,0:T(1,128)} %lists_ref.1) | copy-start | bytes 4612
  11.9 0.7 %copy-start.3 = (s32[16]{0:T(128)S(1)}, s32[16]{0:T(128)}, u32[]{:S(2)}) copy-start(s32[16]{0:T(128)} %param.14) | copy-start | bytes 196
  11.9 0.7 %copy-start.5 = (s32[32]{0:T(128)S(1)}, s32[32]{0:T(128)}, u32[]{:S(2)}) copy-start(s32[32]{0:T(128)} %param.15) | copy-start | bytes 388

commit v12 on v10

--- a/solution.py
+++ b/solution.py
@@ -29,7 +29,7 @@
 
 
 def firsts(slots):
-    return slots // 4, slots - 2
+    return slots * 5 // 8, slots * 5 // 8
 
 
 def gather_rows(tall):
@@ -59,26 +59,16 @@
     return mask(iota((modules, slots), 0) == layer_row)
 
 
-def pack(layer_hbm, query_hbm, cand_hbm, out_ref, layer_ref, query_ref, cand_ref, wide, sems):
-    arrivals = [
-        pltpu.make_async_copy(source, target, sems.at[i])
-        for i, (source, target) in enumerate(
-            ((layer_hbm, layer_ref), (query_hbm, query_ref), (cand_hbm, cand_ref))
-        )
-    ]
-    for arrival in arrivals:
-        arrival.start()
-    arrivals[0].wait()
+def pack(layer_ref, query_ref, cand_ref, out_ref, wide):
     modules, flat = query_ref.shape[1:]
     slots, height, _ = out_ref.shape
     tall = flat // LANES
     step = height + 1
     one_hot = holds(layer_ref[...], modules, firsts(slots)[0])
-    sources = [(query_ref, r) for r in range(query_ref.shape[0])] + [(cand_ref, r) for r in range(cand_ref.shape[0])]
-    for r, (ref, row) in enumerate(sources):
-        if row == 0:
-            arrivals[1 if ref is query_ref else 2].wait()
-        by_slot = dot(one_hot, ref[row], ((0,), (0,)))
+    sources = [query_ref[r] for r in range(query_ref.shape[0])]
+    sources += [cand_ref[r] for r in range(cand_ref.shape[0])]
+    for r, rows in enumerate(sources):
+        by_slot = dot(one_hot, rows, ((0,), (0,)))
         for j in range(tall):
             wide[pl.ds(r * tall + j, slots, stride=step), :] = by_slot[:, j * LANES : (j + 1) * LANES]
     for k in range(slots):
@@ -222,7 +212,6 @@
     )
 
 
-HBM = pl.BlockSpec(memory_space=pltpu.HBM)
 ANY = pl.BlockSpec(memory_space=pl.ANY)
 SMEM = pl.BlockSpec(memory_space=pltpu.SMEM)
 VMEM = pl.BlockSpec(memory_space=pltpu.VMEM)
@@ -260,16 +249,10 @@
 
     packed = pl.pallas_call(
         pack,
-        out_shape=pltpu.VMEM((slots, height, LANES), bf16),
-        in_specs=[HBM] * 3,
+        out_shape=jax.ShapeDtypeStruct((slots, height, LANES), bf16),
+        in_specs=[VMEM] * 3,
         out_specs=VMEM,
-        scratch_shapes=[
-            pltpu.VMEM(layer_row.shape, jnp.int32),
-            pltpu.VMEM(query_grads.shape, bf16),
-            pltpu.VMEM(cand_grads.shape, bf16),
-            pltpu.VMEM((slots * (height + 1), LANES), f32),
-            pltpu.SemaphoreType.DMA((3,)),
-        ],
+        scratch_shapes=[pltpu.VMEM((slots * (height + 1), LANES), f32)],
         compiler_params=PARAMS,
         name="pack",
     )(in_hbm(layer_row), in_hbm(query_grads), in_hbm(cand_grads))

time: 34.3 us -> 33.7 us (0.983)
  waiting for transfers between devices: 8.91 us -> 7.1 us
  blocking collectives: 10.3 us -> 10.9 us
  starting transfers between devices: 8.01 us -> 8.5 us
    all_to_all x1, waiting for transfers between devices: 8.91 us -> 7.1 us  [swap_over(): lax.all_to_all(x, 'shard', split_axis=0, concat_axis=0, tiled=True, axis_...]
    all_to_all x1, blocking collectives: 10.3 us -> 10.9 us  [swap_over(): lax.all_to_all(x, 'shard', split_axis=0, concat_axis=0, tiled=True, axis_...]
    all_to_all x1, starting transfers between devices: 8.01 us -> 8.5 us  [swap_over(): lax.all_to_all(x, 'shard', split_axis=0, concat_axis=0, tiled=True, axis_...]
where the time goes in v12:
time: 33.7 us; the launch traced here: 33.3 us
  blocking collectives  10.9 us (32%)
  starting transfers between devices  8.5 us (25%)
  waiting for transfers between devices  7.1 us (21%)
  Pallas kernels  4.79 us (14%)
  between operations  1.35 us (4%)
  local copies, waits for them, and re-layouts  0.65 us (2%)
    all_to_all x1, blocking collectives, swap_over(): lax.all_to_all(x, 'shard', split_axis=0, concat_axis=0, tiled=True, axis_...  10.9 us
    all_to_all x1, starting transfers between devices, swap_over(): lax.all_to_all(x, 'shard', split_axis=0, concat_axis=0, tiled=True, axis_...  8.5 us
    all_to_all x1, waiting for transfers between devices, swap_over(): lax.all_to_all(x, 'shard', split_axis=0, concat_axis=0, tiled=True, axis_...  7.1 us
    pallas_call x1, Pallas kernels, body(): pl.pallas_call(pack, out_shape=jax.ShapeDtypeStruct((slots, height, LANES...  2.17 us
    pallas_call x1, Pallas kernels, body(): pl.pallas_call(work, out_shape=jax.ShapeDtypeStruct((slots, send, LANES),...  1.22 us
    pallas_call x1, Pallas kernels, body(): pl.pallas_call(finish, out_shape=(jax.ShapeDtypeStruct(query_grads.shape,...  0.83 us
  transfers between devices with their start and end apart: 1, of which 1 were waited for; matrix products, arithmetic and copies ran while one was open for 0% of the time, Pallas kernels for 2%

profile of v12, /device:TPU:0, one launch (start us, length us, event | category | flops | bytes accessed | tf_op | source)
XLA Modules:
  0.0 33.3 jit_solution(16163613060769048495)
XLA Ops:
  0.6 2.2 %pack.1.after_ref = bf16[16,96,128]{2,1,0:T(8,128)(2,1)} custom-call(s32[1,16]{1,0:T(1,128)} %bitcast.8, bf16[1,16,4096]{2,1,0:T(8,128)(2,1)} %query_ref.1, bf16[2,16,4096]{2,1,0:T(8,128)(2,1)} %cand_ref.1), custom_call_target="tpu_custom_call" | custom-call | tf_op jit(solution)/shard_map/pack/pallas_call | solution.py:250
  2.8 0.0 copy-start
  2.8 0.0 copy-start.1
  2.8 0.0 copy-start.2
  2.8 8.5 %all-to-all-start = ((bf16[16,96,128]{2,1,0:T(8,128)(2,1)}), bf16[16,96,128]{2,1,0:T(8,128)(2,1)S(1)}, u32[]{:S(2)}, u32[]{:S(2)}) async-start(bf16[16,96,128]{2,1,0:T(8,128)(2,1)} %pack.1.after_ref), calls=%async_computation | async-start | bytes 786432 | tf_op jit(solution)/shard_map/all_to_all | solution.py:248
  12.0 0.0 copy-start.4
  12.0 0.0 copy-start.3
  12.0 0.0 copy-start.5
  12.0 0.0 copy-done
  12.0 0.0 copy-done.1
  12.0 0.0 copy-done.2
  12.0 0.6 %copy-done.4 = s32[1,384]{1,0:T(1,128)S(1)} copy-done((s32[1,384]{1,0:T(1,128)S(1)}, s32[1,384]{1,0:T(1,128)}, u32[]{:S(2)}) %copy-start.4) | copy-done | bytes 1560
  12.6 0.0 copy-done.3
  12.6 0.0 copy-done.5
  12.6 0.6 %prepare.1 = (bf16[256,256]{1,0:T(8,128)(2,1)S(1)}, bf16[256,256]{1,0:T(8,128)(2,1)S(1)}, bf16[256,256]{1,0:T(8,128)(2,1)S(1)}, f32[64,128]{1,0:T(8,128)S(1)}, b...) custom-call(s32[1]{0:T(128)S(6)} %copy.11.length_ref, s32[1,16]{1,0:T(1,128)S(1)} %bitcast.9, ...), custom_call_target="tpu_custom_call" | custom-call | tf_op jit(solution)/shard_map/prepare/pallas_call | solution.py:260
  13.2 7.1 %all-to-all-done.moved_ref = bf16[16,96,128]{2,1,0:T(8,128)(2,1)S(1)} async-done(((bf16[16,96,128]{2,1,0:T(8,128)(2,1)}), bf16[16,96,128]{2,1,0:T(8,128)(2,1)S(1)}, u32[]{:S(2)}, u32[]{:S(2)}) %all-to-all-start) | async-done | bytes 393248 | tf_op jit(solution)/shard_map/all_to_all | solution.py:248
  20.3 1.2 %work.1 = bf16[16,40,128]{2,1,0:T(8,128)(2,1)S(1)} custom-call(bf16[16,96,128]{2,1,0:T(8,128)(2,1)S(1)} %all-to-all-done.moved_ref, bf16[256,256]{1,0:T(8,128)(2,1)S(1)} %get-tuple-element.9.enter_ref, bf16[256,256]{1,0:T(8,128)(2,1)S(1)} %get-tuple-element.10.outer_ref, bf16[256,256]{1,0:T(8,128)(2,1)S(1)} %get-tuple-element.11.inner_ref, ...), custom_call_target="tpu_custom_call" | custom-call | tf_op jit(solution)/shard_map/work/pallas_call | solution.py:286
  21.6 10.9 %all_to_all.10.home_ref = bf16[16,40,128]{2,1,0:T(8,128)(2,1)S(1)} all-to-all(bf16[16,40,128]{2,1,0:T(8,128)(2,1)S(1)} %work.1), channel_id=1, replica_groups={{10,11,12,13,14,15,0,1,2,3,4,5,6,7,8,9},{26,27,28,29,30,31,16,17,18,19,..., dimensions={0} | all-to-all | bytes 327680 | tf_op jit(solution)/shard_map/all_to_all | solution.py:248
  32.5 0.8 %finish.1 = (bf16[1,16,4096]{2,1,0:T(8,128)(2,1)}, f32[1,384]{1,0:T(1,128)}) custom-call(bf16[16,40,128]{2,1,0:T(8,128)(2,1)S(1)} %all_to_all.10.home_ref, bf16[16,16]{1,0:T(8,128)(2,1)S(1)} %get-tuple-element.14.holds_ref, f32[32,384]{1,0:T(8,128)S(1)} %get-tuple-element.15.chosen_ref), custom_call_target="tpu_custom_call" | custom-call | tf_op jit(solution)/shard_map/finish/pallas_call | solution.py:296
Async XLA Ops:
  2.8 9.2 %copy-start = (bf16[1,64,64]{2,1,0:T(8,128)(2,1)S(1)}, bf16[1,64,64]{2,1,0:T(8,128)(2,1)}, u32[]{:S(2)}) copy-start(bf16[1,64,64]{2,1,0:T(8,128)(2,1)} %param.11) | copy-start | bytes 24580
  2.8 9.2 %copy-start.1 = (bf16[1,64,64]{2,1,0:T(8,128)(2,1)S(1)}, bf16[1,64,64]{2,1,0:T(8,128)(2,1)}, u32[]{:S(2)}) copy-start(bf16[1,64,64]{2,1,0:T(8,128)(2,1)} %param.12) | copy-start | bytes 24580
  2.8 9.2 %copy-start.2 = (f32[1,4096]{1,0:T(1,128)S(1)}, f32[1,4096]{1,0:T(1,128)}, u32[]{:S(2)}) copy-start(f32[1,4096]{1,0:T(1,128)} %param.13) | copy-start | bytes 49156
  2.8 17.5 %all-to-all-start = ((bf16[16,96,128]{2,1,0:T(8,128)(2,1)}), bf16[16,96,128]{2,1,0:T(8,128)(2,1)S(1)}, u32[]{:S(2)}, u32[]{:S(2)}) async-start(bf16[16,96,128]{2,1,0:T(8,128)(2,1)} %pack.1.after_ref), calls=%async_computation | async-start | bytes 786432 | tf_op jit(solution)/shard_map/all_to_all | solution.py:248
  12.0 0.7 %copy-start.4 = (s32[1,384]{1,0:T(1,128)S(1)}, s32[1,384]{1,0:T(1,128)}, u32[]{:S(2)}) copy-start(s32[1,384]{1,0:T(1,128)} %lists_ref.1) | copy-start | bytes 4612
  12.0 0.7 %copy-start.3 = (s32[16]{0:T(128)S(1)}, s32[16]{0:T(128)}, u32[]{:S(2)}) copy-start(s32[16]{0:T(128)} %param.14) | copy-start | bytes 196
  12.0 0.7 %copy-start.5 = (s32[32]{0:T(128)S(1)}, s32[32]{0:T(128)}, u32[]{:S(2)}) copy-start(s32[32]{0:T(128)} %param.15) | copy-start | bytes 388

commit v13 on v12

--- a/solution.py
+++ b/solution.py
@@ -9,6 +9,7 @@
 LANES = 128
 SUBLANES = 8
 PIECES = 3
+PARTS = 4
 f32, bf16 = jnp.float32, jnp.bfloat16
 
 
@@ -24,12 +25,17 @@
     return condition.astype(f32).astype(bf16)
 
 
-def order_of(slots, first):
-    return [(first + k) % slots for k in range(slots)]
-
-
-def firsts(slots):
-    return slots * 5 // 8, slots * 5 // 8
+def reversed_bits(k, slots):
+    bits = (slots - 1).bit_length()
+    return sum(((k >> b) & 1) << (bits - 1 - b) for b in range(bits))
+
+
+def centre(slots):
+    return slots * 5 // 8
+
+
+def order_of(slots):
+    return [reversed_bits(k, slots) ^ centre(slots) for k in range(slots)]
 
 
 def gather_rows(tall):
@@ -52,25 +58,44 @@
     return half(top, swap(low)), half(swap(top), low)
 
 
-def holds(layer_row, modules, first):
+def holds(layer_row, modules):
     slots = layer_row.shape[1]
-    if first:
-        layer_row = jnp.concatenate([layer_row[:, first:], layer_row[:, :first]], axis=1)
-    return mask(iota((modules, slots), 0) == layer_row)
-
-
-def pack(layer_ref, query_ref, cand_ref, out_ref, wide):
+    order = reversed_bits(iota((slots, slots), 1), slots) ^ centre(slots)
+    placed = mask(iota((slots, slots), 0) == order)
+    return dot(mask(iota((modules, slots), 0) == layer_row), placed).astype(bf16)
+
+
+def pack(layer_hbm, query_hbm, cand_hbm, out_ref, layer_ref, query_ref, cand_ref, wide, sems):
     modules, flat = query_ref.shape[1:]
     slots, height, _ = out_ref.shape
     tall = flat // LANES
     step = height + 1
-    one_hot = holds(layer_ref[...], modules, firsts(slots)[0])
-    sources = [query_ref[r] for r in range(query_ref.shape[0])]
-    sources += [cand_ref[r] for r in range(cand_ref.shape[0])]
-    for r, rows in enumerate(sources):
-        by_slot = dot(one_hot, rows, ((0,), (0,)))
-        for j in range(tall):
-            wide[pl.ds(r * tall + j, slots, stride=step), :] = by_slot[:, j * LANES : (j + 1) * LANES]
+    first = pltpu.make_async_copy(layer_hbm, layer_ref, sems.at[2 * PARTS])
+    first.start()
+    arrivals = []
+    for g in range(PARTS):
+        part = pl.ds(g * flat // PARTS, flat // PARTS)
+        arrivals.append(
+            [
+                pltpu.make_async_copy(source.at[:, :, part], target.at[:, :, part], sems.at[2 * g + i])
+                for i, (source, target) in enumerate(((query_hbm, query_ref), (cand_hbm, cand_ref)))
+            ]
+        )
+        for arrival in arrivals[-1]:
+            arrival.start()
+    first.wait()
+    one_hot = holds(layer_ref[...], modules)
+    for g in range(PARTS):
+        part = slice(g * flat // PARTS, (g + 1) * flat // PARTS)
+        r = 0
+        for arrival, ref in zip(arrivals[g], (query_ref, cand_ref)):
+            arrival.wait()
+            for row in range(ref.shape[0]):
+                by_slot = dot(one_hot, ref[row, :, part], ((0,), (0,)))
+                for j in range(tall // PARTS):
+                    place = r * tall + g * tall // PARTS + j
+                    wide[pl.ds(place, slots, stride=step), :] = by_slot[:, j * LANES : (j + 1) * LANES]
+                r += 1
     for k in range(slots):
         out_ref[k] = wide[pl.ds(k * step, height), :].astype(bf16)
 
@@ -103,7 +128,7 @@
     factor_ref[...] = 1.0 / (jnp.concatenate([half(eigen, turned), half(turned, eigen)], axis=0) + damping)
     gather_ref[...] = gather_rows(tall)
     modules, slots = holds_ref.shape
-    holds_ref[...] = holds(layer_ref[...], modules, firsts(slots)[1])
+    holds_ref[...] = holds(layer_ref[...], modules)
 
     count = rows_ref.shape[1]
     lists = lists_ref[...]
@@ -123,8 +148,7 @@
     count = sources * per
     pairs = sources // 2
     stacks = pairs // 4
-    arrive, leave = firsts(sources)
-    places = [(d - leave) % sources for d in order_of(sources, arrive)]
+    order = order_of(sources)
     outer, inner, gather = outer_ref[...], inner_ref[...], gather_ref[...]
     factor = factor_ref[...]
 
@@ -150,7 +174,7 @@
     for p in range(pairs):
         t, u = p // 4, p % 4
         block = precond[u * side : (u + 1) * side, t * LANES : (t + 1) * LANES]
-        homes[places[2 * p]], homes[places[2 * p + 1]] = unpaired(block)
+        homes[2 * p], homes[2 * p + 1] = unpaired(block)
 
     def flat(blocks):
         groups = [
@@ -172,7 +196,7 @@
         )
 
     cands = [
-        moved_ref[(d - arrive) % sources, (1 + c) * tall : (2 + c) * tall, :]
+        moved_ref[order.index(d), (1 + c) * tall : (2 + c) * tall, :]
         for d in range(sources)
         for c in range(per)
     ]
@@ -212,6 +236,7 @@
     )
 
 
+HBM = pl.BlockSpec(memory_space=pltpu.HBM)
 ANY = pl.BlockSpec(memory_space=pl.ANY)
 SMEM = pl.BlockSpec(memory_space=pltpu.SMEM)
 VMEM = pl.BlockSpec(memory_space=pltpu.VMEM)
@@ -243,16 +268,22 @@
     def in_hbm(x):
         return pltpu.with_memory_space_constraint(x, pltpu.HBM)
 
-    def swap_over(x, first):
-        groups = [order_of(slots, first)]
+    def swap_over(x):
+        groups = [order_of(slots)]
         return lax.all_to_all(x, "shard", split_axis=0, concat_axis=0, tiled=True, axis_index_groups=groups)
 
     packed = pl.pallas_call(
         pack,
         out_shape=jax.ShapeDtypeStruct((slots, height, LANES), bf16),
-        in_specs=[VMEM] * 3,
+        in_specs=[HBM] * 3,
         out_specs=VMEM,
-        scratch_shapes=[pltpu.VMEM((slots * (height + 1), LANES), f32)],
+        scratch_shapes=[
+            pltpu.VMEM(layer_row.shape, jnp.int32),
+            pltpu.VMEM(query_grads.shape, bf16),
+            pltpu.VMEM(cand_grads.shape, bf16),
+            pltpu.VMEM((slots * (height + 1), LANES), f32),
+            pltpu.SemaphoreType.DMA((2 * PARTS + 1,)),
+        ],
         compiler_params=PARAMS,
         name="pack",
     )(in_hbm(layer_row), in_hbm(query_grads), in_hbm(cand_grads))
@@ -282,7 +313,7 @@
         cand_lists,
         packed,
     )
-    moved = swap_over(packed, firsts(slots)[0])
+    moved = swap_over(packed)
     homes = pl.pallas_call(
         work,
         out_shape=jax.ShapeDtypeStruct((slots, send, LANES), bf16),
@@ -292,7 +323,7 @@
         compiler_params=PARAMS,
         name="work",
     )(moved, enter, outer, inner, factor, gather)
-    home = swap_over(homes, firsts(slots)[1])
+    home = swap_over(homes)
     return pl.pallas_call(
         finish,
         out_shape=(

time: 33.7 us -> 34.7 us (1.030)
  Pallas kernels: 4.79 us -> 5.34 us
    pallas_call x1, Pallas kernels: 2.17 us -> 2.72 us  [body(): pl.pallas_call(pack, out_shape=jax.ShapeDtypeStruct((slots, height, LANES...]
where the time goes in v13:
time: 34.7 us; the launch traced here: 34.3 us
  blocking collectives  11.1 us (32%)
  starting transfers between devices  8.5 us (24%)
  waiting for transfers between devices  7.29 us (21%)
  Pallas kernels  5.34 us (15%)
  between operations  1.38 us (4%)
  local copies, waits for them, and re-layouts  0.65 us (2%)
    all_to_all x1, blocking collectives, swap_over(): lax.all_to_all(x, 'shard', split_axis=0, concat_axis=0, tiled=True, axis_...  11.1 us
    all_to_all x1, starting transfers between devices, swap_over(): lax.all_to_all(x, 'shard', split_axis=0, concat_axis=0, tiled=True, axis_...  8.5 us
    all_to_all x1, waiting for transfers between devices, swap_over(): lax.all_to_all(x, 'shard', split_axis=0, concat_axis=0, tiled=True, axis_...  7.29 us
    pallas_call x1, Pallas kernels, body(): pl.pallas_call(pack, out_shape=jax.ShapeDtypeStruct((slots, height, LANES...  2.72 us
    pallas_call x1, Pallas kernels, body(): pl.pallas_call(work, out_shape=jax.ShapeDtypeStruct((slots, send, LANES),...  1.22 us
    pallas_call x1, Pallas kernels, body(): pl.pallas_call(finish, out_shape=(jax.ShapeDtypeStruct(query_grads.shape,...  0.84 us
  transfers between devices with their start and end apart: 1, of which 1 were waited for; matrix products, arithmetic and copies ran while one was open for 0% of the time, Pallas kernels for 2%

profile of v13, /device:TPU:0, one launch (start us, length us, event | category | flops | bytes accessed | tf_op | source)
XLA Modules:
  0.0 34.3 jit_solution(12135876729021230844)
XLA Ops:
  0.6 2.7 %pack.1.after_ref = bf16[16,96,128]{2,1,0:T(8,128)(2,1)} custom-call(s32[1,16]{1,0:T(1,128)} %bitcast.8, bf16[1,16,4096]{2,1,0:T(8,128)(2,1)} %query_hbm.1, bf16[2,16,4096]{2,1,0:T(8,128)(2,1)} %cand_hbm.1), custom_call_target="tpu_custom_call" | custom-call | tf_op jit(solution)/shard_map/pack/pallas_call | solution.py:275
  3.4 0.0 copy-start
  3.4 0.0 copy-start.1
  3.4 0.0 copy-start.2
  3.4 8.5 %all-to-all-start = ((bf16[16,96,128]{2,1,0:T(8,128)(2,1)}), bf16[16,96,128]{2,1,0:T(8,128)(2,1)S(1)}, u32[]{:S(2)}, u32[]{:S(2)}) async-start(bf16[16,96,128]{2,1,0:T(8,128)(2,1)} %pack.1.after_ref), calls=%async_computation | async-start | bytes 786432 | tf_op jit(solution)/shard_map/all_to_all | solution.py:273
  12.5 0.0 copy-start.4
  12.6 0.0 copy-start.3
  12.6 0.0 copy-start.5
  12.6 0.0 copy-done
  12.6 0.0 copy-done.1
  12.6 0.0 copy-done.2
  12.6 0.6 %copy-done.4 = s32[1,384]{1,0:T(1,128)S(1)} copy-done((s32[1,384]{1,0:T(1,128)S(1)}, s32[1,384]{1,0:T(1,128)}, u32[]{:S(2)}) %copy-start.4) | copy-done | bytes 1560
  13.2 0.0 copy-done.3
  13.2 0.0 copy-done.5
  13.2 0.6 %prepare.1 = (bf16[256,256]{1,0:T(8,128)(2,1)S(1)}, bf16[256,256]{1,0:T(8,128)(2,1)S(1)}, bf16[256,256]{1,0:T(8,128)(2,1)S(1)}, f32[64,128]{1,0:T(8,128)S(1)}, b...) custom-call(s32[1]{0:T(128)S(6)} %copy.11.length_ref, s32[1,16]{1,0:T(1,128)S(1)} %bitcast.9, ...), custom_call_target="tpu_custom_call" | custom-call | tf_op jit(solution)/shard_map/prepare/pallas_call | solution.py:291
  13.8 7.3 %all-to-all-done.moved_ref = bf16[16,96,128]{2,1,0:T(8,128)(2,1)S(1)} async-done(((bf16[16,96,128]{2,1,0:T(8,128)(2,1)}), bf16[16,96,128]{2,1,0:T(8,128)(2,1)S(1)}, u32[]{:S(2)}, u32[]{:S(2)}) %all-to-all-start) | async-done | bytes 393248 | tf_op jit(solution)/shard_map/all_to_all | solution.py:273
  21.1 1.2 %work.1 = bf16[16,40,128]{2,1,0:T(8,128)(2,1)S(1)} custom-call(bf16[16,96,128]{2,1,0:T(8,128)(2,1)S(1)} %all-to-all-done.moved_ref, bf16[256,256]{1,0:T(8,128)(2,1)S(1)} %get-tuple-element.9.enter_ref, bf16[256,256]{1,0:T(8,128)(2,1)S(1)} %get-tuple-element.10.outer_ref, bf16[256,256]{1,0:T(8,128)(2,1)S(1)} %get-tuple-element.11.inner_ref, ...), custom_call_target="tpu_custom_call" | custom-call | tf_op jit(solution)/shard_map/work/pallas_call | solution.py:317
  22.3 11.1 %all_to_all.10.home_ref = bf16[16,40,128]{2,1,0:T(8,128)(2,1)S(1)} all-to-all(bf16[16,40,128]{2,1,0:T(8,128)(2,1)S(1)} %work.1), channel_id=1, replica_groups={{10,2,14,6,8,0,12,4,11,3,15,7,9,1,13,5},{26,18,30,22,24,16,28,20,27,19,..., dimensions={0} | all-to-all | bytes 327680 | tf_op jit(solution)/shard_map/all_to_all | solution.py:273
  33.4 0.8 %finish.1 = (bf16[1,16,4096]{2,1,0:T(8,128)(2,1)}, f32[1,384]{1,0:T(1,128)}) custom-call(bf16[16,40,128]{2,1,0:T(8,128)(2,1)S(1)} %all_to_all.10.home_ref, bf16[16,16]{1,0:T(8,128)(2,1)S(1)} %get-tuple-element.14.holds_ref, f32[32,384]{1,0:T(8,128)S(1)} %get-tuple-element.15.chosen_ref), custom_call_target="tpu_custom_call" | custom-call | tf_op jit(solution)/shard_map/finish/pallas_call | solution.py:327
Async XLA Ops:
  3.4 9.2 %copy-start = (bf16[1,64,64]{2,1,0:T(8,128)(2,1)S(1)}, bf16[1,64,64]{2,1,0:T(8,128)(2,1)}, u32[]{:S(2)}) copy-start(bf16[1,64,64]{2,1,0:T(8,128)(2,1)} %param.11) | copy-start | bytes 24580
  3.4 9.2 %copy-start.1 = (bf16[1,64,64]{2,1,0:T(8,128)(2,1)S(1)}, bf16[1,64,64]{2,1,0:T(8,128)(2,1)}, u32[]{:S(2)}) copy-start(bf16[1,64,64]{2,1,0:T(8,128)(2,1)} %param.12) | copy-start | bytes 24580
  3.4 9.2 %copy-start.2 = (f32[1,4096]{1,0:T(1,128)S(1)}, f32[1,4096]{1,0:T(1,128)}, u32[]{:S(2)}) copy-start(f32[1,4096]{1,0:T(1,128)} %param.13) | copy-start | bytes 49156
  3.4 17.7 %all-to-all-start = ((bf16[16,96,128]{2,1,0:T(8,128)(2,1)}), bf16[16,96,128]{2,1,0:T(8,128)(2,1)S(1)}, u32[]{:S(2)}, u32[]{:S(2)}) async-start(bf16[16,96,128]{2,1,0:T(8,128)(2,1)} %pack.1.after_ref), calls=%async_computation | async-start | bytes 786432 | tf_op jit(solution)/shard_map/all_to_all | solution.py:273
  12.5 0.7 %copy-start.4 = (s32[1,384]{1,0:T(1,128)S(1)}, s32[1,384]{1,0:T(1,128)}, u32[]{:S(2)}) copy-start(s32[1,384]{1,0:T(1,128)} %lists_ref.1) | copy-start | bytes 4612
  12.6 0.7 %copy-start.3 = (s32[16]{0:T(128)S(1)}, s32[16]{0:T(128)}, u32[]{:S(2)}) copy-start(s32[16]{0:T(128)} %param.14) | copy-start | bytes 196
  12.6 0.7 %copy-start.5 = (s32[32]{0:T(128)S(1)}, s32[32]{0:T(128)}, u32[]{:S(2)}) copy-start(s32[32]{0:T(128)} %param.15) | copy-start | bytes 388

commit v14 on v12

--- a/solution.py
+++ b/solution.py
@@ -38,6 +38,12 @@
     return mask(row // SUBLANES + tall * (row % SUBLANES) == iota((size, size), 1))
 
 
+def scatter_rows(tall):
+    size = SUBLANES * tall
+    row = iota((size, size), 0)
+    return mask(row // tall + SUBLANES * (row % tall) == iota((size, size), 1))
+
+
 def half(left, right):
     return jnp.where(iota(left.shape, 1) < LANES // 2, left, right)
 
@@ -59,33 +65,7 @@
     return mask(iota((modules, slots), 0) == layer_row)
 
 
-def pack(layer_ref, query_ref, cand_ref, out_ref, wide):
-    modules, flat = query_ref.shape[1:]
-    slots, height, _ = out_ref.shape
-    tall = flat // LANES
-    step = height + 1
-    one_hot = holds(layer_ref[...], modules, firsts(slots)[0])
-    sources = [query_ref[r] for r in range(query_ref.shape[0])]
-    sources += [cand_ref[r] for r in range(cand_ref.shape[0])]
-    for r, rows in enumerate(sources):
-        by_slot = dot(one_hot, rows, ((0,), (0,)))
-        for j in range(tall):
-            wide[pl.ds(r * tall + j, slots, stride=step), :] = by_slot[:, j * LANES : (j + 1) * LANES]
-    for k in range(slots):
-        out_ref[k] = wide[pl.ds(k * step, height), :].astype(bf16)
-
-
-def upright(row, count):
-    shape = (count, row.shape[1])
-    return jnp.sum(jnp.where(iota(shape, 0) == iota(shape, 1), row, 0.0), axis=1, keepdims=True)
-
-
-def prepare(
-    length_ref, layer_ref, out_basis_ref, in_basis_ref, eigen_ref, rows_ref, lists_ref, after_ref,
-    enter_ref, outer_ref, inner_ref, factor_ref, gather_ref, holds_ref, chosen_ref,
-):
-    del after_ref
-    out_basis, in_basis = out_basis_ref[...], in_basis_ref[...]
+def spread_bases(out_basis, in_basis, eigen, enter_ref, outer_ref, inner_ref, factor_ref):
     side = out_basis.shape[0]
     tall = side // 2
     size = enter_ref.shape[0]
@@ -98,20 +78,82 @@
     outer_ref[...] = jnp.where(row == column, outer, 0.0).astype(bf16)
     inner_ref[...] = jnp.where(row == column, inner, 0.0).astype(bf16)
     enter_ref[...] = jnp.where(row == 2 * (column % 2) + column // 2, inner, 0.0).astype(bf16)
-    eigen = eigen_ref[...]
     turned = swap(eigen)
     factor_ref[...] = 1.0 / (jnp.concatenate([half(eigen, turned), half(turned, eigen)], axis=0) + damping)
+
+
+def pack(
+    layer_hbm, out_basis_hbm, in_basis_hbm, eigen_hbm, query_hbm, cand_hbm,
+    out_ref, enter_ref, outer_ref, inner_ref, factor_ref, gather_ref,
+    layer_ref, out_basis_ref, in_basis_ref, eigen_ref, query_ref, cand_ref, by_module, sems,
+):
+    arrivals = [
+        pltpu.make_async_copy(source, target, sems.at[i])
+        for i, (source, target) in enumerate(
+            (
+                (layer_hbm, layer_ref),
+                (out_basis_hbm, out_basis_ref),
+                (in_basis_hbm, in_basis_ref),
+                (eigen_hbm, eigen_ref),
+                (query_hbm, query_ref),
+                (cand_hbm, cand_ref),
+            )
+        )
+    ]
+    for arrival in arrivals:
+        arrival.start()
+    modules, flat = query_ref.shape[1:]
+    slots = out_ref.shape[0]
+    tall = flat // LANES
+    order = order_of(slots, firsts(slots)[0])
     gather_ref[...] = gather_rows(tall)
-    modules, slots = holds_ref.shape
-    holds_ref[...] = holds(layer_ref[...], modules, firsts(slots)[1])
-
-    count = rows_ref.shape[1]
-    lists = lists_ref[...]
-    longest = lists.shape[1]
-    rows = upright(rows_ref[...].astype(f32), count)
-    place = jnp.sum(jnp.where(iota((count, longest), 0) == lists, rows, 0.0), axis=0, keepdims=True)
-    place = jnp.where(iota((1, longest), 1) < length_ref[0], place.astype(jnp.int32), -1)
-    chosen_ref[...] = (iota((count, longest), 0) == place).astype(f32)
+    for arrival in arrivals[:4]:
+        arrival.wait()
+    spread_bases(
+        out_basis_ref[...], in_basis_ref[...], eigen_ref[...], enter_ref, outer_ref, inner_ref, factor_ref
+    )
+    at_once = slots * tall <= 512
+    if at_once:
+        shape = (tall, tall * modules)
+        offset = iota(shape, 1) - modules * iota(shape, 0)
+        place = jnp.concatenate([mask(offset == layer_ref[s]) for s in order], axis=0)
+    else:
+        place = scatter_rows(tall)
+    r = 0
+    for arrival, ref in zip(arrivals[4:], (query_ref, cand_ref)):
+        arrival.wait()
+        many = ref.shape[0]
+        if at_once:
+            tiles = [
+                jnp.concatenate([ref[i, :, j * LANES : (j + 1) * LANES] for j in range(tall)], axis=0)
+                for i in range(many)
+            ]
+            blocks = dot(place, jnp.concatenate(tiles, axis=1)).astype(bf16)
+            for k in range(slots):
+                for i in range(many):
+                    part = blocks[k * tall : (k + 1) * tall, i * LANES : (i + 1) * LANES]
+                    out_ref[k, (r + i) * tall : (r + i + 1) * tall, :] = part
+        else:
+            for i in range(many):
+                rows = ref[i].astype(f32)
+                columns = []
+                for m in range(0, modules, SUBLANES):
+                    tiles = [rows[m : m + SUBLANES, j * LANES : (j + 1) * LANES] for j in range(tall)]
+                    columns.append(jnp.concatenate(tiles, axis=0).astype(bf16))
+                blocks = dot(place, jnp.concatenate(columns, axis=1)).astype(bf16)
+                for m in range(modules):
+                    c, g = m % SUBLANES, m // SUBLANES
+                    part = blocks[c * tall : (c + 1) * tall, g * LANES : (g + 1) * LANES]
+                    by_module[m, (r + i) * tall : (r + i + 1) * tall, :] = part
+        r += many
+    if not at_once:
+        for k, s in enumerate(order):
+            out_ref[k] = by_module[layer_ref[s]]
+
+
+def upright(row, count):
+    shape = (count, row.shape[1])
+    return jnp.sum(jnp.where(iota(shape, 0) == iota(shape, 1), row, 0.0), axis=1, keepdims=True)
 
 
 def work(moved_ref, enter_ref, outer_ref, inner_ref, factor_ref, gather_ref, out_ref, tails):
@@ -191,16 +233,22 @@
         out_ref[k] = jnp.concatenate([homes[k], tails[k * tail : (k + 1) * tail, :]], axis=0).astype(bf16)
 
 
-def finish(home_ref, holds_ref, chosen_ref, precond_ref, scores_ref, wide):
+def finish(length_ref, layer_ref, rows_ref, lists_ref, home_ref, precond_ref, scores_ref, wide):
     slots, send, _ = home_ref.shape
-    _, flat = precond_ref.shape[1:]
-    count = chosen_ref.shape[0]
+    modules, flat = precond_ref.shape[1:]
     tall = flat // LANES
     step = send + 1
     for k in range(slots):
         wide[pl.ds(k * step, send), :] = home_ref[k].astype(f32)
     by_slot = jnp.concatenate([wide[pl.ds(j, slots, stride=step), :].astype(bf16) for j in range(tall)], axis=1)
-    precond_ref[0] = dot(holds_ref[...], by_slot).astype(bf16)
+    precond_ref[0] = dot(holds(layer_ref[...], modules, firsts(slots)[1]), by_slot).astype(bf16)
+
+    count = rows_ref.shape[1]
+    lists = lists_ref[...]
+    longest = lists.shape[1]
+    rows = upright(rows_ref[...].astype(f32), count)
+    place = jnp.sum(jnp.where(iota((count, longest), 0) == lists, rows, 0.0), axis=0, keepdims=True)
+    place = jnp.where(iota((1, longest), 1) < length_ref[...], place.astype(jnp.int32), -1)
     groups = -(-count // LANES)
     parts = []
     for t in range(groups):
@@ -208,12 +256,11 @@
         parts.append(jnp.sum((pieces[2] + pieces[1]) + pieces[0], axis=0, keepdims=True))
     dense = parts[0] if groups == 1 else jnp.concatenate(parts, axis=1)
     scores_ref[...] = jnp.sum(
-        jnp.where(chosen_ref[...] > 0.0, upright(dense, count), 0.0), axis=0, keepdims=True
+        jnp.where(iota((count, longest), 0) == place, upright(dense, count), 0.0), axis=0, keepdims=True
     )
 
 
-ANY = pl.BlockSpec(memory_space=pl.ANY)
-SMEM = pl.BlockSpec(memory_space=pltpu.SMEM)
+HBM = pl.BlockSpec(memory_space=pltpu.HBM)
 VMEM = pl.BlockSpec(memory_space=pltpu.VMEM)
 PARAMS = pltpu.CompilerParams(vmem_limit_bytes=40 * 1024 * 1024)
 
@@ -247,41 +294,33 @@
         groups = [order_of(slots, first)]
         return lax.all_to_all(x, "shard", split_axis=0, concat_axis=0, tiled=True, axis_index_groups=groups)
 
-    packed = pl.pallas_call(
+    square = pltpu.VMEM((size, size), bf16)
+    operands = (
+        layer_map,
+        basis_out.reshape(basis_out.shape[1:]),
+        basis_in.reshape(basis_in.shape[1:]),
+        eigvals.reshape(tall, LANES),
+        query_grads,
+        cand_grads,
+    )
+    packed, enter, outer, inner, factor, gather = pl.pallas_call(
         pack,
-        out_shape=jax.ShapeDtypeStruct((slots, height, LANES), bf16),
-        in_specs=[VMEM] * 3,
-        out_specs=VMEM,
-        scratch_shapes=[pltpu.VMEM((slots * (height + 1), LANES), f32)],
-        compiler_params=PARAMS,
-        name="pack",
-    )(in_hbm(layer_row), in_hbm(query_grads), in_hbm(cand_grads))
-    square = jax.ShapeDtypeStruct((size, size), bf16)
-    enter, outer, inner, factor, gather, held, chosen = pl.pallas_call(
-        prepare,
         out_shape=(
+            pltpu.VMEM((slots, height, LANES), bf16),
             square,
             square,
             square,
-            jax.ShapeDtypeStruct((side, LANES), f32),
+            pltpu.VMEM((side, LANES), f32),
             square,
-            jax.ShapeDtypeStruct((modules, slots), bf16),
-            jax.ShapeDtypeStruct((count, cand_lists.shape[1]), f32),
         ),
-        in_specs=[SMEM] + [VMEM] * 6 + [ANY],
-        out_specs=[VMEM] * 7,
+        in_specs=[HBM] * len(operands),
+        out_specs=[VMEM] * 6,
+        scratch_shapes=[pltpu.SMEM(layer_map.shape, jnp.int32)]
+        + [pltpu.VMEM(x.shape, x.dtype) for x in operands[1:]]
+        + [pltpu.VMEM((modules, height, LANES), bf16), pltpu.SemaphoreType.DMA((len(operands),))],
         compiler_params=PARAMS,
-        name="prepare",
-    )(
-        list_lengths,
-        layer_row,
-        basis_out.reshape(basis_out.shape[1:]),
-        basis_in.reshape(basis_in.shape[1:]),
-        eigvals.reshape(tall, LANES),
-        cand_rows.reshape(1, count),
-        cand_lists,
-        packed,
-    )
+        name="pack",
+    )(*(in_hbm(x) for x in operands))
     moved = swap_over(packed, firsts(slots)[0])
     homes = pl.pallas_call(
         work,
@@ -299,12 +338,12 @@
             jax.ShapeDtypeStruct(query_grads.shape, bf16),
             jax.ShapeDtypeStruct(cand_lists.shape, f32),
         ),
-        in_specs=[VMEM] * 3,
+        in_specs=[VMEM] * 5,
         out_specs=(VMEM, VMEM),
         scratch_shapes=[pltpu.VMEM((slots * (send + 1), LANES), f32)],
         compiler_params=PARAMS,
         name="finish",
-    )(home, held, chosen)
+    )(list_lengths.reshape(1, 1), layer_row, cand_rows.reshape(1, count), cand_lists, home)
 
 
 def solution(mesh):

time: 33.7 us -> 34.6 us (1.027)
  blocking collectives: 10.9 us -> 16.7 us
  starting transfers between devices: 8.5 us -> 5.81 us
  waiting for transfers between devices: 7.1 us -> 4.79 us
    all_to_all x1, blocking collectives: 10.9 us -> 16.7 us  [swap_over(): lax.all_to_all(x, 'shard', split_axis=0, concat_axis=0, tiled=True, axis_...]
    all_to_all x1, starting transfers between devices: 8.5 us -> 5.81 us  [swap_over(): lax.all_to_all(x, 'shard', split_axis=0, concat_axis=0, tiled=True, axis_...]
    all_to_all x1, waiting for transfers between devices: 7.1 us -> 4.79 us  [swap_over(): lax.all_to_all(x, 'shard', split_axis=0, concat_axis=0, tiled=True, axis_...]
    pallas_call x1, Pallas kernels: 1.22 us -> 1.89 us  [body(): pl.pallas_call(work, out_shape=jax.ShapeDtypeStruct((slots, send, LANES),...]
    pallas_call x2 -> x1, Pallas kernels: 2.73 us -> 2.22 us  [body(): pl.pallas_call(pack, out_shape=(pltpu.VMEM((slots, height, LANES), bf16),...]
  transfers between devices with their start and end apart: 1 -> 1, of which waited for: 1 -> 1; matrix products, arithmetic and copies ran while one was open for 0% -> 0% of each run, Pallas kernels for 2% -> 0%
where the time goes in v14:
time: 34.6 us; the launch traced here: 34.3 us
  blocking collectives  16.7 us (48%)
  starting transfers between devices  5.81 us (17%)
  Pallas kernels  5 us (14%)
  waiting for transfers between devices  4.79 us (14%)
  between operations  1.3 us (4%)
  local copies, waits for them, and re-layouts  0.68 us (2%)
    all_to_all x1, blocking collectives, swap_over(): lax.all_to_all(x, 'shard', split_axis=0, concat_axis=0, tiled=True, axis_...  16.7 us
    all_to_all x1, starting transfers between devices, swap_over(): lax.all_to_all(x, 'shard', split_axis=0, concat_axis=0, tiled=True, axis_...  5.81 us
    all_to_all x1, waiting for transfers between devices, swap_over(): lax.all_to_all(x, 'shard', split_axis=0, concat_axis=0, tiled=True, axis_...  4.79 us
    pallas_call x1, Pallas kernels, body(): pl.pallas_call(pack, out_shape=(pltpu.VMEM((slots, height, LANES), bf16),...  2.22 us
    pallas_call x1, Pallas kernels, body(): pl.pallas_call(work, out_shape=jax.ShapeDtypeStruct((slots, send, LANES),...  1.89 us
    pallas_call x1, Pallas kernels, body(): pl.pallas_call(finish, out_shape=(jax.ShapeDtypeStruct(query_grads.shape,...  0.89 us
  transfers between devices with their start and end apart: 1, of which 1 were waited for; matrix products, arithmetic and copies ran while one was open for 0% of the time, Pallas kernels for 0%

profile of v14, /device:TPU:0, one launch (start us, length us, event | category | flops | bytes accessed | tf_op | source)
XLA Modules:
  0.0 34.3 jit_solution(789845017610972715)
XLA Ops:
  0.6 2.2 %pack.1 = (bf16[16,96,128]{2,1,0:T(8,128)(2,1)S(1)}, bf16[256,256]{1,0:T(8,128)(2,1)S(1)}, bf16[256,256]{1,0:T(8,128)(2,1)S(1)}, bf16[256,256]{1,0:T(8,128)(2,1)...) custom-call(s32[16]{0:T(128)} %layer_hbm.1, bf16[64,64]{1,0:T(8,128)(2,1)} %bitcast.9, ...), custom_call_target="tpu_custom_call" | custom-call | tf_op jit(solution)/shard_map/pack/pallas_call | solution.py:306
  2.9 16.7 %all_to_all.10.moved_ref = bf16[16,96,128]{2,1,0:T(8,128)(2,1)S(1)} all-to-all(bf16[16,96,128]{2,1,0:T(8,128)(2,1)S(1)} %get-tuple-element.8), channel_id=1, replica_groups={{10,11,12,13,14,15,0,1,2,3,4,5,6,7,8,9},{26,27,28,29,30,31,16,17,18,19,..., dimensions={0} | all-to-all | bytes 786432 | tf_op jit(solution)/shard_map/all_to_all | solution.py:295
  19.5 1.9 %work.1 = bf16[16,40,128]{2,1,0:T(8,128)(2,1)} custom-call(bf16[16,96,128]{2,1,0:T(8,128)(2,1)S(1)} %all_to_all.10.moved_ref, bf16[256,256]{1,0:T(8,128)(2,1)S(1)} %get-tuple-element.9.enter_ref, bf16[256,256]{1,0:T(8,128)(2,1)S(1)} %get-tuple-element.10.outer_ref, bf16[256,256]{1,0:T(8,128)(2,1)S(1)} %get-tuple-element.11.inner_ref, ...), custom_call_target="tpu_custom_call" | custom-call | tf_op jit(solution)/shard_map/work/pallas_call | solution.py:325
  21.4 5.8 %all-to-all-start.1 = ((bf16[16,40,128]{2,1,0:T(8,128)(2,1)}), bf16[16,40,128]{2,1,0:T(8,128)(2,1)S(1)}, u32[]{:S(2)}, u32[]{:S(2)}) async-start(bf16[16,40,128]{2,1,0:T(8,128)(2,1)} %work.1), calls=%async_computation.1 | async-start | bytes 327680 | tf_op jit(solution)/shard_map/all_to_all | solution.py:295
  27.9 4.8 %all-to-all-done.1.home_ref = bf16[16,40,128]{2,1,0:T(8,128)(2,1)S(1)} async-done(((bf16[16,40,128]{2,1,0:T(8,128)(2,1)}), bf16[16,40,128]{2,1,0:T(8,128)(2,1)S(1)}, u32[]{:S(2)}, u32[]{:S(2)}) %all-to-all-start.1) | async-done | bytes 163872 | tf_op jit(solution)/shard_map/all_to_all | solution.py:295
  32.7 0.0 copy-start.1
  32.7 0.0 copy-start
  32.7 0.0 copy-start.2
  32.7 0.7 %copy-done.1 = s32[1,384]{1,0:T(1,128)S(1)} copy-done((s32[1,384]{1,0:T(1,128)S(1)}, s32[1,384]{1,0:T(1,128)}, u32[]{:S(2)}) %copy-start.1) | copy-done | bytes 1560
  33.4 0.0 copy-done
  33.4 0.0 copy-done.2
  33.4 0.9 %finish.1 = (bf16[1,16,4096]{2,1,0:T(8,128)(2,1)}, f32[1,384]{1,0:T(1,128)}) custom-call(s32[1,1]{1,0:T(1,128)} %bitcast.6.length_ref, s32[1,16]{1,0:T(1,128)S(1)} %bitcast.7, s32[1,32]{1,0:T(1,128)S(1)} %bitcast.8, s32[1,384]{1,0:T(1,128)S(1)} %copy-done.1, bf16[16,40,128]{2,1,0:T(8,128)(2,1)S(1)} %all-to-all-done.1.home_ref), custom_call_target="tpu_custom_call" | custom-call | tf_op jit(solution)/shard_map/finish/pallas_call | solution.py:335
Async XLA Ops:
  21.4 11.2 %all-to-all-start.1 = ((bf16[16,40,128]{2,1,0:T(8,128)(2,1)}), bf16[16,40,128]{2,1,0:T(8,128)(2,1)S(1)}, u32[]{:S(2)}, u32[]{:S(2)}) async-start(bf16[16,40,128]{2,1,0:T(8,128)(2,1)} %work.1), calls=%async_computation.1 | async-start | bytes 327680 | tf_op jit(solution)/shard_map/all_to_all | solution.py:295
  32.7 0.7 %copy-start.1 = (s32[1,384]{1,0:T(1,128)S(1)}, s32[1,384]{1,0:T(1,128)}, u32[]{:S(2)}) copy-start(s32[1,384]{1,0:T(1,128)} %lists_ref.1) | copy-start | bytes 4612
  32.7 0.7 %copy-start = (s32[16]{0:T(128)S(1)}, s32[16]{0:T(128)}, u32[]{:S(2)}) copy-start(s32[16]{0:T(128)} %layer_hbm.1) | copy-start | bytes 196
  32.7 0.7 %copy-start.2 = (s32[32]{0:T(128)S(1)}, s32[32]{0:T(128)}, u32[]{:S(2)}) copy-start(s32[32]{0:T(128)} %param.15) | copy-start | bytes 388

commit v15 on v14

--- a/solution.py
+++ b/solution.py
@@ -58,46 +58,11 @@
     return half(top, swap(low)), half(swap(top), low)
 
 
-def holds(layer_row, modules, first):
-    slots = layer_row.shape[1]
-    if first:
-        layer_row = jnp.concatenate([layer_row[:, first:], layer_row[:, :first]], axis=1)
-    return mask(iota((modules, slots), 0) == layer_row)
-
-
-def spread_bases(out_basis, in_basis, eigen, enter_ref, outer_ref, inner_ref, factor_ref):
-    side = out_basis.shape[0]
-    tall = side // 2
-    size = enter_ref.shape[0]
-    order = mask(iota((side, side), 1) == 2 * (iota((side, side), 0) % tall) + iota((side, side), 0) // tall)
-    basis = dot(dot(order, out_basis).astype(bf16), order, ((1,), (1,))).astype(bf16)
-    spread = mask(iota((size, side), 0) % side == iota((size, side), 1))
-    row, column = iota((size, size), 0) // side, iota((size, size), 1) // side
-    outer = dot(dot(spread, basis).astype(bf16), spread, ((1,), (1,)))
-    inner = dot(dot(spread, in_basis).astype(bf16), spread, ((1,), (1,)))
-    outer_ref[...] = jnp.where(row == column, outer, 0.0).astype(bf16)
-    inner_ref[...] = jnp.where(row == column, inner, 0.0).astype(bf16)
-    enter_ref[...] = jnp.where(row == 2 * (column % 2) + column // 2, inner, 0.0).astype(bf16)
-    turned = swap(eigen)
-    factor_ref[...] = 1.0 / (jnp.concatenate([half(eigen, turned), half(turned, eigen)], axis=0) + damping)
-
-
-def pack(
-    layer_hbm, out_basis_hbm, in_basis_hbm, eigen_hbm, query_hbm, cand_hbm,
-    out_ref, enter_ref, outer_ref, inner_ref, factor_ref, gather_ref,
-    layer_ref, out_basis_ref, in_basis_ref, eigen_ref, query_ref, cand_ref, by_module, sems,
-):
+def pack(layer_hbm, query_hbm, cand_hbm, out_ref, holds_ref, layer_ref, query_ref, cand_ref, by_module, sems):
     arrivals = [
         pltpu.make_async_copy(source, target, sems.at[i])
         for i, (source, target) in enumerate(
-            (
-                (layer_hbm, layer_ref),
-                (out_basis_hbm, out_basis_ref),
-                (in_basis_hbm, in_basis_ref),
-                (eigen_hbm, eigen_ref),
-                (query_hbm, query_ref),
-                (cand_hbm, cand_ref),
-            )
+            ((layer_hbm, layer_ref), (query_hbm, query_ref), (cand_hbm, cand_ref))
         )
     ]
     for arrival in arrivals:
@@ -106,12 +71,12 @@
     slots = out_ref.shape[0]
     tall = flat // LANES
     order = order_of(slots, firsts(slots)[0])
-    gather_ref[...] = gather_rows(tall)
-    for arrival in arrivals[:4]:
-        arrival.wait()
-    spread_bases(
-        out_basis_ref[...], in_basis_ref[...], eigen_ref[...], enter_ref, outer_ref, inner_ref, factor_ref
-    )
+    arrivals[0].wait()
+    module, slot = iota((modules, slots), 0), iota((modules, slots), 1)
+    held = jnp.zeros((modules, slots), f32)
+    for k, s in enumerate(order_of(slots, firsts(slots)[1])):
+        held = jnp.where((slot == k) & (module == layer_ref[s]), 1.0, held)
+    holds_ref[...] = held.astype(bf16)
     at_once = slots * tall <= 512
     if at_once:
         shape = (tall, tall * modules)
@@ -120,7 +85,7 @@
     else:
         place = scatter_rows(tall)
     r = 0
-    for arrival, ref in zip(arrivals[4:], (query_ref, cand_ref)):
+    for arrival, ref in zip(arrivals[1:], (query_ref, cand_ref)):
         arrival.wait()
         many = ref.shape[0]
         if at_once:
@@ -156,22 +121,49 @@
     return jnp.sum(jnp.where(iota(shape, 0) == iota(shape, 1), row, 0.0), axis=1, keepdims=True)
 
 
-def work(moved_ref, enter_ref, outer_ref, inner_ref, factor_ref, gather_ref, out_ref, tails):
+def work(
+    moved_ref, out_basis_ref, in_basis_ref, eigen_ref, length_ref, rows_hbm, lists_hbm,
+    out_ref, chosen_ref, tails, rows_ref, lists_ref, sems,
+):
+    arrivals = [
+        pltpu.make_async_copy(source, target, sems.at[i])
+        for i, (source, target) in enumerate(
+            ((rows_hbm, rows_ref), (lists_hbm, lists_ref))
+        )
+    ]
+    for arrival in arrivals:
+        arrival.start()
     sources, height, _ = moved_ref.shape
     _, send, _ = out_ref.shape
-    size = enter_ref.shape[0]
-    side, tall = size // 4, size // SUBLANES
+    side = out_basis_ref.shape[0]
+    tall = side // 2
+    size = SUBLANES * tall
     per = height // tall - 1
     count = sources * per
     pairs = sources // 2
     stacks = pairs // 4
     arrive, leave = firsts(sources)
     places = [(d - leave) % sources for d in order_of(sources, arrive)]
-    outer, inner, gather = outer_ref[...], inner_ref[...], gather_ref[...]
-    factor = factor_ref[...]
+
+    def spread(basis):
+        wide = jnp.concatenate([basis] * 4, axis=1)
+        return jnp.concatenate([wide] * 4, axis=0)
+
+    row, column = iota((size, size), 0) // side, iota((size, size), 1) // side
+    bases = spread(in_basis_ref[...].astype(f32))
+    enter = jnp.where(row == 2 * (column % 2) + column // 2, bases, 0.0).astype(bf16)
+    inner = jnp.where(row == column, bases, 0.0).astype(bf16)
+    turn = mask(iota((side, side), 1) == 2 * (iota((side, side), 0) % tall) + iota((side, side), 0) // tall)
+    bases = spread(dot(dot(turn, out_basis_ref[...]).astype(bf16), turn, ((1,), (1,))))
+    outer = jnp.where(row == column, bases, 0.0).astype(bf16)
+    eigen = eigen_ref[...]
+    turned = swap(eigen)
+    factor = 1.0 / (jnp.concatenate([half(eigen, turned), half(turned, eigen)], axis=0) + damping)
+    gather = gather_rows(tall)
+
 
     queries = [jnp.concatenate([moved_ref[2 * p, :tall, :], moved_ref[2 * p + 1, :tall, :]], axis=1) for p in range(pairs)]
-    entered = dot(jnp.concatenate(queries, axis=0), enter_ref[...]).astype(bf16)
+    entered = dot(jnp.concatenate(queries, axis=0), enter).astype(bf16)
     columns = []
     for t in range(stacks):
         tiles = []
@@ -232,23 +224,26 @@
     for k in range(sources):
         out_ref[k] = jnp.concatenate([homes[k], tails[k * tail : (k + 1) * tail, :]], axis=0).astype(bf16)
 
-
-def finish(length_ref, layer_ref, rows_ref, lists_ref, home_ref, precond_ref, scores_ref, wide):
+    for arrival in arrivals:
+        arrival.wait()
+    lists = lists_ref[...]
+    longest = lists.shape[1]
+    rows = upright(rows_ref[...].astype(f32), count)
+    place = jnp.sum(jnp.where(iota((count, longest), 0) == lists, rows, 0.0), axis=0, keepdims=True)
+    place = jnp.where(iota((1, longest), 1) < length_ref[0], place.astype(jnp.int32), -1)
+    chosen_ref[...] = (iota((count, longest), 0) == place).astype(f32)
+
+
+def finish(home_ref, holds_ref, chosen_ref, precond_ref, scores_ref, wide):
     slots, send, _ = home_ref.shape
-    modules, flat = precond_ref.shape[1:]
+    _, flat = precond_ref.shape[1:]
+    count = chosen_ref.shape[0]
     tall = flat // LANES
     step = send + 1
     for k in range(slots):
         wide[pl.ds(k * step, send), :] = home_ref[k].astype(f32)
     by_slot = jnp.concatenate([wide[pl.ds(j, slots, stride=step), :].astype(bf16) for j in range(tall)], axis=1)
-    precond_ref[0] = dot(holds(layer_ref[...], modules, firsts(slots)[1]), by_slot).astype(bf16)
-
-    count = rows_ref.shape[1]
-    lists = lists_ref[...]
-    longest = lists.shape[1]
-    rows = upright(rows_ref[...].astype(f32), count)
-    place = jnp.sum(jnp.where(iota((count, longest), 0) == lists, rows, 0.0), axis=0, keepdims=True)
-    place = jnp.where(iota((1, longest), 1) < length_ref[...], place.astype(jnp.int32), -1)
+    precond_ref[0] = dot(holds_ref[...], by_slot).astype(bf16)
     groups = -(-count // LANES)
     parts = []
     for t in range(groups):
@@ -256,10 +251,11 @@
         parts.append(jnp.sum((pieces[2] + pieces[1]) + pieces[0], axis=0, keepdims=True))
     dense = parts[0] if groups == 1 else jnp.concatenate(parts, axis=1)
     scores_ref[...] = jnp.sum(
-        jnp.where(iota((count, longest), 0) == place, upright(dense, count), 0.0), axis=0, keepdims=True
+        jnp.where(chosen_ref[...] > 0.0, upright(dense, count), 0.0), axis=0, keepdims=True
     )
 
 
+SMEM = pl.BlockSpec(memory_space=pltpu.SMEM)
 HBM = pl.BlockSpec(memory_space=pltpu.HBM)
 VMEM = pl.BlockSpec(memory_space=pltpu.VMEM)
 PARAMS = pltpu.CompilerParams(vmem_limit_bytes=40 * 1024 * 1024)
@@ -279,10 +275,7 @@
     own, modules, flat = query_grads.shape
     per = cand_grads.shape[0]
     slots = layer_map.shape[0]
-    layer_row = layer_map.reshape(1, slots)
     tall = flat // LANES
-    side = basis_out.shape[1]
-    size = SUBLANES * tall
     count = cand_rows.shape[0]
     height = (own + per) * tall
     send = tall + -(-PIECES * -(-count // LANES) // SUBLANES) * SUBLANES
@@ -294,43 +287,45 @@
         groups = [order_of(slots, first)]
         return lax.all_to_all(x, "shard", split_axis=0, concat_axis=0, tiled=True, axis_index_groups=groups)
 
-    square = pltpu.VMEM((size, size), bf16)
-    operands = (
-        layer_map,
-        basis_out.reshape(basis_out.shape[1:]),
-        basis_in.reshape(basis_in.shape[1:]),
-        eigvals.reshape(tall, LANES),
-        query_grads,
-        cand_grads,
-    )
-    packed, enter, outer, inner, factor, gather = pl.pallas_call(
+    operands = (layer_map, query_grads, cand_grads)
+    packed, held = pl.pallas_call(
         pack,
-        out_shape=(
-            pltpu.VMEM((slots, height, LANES), bf16),
-            square,
-            square,
-            square,
-            pltpu.VMEM((side, LANES), f32),
-            square,
-        ),
-        in_specs=[HBM] * len(operands),
-        out_specs=[VMEM] * 6,
-        scratch_shapes=[pltpu.SMEM(layer_map.shape, jnp.int32)]
-        + [pltpu.VMEM(x.shape, x.dtype) for x in operands[1:]]
-        + [pltpu.VMEM((modules, height, LANES), bf16), pltpu.SemaphoreType.DMA((len(operands),))],
+        out_shape=(pltpu.VMEM((slots, height, LANES), bf16), pltpu.VMEM((modules, slots), bf16)),
+        in_specs=[HBM] * 3,
+        out_specs=(VMEM, VMEM),
+        scratch_shapes=[
+            pltpu.SMEM(layer_map.shape, jnp.int32),
+            pltpu.VMEM(query_grads.shape, bf16),
+            pltpu.VMEM(cand_grads.shape, bf16),
+            pltpu.VMEM((modules, height, LANES), bf16),
+            pltpu.SemaphoreType.DMA((3,)),
+        ],
         compiler_params=PARAMS,
         name="pack",
     )(*(in_hbm(x) for x in operands))
     moved = swap_over(packed, firsts(slots)[0])
-    homes = pl.pallas_call(
+    small = (cand_rows.reshape(1, count), cand_lists)
+    homes, chosen = pl.pallas_call(
         work,
-        out_shape=jax.ShapeDtypeStruct((slots, send, LANES), bf16),
-        in_specs=[VMEM] * 6,
-        out_specs=VMEM,
-        scratch_shapes=[pltpu.VMEM((slots * (send - tall), LANES), f32)],
+        out_shape=(
+            jax.ShapeDtypeStruct((slots, send, LANES), bf16),
+            jax.ShapeDtypeStruct((count, cand_lists.shape[1]), f32),
+        ),
+        in_specs=[VMEM] * 4 + [SMEM] + [HBM] * 2,
+        out_specs=[VMEM] * 2,
+        scratch_shapes=[pltpu.VMEM((slots * (send - tall), LANES), f32)]
+        + [pltpu.VMEM(x.shape, jnp.int32) for x in small]
+        + [pltpu.SemaphoreType.DMA((2,))],
         compiler_params=PARAMS,
         name="work",
-    )(moved, enter, outer, inner, factor, gather)
+    )(
+        moved,
+        basis_out.reshape(basis_out.shape[1:]),
+        basis_in.reshape(basis_in.shape[1:]),
+        eigvals.reshape(tall, LANES),
+        list_lengths,
+        *(in_hbm(x) for x in small),
+    )
     home = swap_over(homes, firsts(slots)[1])
     return pl.pallas_call(
         finish,
@@ -338,12 +333,12 @@
             jax.ShapeDtypeStruct(query_grads.shape, bf16),
             jax.ShapeDtypeStruct(cand_lists.shape, f32),
         ),
-        in_specs=[VMEM] * 5,
+        in_specs=[VMEM] * 3,
         out_specs=(VMEM, VMEM),
         scratch_shapes=[pltpu.VMEM((slots * (send + 1), LANES), f32)],
         compiler_params=PARAMS,
         name="finish",
-    )(list_lengths.reshape(1, 1), layer_row, cand_rows.reshape(1, count), cand_lists, home)
+    )(home, held, chosen)
 
 
 def solution(mesh):

time: 34.6 us -> 34.6 us (level)
  blocking collectives: 16.7 us -> 10.9 us
  waiting for transfers between devices: 4.79 us -> 8.36 us
  starting transfers between devices: 5.81 us -> 8.51 us
  local copies, waits for them, and re-layouts: 0.68 us -> 0.02 us
    all_to_all x1, blocking collectives: 16.7 us -> 10.9 us  [swap_over(): lax.all_to_all(x, 'shard', split_axis=0, concat_axis=0, tiled=True, axis_...]
    all_to_all x1, waiting for transfers between devices: 4.79 us -> 8.36 us  [swap_over(): lax.all_to_all(x, 'shard', split_axis=0, concat_axis=0, tiled=True, axis_...]
    all_to_all x1, starting transfers between devices: 5.81 us -> 8.51 us  [swap_over(): lax.all_to_all(x, 'shard', split_axis=0, concat_axis=0, tiled=True, axis_...]
    unnamed x6, local copies, waits for them, and re-layouts: 0.68 us -> 0.02 us
where the time goes in v15:
time: 34.6 us; the launch traced here: 34.3 us
  blocking collectives  10.9 us (32%)
  starting transfers between devices  8.51 us (25%)
  waiting for transfers between devices  8.36 us (24%)
  Pallas kernels  5.15 us (15%)
  between operations  1.33 us (4%)
    all_to_all x1, blocking collectives, swap_over(): lax.all_to_all(x, 'shard', split_axis=0, concat_axis=0, tiled=True, axis_...  10.9 us
    all_to_all x1, starting transfers between devices, swap_over(): lax.all_to_all(x, 'shard', split_axis=0, concat_axis=0, tiled=True, axis_...  8.51 us
    all_to_all x1, waiting for transfers between devices, swap_over(): lax.all_to_all(x, 'shard', split_axis=0, concat_axis=0, tiled=True, axis_...  8.36 us
    pallas_call x1, Pallas kernels, body(): pl.pallas_call(pack, out_shape=(pltpu.VMEM((slots, height, LANES), bf16),...  2.53 us
    pallas_call x1, Pallas kernels, body(): pl.pallas_call(work, out_shape=(jax.ShapeDtypeStruct((slots, send, LANES)...  1.78 us
    pallas_call x1, Pallas kernels, body(): pl.pallas_call(finish, out_shape=(jax.ShapeDtypeStruct(query_grads.shape,...  0.84 us
  transfers between devices with their start and end apart: 1, of which 1 were waited for; matrix products, arithmetic and copies ran while one was open for 0% of the time, Pallas kernels for 0%

profile of v15, /device:TPU:0, one launch (start us, length us, event | category | flops | bytes accessed | tf_op | source)
XLA Modules:
  0.0 34.3 jit_solution(8727685839319703514)
XLA Ops:
  0.6 2.5 %pack.1 = (bf16[16,96,128]{2,1,0:T(8,128)(2,1)}, bf16[16,16]{1,0:T(8,128)(2,1)S(1)}) custom-call(s32[16]{0:T(128)} %layer_hbm.1, bf16[1,16,4096]{2,1,0:T(8,128)(2,1)} %query_hbm.1, bf16[2,16,4096]{2,1,0:T(8,128)(2,1)} %cand_hbm.1), custom_call_target="tpu_custom_call" | custom-call | tf_op jit(solution)/shard_map/pack/pallas_call | solution.py:291
  3.2 0.0 copy-start
  3.2 0.0 copy-start.1
  3.2 0.0 copy-start.2
  3.2 8.5 %all-to-all-start = ((bf16[16,96,128]{2,1,0:T(8,128)(2,1)}), bf16[16,96,128]{2,1,0:T(8,128)(2,1)S(1)}, u32[]{:S(2)}, u32[]{:S(2)}) async-start(bf16[16,96,128]{2,1,0:T(8,128)(2,1)} %get-tuple-element.6), calls=%async_computation | async-start | bytes 786432 | tf_op jit(solution)/shard_map/all_to_all | solution.py:288
  12.4 8.4 %all-to-all-done.moved_ref = bf16[16,96,128]{2,1,0:T(8,128)(2,1)S(1)} async-done(((bf16[16,96,128]{2,1,0:T(8,128)(2,1)}), bf16[16,96,128]{2,1,0:T(8,128)(2,1)S(1)}, u32[]{:S(2)}, u32[]{:S(2)}) %all-to-all-start) | async-done | bytes 393248 | tf_op jit(solution)/shard_map/all_to_all | solution.py:288
  20.7 0.0 copy-done
  20.7 0.0 copy-done.1
  20.7 0.0 copy-done.2
  20.7 1.8 %work.1 = (bf16[16,40,128]{2,1,0:T(8,128)(2,1)S(1)}, f32[32,384]{1,0:T(8,128)S(1)}) custom-call(bf16[16,96,128]{2,1,0:T(8,128)(2,1)S(1)} %all-to-all-done.moved_ref, bf16[64,64]{1,0:T(8,128)(2,1)S(1)} %bitcast.4, bf16[64,64]{1,0:T(8,128)(2,1)S(1)} %bitcast.5, f32[32,128]{1,0:T(8,128)S(1)} %bitcast.6, s32[1]{0:T(128)S(6)} %copy.11.length_ref, ...), custom_call_target="tpu_custom_call" | custom-call | tf_op jit(solution)/shard_map/work/pallas_call | solution.py:308
  22.5 10.9 %all_to_all.10.home_ref = bf16[16,40,128]{2,1,0:T(8,128)(2,1)S(1)} all-to-all(bf16[16,40,128]{2,1,0:T(8,128)(2,1)S(1)} %get-tuple-element.7), channel_id=1, replica_groups={{10,11,12,13,14,15,0,1,2,3,4,5,6,7,8,9},{26,27,28,29,30,31,16,17,18,19,..., dimensions={0} | all-to-all | bytes 327680 | tf_op jit(solution)/shard_map/all_to_all | solution.py:288
  33.5 0.8 %finish.1 = (bf16[1,16,4096]{2,1,0:T(8,128)(2,1)}, f32[1,384]{1,0:T(1,128)}) custom-call(bf16[16,40,128]{2,1,0:T(8,128)(2,1)S(1)} %all_to_all.10.home_ref, bf16[16,16]{1,0:T(8,128)(2,1)S(1)} %get-tuple-element.8.holds_ref, f32[32,384]{1,0:T(8,128)S(1)} %get-tuple-element.9.chosen_ref), custom_call_target="tpu_custom_call" | custom-call | tf_op jit(solution)/shard_map/finish/pallas_call | solution.py:330
Async XLA Ops:
  3.2 17.6 %copy-start = (bf16[1,64,64]{2,1,0:T(8,128)(2,1)S(1)}, bf16[1,64,64]{2,1,0:T(8,128)(2,1)}, u32[]{:S(2)}) copy-start(bf16[1,64,64]{2,1,0:T(8,128)(2,1)} %param.11) | copy-start | bytes 24580
  3.2 17.6 %copy-start.1 = (bf16[1,64,64]{2,1,0:T(8,128)(2,1)S(1)}, bf16[1,64,64]{2,1,0:T(8,128)(2,1)}, u32[]{:S(2)}) copy-start(bf16[1,64,64]{2,1,0:T(8,128)(2,1)} %param.12) | copy-start | bytes 24580
  3.2 17.5 %copy-start.2 = (f32[1,4096]{1,0:T(1,128)S(1)}, f32[1,4096]{1,0:T(1,128)}, u32[]{:S(2)}) copy-start(f32[1,4096]{1,0:T(1,128)} %param.13) | copy-start | bytes 49156
  3.2 17.5 %all-to-all-start = ((bf16[16,96,128]{2,1,0:T(8,128)(2,1)}), bf16[16,96,128]{2,1,0:T(8,128)(2,1)S(1)}, u32[]{:S(2)}, u32[]{:S(2)}) async-start(bf16[16,96,128]{2,1,0:T(8,128)(2,1)} %get-tuple-element.6), calls=%async_computation | async-start | bytes 786432 | tf_op jit(solution)/shard_map/all_to_all | solution.py:288

commit v16 on v10

--- a/solution.py
+++ b/solution.py
@@ -29,7 +29,7 @@
 
 
 def firsts(slots):
-    return slots // 4, slots - 2
+    return slots * 3 // 4, slots * 3 // 4
 
 
 def gather_rows(tall):
@@ -260,7 +260,7 @@
 
     packed = pl.pallas_call(
         pack,
-        out_shape=pltpu.VMEM((slots, height, LANES), bf16),
+        out_shape=jax.ShapeDtypeStruct((slots, height, LANES), bf16),
         in_specs=[HBM] * 3,
         out_specs=VMEM,
         scratch_shapes=[

time: 34.3 us -> 34.2 us (level)
  waiting for transfers between devices: 8.91 us -> 7.54 us
  blocking collectives: 10.3 us -> 11 us
  starting transfers between devices: 8.01 us -> 8.56 us
    all_to_all x1, waiting for transfers between devices: 8.91 us -> 7.54 us  [swap_over(): lax.all_to_all(x, 'shard', split_axis=0, concat_axis=0, tiled=True, axis_...]
    all_to_all x1, blocking collectives: 10.3 us -> 11 us  [swap_over(): lax.all_to_all(x, 'shard', split_axis=0, concat_axis=0, tiled=True, axis_...]
    all_to_all x1, starting transfers between devices: 8.01 us -> 8.56 us  [swap_over(): lax.all_to_all(x, 'shard', split_axis=0, concat_axis=0, tiled=True, axis_...]
where the time goes in v16:
time: 34.2 us; the launch traced here: 33.8 us
  blocking collectives  11 us (32%)
  starting transfers between devices  8.56 us (25%)
  waiting for transfers between devices  7.54 us (22%)
  Pallas kernels  4.69 us (14%)
  between operations  1.38 us (4%)
  local copies, waits for them, and re-layouts  0.65 us (2%)
    all_to_all x1, blocking collectives, swap_over(): lax.all_to_all(x, 'shard', split_axis=0, concat_axis=0, tiled=True, axis_...  11 us
    all_to_all x1, starting transfers between devices, swap_over(): lax.all_to_all(x, 'shard', split_axis=0, concat_axis=0, tiled=True, axis_...  8.56 us
    all_to_all x1, waiting for transfers between devices, swap_over(): lax.all_to_all(x, 'shard', split_axis=0, concat_axis=0, tiled=True, axis_...  7.54 us
    pallas_call x1, Pallas kernels, body(): pl.pallas_call(pack, out_shape=jax.ShapeDtypeStruct((slots, height, LANES...  2.07 us
    pallas_call x1, Pallas kernels, body(): pl.pallas_call(work, out_shape=jax.ShapeDtypeStruct((slots, send, LANES),...  1.22 us
    pallas_call x1, Pallas kernels, body(): pl.pallas_call(finish, out_shape=(jax.ShapeDtypeStruct(query_grads.shape,...  0.83 us
  transfers between devices with their start and end apart: 1, of which 1 were waited for; matrix products, arithmetic and copies ran while one was open for 0% of the time, Pallas kernels for 2%

profile of v16, /device:TPU:0, one launch (start us, length us, event | category | flops | bytes accessed | tf_op | source)
XLA Modules:
  0.0 33.8 jit_solution(7350650874075267994)
XLA Ops:
  0.6 2.1 %pack.1.after_ref = bf16[16,96,128]{2,1,0:T(8,128)(2,1)} custom-call(s32[1,16]{1,0:T(1,128)} %bitcast.8, bf16[1,16,4096]{2,1,0:T(8,128)(2,1)} %query_hbm.1, bf16[2,16,4096]{2,1,0:T(8,128)(2,1)} %cand_hbm.1), custom_call_target="tpu_custom_call" | custom-call | tf_op jit(solution)/shard_map/pack/pallas_call | solution.py:261
  2.7 0.0 copy-start
  2.7 0.0 copy-start.1
  2.7 0.0 copy-start.2
  2.7 8.6 %all-to-all-start = ((bf16[16,96,128]{2,1,0:T(8,128)(2,1)}), bf16[16,96,128]{2,1,0:T(8,128)(2,1)S(1)}, u32[]{:S(2)}, u32[]{:S(2)}) async-start(bf16[16,96,128]{2,1,0:T(8,128)(2,1)} %pack.1.after_ref), calls=%async_computation | async-start | bytes 786432 | tf_op jit(solution)/shard_map/all_to_all | solution.py:259
  12.0 0.0 copy-start.4
  12.0 0.0 copy-start.3
  12.0 0.0 copy-start.5
  12.0 0.0 copy-done
  12.0 0.0 copy-done.1
  12.0 0.0 copy-done.2
  12.0 0.6 %copy-done.4 = s32[1,384]{1,0:T(1,128)S(1)} copy-done((s32[1,384]{1,0:T(1,128)S(1)}, s32[1,384]{1,0:T(1,128)}, u32[]{:S(2)}) %copy-start.4) | copy-done | bytes 1560
  12.6 0.0 copy-done.3
  12.6 0.0 copy-done.5
  12.6 0.6 %prepare.1 = (bf16[256,256]{1,0:T(8,128)(2,1)S(1)}, bf16[256,256]{1,0:T(8,128)(2,1)S(1)}, bf16[256,256]{1,0:T(8,128)(2,1)S(1)}, f32[64,128]{1,0:T(8,128)S(1)}, b...) custom-call(s32[1]{0:T(128)S(6)} %copy.11.length_ref, s32[1,16]{1,0:T(1,128)S(1)} %bitcast.9, ...), custom_call_target="tpu_custom_call" | custom-call | tf_op jit(solution)/shard_map/prepare/pallas_call | solution.py:277
  13.2 7.5 %all-to-all-done.moved_ref = bf16[16,96,128]{2,1,0:T(8,128)(2,1)S(1)} async-done(((bf16[16,96,128]{2,1,0:T(8,128)(2,1)}), bf16[16,96,128]{2,1,0:T(8,128)(2,1)S(1)}, u32[]{:S(2)}, u32[]{:S(2)}) %all-to-all-start) | async-done | bytes 393248 | tf_op jit(solution)/shard_map/all_to_all | solution.py:259
  20.8 1.2 %work.1 = bf16[16,40,128]{2,1,0:T(8,128)(2,1)S(1)} custom-call(bf16[16,96,128]{2,1,0:T(8,128)(2,1)S(1)} %all-to-all-done.moved_ref, bf16[256,256]{1,0:T(8,128)(2,1)S(1)} %get-tuple-element.9.enter_ref, bf16[256,256]{1,0:T(8,128)(2,1)S(1)} %get-tuple-element.10.outer_ref, bf16[256,256]{1,0:T(8,128)(2,1)S(1)} %get-tuple-element.11.inner_ref, ...), custom_call_target="tpu_custom_call" | custom-call | tf_op jit(solution)/shard_map/work/pallas_call | solution.py:303
  22.0 11.0 %all_to_all.10.home_ref = bf16[16,40,128]{2,1,0:T(8,128)(2,1)S(1)} all-to-all(bf16[16,40,128]{2,1,0:T(8,128)(2,1)S(1)} %work.1), channel_id=1, replica_groups={{12,13,14,15,0,1,2,3,4,5,6,7,8,9,10,11},{28,29,30,31,16,17,18,19,20,21,..., dimensions={0} | all-to-all | bytes 327680 | tf_op jit(solution)/shard_map/all_to_all | solution.py:259
  33.0 0.8 %finish.1 = (bf16[1,16,4096]{2,1,0:T(8,128)(2,1)}, f32[1,384]{1,0:T(1,128)}) custom-call(bf16[16,40,128]{2,1,0:T(8,128)(2,1)S(1)} %all_to_all.10.home_ref, bf16[16,16]{1,0:T(8,128)(2,1)S(1)} %get-tuple-element.14.holds_ref, f32[32,384]{1,0:T(8,128)S(1)} %get-tuple-element.15.chosen_ref), custom_call_target="tpu_custom_call" | custom-call | tf_op jit(solution)/shard_map/finish/pallas_call | solution.py:313
Async XLA Ops:
  2.7 9.3 %copy-start = (bf16[1,64,64]{2,1,0:T(8,128)(2,1)S(1)}, bf16[1,64,64]{2,1,0:T(8,128)(2,1)}, u32[]{:S(2)}) copy-start(bf16[1,64,64]{2,1,0:T(8,128)(2,1)} %param.11) | copy-start | bytes 24580
  2.7 9.3 %copy-start.1 = (bf16[1,64,64]{2,1,0:T(8,128)(2,1)S(1)}, bf16[1,64,64]{2,1,0:T(8,128)(2,1)}, u32[]{:S(2)}) copy-start(bf16[1,64,64]{2,1,0:T(8,128)(2,1)} %param.12) | copy-start | bytes 24580
  2.7 9.3 %copy-start.2 = (f32[1,4096]{1,0:T(1,128)S(1)}, f32[1,4096]{1,0:T(1,128)}, u32[]{:S(2)}) copy-start(f32[1,4096]{1,0:T(1,128)} %param.13) | copy-start | bytes 49156
  2.7 18.0 %all-to-all-start = ((bf16[16,96,128]{2,1,0:T(8,128)(2,1)}), bf16[16,96,128]{2,1,0:T(8,128)(2,1)S(1)}, u32[]{:S(2)}, u32[]{:S(2)}) async-start(bf16[16,96,128]{2,1,0:T(8,128)(2,1)} %pack.1.after_ref), calls=%async_computation | async-start | bytes 786432 | tf_op jit(solution)/shard_map/all_to_all | solution.py:259
  12.0 0.7 %copy-start.4 = (s32[1,384]{1,0:T(1,128)S(1)}, s32[1,384]{1,0:T(1,128)}, u32[]{:S(2)}) copy-start(s32[1,384]{1,0:T(1,128)} %lists_ref.1) | copy-start | bytes 4612
  12.0 0.7 %copy-start.3 = (s32[16]{0:T(128)S(1)}, s32[16]{0:T(128)}, u32[]{:S(2)}) copy-start(s32[16]{0:T(128)} %param.14) | copy-start | bytes 196
  12.0 0.7 %copy-start.5 = (s32[32]{0:T(128)S(1)}, s32[32]{0:T(128)}, u32[]{:S(2)}) copy-start(s32[32]{0:T(128)} %param.15) | copy-start | bytes 388

commit v17 on v16

--- a/solution.py
+++ b/solution.py
@@ -29,7 +29,7 @@
 
 
 def firsts(slots):
-    return slots * 3 // 4, slots * 3 // 4
+    return slots * 5 // 8, slots * 5 // 8
 
 
 def gather_rows(tall):
@@ -68,21 +68,25 @@
     ]
     for arrival in arrivals:
         arrival.start()
-    arrivals[0].wait()
     modules, flat = query_ref.shape[1:]
     slots, height, _ = out_ref.shape
     tall = flat // LANES
-    step = height + 1
-    one_hot = holds(layer_ref[...], modules, firsts(slots)[0])
-    sources = [(query_ref, r) for r in range(query_ref.shape[0])] + [(cand_ref, r) for r in range(cand_ref.shape[0])]
-    for r, (ref, row) in enumerate(sources):
-        if row == 0:
-            arrivals[1 if ref is query_ref else 2].wait()
-        by_slot = dot(one_hot, ref[row], ((0,), (0,)))
-        for j in range(tall):
-            wide[pl.ds(r * tall + j, slots, stride=step), :] = by_slot[:, j * LANES : (j + 1) * LANES]
+    slot, module = iota((slots, modules), 0), iota((slots, modules), 1)
+    arrivals[0].wait()
+    one_hot = jnp.zeros((slots, modules), f32)
+    for k, s in enumerate(order_of(slots, firsts(slots)[0])):
+        one_hot = jnp.where((slot == k) & (module == layer_ref[s]), 1.0, one_hot)
+    one_hot = one_hot.astype(bf16)
+    r = 0
+    for arrival, ref in zip(arrivals[1:], (query_ref, cand_ref)):
+        arrival.wait()
+        for row in range(ref.shape[0]):
+            by_slot = dot(one_hot, ref[row])
+            for j in range(tall):
+                wide[pl.ds(r * tall + j, slots, stride=height), :] = by_slot[:, j * LANES : (j + 1) * LANES]
+            r += 1
     for k in range(slots):
-        out_ref[k] = wide[pl.ds(k * step, height), :].astype(bf16)
+        out_ref[k] = wide[k * height : (k + 1) * height, :].astype(bf16)
 
 
 def upright(row, count):
@@ -264,15 +268,15 @@
         in_specs=[HBM] * 3,
         out_specs=VMEM,
         scratch_shapes=[
-            pltpu.VMEM(layer_row.shape, jnp.int32),
+            pltpu.SMEM(layer_map.shape, jnp.int32),
             pltpu.VMEM(query_grads.shape, bf16),
             pltpu.VMEM(cand_grads.shape, bf16),
-            pltpu.VMEM((slots * (height + 1), LANES), f32),
+            pltpu.VMEM((slots * height, LANES), f32),
             pltpu.SemaphoreType.DMA((3,)),
         ],
         compiler_params=PARAMS,
         name="pack",
-    )(in_hbm(layer_row), in_hbm(query_grads), in_hbm(cand_grads))
+    )(in_hbm(layer_map), in_hbm(query_grads), in_hbm(cand_grads))
     square = jax.ShapeDtypeStruct((size, size), bf16)
     enter, outer, inner, factor, gather, held, chosen = pl.pallas_call(
         prepare,

time: 34.2 us -> 34 us (level)
  waiting for transfers between devices: 7.54 us -> 7.1 us
  Pallas kernels: 4.69 us -> 5.04 us
    all_to_all x1, waiting for transfers between devices: 7.54 us -> 7.1 us  [swap_over(): lax.all_to_all(x, 'shard', split_axis=0, concat_axis=0, tiled=True, axis_...]
    pallas_call x1, Pallas kernels: 2.07 us -> 2.42 us  [body(): pl.pallas_call(pack, out_shape=jax.ShapeDtypeStruct((slots, height, LANES...]
where the time goes in v17:
time: 34 us; the launch traced here: 33.6 us
  blocking collectives  10.9 us (32%)
  starting transfers between devices  8.51 us (25%)
  waiting for transfers between devices  7.1 us (21%)
  Pallas kernels  5.04 us (15%)
  between operations  1.38 us (4%)
  local copies, waits for them, and re-layouts  0.65 us (2%)
    all_to_all x1, blocking collectives, swap_over(): lax.all_to_all(x, 'shard', split_axis=0, concat_axis=0, tiled=True, axis_...  10.9 us
    all_to_all x1, starting transfers between devices, swap_over(): lax.all_to_all(x, 'shard', split_axis=0, concat_axis=0, tiled=True, axis_...  8.51 us
    all_to_all x1, waiting for transfers between devices, swap_over(): lax.all_to_all(x, 'shard', split_axis=0, concat_axis=0, tiled=True, axis_...  7.1 us
    pallas_call x1, Pallas kernels, body(): pl.pallas_call(pack, out_shape=jax.ShapeDtypeStruct((slots, height, LANES...  2.42 us
    pallas_call x1, Pallas kernels, body(): pl.pallas_call(work, out_shape=jax.ShapeDtypeStruct((slots, send, LANES),...  1.22 us
    pallas_call x1, Pallas kernels, body(): pl.pallas_call(finish, out_shape=(jax.ShapeDtypeStruct(query_grads.shape,...  0.83 us
  transfers between devices with their start and end apart: 1, of which 1 were waited for; matrix products, arithmetic and copies ran while one was open for 0% of the time, Pallas kernels for 2%

profile of v17, /device:TPU:0, one launch (start us, length us, event | category | flops | bytes accessed | tf_op | source)
XLA Modules:
  0.0 33.6 jit_solution(1650268776738755242)
XLA Ops:
  0.6 2.4 %pack.1.after_ref = bf16[16,96,128]{2,1,0:T(8,128)(2,1)} custom-call(s32[16]{0:T(128)} %layer_hbm.1, bf16[1,16,4096]{2,1,0:T(8,128)(2,1)} %query_hbm.1, bf16[2,16,4096]{2,1,0:T(8,128)(2,1)} %cand_hbm.1), custom_call_target="tpu_custom_call" | custom-call | tf_op jit(solution)/shard_map/pack/pallas_call | solution.py:265
  3.1 0.0 copy-start
  3.1 0.0 copy-start.1
  3.1 0.0 copy-start.2
  3.1 8.5 %all-to-all-start = ((bf16[16,96,128]{2,1,0:T(8,128)(2,1)}), bf16[16,96,128]{2,1,0:T(8,128)(2,1)S(1)}, u32[]{:S(2)}, u32[]{:S(2)}) async-start(bf16[16,96,128]{2,1,0:T(8,128)(2,1)} %pack.1.after_ref), calls=%async_computation | async-start | bytes 786432 | tf_op jit(solution)/shard_map/all_to_all | solution.py:263
  12.3 0.0 copy-start.4
  12.3 0.0 copy-start.3
  12.3 0.0 copy-start.5
  12.3 0.0 copy-done
  12.3 0.0 copy-done.1
  12.3 0.0 copy-done.2
  12.3 0.6 %copy-done.4 = s32[1,384]{1,0:T(1,128)S(1)} copy-done((s32[1,384]{1,0:T(1,128)S(1)}, s32[1,384]{1,0:T(1,128)}, u32[]{:S(2)}) %copy-start.4) | copy-done | bytes 1560
  12.9 0.0 copy-done.3
  12.9 0.0 copy-done.5
  12.9 0.6 %prepare.1 = (bf16[256,256]{1,0:T(8,128)(2,1)S(1)}, bf16[256,256]{1,0:T(8,128)(2,1)S(1)}, bf16[256,256]{1,0:T(8,128)(2,1)S(1)}, f32[64,128]{1,0:T(8,128)S(1)}, b...) custom-call(s32[1]{0:T(128)S(6)} %copy.11.length_ref, s32[1,16]{1,0:T(1,128)S(1)} %bitcast.8, ...), custom_call_target="tpu_custom_call" | custom-call | tf_op jit(solution)/shard_map/prepare/pallas_call | solution.py:281
  13.5 7.1 %all-to-all-done.moved_ref = bf16[16,96,128]{2,1,0:T(8,128)(2,1)S(1)} async-done(((bf16[16,96,128]{2,1,0:T(8,128)(2,1)}), bf16[16,96,128]{2,1,0:T(8,128)(2,1)S(1)}, u32[]{:S(2)}, u32[]{:S(2)}) %all-to-all-start) | async-done | bytes 393248 | tf_op jit(solution)/shard_map/all_to_all | solution.py:263
  20.6 1.2 %work.1 = bf16[16,40,128]{2,1,0:T(8,128)(2,1)S(1)} custom-call(bf16[16,96,128]{2,1,0:T(8,128)(2,1)S(1)} %all-to-all-done.moved_ref, bf16[256,256]{1,0:T(8,128)(2,1)S(1)} %get-tuple-element.9.enter_ref, bf16[256,256]{1,0:T(8,128)(2,1)S(1)} %get-tuple-element.10.outer_ref, bf16[256,256]{1,0:T(8,128)(2,1)S(1)} %get-tuple-element.11.inner_ref, ...), custom_call_target="tpu_custom_call" | custom-call | tf_op jit(solution)/shard_map/work/pallas_call | solution.py:307
  21.8 10.9 %all_to_all.10.home_ref = bf16[16,40,128]{2,1,0:T(8,128)(2,1)S(1)} all-to-all(bf16[16,40,128]{2,1,0:T(8,128)(2,1)S(1)} %work.1), channel_id=1, replica_groups={{10,11,12,13,14,15,0,1,2,3,4,5,6,7,8,9},{26,27,28,29,30,31,16,17,18,19,..., dimensions={0} | all-to-all | bytes 327680 | tf_op jit(solution)/shard_map/all_to_all | solution.py:263
  32.8 0.8 %finish.1 = (bf16[1,16,4096]{2,1,0:T(8,128)(2,1)}, f32[1,384]{1,0:T(1,128)}) custom-call(bf16[16,40,128]{2,1,0:T(8,128)(2,1)S(1)} %all_to_all.10.home_ref, bf16[16,16]{1,0:T(8,128)(2,1)S(1)} %get-tuple-element.14.holds_ref, f32[32,384]{1,0:T(8,128)S(1)} %get-tuple-element.15.chosen_ref), custom_call_target="tpu_custom_call" | custom-call | tf_op jit(solution)/shard_map/finish/pallas_call | solution.py:317
Async XLA Ops:
  3.1 9.2 %copy-start = (bf16[1,64,64]{2,1,0:T(8,128)(2,1)S(1)}, bf16[1,64,64]{2,1,0:T(8,128)(2,1)}, u32[]{:S(2)}) copy-start(bf16[1,64,64]{2,1,0:T(8,128)(2,1)} %param.11) | copy-start | bytes 24580
  3.1 9.2 %copy-start.1 = (bf16[1,64,64]{2,1,0:T(8,128)(2,1)S(1)}, bf16[1,64,64]{2,1,0:T(8,128)(2,1)}, u32[]{:S(2)}) copy-start(bf16[1,64,64]{2,1,0:T(8,128)(2,1)} %param.12) | copy-start | bytes 24580
  3.1 9.2 %copy-start.2 = (f32[1,4096]{1,0:T(1,128)S(1)}, f32[1,4096]{1,0:T(1,128)}, u32[]{:S(2)}) copy-start(f32[1,4096]{1,0:T(1,128)} %param.13) | copy-start | bytes 49156
  3.1 17.5 %all-to-all-start = ((bf16[16,96,128]{2,1,0:T(8,128)(2,1)}), bf16[16,96,128]{2,1,0:T(8,128)(2,1)S(1)}, u32[]{:S(2)}, u32[]{:S(2)}) async-start(bf16[16,96,128]{2,1,0:T(8,128)(2,1)} %pack.1.after_ref), calls=%async_computation | async-start | bytes 786432 | tf_op jit(solution)/shard_map/all_to_all | solution.py:263
  12.3 0.7 %copy-start.4 = (s32[1,384]{1,0:T(1,128)S(1)}, s32[1,384]{1,0:T(1,128)}, u32[]{:S(2)}) copy-start(s32[1,384]{1,0:T(1,128)} %lists_ref.1) | copy-start | bytes 4612
  12.3 0.7 %copy-start.3 = (s32[16]{0:T(128)S(1)}, s32[16]{0:T(128)}, u32[]{:S(2)}) copy-start(s32[16]{0:T(128)} %layer_hbm.1) | copy-start | bytes 196
  12.3 0.7 %copy-start.5 = (s32[32]{0:T(128)S(1)}, s32[32]{0:T(128)}, u32[]{:S(2)}) copy-start(s32[32]{0:T(128)} %param.15) | copy-start | bytes 388

commit v18 on v16

--- a/solution.py
+++ b/solution.py
@@ -29,7 +29,7 @@
 
 
 def firsts(slots):
-    return slots * 3 // 4, slots * 3 // 4
+    return slots // 2, slots * 5 // 8
 
 
 def gather_rows(tall):
@@ -60,24 +60,23 @@
 
 
 def pack(layer_hbm, query_hbm, cand_hbm, out_ref, layer_ref, query_ref, cand_ref, wide, sems):
+    sources = [(query_hbm, query_ref, r) for r in range(query_ref.shape[0])]
+    sources += [(cand_hbm, cand_ref, r) for r in range(cand_ref.shape[0])]
+    first = pltpu.make_async_copy(layer_hbm, layer_ref, sems.at[len(sources)])
+    first.start()
     arrivals = [
-        pltpu.make_async_copy(source, target, sems.at[i])
-        for i, (source, target) in enumerate(
-            ((layer_hbm, layer_ref), (query_hbm, query_ref), (cand_hbm, cand_ref))
-        )
+        pltpu.make_async_copy(hbm.at[row], ref.at[row], sems.at[i]) for i, (hbm, ref, row) in enumerate(sources)
     ]
     for arrival in arrivals:
         arrival.start()
-    arrivals[0].wait()
+    first.wait()
     modules, flat = query_ref.shape[1:]
     slots, height, _ = out_ref.shape
     tall = flat // LANES
     step = height + 1
     one_hot = holds(layer_ref[...], modules, firsts(slots)[0])
-    sources = [(query_ref, r) for r in range(query_ref.shape[0])] + [(cand_ref, r) for r in range(cand_ref.shape[0])]
-    for r, (ref, row) in enumerate(sources):
-        if row == 0:
-            arrivals[1 if ref is query_ref else 2].wait()
+    for r, (_, ref, row) in enumerate(sources):
+        arrivals[r].wait()
         by_slot = dot(one_hot, ref[row], ((0,), (0,)))
         for j in range(tall):
             wide[pl.ds(r * tall + j, slots, stride=step), :] = by_slot[:, j * LANES : (j + 1) * LANES]
@@ -268,7 +267,7 @@
             pltpu.VMEM(query_grads.shape, bf16),
             pltpu.VMEM(cand_grads.shape, bf16),
             pltpu.VMEM((slots * (height + 1), LANES), f32),
-            pltpu.SemaphoreType.DMA((3,)),
+            pltpu.SemaphoreType.DMA((own + per + 1,)),
         ],
         compiler_params=PARAMS,
         name="pack",

time: 34.2 us -> 33.7 us (0.985)
  starting transfers between devices: 8.56 us -> 8.01 us
  blocking collectives: 11 us -> 10.5 us
  waiting for transfers between devices: 7.54 us -> 8.02 us
    all_to_all x1, starting transfers between devices: 8.56 us -> 8.01 us  [swap_over(): lax.all_to_all(x, 'shard', split_axis=0, concat_axis=0, tiled=True, axis_...]
    all_to_all x1, blocking collectives: 11 us -> 10.5 us  [swap_over(): lax.all_to_all(x, 'shard', split_axis=0, concat_axis=0, tiled=True, axis_...]
    all_to_all x1, waiting for transfers between devices: 7.54 us -> 8.02 us  [swap_over(): lax.all_to_all(x, 'shard', split_axis=0, concat_axis=0, tiled=True, axis_...]
where the time goes in v18:
time: 33.7 us; the launch traced here: 33.3 us
  blocking collectives  10.5 us (31%)
  waiting for transfers between devices  8.02 us (24%)
  starting transfers between devices  8.01 us (24%)
  Pallas kernels  4.82 us (14%)
  between operations  1.38 us (4%)
  local copies, waits for them, and re-layouts  0.65 us (2%)
    all_to_all x1, blocking collectives, swap_over(): lax.all_to_all(x, 'shard', split_axis=0, concat_axis=0, tiled=True, axis_...  10.5 us
    all_to_all x1, waiting for transfers between devices, swap_over(): lax.all_to_all(x, 'shard', split_axis=0, concat_axis=0, tiled=True, axis_...  8.02 us
    all_to_all x1, starting transfers between devices, swap_over(): lax.all_to_all(x, 'shard', split_axis=0, concat_axis=0, tiled=True, axis_...  8.01 us
    pallas_call x1, Pallas kernels, body(): pl.pallas_call(pack, out_shape=jax.ShapeDtypeStruct((slots, height, LANES...  2.19 us
    pallas_call x1, Pallas kernels, body(): pl.pallas_call(work, out_shape=jax.ShapeDtypeStruct((slots, send, LANES),...  1.23 us
    pallas_call x1, Pallas kernels, body(): pl.pallas_call(finish, out_shape=(jax.ShapeDtypeStruct(query_grads.shape,...  0.84 us
  transfers between devices with their start and end apart: 1, of which 1 were waited for; matrix products, arithmetic and copies ran while one was open for 0% of the time, Pallas kernels for 2%

profile of v18, /device:TPU:0, one launch (start us, length us, event | category | flops | bytes accessed | tf_op | source)
XLA Modules:
  0.0 33.3 jit_solution(17460016464917855556)
XLA Ops:
  0.6 2.2 %pack.1.after_ref = bf16[16,96,128]{2,1,0:T(8,128)(2,1)} custom-call(s32[1,16]{1,0:T(1,128)} %bitcast.8, bf16[1,16,4096]{2,1,0:T(8,128)(2,1)} %query_hbm.1, bf16[2,16,4096]{2,1,0:T(8,128)(2,1)} %cand_hbm.1), custom_call_target="tpu_custom_call" | custom-call | tf_op jit(solution)/shard_map/pack/pallas_call | solution.py:260
  2.8 0.0 copy-start
  2.8 0.0 copy-start.1
  2.9 0.0 copy-start.2
  2.9 8.0 %all-to-all-start = ((bf16[16,96,128]{2,1,0:T(8,128)(2,1)}), bf16[16,96,128]{2,1,0:T(8,128)(2,1)S(1)}, u32[]{:S(2)}, u32[]{:S(2)}) async-start(bf16[16,96,128]{2,1,0:T(8,128)(2,1)} %pack.1.after_ref), calls=%async_computation | async-start | bytes 786432 | tf_op jit(solution)/shard_map/all_to_all | solution.py:258
  11.5 0.0 copy-start.4
  11.5 0.0 copy-start.3
  11.6 0.0 copy-start.5
  11.6 0.0 copy-done
  11.6 0.0 copy-done.1
  11.6 0.0 copy-done.2
  11.6 0.6 %copy-done.4 = s32[1,384]{1,0:T(1,128)S(1)} copy-done((s32[1,384]{1,0:T(1,128)S(1)}, s32[1,384]{1,0:T(1,128)}, u32[]{:S(2)}) %copy-start.4) | copy-done | bytes 1560
  12.2 0.0 copy-done.3
  12.2 0.0 copy-done.5
  12.2 0.6 %prepare.1 = (bf16[256,256]{1,0:T(8,128)(2,1)S(1)}, bf16[256,256]{1,0:T(8,128)(2,1)S(1)}, bf16[256,256]{1,0:T(8,128)(2,1)S(1)}, f32[64,128]{1,0:T(8,128)S(1)}, b...) custom-call(s32[1]{0:T(128)S(6)} %copy.11.length_ref, s32[1,16]{1,0:T(1,128)S(1)} %bitcast.9, ...), custom_call_target="tpu_custom_call" | custom-call | tf_op jit(solution)/shard_map/prepare/pallas_call | solution.py:276
  12.8 8.0 %all-to-all-done.moved_ref = bf16[16,96,128]{2,1,0:T(8,128)(2,1)S(1)} async-done(((bf16[16,96,128]{2,1,0:T(8,128)(2,1)}), bf16[16,96,128]{2,1,0:T(8,128)(2,1)S(1)}, u32[]{:S(2)}, u32[]{:S(2)}) %all-to-all-start) | async-done | bytes 393248 | tf_op jit(solution)/shard_map/all_to_all | solution.py:258
  20.8 1.2 %work.1 = bf16[16,40,128]{2,1,0:T(8,128)(2,1)S(1)} custom-call(bf16[16,96,128]{2,1,0:T(8,128)(2,1)S(1)} %all-to-all-done.moved_ref, bf16[256,256]{1,0:T(8,128)(2,1)S(1)} %get-tuple-element.9.enter_ref, bf16[256,256]{1,0:T(8,128)(2,1)S(1)} %get-tuple-element.10.outer_ref, bf16[256,256]{1,0:T(8,128)(2,1)S(1)} %get-tuple-element.11.inner_ref, ...), custom_call_target="tpu_custom_call" | custom-call | tf_op jit(solution)/shard_map/work/pallas_call | solution.py:302
  22.0 10.5 %all_to_all.10.home_ref = bf16[16,40,128]{2,1,0:T(8,128)(2,1)S(1)} all-to-all(bf16[16,40,128]{2,1,0:T(8,128)(2,1)S(1)} %work.1), channel_id=1, replica_groups={{10,11,12,13,14,15,0,1,2,3,4,5,6,7,8,9},{26,27,28,29,30,31,16,17,18,19,..., dimensions={0} | all-to-all | bytes 327680 | tf_op jit(solution)/shard_map/all_to_all | solution.py:258
  32.5 0.8 %finish.1 = (bf16[1,16,4096]{2,1,0:T(8,128)(2,1)}, f32[1,384]{1,0:T(1,128)}) custom-call(bf16[16,40,128]{2,1,0:T(8,128)(2,1)S(1)} %all_to_all.10.home_ref, bf16[16,16]{1,0:T(8,128)(2,1)S(1)} %get-tuple-element.14.holds_ref, f32[32,384]{1,0:T(8,128)S(1)} %get-tuple-element.15.chosen_ref), custom_call_target="tpu_custom_call" | custom-call | tf_op jit(solution)/shard_map/finish/pallas_call | solution.py:312
Async XLA Ops:
  2.8 8.7 %copy-start = (bf16[1,64,64]{2,1,0:T(8,128)(2,1)S(1)}, bf16[1,64,64]{2,1,0:T(8,128)(2,1)}, u32[]{:S(2)}) copy-start(bf16[1,64,64]{2,1,0:T(8,128)(2,1)} %param.11) | copy-start | bytes 24580
  2.8 8.7 %copy-start.1 = (bf16[1,64,64]{2,1,0:T(8,128)(2,1)S(1)}, bf16[1,64,64]{2,1,0:T(8,128)(2,1)}, u32[]{:S(2)}) copy-start(bf16[1,64,64]{2,1,0:T(8,128)(2,1)} %param.12) | copy-start | bytes 24580
  2.9 8.7 %copy-start.2 = (f32[1,4096]{1,0:T(1,128)S(1)}, f32[1,4096]{1,0:T(1,128)}, u32[]{:S(2)}) copy-start(f32[1,4096]{1,0:T(1,128)} %param.13) | copy-start | bytes 49156
  2.9 17.9 %all-to-all-start = ((bf16[16,96,128]{2,1,0:T(8,128)(2,1)}), bf16[16,96,128]{2,1,0:T(8,128)(2,1)S(1)}, u32[]{:S(2)}, u32[]{:S(2)}) async-start(bf16[16,96,128]{2,1,0:T(8,128)(2,1)} %pack.1.after_ref), calls=%async_computation | async-start | bytes 786432 | tf_op jit(solution)/shard_map/all_to_all | solution.py:258
  11.5 0.7 %copy-start.4 = (s32[1,384]{1,0:T(1,128)S(1)}, s32[1,384]{1,0:T(1,128)}, u32[]{:S(2)}) copy-start(s32[1,384]{1,0:T(1,128)} %lists_ref.1) | copy-start | bytes 4612
  11.5 0.7 %copy-start.3 = (s32[16]{0:T(128)S(1)}, s32[16]{0:T(128)}, u32[]{:S(2)}) copy-start(s32[16]{0:T(128)} %param.14) | copy-start | bytes 196
  11.6 0.7 %copy-start.5 = (s32[32]{0:T(128)S(1)}, s32[32]{0:T(128)}, u32[]{:S(2)}) copy-start(s32[32]{0:T(128)} %param.15) | copy-start | bytes 388

commit v19 on v18

--- a/solution.py
+++ b/solution.py
@@ -91,7 +91,7 @@
 
 def prepare(
     length_ref, layer_ref, out_basis_ref, in_basis_ref, eigen_ref, rows_ref, lists_ref, after_ref,
-    enter_ref, outer_ref, inner_ref, factor_ref, gather_ref, holds_ref, chosen_ref,
+    enter_ref, outer_ref, turned_ref, back_ref, factor_ref, gather_ref, holds_ref, chosen_ref,
 ):
     del after_ref
     out_basis, in_basis = out_basis_ref[...], in_basis_ref[...]
@@ -104,8 +104,10 @@
     row, column = iota((size, size), 0) // side, iota((size, size), 1) // side
     outer = dot(dot(spread, basis).astype(bf16), spread, ((1,), (1,)))
     inner = dot(dot(spread, in_basis).astype(bf16), spread, ((1,), (1,)))
-    outer_ref[...] = jnp.where(row == column, outer, 0.0).astype(bf16)
-    inner_ref[...] = jnp.where(row == column, inner, 0.0).astype(bf16)
+    outer = jnp.where(row == column, outer, 0.0)
+    outer_ref[...] = outer.astype(bf16)
+    turned_ref[...] = outer.T.astype(bf16)
+    back_ref[...] = jnp.where(row == column, inner, 0.0).T.astype(bf16)
     enter_ref[...] = jnp.where(row == 2 * (column % 2) + column // 2, inner, 0.0).astype(bf16)
     eigen = eigen_ref[...]
     turned = swap(eigen)
@@ -123,7 +125,7 @@
     chosen_ref[...] = (iota((count, longest), 0) == place).astype(f32)
 
 
-def work(moved_ref, enter_ref, outer_ref, inner_ref, factor_ref, gather_ref, out_ref, tails):
+def work(moved_ref, enter_ref, outer_ref, turned_ref, back_ref, factor_ref, gather_ref, out_ref, tails):
     sources, height, _ = moved_ref.shape
     _, send, _ = out_ref.shape
     size = enter_ref.shape[0]
@@ -134,7 +136,7 @@
     stacks = pairs // 4
     arrive, leave = firsts(sources)
     places = [(d - leave) % sources for d in order_of(sources, arrive)]
-    outer, inner, gather = outer_ref[...], inner_ref[...], gather_ref[...]
+    gather = gather_ref[...]
     factor = factor_ref[...]
 
     queries = [jnp.concatenate([moved_ref[2 * p, :tall, :], moved_ref[2 * p + 1, :tall, :]], axis=1) for p in range(pairs)]
@@ -146,14 +148,14 @@
             rows = entered[p * tall : (p + 1) * tall]
             tiles += [rows[:, :LANES], rows[:, LANES:]]
         columns.append(jnp.concatenate(tiles, axis=0))
-    rotated = dot(outer, jnp.concatenate(columns, axis=1), ((0,), (0,)))
+    rotated = dot(turned_ref[...], jnp.concatenate(columns, axis=1))
     tile = jnp.concatenate([jnp.concatenate([factor] * 4, axis=0)] * 2, axis=1)
     scaled = [
         (rotated[:, t * LANES : (t + 2) * LANES] * tile).astype(bf16) for t in range(0, stacks, 2)
     ]
-    returned = dot(jnp.concatenate(scaled, axis=0), inner, ((1,), (1,))).astype(bf16)
+    returned = dot(jnp.concatenate(scaled, axis=0), back_ref[...]).astype(bf16)
     returned = jnp.concatenate([returned[t * size : (t + 1) * size] for t in range(stacks // 2)], axis=1)
-    precond = dot(outer, returned).astype(bf16).astype(f32)
+    precond = dot(outer_ref[...], returned).astype(bf16).astype(f32)
 
     homes = [None] * sources
     for p in range(pairs):
@@ -273,9 +275,10 @@
         name="pack",
     )(in_hbm(layer_row), in_hbm(query_grads), in_hbm(cand_grads))
     square = jax.ShapeDtypeStruct((size, size), bf16)
-    enter, outer, inner, factor, gather, held, chosen = pl.pallas_call(
+    enter, outer, turned, back, factor, gather, held, chosen = pl.pallas_call(
         prepare,
         out_shape=(
+            square,
             square,
             square,
             square,
@@ -285,7 +288,7 @@
             jax.ShapeDtypeStruct((count, cand_lists.shape[1]), f32),
         ),
         in_specs=[SMEM] + [VMEM] * 6 + [ANY],
-        out_specs=[VMEM] * 7,
+        out_specs=[VMEM] * 8,
         compiler_params=PARAMS,
         name="prepare",
     )(
@@ -302,12 +305,12 @@
     homes = pl.pallas_call(
         work,
         out_shape=jax.ShapeDtypeStruct((slots, send, LANES), bf16),
-        in_specs=[VMEM] * 6,
+        in_specs=[VMEM] * 7,
         out_specs=VMEM,
         scratch_shapes=[pltpu.VMEM((slots * (send - tall), LANES), f32)],
         compiler_params=PARAMS,
         name="work",
-    )(moved, enter, outer, inner, factor, gather)
+    )(moved, enter, outer, turned, back, factor, gather)
     home = swap_over(homes, firsts(slots)[1])
     return pl.pallas_call(
         finish,

time: 33.7 us -> 33.7 us (level)
  no operation moved by 1% of the time
where the time goes in v19:
time: 33.7 us; the launch traced here: 33.4 us
  blocking collectives  10.5 us (31%)
  starting transfers between devices  8.01 us (24%)
  waiting for transfers between devices  7.87 us (23%)
  Pallas kernels  4.99 us (15%)
  between operations  1.37 us (4%)
  local copies, waits for them, and re-layouts  0.65 us (2%)
    all_to_all x1, blocking collectives, swap_over(): lax.all_to_all(x, 'shard', split_axis=0, concat_axis=0, tiled=True, axis_...  10.5 us
    all_to_all x1, starting transfers between devices, swap_over(): lax.all_to_all(x, 'shard', split_axis=0, concat_axis=0, tiled=True, axis_...  8.01 us
    all_to_all x1, waiting for transfers between devices, swap_over(): lax.all_to_all(x, 'shard', split_axis=0, concat_axis=0, tiled=True, axis_...  7.87 us
    pallas_call x1, Pallas kernels, body(): pl.pallas_call(pack, out_shape=jax.ShapeDtypeStruct((slots, height, LANES...  2.19 us
    pallas_call x1, Pallas kernels, body(): pl.pallas_call(work, out_shape=jax.ShapeDtypeStruct((slots, send, LANES),...  1.25 us
    pallas_call x1, Pallas kernels, body(): pl.pallas_call(finish, out_shape=(jax.ShapeDtypeStruct(query_grads.shape,...  0.84 us
    pallas_call x1, Pallas kernels, body(): pl.pallas_call(prepare, out_shape=(square, square, square, square, jax.Sh...  0.72 us
  transfers between devices with their start and end apart: 1, of which 1 were waited for; matrix products, arithmetic and copies ran while one was open for 0% of the time, Pallas kernels for 2%

profile of v19, /device:TPU:0, one launch (start us, length us, event | category | flops | bytes accessed | tf_op | source)
XLA Modules:
  0.0 33.4 jit_solution(7171504795585150836)
XLA Ops:
  0.6 2.2 %pack.1.after_ref = bf16[16,96,128]{2,1,0:T(8,128)(2,1)} custom-call(s32[1,16]{1,0:T(1,128)} %bitcast.8, bf16[1,16,4096]{2,1,0:T(8,128)(2,1)} %query_hbm.1, bf16[2,16,4096]{2,1,0:T(8,128)(2,1)} %cand_hbm.1), custom_call_target="tpu_custom_call" | custom-call | tf_op jit(solution)/shard_map/pack/pallas_call | solution.py:262
  2.8 0.0 copy-start
  2.8 0.0 copy-start.1
  2.9 0.0 copy-start.2
  2.9 8.0 %all-to-all-start = ((bf16[16,96,128]{2,1,0:T(8,128)(2,1)}), bf16[16,96,128]{2,1,0:T(8,128)(2,1)S(1)}, u32[]{:S(2)}, u32[]{:S(2)}) async-start(bf16[16,96,128]{2,1,0:T(8,128)(2,1)} %pack.1.after_ref), calls=%async_computation | async-start | bytes 786432 | tf_op jit(solution)/shard_map/all_to_all | solution.py:260
  11.5 0.0 copy-start.4
  11.5 0.0 copy-start.3
  11.6 0.0 copy-start.5
  11.6 0.0 copy-done
  11.6 0.0 copy-done.1
  11.6 0.0 copy-done.2
  11.6 0.6 %copy-done.4 = s32[1,384]{1,0:T(1,128)S(1)} copy-done((s32[1,384]{1,0:T(1,128)S(1)}, s32[1,384]{1,0:T(1,128)}, u32[]{:S(2)}) %copy-start.4) | copy-done | bytes 1560
  12.2 0.0 copy-done.3
  12.2 0.0 copy-done.5
  12.2 0.7 %prepare.1 = (bf16[256,256]{1,0:T(8,128)(2,1)S(1)}, bf16[256,256]{1,0:T(8,128)(2,1)S(1)}, bf16[256,256]{1,0:T(8,128)(2,1)S(1)}, bf16[256,256]{1,0:T(8,128)(2,1)S...) custom-call(s32[1]{0:T(128)S(6)} %copy.11.length_ref, ...), custom_call_target="tpu_custom_call" | custom-call | tf_op jit(solution)/shard_map/prepare/pallas_call | solution.py:278
  12.9 7.9 %all-to-all-done.moved_ref = bf16[16,96,128]{2,1,0:T(8,128)(2,1)S(1)} async-done(((bf16[16,96,128]{2,1,0:T(8,128)(2,1)}), bf16[16,96,128]{2,1,0:T(8,128)(2,1)S(1)}, u32[]{:S(2)}, u32[]{:S(2)}) %all-to-all-start) | async-done | bytes 393248 | tf_op jit(solution)/shard_map/all_to_all | solution.py:260
  20.8 1.2 %work.1 = bf16[16,40,128]{2,1,0:T(8,128)(2,1)S(1)} custom-call(bf16[16,96,128]{2,1,0:T(8,128)(2,1)S(1)} %all-to-all-done.moved_ref, bf16[256,256]{1,0:T(8,128)(2,1)S(1)} %get-tuple-element.10.enter_ref, bf16[256,256]{1,0:T(8,128)(2,1)S(1)} %get-tuple-element.11.outer_ref, bf16[256,256]{1,0:T(8,128)(2,1)S(1)} %get-tuple-element.12.turned_ref, ...), custom_call_target="tpu_custom_call" | custom-call | tf_op jit(solution)/shard_map/work/pallas_call | solution.py:305
  22.1 10.5 %all_to_all.10.home_ref = bf16[16,40,128]{2,1,0:T(8,128)(2,1)S(1)} all-to-all(bf16[16,40,128]{2,1,0:T(8,128)(2,1)S(1)} %work.1), channel_id=1, replica_groups={{10,11,12,13,14,15,0,1,2,3,4,5,6,7,8,9},{26,27,28,29,30,31,16,17,18,19,..., dimensions={0} | all-to-all | bytes 327680 | tf_op jit(solution)/shard_map/all_to_all | solution.py:260
  32.5 0.8 %finish.1 = (bf16[1,16,4096]{2,1,0:T(8,128)(2,1)}, f32[1,384]{1,0:T(1,128)}) custom-call(bf16[16,40,128]{2,1,0:T(8,128)(2,1)S(1)} %all_to_all.10.home_ref, bf16[16,16]{1,0:T(8,128)(2,1)S(1)} %get-tuple-element.16.holds_ref, f32[32,384]{1,0:T(8,128)S(1)} %get-tuple-element.17.chosen_ref), custom_call_target="tpu_custom_call" | custom-call | tf_op jit(solution)/shard_map/finish/pallas_call | solution.py:315
Async XLA Ops:
  2.8 8.7 %copy-start = (bf16[1,64,64]{2,1,0:T(8,128)(2,1)S(1)}, bf16[1,64,64]{2,1,0:T(8,128)(2,1)}, u32[]{:S(2)}) copy-start(bf16[1,64,64]{2,1,0:T(8,128)(2,1)} %param.11) | copy-start | bytes 24580
  2.8 8.7 %copy-start.1 = (bf16[1,64,64]{2,1,0:T(8,128)(2,1)S(1)}, bf16[1,64,64]{2,1,0:T(8,128)(2,1)}, u32[]{:S(2)}) copy-start(bf16[1,64,64]{2,1,0:T(8,128)(2,1)} %param.12) | copy-start | bytes 24580
  2.9 8.7 %copy-start.2 = (f32[1,4096]{1,0:T(1,128)S(1)}, f32[1,4096]{1,0:T(1,128)}, u32[]{:S(2)}) copy-start(f32[1,4096]{1,0:T(1,128)} %param.13) | copy-start | bytes 49156
  2.9 17.9 %all-to-all-start = ((bf16[16,96,128]{2,1,0:T(8,128)(2,1)}), bf16[16,96,128]{2,1,0:T(8,128)(2,1)S(1)}, u32[]{:S(2)}, u32[]{:S(2)}) async-start(bf16[16,96,128]{2,1,0:T(8,128)(2,1)} %pack.1.after_ref), calls=%async_computation | async-start | bytes 786432 | tf_op jit(solution)/shard_map/all_to_all | solution.py:260
  11.5 0.7 %copy-start.4 = (s32[1,384]{1,0:T(1,128)S(1)}, s32[1,384]{1,0:T(1,128)}, u32[]{:S(2)}) copy-start(s32[1,384]{1,0:T(1,128)} %lists_ref.1) | copy-start | bytes 4612
  11.5 0.7 %copy-start.3 = (s32[16]{0:T(128)S(1)}, s32[16]{0:T(128)}, u32[]{:S(2)}) copy-start(s32[16]{0:T(128)} %param.14) | copy-start | bytes 196
  11.6 0.7 %copy-start.5 = (s32[32]{0:T(128)S(1)}, s32[32]{0:T(128)}, u32[]{:S(2)}) copy-start(s32[32]{0:T(128)} %param.15) | copy-start | bytes 388

commit v20 on v14

--- a/solution.py
+++ b/solution.py
@@ -38,12 +38,6 @@
     return mask(row // SUBLANES + tall * (row % SUBLANES) == iota((size, size), 1))
 
 
-def scatter_rows(tall):
-    size = SUBLANES * tall
-    row = iota((size, size), 0)
-    return mask(row // tall + SUBLANES * (row % tall) == iota((size, size), 1))
-
-
 def half(left, right):
     return jnp.where(iota(left.shape, 1) < LANES // 2, left, right)
 
@@ -65,27 +59,31 @@
     return mask(iota((modules, slots), 0) == layer_row)
 
 
-def spread_bases(out_basis, in_basis, eigen, enter_ref, outer_ref, inner_ref, factor_ref):
+def block_bases(out_basis, in_basis, eigen):
     side = out_basis.shape[0]
     tall = side // 2
-    size = enter_ref.shape[0]
-    order = mask(iota((side, side), 1) == 2 * (iota((side, side), 0) % tall) + iota((side, side), 0) // tall)
-    basis = dot(dot(order, out_basis).astype(bf16), order, ((1,), (1,))).astype(bf16)
-    spread = mask(iota((size, side), 0) % side == iota((size, side), 1))
+    size = 4 * side
+
+    def spread(basis):
+        wide = jnp.concatenate([basis] * 4, axis=1)
+        return jnp.concatenate([wide] * 4, axis=0)
+
     row, column = iota((size, size), 0) // side, iota((size, size), 1) // side
-    outer = dot(dot(spread, basis).astype(bf16), spread, ((1,), (1,)))
-    inner = dot(dot(spread, in_basis).astype(bf16), spread, ((1,), (1,)))
-    outer_ref[...] = jnp.where(row == column, outer, 0.0).astype(bf16)
-    inner_ref[...] = jnp.where(row == column, inner, 0.0).astype(bf16)
-    enter_ref[...] = jnp.where(row == 2 * (column % 2) + column // 2, inner, 0.0).astype(bf16)
+    turn = mask(iota((side, side), 1) == 2 * (iota((side, side), 0) % tall) + iota((side, side), 0) // tall)
+    bases = spread(dot(dot(turn, out_basis).astype(bf16), turn, ((1,), (1,))))
+    outer = jnp.where(row == column, bases, 0.0).astype(bf16)
+    bases = spread(in_basis.astype(f32))
+    enter = jnp.where(row == 2 * (column % 2) + column // 2, bases, 0.0).astype(bf16)
+    inner = jnp.where(row == column, bases, 0.0).astype(bf16)
     turned = swap(eigen)
-    factor_ref[...] = 1.0 / (jnp.concatenate([half(eigen, turned), half(turned, eigen)], axis=0) + damping)
+    factor = 1.0 / (jnp.concatenate([half(eigen, turned), half(turned, eigen)], axis=0) + damping)
+    return enter, outer, inner, factor
 
 
 def pack(
-    layer_hbm, out_basis_hbm, in_basis_hbm, eigen_hbm, query_hbm, cand_hbm,
-    out_ref, enter_ref, outer_ref, inner_ref, factor_ref, gather_ref,
-    layer_ref, out_basis_ref, in_basis_ref, eigen_ref, query_ref, cand_ref, by_module, sems,
+    length_ref, layer_hbm, out_basis_hbm, in_basis_hbm, eigen_hbm, query_hbm, cand_hbm,
+    out_ref, enter_ref, outer_ref, inner_ref, factor_ref, gather_ref, holds_ref, limit_ref,
+    layer_ref, out_basis_ref, in_basis_ref, eigen_ref, query_ref, cand_ref, wide, sems,
 ):
     arrivals = [
         pltpu.make_async_copy(source, target, sems.at[i])
@@ -103,52 +101,28 @@
     for arrival in arrivals:
         arrival.start()
     modules, flat = query_ref.shape[1:]
-    slots = out_ref.shape[0]
+    slots, height, _ = out_ref.shape
     tall = flat // LANES
-    order = order_of(slots, firsts(slots)[0])
+    step = height + 1
     gather_ref[...] = gather_rows(tall)
+    limit_ref[...] = jnp.full(limit_ref.shape, length_ref[0])
     for arrival in arrivals[:4]:
         arrival.wait()
-    spread_bases(
-        out_basis_ref[...], in_basis_ref[...], eigen_ref[...], enter_ref, outer_ref, inner_ref, factor_ref
+    one_hot = holds(layer_ref[...], modules, firsts(slots)[0])
+    holds_ref[...] = holds(layer_ref[...], modules, firsts(slots)[1])
+    enter_ref[...], outer_ref[...], inner_ref[...], factor_ref[...] = block_bases(
+        out_basis_ref[...], in_basis_ref[...], eigen_ref[...]
     )
-    at_once = slots * tall <= 512
-    if at_once:
-        shape = (tall, tall * modules)
-        offset = iota(shape, 1) - modules * iota(shape, 0)
-        place = jnp.concatenate([mask(offset == layer_ref[s]) for s in order], axis=0)
-    else:
-        place = scatter_rows(tall)
     r = 0
     for arrival, ref in zip(arrivals[4:], (query_ref, cand_ref)):
         arrival.wait()
-        many = ref.shape[0]
-        if at_once:
-            tiles = [
-                jnp.concatenate([ref[i, :, j * LANES : (j + 1) * LANES] for j in range(tall)], axis=0)
-                for i in range(many)
-            ]
-            blocks = dot(place, jnp.concatenate(tiles, axis=1)).astype(bf16)
-            for k in range(slots):
-                for i in range(many):
-                    part = blocks[k * tall : (k + 1) * tall, i * LANES : (i + 1) * LANES]
-                    out_ref[k, (r + i) * tall : (r + i + 1) * tall, :] = part
-        else:
-            for i in range(many):
-                rows = ref[i].astype(f32)
-                columns = []
-                for m in range(0, modules, SUBLANES):
-                    tiles = [rows[m : m + SUBLANES, j * LANES : (j + 1) * LANES] for j in range(tall)]
-                    columns.append(jnp.concatenate(tiles, axis=0).astype(bf16))
-                blocks = dot(place, jnp.concatenate(columns, axis=1)).astype(bf16)
-                for m in range(modules):
-                    c, g = m % SUBLANES, m // SUBLANES
-                    part = blocks[c * tall : (c + 1) * tall, g * LANES : (g + 1) * LANES]
-                    by_module[m, (r + i) * tall : (r + i + 1) * tall, :] = part
-        r += many
-    if not at_once:
-        for k, s in enumerate(order):
-            out_ref[k] = by_module[layer_ref[s]]
+        for row in range(ref.shape[0]):
+            by_slot = dot(one_hot, ref[row], ((0,), (0,)))
+            for j in range(tall):
+                wide[pl.ds(r * tall + j, slots, stride=step), :] = by_slot[:, j * LANES : (j + 1) * LANES]
+            r += 1
+    for k in range(slots):
+        out_ref[k] = wide[pl.ds(k * step, height), :].astype(bf16)
 
 
 def upright(row, count):
@@ -156,7 +130,16 @@
     return jnp.sum(jnp.where(iota(shape, 0) == iota(shape, 1), row, 0.0), axis=1, keepdims=True)
 
 
-def work(moved_ref, enter_ref, outer_ref, inner_ref, factor_ref, gather_ref, out_ref, tails):
+def work(
+    moved_ref, enter_ref, outer_ref, inner_ref, factor_ref, gather_ref, limit_ref, rows_hbm, lists_hbm,
+    out_ref, chosen_ref, tails, rows_ref, lists_ref, sems,
+):
+    arrivals = [
+        pltpu.make_async_copy(rows_hbm, rows_ref, sems.at[0]),
+        pltpu.make_async_copy(lists_hbm, lists_ref, sems.at[1]),
+    ]
+    for arrival in arrivals:
+        arrival.start()
     sources, height, _ = moved_ref.shape
     _, send, _ = out_ref.shape
     size = enter_ref.shape[0]
@@ -232,23 +215,26 @@
     for k in range(sources):
         out_ref[k] = jnp.concatenate([homes[k], tails[k * tail : (k + 1) * tail, :]], axis=0).astype(bf16)
 
-
-def finish(length_ref, layer_ref, rows_ref, lists_ref, home_ref, precond_ref, scores_ref, wide):
+    for arrival in arrivals:
+        arrival.wait()
+    lists = lists_ref[...]
+    longest = lists.shape[1]
+    rows = upright(rows_ref[...].astype(f32), count)
+    place = jnp.sum(jnp.where(iota((count, longest), 0) == lists, rows, 0.0), axis=0, keepdims=True)
+    place = jnp.where(iota((1, longest), 1) < limit_ref[:, :1], place.astype(jnp.int32), -1)
+    chosen_ref[...] = (iota((count, longest), 0) == place).astype(f32)
+
+
+def finish(home_ref, holds_ref, chosen_ref, precond_ref, scores_ref, wide):
     slots, send, _ = home_ref.shape
-    modules, flat = precond_ref.shape[1:]
+    _, flat = precond_ref.shape[1:]
+    count = chosen_ref.shape[0]
     tall = flat // LANES
     step = send + 1
     for k in range(slots):
         wide[pl.ds(k * step, send), :] = home_ref[k].astype(f32)
     by_slot = jnp.concatenate([wide[pl.ds(j, slots, stride=step), :].astype(bf16) for j in range(tall)], axis=1)
-    precond_ref[0] = dot(holds(layer_ref[...], modules, firsts(slots)[1]), by_slot).astype(bf16)
-
-    count = rows_ref.shape[1]
-    lists = lists_ref[...]
-    longest = lists.shape[1]
-    rows = upright(rows_ref[...].astype(f32), count)
-    place = jnp.sum(jnp.where(iota((count, longest), 0) == lists, rows, 0.0), axis=0, keepdims=True)
-    place = jnp.where(iota((1, longest), 1) < length_ref[...], place.astype(jnp.int32), -1)
+    precond_ref[0] = dot(holds_ref[...], by_slot).astype(bf16)
     groups = -(-count // LANES)
     parts = []
     for t in range(groups):
@@ -256,10 +242,11 @@
         parts.append(jnp.sum((pieces[2] + pieces[1]) + pieces[0], axis=0, keepdims=True))
     dense = parts[0] if groups == 1 else jnp.concatenate(parts, axis=1)
     scores_ref[...] = jnp.sum(
-        jnp.where(iota((count, longest), 0) == place, upright(dense, count), 0.0), axis=0, keepdims=True
+        jnp.where(chosen_ref[...] > 0.0, upright(dense, count), 0.0), axis=0, keepdims=True
     )
 
 
+SMEM = pl.BlockSpec(memory_space=pltpu.SMEM)
 HBM = pl.BlockSpec(memory_space=pltpu.HBM)
 VMEM = pl.BlockSpec(memory_space=pltpu.VMEM)
 PARAMS = pltpu.CompilerParams(vmem_limit_bytes=40 * 1024 * 1024)
@@ -279,7 +266,6 @@
     own, modules, flat = query_grads.shape
     per = cand_grads.shape[0]
     slots = layer_map.shape[0]
-    layer_row = layer_map.reshape(1, slots)
     tall = flat // LANES
     side = basis_out.shape[1]
     size = SUBLANES * tall
@@ -296,14 +282,14 @@
 
     square = pltpu.VMEM((size, size), bf16)
     operands = (
-        layer_map,
+        layer_map.reshape(1, slots),
         basis_out.reshape(basis_out.shape[1:]),
         basis_in.reshape(basis_in.shape[1:]),
         eigvals.reshape(tall, LANES),
         query_grads,
         cand_grads,
     )
-    packed, enter, outer, inner, factor, gather = pl.pallas_call(
+    packed, enter, outer, inner, factor, gather, held, limit = pl.pallas_call(
         pack,
         out_shape=(
             pltpu.VMEM((slots, height, LANES), bf16),
@@ -312,25 +298,32 @@
             square,
             pltpu.VMEM((side, LANES), f32),
             square,
+            pltpu.VMEM((modules, slots), bf16),
+            pltpu.VMEM((1, LANES), jnp.int32),
         ),
-        in_specs=[HBM] * len(operands),
-        out_specs=[VMEM] * 6,
-        scratch_shapes=[pltpu.SMEM(layer_map.shape, jnp.int32)]
-        + [pltpu.VMEM(x.shape, x.dtype) for x in operands[1:]]
-        + [pltpu.VMEM((modules, height, LANES), bf16), pltpu.SemaphoreType.DMA((len(operands),))],
+        in_specs=[SMEM] + [HBM] * len(operands),
+        out_specs=[VMEM] * 8,
+        scratch_shapes=[pltpu.VMEM(x.shape, x.dtype) for x in operands]
+        + [pltpu.VMEM((slots * (height + 1), LANES), f32), pltpu.SemaphoreType.DMA((len(operands),))],
         compiler_params=PARAMS,
         name="pack",
-    )(*(in_hbm(x) for x in operands))
+    )(list_lengths, *(in_hbm(x) for x in operands))
     moved = swap_over(packed, firsts(slots)[0])
-    homes = pl.pallas_call(
+    small = (cand_rows.reshape(1, count), cand_lists)
+    homes, chosen = pl.pallas_call(
         work,
-        out_shape=jax.ShapeDtypeStruct((slots, send, LANES), bf16),
-        in_specs=[VMEM] * 6,
-        out_specs=VMEM,
-        scratch_shapes=[pltpu.VMEM((slots * (send - tall), LANES), f32)],
+        out_shape=(
+            jax.ShapeDtypeStruct((slots, send, LANES), bf16),
+            jax.ShapeDtypeStruct((count, cand_lists.shape[1]), f32),
+        ),
+        in_specs=[VMEM] * 7 + [HBM] * 2,
+        out_specs=[VMEM] * 2,
+        scratch_shapes=[pltpu.VMEM((slots * (send - tall), LANES), f32)]
+        + [pltpu.VMEM(x.shape, jnp.int32) for x in small]
+        + [pltpu.SemaphoreType.DMA((2,))],
         compiler_params=PARAMS,
         name="work",
-    )(moved, enter, outer, inner, factor, gather)
+    )(moved, enter, outer, inner, factor, gather, limit, *(in_hbm(x) for x in small))
     home = swap_over(homes, firsts(slots)[1])
     return pl.pallas_call(
         finish,
@@ -338,12 +331,12 @@
             jax.ShapeDtypeStruct(query_grads.shape, bf16),
             jax.ShapeDtypeStruct(cand_lists.shape, f32),
         ),
-        in_specs=[VMEM] * 5,
+        in_specs=[VMEM] * 3,
         out_specs=(VMEM, VMEM),
         scratch_shapes=[pltpu.VMEM((slots * (send + 1), LANES), f32)],
         compiler_params=PARAMS,
         name="finish",
-    )(list_lengths.reshape(1, 1), layer_row, cand_rows.reshape(1, count), cand_lists, home)
+    )(home, held, chosen)
 
 
 def solution(mesh):

time: 34.6 us -> 33.2 us (0.960)
  blocking collectives: 16.7 us -> 27.6 us
  starting transfers between devices: 5.81 us -> 0 us
  waiting for transfers between devices: 4.79 us -> 0 us
  Pallas kernels: 5 us -> 4.07 us
  local copies, waits for them, and re-layouts: 0.68 us -> 0 us
    all_to_all x1 -> x2, blocking collectives: 16.7 us -> 27.6 us  [swap_over(): lax.all_to_all(x, 'shard', split_axis=0, concat_axis=0, tiled=True, axis_...]
    all_to_all x1 -> x0, starting transfers between devices: 5.81 us -> none  [swap_over(): lax.all_to_all(x, 'shard', split_axis=0, concat_axis=0, tiled=True, axis_...]
    all_to_all x1 -> x0, waiting for transfers between devices: 4.79 us -> none  [swap_over(): lax.all_to_all(x, 'shard', split_axis=0, concat_axis=0, tiled=True, axis_...]
    unnamed x6 -> x0, local copies, waits for them, and re-layouts: 0.68 us -> none
    pallas_call x1, Pallas kernels: 2.22 us -> 1.62 us  [body(): pl.pallas_call(pack, out_shape=(pltpu.VMEM((slots, height, LANES), bf16),...]
  transfers between devices with their start and end apart: 1 -> 0, of which waited for: 1 -> 0; matrix products, arithmetic and copies ran while one was open for 0% -> 0% of each run, Pallas kernels for 0% -> 0%
where the time goes in v20:
time: 33.2 us; the launch traced here: 32.9 us
  blocking collectives  27.6 us (83%)
  Pallas kernels  4.07 us (12%)
  between operations  1.3 us (4%)
    all_to_all x2, blocking collectives, swap_over(): lax.all_to_all(x, 'shard', split_axis=0, concat_axis=0, tiled=True, axis_...  27.6 us
    pallas_call x1, Pallas kernels, body(): pl.pallas_call(pack, out_shape=(pltpu.VMEM((slots, height, LANES), bf16),...  1.62 us
    pallas_call x1, Pallas kernels, body(): pl.pallas_call(work, out_shape=(jax.ShapeDtypeStruct((slots, send, LANES)...  1.61 us
    pallas_call x1, Pallas kernels, body(): pl.pallas_call(finish, out_shape=(jax.ShapeDtypeStruct(query_grads.shape,...  0.84 us

profile of v20, /device:TPU:0, one launch (start us, length us, event | category | flops | bytes accessed | tf_op | source)
XLA Modules:
  0.0 32.9 jit_solution(4735512234084177196)
XLA Ops:
  1.3 1.6 %pack.1 = (bf16[16,96,128]{2,1,0:T(8,128)(2,1)S(1)}, bf16[256,256]{1,0:T(8,128)(2,1)S(1)}, bf16[256,256]{1,0:T(8,128)(2,1)S(1)}, bf16[256,256]{1,0:T(8,128)(2,1)...) custom-call(s32[1]{0:T(128)S(6)} %copy.11.length_ref, ...), custom_call_target="tpu_custom_call" | custom-call | tf_op jit(solution)/shard_map/pack/pallas_call | solution.py:292
  2.9 16.7 %all_to_all.10.moved_ref = bf16[16,96,128]{2,1,0:T(8,128)(2,1)S(1)} all-to-all(bf16[16,96,128]{2,1,0:T(8,128)(2,1)S(1)} %get-tuple-element.12), channel_id=1, replica_groups={{10,11,12,13,14,15,0,1,2,3,4,5,6,7,8,9},{26,27,28,29,30,31,16,17,18,19,..., dimensions={0} | all-to-all | bytes 786432 | tf_op jit(solution)/shard_map/all_to_all | solution.py:281
  19.6 1.6 %work.1 = (bf16[16,40,128]{2,1,0:T(8,128)(2,1)S(1)}, f32[32,384]{1,0:T(8,128)S(1)}) custom-call(bf16[16,96,128]{2,1,0:T(8,128)(2,1)S(1)} %all_to_all.10.moved_ref, bf16[256,256]{1,0:T(8,128)(2,1)S(1)} %get-tuple-element.13.enter_ref, bf16[256,256]{1,0:T(8,128)(2,1)S(1)} %get-tuple-element.14.outer_ref, bf16[256,256]{1,0:T(8,128)(2,1)S(1)} %get-tuple-element.15.inner_ref, ...), custom_call_target="tpu_custom_call" | custom-call | tf_op jit(solution)/shard_map/work/pallas_call | solution.py:313
  21.2 10.9 %all_to_all.11.home_ref = bf16[16,40,128]{2,1,0:T(8,128)(2,1)S(1)} all-to-all(bf16[16,40,128]{2,1,0:T(8,128)(2,1)S(1)} %get-tuple-element.19), channel_id=1, replica_groups={{10,11,12,13,14,15,0,1,2,3,4,5,6,7,8,9},{26,27,28,29,30,31,16,17,18,19,..., dimensions={0} | all-to-all | bytes 327680 | tf_op jit(solution)/shard_map/all_to_all | solution.py:281
  32.1 0.8 %finish.1 = (bf16[1,16,4096]{2,1,0:T(8,128)(2,1)}, f32[1,384]{1,0:T(1,128)}) custom-call(bf16[16,40,128]{2,1,0:T(8,128)(2,1)S(1)} %all_to_all.11.home_ref, bf16[16,16]{1,0:T(8,128)(2,1)S(1)} %get-tuple-element.20.holds_ref, f32[32,384]{1,0:T(8,128)S(1)} %get-tuple-element.21.chosen_ref), custom_call_target="tpu_custom_call" | custom-call | tf_op jit(solution)/shard_map/finish/pallas_call | solution.py:328

commit v21 on v20

--- a/solution.py
+++ b/solution.py
@@ -81,20 +81,22 @@
 
 
 def pack(
-    length_ref, layer_hbm, out_basis_hbm, in_basis_hbm, eigen_hbm, query_hbm, cand_hbm,
-    out_ref, enter_ref, outer_ref, inner_ref, factor_ref, gather_ref, holds_ref, limit_ref,
-    layer_ref, out_basis_ref, in_basis_ref, eigen_ref, query_ref, cand_ref, wide, sems,
+    length_ref, query_hbm, cand_hbm, layer_hbm, out_basis_hbm, in_basis_hbm, eigen_hbm, rows_hbm, lists_hbm,
+    out_ref, enter_ref, outer_ref, inner_ref, factor_ref, gather_ref, holds_ref, chosen_ref,
+    query_ref, cand_ref, layer_ref, out_basis_ref, in_basis_ref, eigen_ref, rows_ref, lists_ref, wide, sems,
 ):
     arrivals = [
         pltpu.make_async_copy(source, target, sems.at[i])
         for i, (source, target) in enumerate(
             (
+                (query_hbm, query_ref),
+                (cand_hbm, cand_ref),
                 (layer_hbm, layer_ref),
                 (out_basis_hbm, out_basis_ref),
                 (in_basis_hbm, in_basis_ref),
                 (eigen_hbm, eigen_ref),
-                (query_hbm, query_ref),
-                (cand_hbm, cand_ref),
+                (rows_hbm, rows_ref),
+                (lists_hbm, lists_ref),
             )
         )
     ]
@@ -105,16 +107,21 @@
     tall = flat // LANES
     step = height + 1
     gather_ref[...] = gather_rows(tall)
-    limit_ref[...] = jnp.full(limit_ref.shape, length_ref[0])
-    for arrival in arrivals[:4]:
+    for arrival in arrivals[2:]:
         arrival.wait()
     one_hot = holds(layer_ref[...], modules, firsts(slots)[0])
     holds_ref[...] = holds(layer_ref[...], modules, firsts(slots)[1])
     enter_ref[...], outer_ref[...], inner_ref[...], factor_ref[...] = block_bases(
         out_basis_ref[...], in_basis_ref[...], eigen_ref[...]
     )
+    lists = lists_ref[...]
+    count, longest = rows_ref.shape[1], lists.shape[1]
+    rows = upright(rows_ref[...].astype(f32), count)
+    place = jnp.sum(jnp.where(iota((count, longest), 0) == lists, rows, 0.0), axis=0, keepdims=True)
+    place = jnp.where(iota((1, longest), 1) < length_ref[0], place.astype(jnp.int32), -1)
+    chosen_ref[...] = (iota((count, longest), 0) == place).astype(f32)
     r = 0
-    for arrival, ref in zip(arrivals[4:], (query_ref, cand_ref)):
+    for arrival, ref in zip(arrivals, (query_ref, cand_ref)):
         arrival.wait()
         for row in range(ref.shape[0]):
             by_slot = dot(one_hot, ref[row], ((0,), (0,)))
@@ -130,16 +137,7 @@
     return jnp.sum(jnp.where(iota(shape, 0) == iota(shape, 1), row, 0.0), axis=1, keepdims=True)
 
 
-def work(
-    moved_ref, enter_ref, outer_ref, inner_ref, factor_ref, gather_ref, limit_ref, rows_hbm, lists_hbm,
-    out_ref, chosen_ref, tails, rows_ref, lists_ref, sems,
-):
-    arrivals = [
-        pltpu.make_async_copy(rows_hbm, rows_ref, sems.at[0]),
-        pltpu.make_async_copy(lists_hbm, lists_ref, sems.at[1]),
-    ]
-    for arrival in arrivals:
-        arrival.start()
+def work(moved_ref, enter_ref, outer_ref, inner_ref, factor_ref, gather_ref, out_ref, tails):
     sources, height, _ = moved_ref.shape
     _, send, _ = out_ref.shape
     size = enter_ref.shape[0]
@@ -214,15 +212,6 @@
             tails[pl.ds(k * wide + t, sources, stride=tail), :] = piece[:, t * LANES : (t + 1) * LANES]
     for k in range(sources):
         out_ref[k] = jnp.concatenate([homes[k], tails[k * tail : (k + 1) * tail, :]], axis=0).astype(bf16)
-
-    for arrival in arrivals:
-        arrival.wait()
-    lists = lists_ref[...]
-    longest = lists.shape[1]
-    rows = upright(rows_ref[...].astype(f32), count)
-    place = jnp.sum(jnp.where(iota((count, longest), 0) == lists, rows, 0.0), axis=0, keepdims=True)
-    place = jnp.where(iota((1, longest), 1) < limit_ref[:, :1], place.astype(jnp.int32), -1)
-    chosen_ref[...] = (iota((count, longest), 0) == place).astype(f32)
 
 
 def finish(home_ref, holds_ref, chosen_ref, precond_ref, scores_ref, wide):
@@ -282,14 +271,16 @@
 
     square = pltpu.VMEM((size, size), bf16)
     operands = (
+        query_grads,
+        cand_grads,
         layer_map.reshape(1, slots),
         basis_out.reshape(basis_out.shape[1:]),
         basis_in.reshape(basis_in.shape[1:]),
         eigvals.reshape(tall, LANES),
-        query_grads,
-        cand_grads,
+        cand_rows.reshape(1, count),
+        cand_lists,
     )
-    packed, enter, outer, inner, factor, gather, held, limit = pl.pallas_call(
+    packed, enter, outer, inner, factor, gather, held, chosen = pl.pallas_call(
         pack,
         out_shape=(
             pltpu.VMEM((slots, height, LANES), bf16),
@@ -299,7 +290,7 @@
             pltpu.VMEM((side, LANES), f32),
             square,
             pltpu.VMEM((modules, slots), bf16),
-            pltpu.VMEM((1, LANES), jnp.int32),
+            pltpu.VMEM((count, cand_lists.shape[1]), f32),
         ),
         in_specs=[SMEM] + [HBM] * len(operands),
         out_specs=[VMEM] * 8,
@@ -309,21 +300,15 @@
         name="pack",
     )(list_lengths, *(in_hbm(x) for x in operands))
     moved = swap_over(packed, firsts(slots)[0])
-    small = (cand_rows.reshape(1, count), cand_lists)
-    homes, chosen = pl.pallas_call(
+    homes = pl.pallas_call(
         work,
-        out_shape=(
-            jax.ShapeDtypeStruct((slots, send, LANES), bf16),
-            jax.ShapeDtypeStruct((count, cand_lists.shape[1]), f32),
-        ),
-        in_specs=[VMEM] * 7 + [HBM] * 2,
-        out_specs=[VMEM] * 2,
-        scratch_shapes=[pltpu.VMEM((slots * (send - tall), LANES), f32)]
-        + [pltpu.VMEM(x.shape, jnp.int32) for x in small]
-        + [pltpu.SemaphoreType.DMA((2,))],
+        out_shape=jax.ShapeDtypeStruct((slots, send, LANES), bf16),
+        in_specs=[VMEM] * 6,
+        out_specs=VMEM,
+        scratch_shapes=[pltpu.VMEM((slots * (send - tall), LANES), f32)],
         compiler_params=PARAMS,
         name="work",
-    )(moved, enter, outer, inner, factor, gather, limit, *(in_hbm(x) for x in small))
+    )(moved, enter, outer, inner, factor, gather)
     home = swap_over(homes, firsts(slots)[1])
     return pl.pallas_call(
         finish,

time: 33.2 us -> 33 us (level)
    pallas_call x1, Pallas kernels: 1.61 us -> 1.22 us  [body(): pl.pallas_call(work, out_shape=jax.ShapeDtypeStruct((slots, send, LANES),...]
where the time goes in v21:
time: 33 us; the launch traced here: 32.7 us
  blocking collectives  27.6 us (84%)
  Pallas kernels  3.85 us (12%)
  between operations  1.3 us (4%)
    all_to_all x2, blocking collectives, swap_over(): lax.all_to_all(x, 'shard', split_axis=0, concat_axis=0, tiled=True, axis_...  27.6 us
    pallas_call x1, Pallas kernels, body(): pl.pallas_call(pack, out_shape=(pltpu.VMEM((slots, height, LANES), bf16),...  1.79 us
    pallas_call x1, Pallas kernels, body(): pl.pallas_call(work, out_shape=jax.ShapeDtypeStruct((slots, send, LANES),...  1.22 us
    pallas_call x1, Pallas kernels, body(): pl.pallas_call(finish, out_shape=(jax.ShapeDtypeStruct(query_grads.shape,...  0.84 us

profile of v21, /device:TPU:0, one launch (start us, length us, event | category | flops | bytes accessed | tf_op | source)
XLA Modules:
  0.0 32.7 jit_solution(14746232692420266367)
XLA Ops:
  1.3 1.8 %pack.1 = (bf16[16,96,128]{2,1,0:T(8,128)(2,1)S(1)}, bf16[256,256]{1,0:T(8,128)(2,1)S(1)}, bf16[256,256]{1,0:T(8,128)(2,1)S(1)}, bf16[256,256]{1,0:T(8,128)(2,1)...) custom-call(s32[1]{0:T(128)S(6)} %copy.11.length_ref, ...), custom_call_target="tpu_custom_call" | custom-call | tf_op jit(solution)/shard_map/pack/pallas_call | solution.py:283
  3.1 16.7 %all_to_all.10.moved_ref = bf16[16,96,128]{2,1,0:T(8,128)(2,1)S(1)} all-to-all(bf16[16,96,128]{2,1,0:T(8,128)(2,1)S(1)} %get-tuple-element.10), channel_id=1, replica_groups={{10,11,12,13,14,15,0,1,2,3,4,5,6,7,8,9},{26,27,28,29,30,31,16,17,18,19,..., dimensions={0} | all-to-all | bytes 786432 | tf_op jit(solution)/shard_map/all_to_all | solution.py:270
  19.8 1.2 %work.1 = bf16[16,40,128]{2,1,0:T(8,128)(2,1)S(1)} custom-call(bf16[16,96,128]{2,1,0:T(8,128)(2,1)S(1)} %all_to_all.10.moved_ref, bf16[256,256]{1,0:T(8,128)(2,1)S(1)} %get-tuple-element.11.enter_ref, bf16[256,256]{1,0:T(8,128)(2,1)S(1)} %get-tuple-element.12.outer_ref, bf16[256,256]{1,0:T(8,128)(2,1)S(1)} %get-tuple-element.13.inner_ref, ...), custom_call_target="tpu_custom_call" | custom-call | tf_op jit(solution)/shard_map/work/pallas_call | solution.py:303
  21.0 10.9 %all_to_all.11.home_ref = bf16[16,40,128]{2,1,0:T(8,128)(2,1)S(1)} all-to-all(bf16[16,40,128]{2,1,0:T(8,128)(2,1)S(1)} %work.1), channel_id=1, replica_groups={{10,11,12,13,14,15,0,1,2,3,4,5,6,7,8,9},{26,27,28,29,30,31,16,17,18,19,..., dimensions={0} | all-to-all | bytes 327680 | tf_op jit(solution)/shard_map/all_to_all | solution.py:270
  31.9 0.8 %finish.1 = (bf16[1,16,4096]{2,1,0:T(8,128)(2,1)}, f32[1,384]{1,0:T(1,128)}) custom-call(bf16[16,40,128]{2,1,0:T(8,128)(2,1)S(1)} %all_to_all.11.home_ref, bf16[16,16]{1,0:T(8,128)(2,1)S(1)} %get-tuple-element.16.holds_ref, f32[32,384]{1,0:T(8,128)S(1)} %get-tuple-element.17.chosen_ref), custom_call_target="tpu_custom_call" | custom-call | tf_op jit(solution)/shard_map/finish/pallas_call | solution.py:313

commit v22 on v21

--- a/solution.py
+++ b/solution.py
@@ -25,7 +25,7 @@
 
 
 def order_of(slots, first):
-    return [(first + k) % slots for k in range(slots)]
+    return [(first - k) % slots for k in range(slots)]
 
 
 def firsts(slots):
@@ -54,9 +54,8 @@
 
 def holds(layer_row, modules, first):
     slots = layer_row.shape[1]
-    if first:
-        layer_row = jnp.concatenate([layer_row[:, first:], layer_row[:, :first]], axis=1)
-    return mask(iota((modules, slots), 0) == layer_row)
+    placed = mask(iota((slots, slots), 0) == (first + slots - iota((slots, slots), 1)) % slots)
+    return dot(mask(iota((modules, slots), 0) == layer_row), placed).astype(bf16)
 
 
 def block_bases(out_basis, in_basis, eigen):
@@ -147,7 +146,8 @@
     pairs = sources // 2
     stacks = pairs // 4
     arrive, leave = firsts(sources)
-    places = [(d - leave) % sources for d in order_of(sources, arrive)]
+    order = order_of(sources, arrive)
+    places = [order_of(sources, leave).index(d) for d in order]
     outer, inner, gather = outer_ref[...], inner_ref[...], gather_ref[...]
     factor = factor_ref[...]
 
@@ -195,7 +195,7 @@
         )
 
     cands = [
-        moved_ref[(d - arrive) % sources, (1 + c) * tall : (2 + c) * tall, :]
+        moved_ref[order.index(d), (1 + c) * tall : (2 + c) * tall, :]
         for d in range(sources)
         for c in range(per)
     ]

time: 33 us -> 32.5 us (0.985)
  blocking collectives: 27.6 us -> 27.1 us
    all_to_all x2, blocking collectives: 27.6 us -> 27.1 us  [swap_over(): lax.all_to_all(x, 'shard', split_axis=0, concat_axis=0, tiled=True, axis_...]
where the time goes in v22:
time: 32.5 us; the launch traced here: 32.2 us
  blocking collectives  27.1 us (83%)
  Pallas kernels  3.84 us (12%)
  between operations  1.3 us (4%)
    all_to_all x2, blocking collectives, swap_over(): lax.all_to_all(x, 'shard', split_axis=0, concat_axis=0, tiled=True, axis_...  27.1 us
    pallas_call x1, Pallas kernels, body(): pl.pallas_call(pack, out_shape=(pltpu.VMEM((slots, height, LANES), bf16),...  1.79 us
    pallas_call x1, Pallas kernels, body(): pl.pallas_call(work, out_shape=jax.ShapeDtypeStruct((slots, send, LANES),...  1.22 us
    pallas_call x1, Pallas kernels, body(): pl.pallas_call(finish, out_shape=(jax.ShapeDtypeStruct(query_grads.shape,...  0.83 us

profile of v22, /device:TPU:0, one launch (start us, length us, event | category | flops | bytes accessed | tf_op | source)
XLA Modules:
  0.0 32.2 jit_solution(7732438824040426440)
XLA Ops:
  1.3 1.8 %pack.1 = (bf16[16,96,128]{2,1,0:T(8,128)(2,1)S(1)}, bf16[256,256]{1,0:T(8,128)(2,1)S(1)}, bf16[256,256]{1,0:T(8,128)(2,1)S(1)}, bf16[256,256]{1,0:T(8,128)(2,1)...) custom-call(s32[1]{0:T(128)S(6)} %copy.11.length_ref, ...), custom_call_target="tpu_custom_call" | custom-call | tf_op jit(solution)/shard_map/pack/pallas_call | solution.py:283
  3.1 17.5 %all_to_all.10.moved_ref = bf16[16,96,128]{2,1,0:T(8,128)(2,1)S(1)} all-to-all(bf16[16,96,128]{2,1,0:T(8,128)(2,1)S(1)} %get-tuple-element.10), channel_id=1, replica_groups={{10,9,8,7,6,5,4,3,2,1,0,15,14,13,12,11},{26,25,24,23,22,21,20,19,18,17,..., dimensions={0} | all-to-all | bytes 786432 | tf_op jit(solution)/shard_map/all_to_all | solution.py:270
  20.5 1.2 %work.1 = bf16[16,40,128]{2,1,0:T(8,128)(2,1)S(1)} custom-call(bf16[16,96,128]{2,1,0:T(8,128)(2,1)S(1)} %all_to_all.10.moved_ref, bf16[256,256]{1,0:T(8,128)(2,1)S(1)} %get-tuple-element.11.enter_ref, bf16[256,256]{1,0:T(8,128)(2,1)S(1)} %get-tuple-element.12.outer_ref, bf16[256,256]{1,0:T(8,128)(2,1)S(1)} %get-tuple-element.13.inner_ref, ...), custom_call_target="tpu_custom_call" | custom-call | tf_op jit(solution)/shard_map/work/pallas_call | solution.py:303
  21.8 9.6 %all_to_all.11.home_ref = bf16[16,40,128]{2,1,0:T(8,128)(2,1)S(1)} all-to-all(bf16[16,40,128]{2,1,0:T(8,128)(2,1)S(1)} %work.1), channel_id=1, replica_groups={{10,9,8,7,6,5,4,3,2,1,0,15,14,13,12,11},{26,25,24,23,22,21,20,19,18,17,..., dimensions={0} | all-to-all | bytes 327680 | tf_op jit(solution)/shard_map/all_to_all | solution.py:270
  31.4 0.8 %finish.1 = (bf16[1,16,4096]{2,1,0:T(8,128)(2,1)}, f32[1,384]{1,0:T(1,128)}) custom-call(bf16[16,40,128]{2,1,0:T(8,128)(2,1)S(1)} %all_to_all.11.home_ref, bf16[16,16]{1,0:T(8,128)(2,1)S(1)} %get-tuple-element.16.holds_ref, f32[32,384]{1,0:T(8,128)S(1)} %get-tuple-element.17.chosen_ref), custom_call_target="tpu_custom_call" | custom-call | tf_op jit(solution)/shard_map/finish/pallas_call | solution.py:313

commit v23 on v22

--- a/solution.py
+++ b/solution.py
@@ -29,7 +29,7 @@
 
 
 def firsts(slots):
-    return slots * 5 // 8, slots * 5 // 8
+    return slots * 5 // 8, slots // 2
 
 
 def gather_rows(tall):

time: 32.5 us -> 32.9 us (1.012)
    all_to_all x2, blocking collectives: 27.1 us -> 27.4 us  [swap_over(): lax.all_to_all(x, 'shard', split_axis=0, concat_axis=0, tiled=True, axis_...]
where the time goes in v23:
time: 32.9 us; the launch traced here: 32.6 us
  blocking collectives  27.4 us (83%)
  Pallas kernels  3.86 us (12%)
  between operations  1.3 us (4%)
    all_to_all x2, blocking collectives, swap_over(): lax.all_to_all(x, 'shard', split_axis=0, concat_axis=0, tiled=True, axis_...  27.4 us
    pallas_call x1, Pallas kernels, body(): pl.pallas_call(pack, out_shape=(pltpu.VMEM((slots, height, LANES), bf16),...  1.8 us
    pallas_call x1, Pallas kernels, body(): pl.pallas_call(work, out_shape=jax.ShapeDtypeStruct((slots, send, LANES),...  1.23 us
    pallas_call x1, Pallas kernels, body(): pl.pallas_call(finish, out_shape=(jax.ShapeDtypeStruct(query_grads.shape,...  0.84 us

profile of v23, /device:TPU:0, one launch (start us, length us, event | category | flops | bytes accessed | tf_op | source)
XLA Modules:
  0.0 32.6 jit_solution(15776680168222790719)
XLA Ops:
  1.3 1.8 %pack.1 = (bf16[16,96,128]{2,1,0:T(8,128)(2,1)S(1)}, bf16[256,256]{1,0:T(8,128)(2,1)S(1)}, bf16[256,256]{1,0:T(8,128)(2,1)S(1)}, bf16[256,256]{1,0:T(8,128)(2,1)...) custom-call(s32[1]{0:T(128)S(6)} %copy.11.length_ref, ...), custom_call_target="tpu_custom_call" | custom-call | tf_op jit(solution)/shard_map/pack/pallas_call | solution.py:283
  3.1 17.5 %all_to_all.10.moved_ref = bf16[16,96,128]{2,1,0:T(8,128)(2,1)S(1)} all-to-all(bf16[16,96,128]{2,1,0:T(8,128)(2,1)S(1)} %get-tuple-element.10), channel_id=1, replica_groups={{10,9,8,7,6,5,4,3,2,1,0,15,14,13,12,11},{26,25,24,23,22,21,20,19,18,17,..., dimensions={0} | all-to-all | bytes 786432 | tf_op jit(solution)/shard_map/all_to_all | solution.py:270
  20.5 1.2 %work.1 = bf16[16,40,128]{2,1,0:T(8,128)(2,1)S(1)} custom-call(bf16[16,96,128]{2,1,0:T(8,128)(2,1)S(1)} %all_to_all.10.moved_ref, bf16[256,256]{1,0:T(8,128)(2,1)S(1)} %get-tuple-element.11.enter_ref, bf16[256,256]{1,0:T(8,128)(2,1)S(1)} %get-tuple-element.12.outer_ref, bf16[256,256]{1,0:T(8,128)(2,1)S(1)} %get-tuple-element.13.inner_ref, ...), custom_call_target="tpu_custom_call" | custom-call | tf_op jit(solution)/shard_map/work/pallas_call | solution.py:303
  21.8 10.0 %all_to_all.11.home_ref = bf16[16,40,128]{2,1,0:T(8,128)(2,1)S(1)} all-to-all(bf16[16,40,128]{2,1,0:T(8,128)(2,1)S(1)} %work.1), channel_id=1, replica_groups={{8,7,6,5,4,3,2,1,0,15,14,13,12,11,10,9},{24,23,22,21,20,19,18,17,16,31,..., dimensions={0} | all-to-all | bytes 327680 | tf_op jit(solution)/shard_map/all_to_all | solution.py:270
  31.8 0.8 %finish.1 = (bf16[1,16,4096]{2,1,0:T(8,128)(2,1)}, f32[1,384]{1,0:T(1,128)}) custom-call(bf16[16,40,128]{2,1,0:T(8,128)(2,1)S(1)} %all_to_all.11.home_ref, bf16[16,16]{1,0:T(8,128)(2,1)S(1)} %get-tuple-element.16.holds_ref, f32[32,384]{1,0:T(8,128)S(1)} %get-tuple-element.17.chosen_ref), custom_call_target="tpu_custom_call" | custom-call | tf_op jit(solution)/shard_map/finish/pallas_call | solution.py:313

commit v24 on v22

--- a/solution.py
+++ b/solution.py
@@ -24,8 +24,18 @@
     return condition.astype(f32).astype(bf16)
 
 
+def ring(place, slots):
+    core, middle = place % 2, slots // 2
+    up = 4 * (place // 2) + core
+    down = 2 * (middle - 1 - 2 * ((place - middle) // 2)) + core
+    if isinstance(place, int):
+        return up if place < middle else down
+    return jnp.where(place < middle, up, down)
+
+
 def order_of(slots, first):
-    return [(first - k) % slots for k in range(slots)]
+    start = [ring(k, slots) for k in range(slots)].index(first)
+    return [ring((start + k) % slots, slots) for k in range(slots)]
 
 
 def firsts(slots):
@@ -54,7 +64,8 @@
 
 def holds(layer_row, modules, first):
     slots = layer_row.shape[1]
-    placed = mask(iota((slots, slots), 0) == (first + slots - iota((slots, slots), 1)) % slots)
+    start = [ring(k, slots) for k in range(slots)].index(first)
+    placed = mask(iota((slots, slots), 0) == ring((start + iota((slots, slots), 1)) % slots, slots))
     return dot(mask(iota((modules, slots), 0) == layer_row), placed).astype(bf16)
 
 

time: 32.5 us -> 31.8 us (0.978)
  blocking collectives: 27.1 us -> 26.3 us
    all_to_all x2, blocking collectives: 27.1 us -> 26.3 us  [swap_over(): lax.all_to_all(x, 'shard', split_axis=0, concat_axis=0, tiled=True, axis_...]
where the time goes in v24:
time: 31.8 us; the launch traced here: 31.4 us
  blocking collectives  26.3 us (83%)
  Pallas kernels  3.85 us (12%)
  between operations  1.3 us (4%)
    all_to_all x2, blocking collectives, swap_over(): lax.all_to_all(x, 'shard', split_axis=0, concat_axis=0, tiled=True, axis_...  26.3 us
    pallas_call x1, Pallas kernels, body(): pl.pallas_call(pack, out_shape=(pltpu.VMEM((slots, height, LANES), bf16),...  1.79 us
    pallas_call x1, Pallas kernels, body(): pl.pallas_call(work, out_shape=jax.ShapeDtypeStruct((slots, send, LANES),...  1.22 us
    pallas_call x1, Pallas kernels, body(): pl.pallas_call(finish, out_shape=(jax.ShapeDtypeStruct(query_grads.shape,...  0.83 us

profile of v24, /device:TPU:0, one launch (start us, length us, event | category | flops | bytes accessed | tf_op | source)
XLA Modules:
  0.0 31.4 jit_solution(15151882021174334379)
XLA Ops:
  1.3 1.8 %pack.1 = (bf16[16,96,128]{2,1,0:T(8,128)(2,1)S(1)}, bf16[256,256]{1,0:T(8,128)(2,1)S(1)}, bf16[256,256]{1,0:T(8,128)(2,1)S(1)}, bf16[256,256]{1,0:T(8,128)(2,1)...) custom-call(s32[1]{0:T(128)S(6)} %copy.11.length_ref, ...), custom_call_target="tpu_custom_call" | custom-call | tf_op jit(solution)/shard_map/pack/pallas_call | solution.py:294
  3.1 16.8 %all_to_all.10.moved_ref = bf16[16,96,128]{2,1,0:T(8,128)(2,1)S(1)} all-to-all(bf16[16,96,128]{2,1,0:T(8,128)(2,1)S(1)} %get-tuple-element.10), channel_id=1, replica_groups={{10,11,6,7,2,3,0,1,4,5,8,9,12,13,14,15},{26,27,22,23,18,19,16,17,20,21,..., dimensions={0} | all-to-all | bytes 786432 | tf_op jit(solution)/shard_map/all_to_all | solution.py:281
  19.9 1.2 %work.1 = bf16[16,40,128]{2,1,0:T(8,128)(2,1)S(1)} custom-call(bf16[16,96,128]{2,1,0:T(8,128)(2,1)S(1)} %all_to_all.10.moved_ref, bf16[256,256]{1,0:T(8,128)(2,1)S(1)} %get-tuple-element.11.enter_ref, bf16[256,256]{1,0:T(8,128)(2,1)S(1)} %get-tuple-element.12.outer_ref, bf16[256,256]{1,0:T(8,128)(2,1)S(1)} %get-tuple-element.13.inner_ref, ...), custom_call_target="tpu_custom_call" | custom-call | tf_op jit(solution)/shard_map/work/pallas_call | solution.py:314
  21.1 9.5 %all_to_all.11.home_ref = bf16[16,40,128]{2,1,0:T(8,128)(2,1)S(1)} all-to-all(bf16[16,40,128]{2,1,0:T(8,128)(2,1)S(1)} %work.1), channel_id=1, replica_groups={{10,11,6,7,2,3,0,1,4,5,8,9,12,13,14,15},{26,27,22,23,18,19,16,17,20,21,..., dimensions={0} | all-to-all | bytes 327680 | tf_op jit(solution)/shard_map/all_to_all | solution.py:281
  30.6 0.8 %finish.1 = (bf16[1,16,4096]{2,1,0:T(8,128)(2,1)}, f32[1,384]{1,0:T(1,128)}) custom-call(bf16[16,40,128]{2,1,0:T(8,128)(2,1)S(1)} %all_to_all.11.home_ref, bf16[16,16]{1,0:T(8,128)(2,1)S(1)} %get-tuple-element.16.holds_ref, f32[32,384]{1,0:T(8,128)S(1)} %get-tuple-element.17.chosen_ref), custom_call_target="tpu_custom_call" | custom-call | tf_op jit(solution)/shard_map/finish/pallas_call | solution.py:324

commit v25 on v24

--- a/solution.py
+++ b/solution.py
@@ -9,6 +9,7 @@
 LANES = 128
 SUBLANES = 8
 PIECES = 3
+STRIDE = 7
 f32, bf16 = jnp.float32, jnp.bfloat16
 
 
@@ -35,7 +36,7 @@
 
 def order_of(slots, first):
     start = [ring(k, slots) for k in range(slots)].index(first)
-    return [ring((start + k) % slots, slots) for k in range(slots)]
+    return [ring((start + STRIDE * k) % slots, slots) for k in range(slots)]
 
 
 def firsts(slots):
@@ -65,7 +66,7 @@
 def holds(layer_row, modules, first):
     slots = layer_row.shape[1]
     start = [ring(k, slots) for k in range(slots)].index(first)
-    placed = mask(iota((slots, slots), 0) == ring((start + iota((slots, slots), 1)) % slots, slots))
+    placed = mask(iota((slots, slots), 0) == ring((start + STRIDE * iota((slots, slots), 1)) % slots, slots))
     return dot(mask(iota((modules, slots), 0) == layer_row), placed).astype(bf16)
 
 

time: 31.8 us -> 31.9 us (level)
  no operation moved by 1% of the time
where the time goes in v25:
time: 31.9 us; the launch traced here: 31.6 us
  blocking collectives  26.5 us (83%)
  Pallas kernels  3.84 us (12%)
  between operations  1.3 us (4%)
    all_to_all x2, blocking collectives, swap_over(): lax.all_to_all(x, 'shard', split_axis=0, concat_axis=0, tiled=True, axis_...  26.5 us
    pallas_call x1, Pallas kernels, body(): pl.pallas_call(pack, out_shape=(pltpu.VMEM((slots, height, LANES), bf16),...  1.79 us
    pallas_call x1, Pallas kernels, body(): pl.pallas_call(work, out_shape=jax.ShapeDtypeStruct((slots, send, LANES),...  1.22 us
    pallas_call x1, Pallas kernels, body(): pl.pallas_call(finish, out_shape=(jax.ShapeDtypeStruct(query_grads.shape,...  0.83 us

profile of v25, /device:TPU:0, one launch (start us, length us, event | category | flops | bytes accessed | tf_op | source)
XLA Modules:
  0.0 31.6 jit_solution(18266659710709042125)
XLA Ops:
  1.3 1.8 %pack.1 = (bf16[16,96,128]{2,1,0:T(8,128)(2,1)S(1)}, bf16[256,256]{1,0:T(8,128)(2,1)S(1)}, bf16[256,256]{1,0:T(8,128)(2,1)S(1)}, bf16[256,256]{1,0:T(8,128)(2,1)...) custom-call(s32[1]{0:T(128)S(6)} %copy.11.length_ref, ...), custom_call_target="tpu_custom_call" | custom-call | tf_op jit(solution)/shard_map/pack/pallas_call | solution.py:295
  3.1 16.0 %all_to_all.10.moved_ref = bf16[16,96,128]{2,1,0:T(8,128)(2,1)S(1)} all-to-all(bf16[16,96,128]{2,1,0:T(8,128)(2,1)S(1)} %get-tuple-element.10), channel_id=1, replica_groups={{10,1,14,3,12,7,8,11,4,15,0,13,2,9,6,5},{26,17,30,19,28,23,24,27,20,31,..., dimensions={0} | all-to-all | bytes 786432 | tf_op jit(solution)/shard_map/all_to_all | solution.py:282
  19.1 1.2 %work.1 = bf16[16,40,128]{2,1,0:T(8,128)(2,1)S(1)} custom-call(bf16[16,96,128]{2,1,0:T(8,128)(2,1)S(1)} %all_to_all.10.moved_ref, bf16[256,256]{1,0:T(8,128)(2,1)S(1)} %get-tuple-element.11.enter_ref, bf16[256,256]{1,0:T(8,128)(2,1)S(1)} %get-tuple-element.12.outer_ref, bf16[256,256]{1,0:T(8,128)(2,1)S(1)} %get-tuple-element.13.inner_ref, ...), custom_call_target="tpu_custom_call" | custom-call | tf_op jit(solution)/shard_map/work/pallas_call | solution.py:315
  20.3 10.5 %all_to_all.11.home_ref = bf16[16,40,128]{2,1,0:T(8,128)(2,1)S(1)} all-to-all(bf16[16,40,128]{2,1,0:T(8,128)(2,1)S(1)} %work.1), channel_id=1, replica_groups={{10,1,14,3,12,7,8,11,4,15,0,13,2,9,6,5},{26,17,30,19,28,23,24,27,20,31,..., dimensions={0} | all-to-all | bytes 327680 | tf_op jit(solution)/shard_map/all_to_all | solution.py:282
  30.8 0.8 %finish.1 = (bf16[1,16,4096]{2,1,0:T(8,128)(2,1)}, f32[1,384]{1,0:T(1,128)}) custom-call(bf16[16,40,128]{2,1,0:T(8,128)(2,1)S(1)} %all_to_all.11.home_ref, bf16[16,16]{1,0:T(8,128)(2,1)S(1)} %get-tuple-element.16.holds_ref, f32[32,384]{1,0:T(8,128)S(1)} %get-tuple-element.17.chosen_ref), custom_call_target="tpu_custom_call" | custom-call | tf_op jit(solution)/shard_map/finish/pallas_call | solution.py:325

commit v26 on v24

--- a/solution.py
+++ b/solution.py
@@ -33,13 +33,13 @@
     return jnp.where(place < middle, up, down)
 
 
-def order_of(slots, first):
+def order_of(slots, first, stride):
     start = [ring(k, slots) for k in range(slots)].index(first)
-    return [ring((start + k) % slots, slots) for k in range(slots)]
-
-
-def firsts(slots):
-    return slots * 5 // 8, slots * 5 // 8
+    return [ring((start + stride * k) % slots, slots) for k in range(slots)]
+
+
+def orders(slots):
+    return (slots * 5 // 8, 7), (slots * 5 // 8, 1)
 
 
 def gather_rows(tall):
@@ -62,10 +62,10 @@
     return half(top, swap(low)), half(swap(top), low)
 
 
-def holds(layer_row, modules, first):
+def holds(layer_row, modules, first, stride):
     slots = layer_row.shape[1]
     start = [ring(k, slots) for k in range(slots)].index(first)
-    placed = mask(iota((slots, slots), 0) == ring((start + iota((slots, slots), 1)) % slots, slots))
+    placed = mask(iota((slots, slots), 0) == ring((start + stride * iota((slots, slots), 1)) % slots, slots))
     return dot(mask(iota((modules, slots), 0) == layer_row), placed).astype(bf16)
 
 
@@ -119,8 +119,8 @@
     gather_ref[...] = gather_rows(tall)
     for arrival in arrivals[2:]:
         arrival.wait()
-    one_hot = holds(layer_ref[...], modules, firsts(slots)[0])
-    holds_ref[...] = holds(layer_ref[...], modules, firsts(slots)[1])
+    one_hot = holds(layer_ref[...], modules, *orders(slots)[0])
+    holds_ref[...] = holds(layer_ref[...], modules, *orders(slots)[1])
     enter_ref[...], outer_ref[...], inner_ref[...], factor_ref[...] = block_bases(
         out_basis_ref[...], in_basis_ref[...], eigen_ref[...]
     )
@@ -156,9 +156,8 @@
     count = sources * per
     pairs = sources // 2
     stacks = pairs // 4
-    arrive, leave = firsts(sources)
-    order = order_of(sources, arrive)
-    places = [order_of(sources, leave).index(d) for d in order]
+    order, later = (order_of(sources, *each) for each in orders(sources))
+    places = [later.index(d) for d in order]
     outer, inner, gather = outer_ref[...], inner_ref[...], gather_ref[...]
     factor = factor_ref[...]
 
@@ -276,8 +275,8 @@
     def in_hbm(x):
         return pltpu.with_memory_space_constraint(x, pltpu.HBM)
 
-    def swap_over(x, first):
-        groups = [order_of(slots, first)]
+    def swap_over(x, first, stride):
+        groups = [order_of(slots, first, stride)]
         return lax.all_to_all(x, "shard", split_axis=0, concat_axis=0, tiled=True, axis_index_groups=groups)
 
     square = pltpu.VMEM((size, size), bf16)
@@ -310,7 +309,7 @@
         compiler_params=PARAMS,
         name="pack",
     )(list_lengths, *(in_hbm(x) for x in operands))
-    moved = swap_over(packed, firsts(slots)[0])
+    moved = swap_over(packed, *orders(slots)[0])
     homes = pl.pallas_call(
         work,
         out_shape=jax.ShapeDtypeStruct((slots, send, LANES), bf16),
@@ -320,7 +319,7 @@
         compiler_params=PARAMS,
         name="work",
     )(moved, enter, outer, inner, factor, gather)
-    home = swap_over(homes, firsts(slots)[1])
+    home = swap_over(homes, *orders(slots)[1])
     return pl.pallas_call(
         finish,
         out_shape=(

time: 31.8 us -> 31.7 us (level)
  no operation moved by 1% of the time
where the time goes in v26:
time: 31.7 us; the launch traced here: 31.4 us
  blocking collectives  26.2 us (83%)
  Pallas kernels  3.87 us (12%)
  between operations  1.3 us (4%)
    all_to_all x2, blocking collectives, swap_over(): lax.all_to_all(x, 'shard', split_axis=0, concat_axis=0, tiled=True, axis_...  26.2 us
    pallas_call x1, Pallas kernels, body(): pl.pallas_call(pack, out_shape=(pltpu.VMEM((slots, height, LANES), bf16),...  1.81 us
    pallas_call x1, Pallas kernels, body(): pl.pallas_call(work, out_shape=jax.ShapeDtypeStruct((slots, send, LANES),...  1.22 us
    pallas_call x1, Pallas kernels, body(): pl.pallas_call(finish, out_shape=(jax.ShapeDtypeStruct(query_grads.shape,...  0.83 us

profile of v26, /device:TPU:0, one launch (start us, length us, event | category | flops | bytes accessed | tf_op | source)
XLA Modules:
  0.0 31.4 jit_solution(17648834230714367317)
XLA Ops:
  1.3 1.8 %pack.1 = (bf16[16,96,128]{2,1,0:T(8,128)(2,1)S(1)}, bf16[256,256]{1,0:T(8,128)(2,1)S(1)}, bf16[256,256]{1,0:T(8,128)(2,1)S(1)}, bf16[256,256]{1,0:T(8,128)(2,1)...) custom-call(s32[1]{0:T(128)S(6)} %copy.11.length_ref, ...), custom_call_target="tpu_custom_call" | custom-call | tf_op jit(solution)/shard_map/pack/pallas_call | solution.py:293
  3.1 16.0 %all_to_all.10.moved_ref = bf16[16,96,128]{2,1,0:T(8,128)(2,1)S(1)} all-to-all(bf16[16,96,128]{2,1,0:T(8,128)(2,1)S(1)} %get-tuple-element.10), channel_id=1, replica_groups={{10,1,14,3,12,7,8,11,4,15,0,13,2,9,6,5},{26,17,30,19,28,23,24,27,20,31,..., dimensions={0} | all-to-all | bytes 786432 | tf_op jit(solution)/shard_map/all_to_all | solution.py:280
  19.1 1.2 %work.1 = bf16[16,40,128]{2,1,0:T(8,128)(2,1)S(1)} custom-call(bf16[16,96,128]{2,1,0:T(8,128)(2,1)S(1)} %all_to_all.10.moved_ref, bf16[256,256]{1,0:T(8,128)(2,1)S(1)} %get-tuple-element.11.enter_ref, bf16[256,256]{1,0:T(8,128)(2,1)S(1)} %get-tuple-element.12.outer_ref, bf16[256,256]{1,0:T(8,128)(2,1)S(1)} %get-tuple-element.13.inner_ref, ...), custom_call_target="tpu_custom_call" | custom-call | tf_op jit(solution)/shard_map/work/pallas_call | solution.py:313
  20.3 10.2 %all_to_all.11.home_ref = bf16[16,40,128]{2,1,0:T(8,128)(2,1)S(1)} all-to-all(bf16[16,40,128]{2,1,0:T(8,128)(2,1)S(1)} %work.1), channel_id=1, replica_groups={{10,11,6,7,2,3,0,1,4,5,8,9,12,13,14,15},{26,27,22,23,18,19,16,17,20,21,..., dimensions={0} | all-to-all | bytes 327680 | tf_op jit(solution)/shard_map/all_to_all | solution.py:280
  30.6 0.8 %finish.1 = (bf16[1,16,4096]{2,1,0:T(8,128)(2,1)}, f32[1,384]{1,0:T(1,128)}) custom-call(bf16[16,40,128]{2,1,0:T(8,128)(2,1)S(1)} %all_to_all.11.home_ref, bf16[16,16]{1,0:T(8,128)(2,1)S(1)} %get-tuple-element.16.holds_ref, f32[32,384]{1,0:T(8,128)S(1)} %get-tuple-element.17.chosen_ref), custom_call_target="tpu_custom_call" | custom-call | tf_op jit(solution)/shard_map/finish/pallas_call | solution.py:323

commit v27 on v26

--- a/solution.py
+++ b/solution.py
@@ -39,7 +39,7 @@
 
 
 def orders(slots):
-    return (slots * 5 // 8, 7), (slots * 5 // 8, 1)
+    return (slots * 5 // 8, 3), (slots * 5 // 8, slots - 1)
 
 
 def gather_rows(tall):

time: 31.7 us -> 32.4 us (1.022)
  blocking collectives: 26.2 us -> 26.8 us
    all_to_all x2, blocking collectives: 26.2 us -> 26.8 us  [swap_over(): lax.all_to_all(x, 'shard', split_axis=0, concat_axis=0, tiled=True, axis_...]
where the time goes in v27:
time: 32.4 us; the launch traced here: 31.9 us
  blocking collectives  26.8 us (83%)
  Pallas kernels  3.87 us (12%)
  between operations  1.3 us (4%)
    all_to_all x2, blocking collectives, swap_over(): lax.all_to_all(x, 'shard', split_axis=0, concat_axis=0, tiled=True, axis_...  26.8 us
    pallas_call x1, Pallas kernels, body(): pl.pallas_call(pack, out_shape=(pltpu.VMEM((slots, height, LANES), bf16),...  1.81 us
    pallas_call x1, Pallas kernels, body(): pl.pallas_call(work, out_shape=jax.ShapeDtypeStruct((slots, send, LANES),...  1.22 us
    pallas_call x1, Pallas kernels, body(): pl.pallas_call(finish, out_shape=(jax.ShapeDtypeStruct(query_grads.shape,...  0.83 us

profile of v27, /device:TPU:0, one launch (start us, length us, event | category | flops | bytes accessed | tf_op | source)
XLA Modules:
  0.0 31.9 jit_solution(12398411043820772889)
XLA Ops:
  1.3 1.8 %pack.1 = (bf16[16,96,128]{2,1,0:T(8,128)(2,1)S(1)}, bf16[256,256]{1,0:T(8,128)(2,1)S(1)}, bf16[256,256]{1,0:T(8,128)(2,1)S(1)}, bf16[256,256]{1,0:T(8,128)(2,1)...) custom-call(s32[1]{0:T(128)S(6)} %copy.11.length_ref, ...), custom_call_target="tpu_custom_call" | custom-call | tf_op jit(solution)/shard_map/pack/pallas_call | solution.py:293
  3.1 17.6 %all_to_all.10.moved_ref = bf16[16,96,128]{2,1,0:T(8,128)(2,1)S(1)} all-to-all(bf16[16,96,128]{2,1,0:T(8,128)(2,1)S(1)} %get-tuple-element.10), channel_id=1, replica_groups={{10,7,0,5,12,15,6,3,4,9,14,11,2,1,8,13},{26,23,16,21,28,31,22,19,20,25,..., dimensions={0} | all-to-all | bytes 786432 | tf_op jit(solution)/shard_map/all_to_all | solution.py:280
  20.7 1.2 %work.1 = bf16[16,40,128]{2,1,0:T(8,128)(2,1)S(1)} custom-call(bf16[16,96,128]{2,1,0:T(8,128)(2,1)S(1)} %all_to_all.10.moved_ref, bf16[256,256]{1,0:T(8,128)(2,1)S(1)} %get-tuple-element.11.enter_ref, bf16[256,256]{1,0:T(8,128)(2,1)S(1)} %get-tuple-element.12.outer_ref, bf16[256,256]{1,0:T(8,128)(2,1)S(1)} %get-tuple-element.13.inner_ref, ...), custom_call_target="tpu_custom_call" | custom-call | tf_op jit(solution)/shard_map/work/pallas_call | solution.py:313
  22.0 9.1 %all_to_all.11.home_ref = bf16[16,40,128]{2,1,0:T(8,128)(2,1)S(1)} all-to-all(bf16[16,40,128]{2,1,0:T(8,128)(2,1)S(1)} %work.1), channel_id=1, replica_groups={{10,15,14,13,12,9,8,5,4,1,0,3,2,7,6,11},{26,31,30,29,28,25,24,21,20,17,..., dimensions={0} | all-to-all | bytes 327680 | tf_op jit(solution)/shard_map/all_to_all | solution.py:280
  31.1 0.8 %finish.1 = (bf16[1,16,4096]{2,1,0:T(8,128)(2,1)}, f32[1,384]{1,0:T(1,128)}) custom-call(bf16[16,40,128]{2,1,0:T(8,128)(2,1)S(1)} %all_to_all.11.home_ref, bf16[16,16]{1,0:T(8,128)(2,1)S(1)} %get-tuple-element.16.holds_ref, f32[32,384]{1,0:T(8,128)S(1)} %get-tuple-element.17.chosen_ref), custom_call_target="tpu_custom_call" | custom-call | tf_op jit(solution)/shard_map/finish/pallas_call | solution.py:323

commit v28 on v27

--- a/solution.py
+++ b/solution.py
@@ -39,7 +39,7 @@
 
 
 def orders(slots):
-    return (slots * 5 // 8, 3), (slots * 5 // 8, slots - 1)
+    return (slots * 5 // 8, 7), (slots * 5 // 8, slots - 1)
 
 
 def gather_rows(tall):

time: 32.4 us -> 31.6 us (0.975)
  blocking collectives: 26.8 us -> 25.9 us
    all_to_all x2, blocking collectives: 26.8 us -> 25.9 us  [swap_over(): lax.all_to_all(x, 'shard', split_axis=0, concat_axis=0, tiled=True, axis_...]
where the time goes in v28:
time: 31.6 us; the launch traced here: 31.1 us
  blocking collectives  25.9 us (82%)
  Pallas kernels  3.87 us (12%)
  between operations  1.3 us (4%)
    all_to_all x2, blocking collectives, swap_over(): lax.all_to_all(x, 'shard', split_axis=0, concat_axis=0, tiled=True, axis_...  25.9 us
    pallas_call x1, Pallas kernels, body(): pl.pallas_call(pack, out_shape=(pltpu.VMEM((slots, height, LANES), bf16),...  1.81 us
    pallas_call x1, Pallas kernels, body(): pl.pallas_call(work, out_shape=jax.ShapeDtypeStruct((slots, send, LANES),...  1.22 us
    pallas_call x1, Pallas kernels, body(): pl.pallas_call(finish, out_shape=(jax.ShapeDtypeStruct(query_grads.shape,...  0.83 us

profile of v28, /device:TPU:0, one launch (start us, length us, event | category | flops | bytes accessed | tf_op | source)
XLA Modules:
  0.0 31.1 jit_solution(6664127679843218686)
XLA Ops:
  1.3 1.8 %pack.1 = (bf16[16,96,128]{2,1,0:T(8,128)(2,1)S(1)}, bf16[256,256]{1,0:T(8,128)(2,1)S(1)}, bf16[256,256]{1,0:T(8,128)(2,1)S(1)}, bf16[256,256]{1,0:T(8,128)(2,1)...) custom-call(s32[1]{0:T(128)S(6)} %copy.11.length_ref, ...), custom_call_target="tpu_custom_call" | custom-call | tf_op jit(solution)/shard_map/pack/pallas_call | solution.py:293
  3.1 16.0 %all_to_all.10.moved_ref = bf16[16,96,128]{2,1,0:T(8,128)(2,1)S(1)} all-to-all(bf16[16,96,128]{2,1,0:T(8,128)(2,1)S(1)} %get-tuple-element.10), channel_id=1, replica_groups={{10,1,14,3,12,7,8,11,4,15,0,13,2,9,6,5},{26,17,30,19,28,23,24,27,20,31,..., dimensions={0} | all-to-all | bytes 786432 | tf_op jit(solution)/shard_map/all_to_all | solution.py:280
  19.1 1.2 %work.1 = bf16[16,40,128]{2,1,0:T(8,128)(2,1)S(1)} custom-call(bf16[16,96,128]{2,1,0:T(8,128)(2,1)S(1)} %all_to_all.10.moved_ref, bf16[256,256]{1,0:T(8,128)(2,1)S(1)} %get-tuple-element.11.enter_ref, bf16[256,256]{1,0:T(8,128)(2,1)S(1)} %get-tuple-element.12.outer_ref, bf16[256,256]{1,0:T(8,128)(2,1)S(1)} %get-tuple-element.13.inner_ref, ...), custom_call_target="tpu_custom_call" | custom-call | tf_op jit(solution)/shard_map/work/pallas_call | solution.py:313
  20.3 9.9 %all_to_all.11.home_ref = bf16[16,40,128]{2,1,0:T(8,128)(2,1)S(1)} all-to-all(bf16[16,40,128]{2,1,0:T(8,128)(2,1)S(1)} %work.1), channel_id=1, replica_groups={{10,15,14,13,12,9,8,5,4,1,0,3,2,7,6,11},{26,31,30,29,28,25,24,21,20,17,..., dimensions={0} | all-to-all | bytes 327680 | tf_op jit(solution)/shard_map/all_to_all | solution.py:280
  30.2 0.8 %finish.1 = (bf16[1,16,4096]{2,1,0:T(8,128)(2,1)}, f32[1,384]{1,0:T(1,128)}) custom-call(bf16[16,40,128]{2,1,0:T(8,128)(2,1)S(1)} %all_to_all.11.home_ref, bf16[16,16]{1,0:T(8,128)(2,1)S(1)} %get-tuple-element.16.holds_ref, f32[32,384]{1,0:T(8,128)S(1)} %get-tuple-element.17.chosen_ref), custom_call_target="tpu_custom_call" | custom-call | tf_op jit(solution)/shard_map/finish/pallas_call | solution.py:323

commit v29 on v28

--- a/solution.py
+++ b/solution.py
@@ -39,7 +39,7 @@
 
 
 def orders(slots):
-    return (slots * 5 // 8, 7), (slots * 5 // 8, slots - 1)
+    return (slots * 5 // 8, slots - 7), (slots * 5 // 8, slots - 1)
 
 
 def gather_rows(tall):

time: 31.6 us -> 31.6 us (level)
  no operation moved by 1% of the time
where the time goes in v29:
time: 31.6 us; the launch traced here: 31.1 us
  blocking collectives  25.9 us (82%)
  Pallas kernels  3.87 us (12%)
  between operations  1.3 us (4%)
    all_to_all x2, blocking collectives, swap_over(): lax.all_to_all(x, 'shard', split_axis=0, concat_axis=0, tiled=True, axis_...  25.9 us
    pallas_call x1, Pallas kernels, body(): pl.pallas_call(pack, out_shape=(pltpu.VMEM((slots, height, LANES), bf16),...  1.81 us
    pallas_call x1, Pallas kernels, body(): pl.pallas_call(work, out_shape=jax.ShapeDtypeStruct((slots, send, LANES),...  1.23 us
    pallas_call x1, Pallas kernels, body(): pl.pallas_call(finish, out_shape=(jax.ShapeDtypeStruct(query_grads.shape,...  0.84 us

profile of v29, /device:TPU:0, one launch (start us, length us, event | category | flops | bytes accessed | tf_op | source)
XLA Modules:
  0.0 31.1 jit_solution(4405085095612042637)
XLA Ops:
  1.3 1.8 %pack.1 = (bf16[16,96,128]{2,1,0:T(8,128)(2,1)S(1)}, bf16[256,256]{1,0:T(8,128)(2,1)S(1)}, bf16[256,256]{1,0:T(8,128)(2,1)S(1)}, bf16[256,256]{1,0:T(8,128)(2,1)...) custom-call(s32[1]{0:T(128)S(6)} %copy.11.length_ref, ...), custom_call_target="tpu_custom_call" | custom-call | tf_op jit(solution)/shard_map/pack/pallas_call | solution.py:293
  3.1 16.4 %all_to_all.10.moved_ref = bf16[16,96,128]{2,1,0:T(8,128)(2,1)S(1)} all-to-all(bf16[16,96,128]{2,1,0:T(8,128)(2,1)S(1)} %get-tuple-element.10), channel_id=1, replica_groups={{10,5,6,9,2,13,0,15,4,11,8,7,12,3,14,1},{26,21,22,25,18,29,16,31,20,27,..., dimensions={0} | all-to-all | bytes 786432 | tf_op jit(solution)/shard_map/all_to_all | solution.py:280
  19.5 1.2 %work.1 = bf16[16,40,128]{2,1,0:T(8,128)(2,1)S(1)} custom-call(bf16[16,96,128]{2,1,0:T(8,128)(2,1)S(1)} %all_to_all.10.moved_ref, bf16[256,256]{1,0:T(8,128)(2,1)S(1)} %get-tuple-element.11.enter_ref, bf16[256,256]{1,0:T(8,128)(2,1)S(1)} %get-tuple-element.12.outer_ref, bf16[256,256]{1,0:T(8,128)(2,1)S(1)} %get-tuple-element.13.inner_ref, ...), custom_call_target="tpu_custom_call" | custom-call | tf_op jit(solution)/shard_map/work/pallas_call | solution.py:313
  20.7 9.5 %all_to_all.11.home_ref = bf16[16,40,128]{2,1,0:T(8,128)(2,1)S(1)} all-to-all(bf16[16,40,128]{2,1,0:T(8,128)(2,1)S(1)} %work.1), channel_id=1, replica_groups={{10,15,14,13,12,9,8,5,4,1,0,3,2,7,6,11},{26,31,30,29,28,25,24,21,20,17,..., dimensions={0} | all-to-all | bytes 327680 | tf_op jit(solution)/shard_map/all_to_all | solution.py:280
  30.3 0.8 %finish.1 = (bf16[1,16,4096]{2,1,0:T(8,128)(2,1)}, f32[1,384]{1,0:T(1,128)}) custom-call(bf16[16,40,128]{2,1,0:T(8,128)(2,1)S(1)} %all_to_all.11.home_ref, bf16[16,16]{1,0:T(8,128)(2,1)S(1)} %get-tuple-element.16.holds_ref, f32[32,384]{1,0:T(8,128)S(1)} %get-tuple-element.17.chosen_ref), custom_call_target="tpu_custom_call" | custom-call | tf_op jit(solution)/shard_map/finish/pallas_call | solution.py:323

commit v30 on v29

--- a/solution.py
+++ b/solution.py
@@ -39,7 +39,7 @@
 
 
 def orders(slots):
-    return (slots * 5 // 8, slots - 7), (slots * 5 // 8, slots - 1)
+    return (slots * 5 // 8, slots - 7), (slots // 2, slots - 1)
 
 
 def gather_rows(tall):

time: 31.6 us -> 32.5 us (1.028)
  blocking collectives: 25.9 us -> 26.8 us
    all_to_all x2, blocking collectives: 25.9 us -> 26.8 us  [swap_over(): lax.all_to_all(x, 'shard', split_axis=0, concat_axis=0, tiled=True, axis_...]
where the time goes in v30:
time: 32.5 us; the launch traced here: 32 us
  blocking collectives  26.8 us (82%)
  Pallas kernels  3.88 us (12%)
  between operations  1.3 us (4%)
    all_to_all x2, blocking collectives, swap_over(): lax.all_to_all(x, 'shard', split_axis=0, concat_axis=0, tiled=True, axis_...  26.8 us
    pallas_call x1, Pallas kernels, body(): pl.pallas_call(pack, out_shape=(pltpu.VMEM((slots, height, LANES), bf16),...  1.81 us
    pallas_call x1, Pallas kernels, body(): pl.pallas_call(work, out_shape=jax.ShapeDtypeStruct((slots, send, LANES),...  1.24 us
    pallas_call x1, Pallas kernels, body(): pl.pallas_call(finish, out_shape=(jax.ShapeDtypeStruct(query_grads.shape,...  0.84 us

profile of v30, /device:TPU:0, one launch (start us, length us, event | category | flops | bytes accessed | tf_op | source)
XLA Modules:
  0.0 32.0 jit_solution(11528938860366081921)
XLA Ops:
  1.3 1.8 %pack.1 = (bf16[16,96,128]{2,1,0:T(8,128)(2,1)S(1)}, bf16[256,256]{1,0:T(8,128)(2,1)S(1)}, bf16[256,256]{1,0:T(8,128)(2,1)S(1)}, bf16[256,256]{1,0:T(8,128)(2,1)...) custom-call(s32[1]{0:T(128)S(6)} %copy.11.length_ref, ...), custom_call_target="tpu_custom_call" | custom-call | tf_op jit(solution)/shard_map/pack/pallas_call | solution.py:293
  3.1 16.4 %all_to_all.10.moved_ref = bf16[16,96,128]{2,1,0:T(8,128)(2,1)S(1)} all-to-all(bf16[16,96,128]{2,1,0:T(8,128)(2,1)S(1)} %get-tuple-element.10), channel_id=1, replica_groups={{10,5,6,9,2,13,0,15,4,11,8,7,12,3,14,1},{26,21,22,25,18,29,16,31,20,27,..., dimensions={0} | all-to-all | bytes 786432 | tf_op jit(solution)/shard_map/all_to_all | solution.py:280
  19.5 1.2 %work.1 = bf16[16,40,128]{2,1,0:T(8,128)(2,1)S(1)} custom-call(bf16[16,96,128]{2,1,0:T(8,128)(2,1)S(1)} %all_to_all.10.moved_ref, bf16[256,256]{1,0:T(8,128)(2,1)S(1)} %get-tuple-element.11.enter_ref, bf16[256,256]{1,0:T(8,128)(2,1)S(1)} %get-tuple-element.12.outer_ref, bf16[256,256]{1,0:T(8,128)(2,1)S(1)} %get-tuple-element.13.inner_ref, ...), custom_call_target="tpu_custom_call" | custom-call | tf_op jit(solution)/shard_map/work/pallas_call | solution.py:313
  20.7 10.4 %all_to_all.11.home_ref = bf16[16,40,128]{2,1,0:T(8,128)(2,1)S(1)} all-to-all(bf16[16,40,128]{2,1,0:T(8,128)(2,1)S(1)} %work.1), channel_id=1, replica_groups={{8,5,4,1,0,3,2,7,6,11,10,15,14,13,12,9},{24,21,20,17,16,19,18,23,22,27,..., dimensions={0} | all-to-all | bytes 327680 | tf_op jit(solution)/shard_map/all_to_all | solution.py:280
  31.2 0.8 %finish.1 = (bf16[1,16,4096]{2,1,0:T(8,128)(2,1)}, f32[1,384]{1,0:T(1,128)}) custom-call(bf16[16,40,128]{2,1,0:T(8,128)(2,1)S(1)} %all_to_all.11.home_ref, bf16[16,16]{1,0:T(8,128)(2,1)S(1)} %get-tuple-element.16.holds_ref, f32[32,384]{1,0:T(8,128)S(1)} %get-tuple-element.17.chosen_ref), custom_call_target="tpu_custom_call" | custom-call | tf_op jit(solution)/shard_map/finish/pallas_call | solution.py:323

commit v31 on v30

--- a/solution.py
+++ b/solution.py
@@ -39,7 +39,7 @@
 
 
 def orders(slots):
-    return (slots * 5 // 8, slots - 7), (slots // 2, slots - 1)
+    return (slots * 5 // 8, slots - 7), (slots - 2, slots - 1)
 
 
 def gather_rows(tall):

time: 32.5 us -> 32.9 us (1.012)
  blocking collectives: 26.8 us -> 27.4 us
    all_to_all x2, blocking collectives: 26.8 us -> 27.4 us  [swap_over(): lax.all_to_all(x, 'shard', split_axis=0, concat_axis=0, tiled=True, axis_...]
where the time goes in v31:
time: 32.9 us; the launch traced here: 32.6 us
  blocking collectives  27.4 us (83%)
  Pallas kernels  3.88 us (12%)
  between operations  1.3 us (4%)
    all_to_all x2, blocking collectives, swap_over(): lax.all_to_all(x, 'shard', split_axis=0, concat_axis=0, tiled=True, axis_...  27.4 us
    pallas_call x1, Pallas kernels, body(): pl.pallas_call(pack, out_shape=(pltpu.VMEM((slots, height, LANES), bf16),...  1.81 us
    pallas_call x1, Pallas kernels, body(): pl.pallas_call(work, out_shape=jax.ShapeDtypeStruct((slots, send, LANES),...  1.24 us
    pallas_call x1, Pallas kernels, body(): pl.pallas_call(finish, out_shape=(jax.ShapeDtypeStruct(query_grads.shape,...  0.83 us

profile of v31, /device:TPU:0, one launch (start us, length us, event | category | flops | bytes accessed | tf_op | source)
XLA Modules:
  0.0 32.6 jit_solution(3523155464479855935)
XLA Ops:
  1.3 1.8 %pack.1 = (bf16[16,96,128]{2,1,0:T(8,128)(2,1)S(1)}, bf16[256,256]{1,0:T(8,128)(2,1)S(1)}, bf16[256,256]{1,0:T(8,128)(2,1)S(1)}, bf16[256,256]{1,0:T(8,128)(2,1)...) custom-call(s32[1]{0:T(128)S(6)} %copy.11.length_ref, ...), custom_call_target="tpu_custom_call" | custom-call | tf_op jit(solution)/shard_map/pack/pallas_call | solution.py:293
  3.1 16.4 %all_to_all.10.moved_ref = bf16[16,96,128]{2,1,0:T(8,128)(2,1)S(1)} all-to-all(bf16[16,96,128]{2,1,0:T(8,128)(2,1)S(1)} %get-tuple-element.10), channel_id=1, replica_groups={{10,5,6,9,2,13,0,15,4,11,8,7,12,3,14,1},{26,21,22,25,18,29,16,31,20,27,..., dimensions={0} | all-to-all | bytes 786432 | tf_op jit(solution)/shard_map/all_to_all | solution.py:280
  19.5 1.2 %work.1 = bf16[16,40,128]{2,1,0:T(8,128)(2,1)S(1)} custom-call(bf16[16,96,128]{2,1,0:T(8,128)(2,1)S(1)} %all_to_all.10.moved_ref, bf16[256,256]{1,0:T(8,128)(2,1)S(1)} %get-tuple-element.11.enter_ref, bf16[256,256]{1,0:T(8,128)(2,1)S(1)} %get-tuple-element.12.outer_ref, bf16[256,256]{1,0:T(8,128)(2,1)S(1)} %get-tuple-element.13.inner_ref, ...), custom_call_target="tpu_custom_call" | custom-call | tf_op jit(solution)/shard_map/work/pallas_call | solution.py:313
  20.7 11.0 %all_to_all.11.home_ref = bf16[16,40,128]{2,1,0:T(8,128)(2,1)S(1)} all-to-all(bf16[16,40,128]{2,1,0:T(8,128)(2,1)S(1)} %work.1), channel_id=1, replica_groups={{14,13,12,9,8,5,4,1,0,3,2,7,6,11,10,15},{30,29,28,25,24,21,20,17,16,19,..., dimensions={0} | all-to-all | bytes 327680 | tf_op jit(solution)/shard_map/all_to_all | solution.py:280
  31.8 0.8 %finish.1 = (bf16[1,16,4096]{2,1,0:T(8,128)(2,1)}, f32[1,384]{1,0:T(1,128)}) custom-call(bf16[16,40,128]{2,1,0:T(8,128)(2,1)S(1)} %all_to_all.11.home_ref, bf16[16,16]{1,0:T(8,128)(2,1)S(1)} %get-tuple-element.16.holds_ref, f32[32,384]{1,0:T(8,128)S(1)} %get-tuple-element.17.chosen_ref), custom_call_target="tpu_custom_call" | custom-call | tf_op jit(solution)/shard_map/finish/pallas_call | solution.py:323

commit v32 on v31

--- a/solution.py
+++ b/solution.py
@@ -39,7 +39,7 @@
 
 
 def orders(slots):
-    return (slots * 5 // 8, slots - 7), (slots - 2, slots - 1)
+    return (slots - 2, slots - 7), (slots * 5 // 8, slots - 1)
 
 
 def gather_rows(tall):

time: 32.9 us -> 32.4 us (0.985)
  blocking collectives: 27.4 us -> 26.7 us
    all_to_all x2, blocking collectives: 27.4 us -> 26.7 us  [swap_over(): lax.all_to_all(x, 'shard', split_axis=0, concat_axis=0, tiled=True, axis_...]
where the time goes in v32:
time: 32.4 us; the launch traced here: 31.9 us
  blocking collectives  26.7 us (82%)
  Pallas kernels  3.88 us (12%)
  between operations  1.3 us (4%)
    all_to_all x2, blocking collectives, swap_over(): lax.all_to_all(x, 'shard', split_axis=0, concat_axis=0, tiled=True, axis_...  26.7 us
    pallas_call x1, Pallas kernels, body(): pl.pallas_call(pack, out_shape=(pltpu.VMEM((slots, height, LANES), bf16),...  1.81 us
    pallas_call x1, Pallas kernels, body(): pl.pallas_call(work, out_shape=jax.ShapeDtypeStruct((slots, send, LANES),...  1.24 us
    pallas_call x1, Pallas kernels, body(): pl.pallas_call(finish, out_shape=(jax.ShapeDtypeStruct(query_grads.shape,...  0.84 us

profile of v32, /device:TPU:0, one launch (start us, length us, event | category | flops | bytes accessed | tf_op | source)
XLA Modules:
  0.0 31.9 jit_solution(12777331056247007452)
XLA Ops:
  1.3 1.8 %pack.1 = (bf16[16,96,128]{2,1,0:T(8,128)(2,1)S(1)}, bf16[256,256]{1,0:T(8,128)(2,1)S(1)}, bf16[256,256]{1,0:T(8,128)(2,1)S(1)}, bf16[256,256]{1,0:T(8,128)(2,1)...) custom-call(s32[1]{0:T(128)S(6)} %copy.11.length_ref, ...), custom_call_target="tpu_custom_call" | custom-call | tf_op jit(solution)/shard_map/pack/pallas_call | solution.py:293
  3.1 17.4 %all_to_all.10.moved_ref = bf16[16,96,128]{2,1,0:T(8,128)(2,1)S(1)} all-to-all(bf16[16,96,128]{2,1,0:T(8,128)(2,1)S(1)} %get-tuple-element.10), channel_id=1, replica_groups={{14,1,10,5,6,9,2,13,0,15,4,11,8,7,12,3},{30,17,26,21,22,25,18,29,16,31,..., dimensions={0} | all-to-all | bytes 786432 | tf_op jit(solution)/shard_map/all_to_all | solution.py:280
  20.5 1.2 %work.1 = bf16[16,40,128]{2,1,0:T(8,128)(2,1)S(1)} custom-call(bf16[16,96,128]{2,1,0:T(8,128)(2,1)S(1)} %all_to_all.10.moved_ref, bf16[256,256]{1,0:T(8,128)(2,1)S(1)} %get-tuple-element.11.enter_ref, bf16[256,256]{1,0:T(8,128)(2,1)S(1)} %get-tuple-element.12.outer_ref, bf16[256,256]{1,0:T(8,128)(2,1)S(1)} %get-tuple-element.13.inner_ref, ...), custom_call_target="tpu_custom_call" | custom-call | tf_op jit(solution)/shard_map/work/pallas_call | solution.py:313
  21.7 9.4 %all_to_all.11.home_ref = bf16[16,40,128]{2,1,0:T(8,128)(2,1)S(1)} all-to-all(bf16[16,40,128]{2,1,0:T(8,128)(2,1)S(1)} %work.1), channel_id=1, replica_groups={{10,15,14,13,12,9,8,5,4,1,0,3,2,7,6,11},{26,31,30,29,28,25,24,21,20,17,..., dimensions={0} | all-to-all | bytes 327680 | tf_op jit(solution)/shard_map/all_to_all | solution.py:280
  31.1 0.8 %finish.1 = (bf16[1,16,4096]{2,1,0:T(8,128)(2,1)}, f32[1,384]{1,0:T(1,128)}) custom-call(bf16[16,40,128]{2,1,0:T(8,128)(2,1)S(1)} %all_to_all.11.home_ref, bf16[16,16]{1,0:T(8,128)(2,1)S(1)} %get-tuple-element.16.holds_ref, f32[32,384]{1,0:T(8,128)S(1)} %get-tuple-element.17.chosen_ref), custom_call_target="tpu_custom_call" | custom-call | tf_op jit(solution)/shard_map/finish/pallas_call | solution.py:323

commit v33 on v32

--- a/solution.py
+++ b/solution.py
@@ -39,7 +39,7 @@
 
 
 def orders(slots):
-    return (slots - 2, slots - 7), (slots * 5 // 8, slots - 1)
+    return (slots // 2, slots - 7), (slots * 5 // 8, slots - 1)
 
 
 def gather_rows(tall):

time: 32.4 us -> 32.5 us (level)
  no operation moved by 1% of the time
where the time goes in v33:
time: 32.5 us; the launch traced here: 32 us
  blocking collectives  26.9 us (83%)
  Pallas kernels  3.88 us (12%)
  between operations  1.3 us (4%)
    all_to_all x2, blocking collectives, swap_over(): lax.all_to_all(x, 'shard', split_axis=0, concat_axis=0, tiled=True, axis_...  26.9 us
    pallas_call x1, Pallas kernels, body(): pl.pallas_call(pack, out_shape=(pltpu.VMEM((slots, height, LANES), bf16),...  1.81 us
    pallas_call x1, Pallas kernels, body(): pl.pallas_call(work, out_shape=jax.ShapeDtypeStruct((slots, send, LANES),...  1.24 us
    pallas_call x1, Pallas kernels, body(): pl.pallas_call(finish, out_shape=(jax.ShapeDtypeStruct(query_grads.shape,...  0.83 us

profile of v33, /device:TPU:0, one launch (start us, length us, event | category | flops | bytes accessed | tf_op | source)
XLA Modules:
  0.0 32.0 jit_solution(12287416254073616682)
XLA Ops:
  1.3 1.8 %pack.1 = (bf16[16,96,128]{2,1,0:T(8,128)(2,1)S(1)}, bf16[256,256]{1,0:T(8,128)(2,1)S(1)}, bf16[256,256]{1,0:T(8,128)(2,1)S(1)}, bf16[256,256]{1,0:T(8,128)(2,1)...) custom-call(s32[1]{0:T(128)S(6)} %copy.11.length_ref, ...), custom_call_target="tpu_custom_call" | custom-call | tf_op jit(solution)/shard_map/pack/pallas_call | solution.py:293
  3.1 16.9 %all_to_all.10.moved_ref = bf16[16,96,128]{2,1,0:T(8,128)(2,1)S(1)} all-to-all(bf16[16,96,128]{2,1,0:T(8,128)(2,1)S(1)} %get-tuple-element.10), channel_id=1, replica_groups={{8,7,12,3,14,1,10,5,6,9,2,13,0,15,4,11},{24,23,28,19,30,17,26,21,22,25,..., dimensions={0} | all-to-all | bytes 786432 | tf_op jit(solution)/shard_map/all_to_all | solution.py:280
  20.0 1.2 %work.1 = bf16[16,40,128]{2,1,0:T(8,128)(2,1)S(1)} custom-call(bf16[16,96,128]{2,1,0:T(8,128)(2,1)S(1)} %all_to_all.10.moved_ref, bf16[256,256]{1,0:T(8,128)(2,1)S(1)} %get-tuple-element.11.enter_ref, bf16[256,256]{1,0:T(8,128)(2,1)S(1)} %get-tuple-element.12.outer_ref, bf16[256,256]{1,0:T(8,128)(2,1)S(1)} %get-tuple-element.13.inner_ref, ...), custom_call_target="tpu_custom_call" | custom-call | tf_op jit(solution)/shard_map/work/pallas_call | solution.py:313
  21.2 10.0 %all_to_all.11.home_ref = bf16[16,40,128]{2,1,0:T(8,128)(2,1)S(1)} all-to-all(bf16[16,40,128]{2,1,0:T(8,128)(2,1)S(1)} %work.1), channel_id=1, replica_groups={{10,15,14,13,12,9,8,5,4,1,0,3,2,7,6,11},{26,31,30,29,28,25,24,21,20,17,..., dimensions={0} | all-to-all | bytes 327680 | tf_op jit(solution)/shard_map/all_to_all | solution.py:280
  31.2 0.8 %finish.1 = (bf16[1,16,4096]{2,1,0:T(8,128)(2,1)}, f32[1,384]{1,0:T(1,128)}) custom-call(bf16[16,40,128]{2,1,0:T(8,128)(2,1)S(1)} %all_to_all.11.home_ref, bf16[16,16]{1,0:T(8,128)(2,1)S(1)} %get-tuple-element.16.holds_ref, f32[32,384]{1,0:T(8,128)S(1)} %get-tuple-element.17.chosen_ref), custom_call_target="tpu_custom_call" | custom-call | tf_op jit(solution)/shard_map/finish/pallas_call | solution.py:323

commit v34 on v33

--- a/solution.py
+++ b/solution.py
@@ -39,7 +39,7 @@
 
 
 def orders(slots):
-    return (slots // 2, slots - 7), (slots * 5 // 8, slots - 1)
+    return (slots * 5 // 8, slots - 5), (slots * 5 // 8, slots - 1)
 
 
 def gather_rows(tall):

time: 32.5 us -> 32.5 us (level)
  no operation moved by 1% of the time
where the time goes in v34:
time: 32.5 us; the launch traced here: 32 us
  blocking collectives  26.8 us (82%)
  Pallas kernels  3.87 us (12%)
  between operations  1.3 us (4%)
    all_to_all x2, blocking collectives, swap_over(): lax.all_to_all(x, 'shard', split_axis=0, concat_axis=0, tiled=True, axis_...  26.8 us
    pallas_call x1, Pallas kernels, body(): pl.pallas_call(pack, out_shape=(pltpu.VMEM((slots, height, LANES), bf16),...  1.81 us
    pallas_call x1, Pallas kernels, body(): pl.pallas_call(work, out_shape=jax.ShapeDtypeStruct((slots, send, LANES),...  1.22 us
    pallas_call x1, Pallas kernels, body(): pl.pallas_call(finish, out_shape=(jax.ShapeDtypeStruct(query_grads.shape,...  0.83 us

profile of v34, /device:TPU:0, one launch (start us, length us, event | category | flops | bytes accessed | tf_op | source)
XLA Modules:
  0.0 32.0 jit_solution(13810133400336751865)
XLA Ops:
  1.3 1.8 %pack.1 = (bf16[16,96,128]{2,1,0:T(8,128)(2,1)S(1)}, bf16[256,256]{1,0:T(8,128)(2,1)S(1)}, bf16[256,256]{1,0:T(8,128)(2,1)S(1)}, bf16[256,256]{1,0:T(8,128)(2,1)...) custom-call(s32[1]{0:T(128)S(6)} %copy.11.length_ref, ...), custom_call_target="tpu_custom_call" | custom-call | tf_op jit(solution)/shard_map/pack/pallas_call | solution.py:293
  3.1 17.6 %all_to_all.10.moved_ref = bf16[16,96,128]{2,1,0:T(8,128)(2,1)S(1)} all-to-all(bf16[16,96,128]{2,1,0:T(8,128)(2,1)S(1)} %get-tuple-element.10), channel_id=1, replica_groups={{10,9,0,11,12,1,6,13,4,7,14,5,2,15,8,3},{26,25,16,27,28,17,22,29,20,23,..., dimensions={0} | all-to-all | bytes 786432 | tf_op jit(solution)/shard_map/all_to_all | solution.py:280
  20.7 1.2 %work.1 = bf16[16,40,128]{2,1,0:T(8,128)(2,1)S(1)} custom-call(bf16[16,96,128]{2,1,0:T(8,128)(2,1)S(1)} %all_to_all.10.moved_ref, bf16[256,256]{1,0:T(8,128)(2,1)S(1)} %get-tuple-element.11.enter_ref, bf16[256,256]{1,0:T(8,128)(2,1)S(1)} %get-tuple-element.12.outer_ref, bf16[256,256]{1,0:T(8,128)(2,1)S(1)} %get-tuple-element.13.inner_ref, ...), custom_call_target="tpu_custom_call" | custom-call | tf_op jit(solution)/shard_map/work/pallas_call | solution.py:313
  22.0 9.2 %all_to_all.11.home_ref = bf16[16,40,128]{2,1,0:T(8,128)(2,1)S(1)} all-to-all(bf16[16,40,128]{2,1,0:T(8,128)(2,1)S(1)} %work.1), channel_id=1, replica_groups={{10,15,14,13,12,9,8,5,4,1,0,3,2,7,6,11},{26,31,30,29,28,25,24,21,20,17,..., dimensions={0} | all-to-all | bytes 327680 | tf_op jit(solution)/shard_map/all_to_all | solution.py:280
  31.1 0.8 %finish.1 = (bf16[1,16,4096]{2,1,0:T(8,128)(2,1)}, f32[1,384]{1,0:T(1,128)}) custom-call(bf16[16,40,128]{2,1,0:T(8,128)(2,1)S(1)} %all_to_all.11.home_ref, bf16[16,16]{1,0:T(8,128)(2,1)S(1)} %get-tuple-element.16.holds_ref, f32[32,384]{1,0:T(8,128)S(1)} %get-tuple-element.17.chosen_ref), custom_call_target="tpu_custom_call" | custom-call | tf_op jit(solution)/shard_map/finish/pallas_call | solution.py:323
